TPU v7x, 32 devices: a whole 2x2x4 slice. The times are simulated.
32 devices in a mesh: wide: 4 (over z), row: 2 (over core), col: 4 (over y, x).
Axes of the slice: x: 2, y: 2, z: 4, core: 2. Of those that a mesh axis runs over, the one named last changes fastest.
Arguments:
- amplitudes: float32 [24, 256, 256], P('wide'), may hold values from -6 to 6
- factors: float32 [8, 512, 512], P(('row', 'col'), 'wide'), may hold values from -0.24 to 0.24
- domains: int32 [24, 4], P('wide'), may hold values from 0 to 7, as said below
- domain_mask: int32 [24, 4], P('wide'), may hold values 0 or 1
- block_mask: int32 [8, 8], replicated, may hold values 0 or 1
Outputs:
- ladder: float32 [24, 256, 256], P('wide', ('row', 'col'))
Inputs may be any that keep to these rules, and one draw needn't show every extreme that they name: `domains`: each row names 4 different virtual blocks.
All inputs are finite; a program needn't handle non-finite values. No bound on the sum of `domain_mask` on one device may be relied on, other than what follows from the above.
Results may differ from a plain program's by a relative error of at most 0.0003.
Values sent between devices are 32-bit elements; how exact they have to be, the bound alone decides.
No kernel may reach another device: no remote copies, remote signals or barrier semaphores. Data moves between devices by JAX's collectives and lax.ppermute only.
A program may use at most 64 MiB of HBM per device.

v0:
```python
import jax
import jax.numpy as jnp
from jax import lax
from jax.sharding import PartitionSpec as P

BS = 64


def contract_rows(tile, blocks, flags, screened):
    block_size = screened.shape[1] // block_count_of(screened)
    offsets = jnp.arange(block_size, dtype=jnp.int32)
    indices = (blocks[:, None] * block_size + offsets[None, :]).reshape(-1)
    weights = jnp.repeat(flags, block_size).astype(jnp.float32)
    subset = screened[:, indices][:, :, indices]
    masked = tile * weights[:, None] * weights[None, :]
    halfway = jnp.einsum("qxu,uw->qxw", subset, masked, precision=lax.Precision.HIGHEST)
    result = jnp.einsum("qxw,qyw->xy", halfway, subset, precision=lax.Precision.HIGHEST)
    return result * weights[:, None] * weights[None, :]


def block_count_of(screened):
    return screened.shape[1] // BS


def screen(factors, block_mask):
    expanded = jnp.repeat(jnp.repeat(block_mask, BS, 0), BS, 1).astype(jnp.float32)
    return factors * expanded[None, :, :]


def all_pairs(amplitudes, domains, domain_mask, screened):

    def one_pair(items):
        return contract_rows(items[0], items[1], items[2], screened)

    return lax.map(one_pair, (amplitudes, domains, domain_mask))


def body(amplitudes, factors, domains, domain_mask, block_mask):
    gathered = lax.all_gather(factors, "wide", axis=1, tiled=True)
    screened = screen(gathered, block_mask)
    partial_terms = all_pairs(amplitudes, domains, domain_mask, screened)
    return lax.psum_scatter(partial_terms, ("row", "col"), scatter_dimension=1, tiled=True)


def solution(mesh):
    return jax.shard_map(
        body,
        mesh=mesh,
        in_specs=(
            P("wide", None, None),
            P(("row", "col"), "wide", None),
            P("wide", None),
            P("wide", None),
            P(),
        ),
        out_specs=P("wide", ("row", "col"), None),
        check_vma=False,
    )
```

profile of v0, /device:TPU:0, one launch (start us, length us, event | category | flops | bytes accessed | tf_op | source)
XLA Modules:
  0.0 118.5 jit_solution(2600795252616677145)
XLA Ops:
  6.5 1.8 %copy.10 = f32[1,128,512]{1,2,0:T(8,128)} copy(f32[1,128,512]{2,1,0:T(8,128)} %param.8) | data formatting | bytes 524288 | tf_op args[1]
  8.4 0.7 convert_element_type.36
  9.1 0.1 copy.11
  9.2 0.1 broadcast_in_dim.12
  9.2 0.1 convert_element_type.37
  9.3 0.8 copy.12
  10.1 0.8 copy.14
  10.9 31.0 %all-gather.2.cloned.1.call-done = f32[1,512,512]{1,2,0:T(8,128)} async-done(((f32[1,128,512]{1,2,0:T(8,128)}), f32[1,512,512]{1,2,0:T(8,128)}) %all-gather.2.cloned.1.call-update) | async-done | bytes 1048592 | tf_op jit(solution)/shard_map/all_gather | solution.py:39
  41.8 1.3 %bitcast_multiply_fusion = f32[1,512,512]{1,2,0:T(8,128)S(1)} fusion(f32[1,512,512]{1,2,0:T(8,128)} %all-gather.2.cloned.1.call-done, f32[512,8]{0,1:T(8,128)S(1)} %convert_element_type.37), kind=kLoop, calls=%fused_computation.23 | loop fusion | flops 262144 | bytes 2113536 | tf_op jit(solution)/shard_map/mul | solution.py:27
  43.2 0.3 copy.13
  43.5 31.1 %while.10 = (s32[]{:T(128)}, f32[6,256,256]{2,1,0:T(8,128)}, s32[6,4]{1,0:T(8,128)S(1)}, f32[1,512,512]{2,1,0:T(8,128)S(1)}, f32[6,256,256]{2,1,0:T(8,128)}, /*index=5*/s32[6,4]{1,0:T(8,128)S(1)}, s32[]{:T(128)}) while((s32[]{:T(128)}, f32[6,256,256]{2,1,0:T(8,128)}, s32[6,4]{1,0:T(8,128)S(1)}, f32[1,512,512]{2,1,0:T(8,128)S(1)}, ...), condition=%wide.region_1.2_spmd, body=%wide.region_0.1_spmd.sunk | while | flops 402917376 | bytes 4214961 | solution.py:35
  43.5 0.1 iota_add_fusion.2
  43.6 0.1 add.55
  43.7 1.0 gather_fusion
  44.7 0.2 copy.16
  44.9 1.0 gather_fusion.1
  45.9 0.1 broadcast_in_dim.30
  45.9 0.1 convert_element_type.43
  46.0 1.6 %fusion.30 = f32[256,256]{1,0:T(8,128)S(1)} fusion(f32[256,256]{1,0:T(8,128)S(1)} %gather_fusion.1, f32[6,256,256]{2,1,0:T(8,128)} %get-tuple-element.123, s32[]{:T(128)} %get-tuple-element.112, f32[256]{0:T(256)S(1)} %convert_element_type.43), kind=kOutput, calls=%fused_computation.6.clone.1 | convolution fusion | flops 201457664 | bytes 788992 | tf_op jit(solution)/shard_map/while/body/eval_jaxpr/qxu,uw->qxw/dot_general | solution.py:16
  47.6 1.1 fusion.31
  48.7 0.1 iota_add_fusion.2
  48.8 0.1 add.55
  48.9 1.0 gather_fusion
  49.9 0.2 copy.16
  50.1 1.0 gather_fusion.1
  51.1 0.1 broadcast_in_dim.30
  51.1 0.1 convert_element_type.43
  51.2 1.6 %fusion.30 = f32[256,256]{1,0:T(8,128)S(1)} fusion(f32[256,256]{1,0:T(8,128)S(1)} %gather_fusion.1, f32[6,256,256]{2,1,0:T(8,128)} %get-tuple-element.123, s32[]{:T(128)} %get-tuple-element.112, f32[256]{0:T(256)S(1)} %convert_element_type.43), kind=kOutput, calls=%fused_computation.6.clone.1 | convolution fusion | flops 201457664 | bytes 788992 | tf_op jit(solution)/shard_map/while/body/eval_jaxpr/qxu,uw->qxw/dot_general | solution.py:16
  52.8 1.1 fusion.31
  53.9 0.1 iota_add_fusion.2
  54.0 0.1 add.55
  54.1 1.0 gather_fusion
  55.1 0.2 copy.16
  55.3 1.0 gather_fusion.1
  56.2 0.1 broadcast_in_dim.30
  56.3 0.1 convert_element_type.43
  56.4 1.6 %fusion.30 = f32[256,256]{1,0:T(8,128)S(1)} fusion(f32[256,256]{1,0:T(8,128)S(1)} %gather_fusion.1, f32[6,256,256]{2,1,0:T(8,128)} %get-tuple-element.123, s32[]{:T(128)} %get-tuple-element.112, f32[256]{0:T(256)S(1)} %convert_element_type.43), kind=kOutput, calls=%fused_computation.6.clone.1 | convolution fusion | flops 201457664 | bytes 788992 | tf_op jit(solution)/shard_map/while/body/eval_jaxpr/qxu,uw->qxw/dot_general | solution.py:16
  58.0 1.1 fusion.31
  59.1 0.1 iota_add_fusion.2
  59.2 0.1 add.55
  59.3 1.0 gather_fusion
  60.2 0.2 copy.16
  60.4 1.0 gather_fusion.1
  61.4 0.1 broadcast_in_dim.30
  61.5 0.1 convert_element_type.43
  61.6 1.6 %fusion.30 = f32[256,256]{1,0:T(8,128)S(1)} fusion(f32[256,256]{1,0:T(8,128)S(1)} %gather_fusion.1, f32[6,256,256]{2,1,0:T(8,128)} %get-tuple-element.123, s32[]{:T(128)} %get-tuple-element.112, f32[256]{0:T(256)S(1)} %convert_element_type.43), kind=kOutput, calls=%fused_computation.6.clone.1 | convolution fusion | flops 201457664 | bytes 788992 | tf_op jit(solution)/shard_map/while/body/eval_jaxpr/qxu,uw->qxw/dot_general | solution.py:16
  63.2 1.1 fusion.31
  64.3 0.1 iota_add_fusion.2
  64.4 0.1 add.55
  64.5 1.0 gather_fusion
  65.4 0.2 copy.16
  65.6 1.0 gather_fusion.1
  66.7 0.1 convert_element_type.43
  66.8 1.6 %fusion.30 = f32[256,256]{1,0:T(8,128)S(1)} fusion(f32[256,256]{1,0:T(8,128)S(1)} %gather_fusion.1, f32[6,256,256]{2,1,0:T(8,128)} %get-tuple-element.123, s32[]{:T(128)} %get-tuple-element.112, f32[256]{0:T(256)S(1)} %convert_element_type.43), kind=kOutput, calls=%fused_computation.6.clone.1 | convolution fusion | flops 201457664 | bytes 788992 | tf_op jit(solution)/shard_map/while/body/eval_jaxpr/qxu,uw->qxw/dot_general | solution.py:16
  68.4 1.1 fusion.31
  69.5 0.1 iota_add_fusion.2
  69.5 0.1 add.55
  69.6 1.0 gather_fusion
  70.6 0.2 copy.16
  70.8 1.0 gather_fusion.1
  71.9 0.1 convert_element_type.43
  71.9 1.6 %fusion.30 = f32[256,256]{1,0:T(8,128)S(1)} fusion(f32[256,256]{1,0:T(8,128)S(1)} %gather_fusion.1, f32[6,256,256]{2,1,0:T(8,128)} %get-tuple-element.123, s32[]{:T(128)} %get-tuple-element.112, f32[256]{0:T(256)S(1)} %convert_element_type.43), kind=kOutput, calls=%fused_computation.6.clone.1 | convolution fusion | flops 201457664 | bytes 788992 | tf_op jit(solution)/shard_map/while/body/eval_jaxpr/qxu,uw->qxw/dot_general | solution.py:16
  73.6 1.1 fusion.31
  74.7 37.0 %reduce-scatter.2.cloned.1.call-done = f32[6,32,256]{2,1,0:T(8,128)} async-done(((f32[6,256,256]{2,1,0:T(8,128)}), f32[6,32,256]{2,1,0:T(8,128)}) %reduce-scatter.2.cloned.1.call-update) | async-done | bytes 196624 | tf_op jit(solution)/shard_map/reduce_scatter | solution.py:42
  (25 shorter events, 0.3 us)
Async XLA Ops:
  6.5 35.3 %all-gather.2.cloned.1.call-start = ((), (), s32[]{:S(2)}) async-start(), calls=%async_computation.1 | async-start | bytes 1310720 | tf_op jit(solution)/shard_map/all_gather | solution.py:39
  8.3 103.3 %reduce-scatter.2.cloned.1.call-start = ((), (), s32[]{:S(2)}) async-start(), calls=%async_computation.2 | async-start | bytes 1769472 | tf_op jit(solution)/shard_map/reduce_scatter | solution.py:42
Sparse Core Ops, SparseCore 0:
  8.9 32.8 all-gather.1
  74.8 36.7 reduce-scatter.1
where the time goes:
time: 119 us; the launch traced here: 118 us
  waiting for transfers between devices  68 us (57%)
  local copies, waits for them, and re-layouts  18.1 us (15%)
  matrix products  16.2 us (14%)
  between operations  13.4 us (11%)
  other arithmetic  2.59 us (2%)
    reduce_scatter x1, waiting for transfers between devices, body(): lax.psum_scatter(partial_terms, ('row', 'col'), scatter_dimension=1, tile...  37 us
    all_gather x1, waiting for transfers between devices, body(): gathered = lax.all_gather(factors, 'wide', axis=1, tiled=True)  31 us
    gather x18, local copies, waits for them, and re-layouts, contract_rows(): subset = screened[:, indices][:, :, indices]  12.8 us
    dot_general x6, matrix products, contract_rows(): jnp.einsum('qxu,uw->qxw', subset, masked, precision=lax.Precision.HIGHEST)  9.64 us
    dot_general x6, matrix products, contract_rows(): jnp.einsum('qxw,qyw->xy', halfway, subset, precision=lax.Precision.HIGHEST)  6.52 us
  transfers between devices with their start and end apart: 2, of which 2 were waited for; matrix products, arithmetic and copies ran while one was open for 2% of the time, Pallas kernels for 0%

commit v1 on v0

v1 whole, which is shorter than its diff:
```python
import functools

import jax
import jax.numpy as jnp
from jax import lax
from jax.experimental import pallas as pl
from jax.experimental.pallas import tpu as pltpu
from jax.sharding import PartitionSpec as P

BS = 64
LANES = 128
LINE = 4
VMEM_LIMIT = 40 * 1024 * 1024
SMEM_SPEC = pl.BlockSpec(memory_space=pltpu.SMEM)
VMEM_SPEC = pl.BlockSpec(memory_space=pltpu.VMEM)


def split(value):
    top = value.astype(jnp.bfloat16)
    return top, (value - top.astype(jnp.float32)).astype(jnp.bfloat16)


def pair_row(left_half, first, second):
    return jnp.where(left_half, first.astype(jnp.float32), second.astype(jnp.float32))


def left_of(rows):
    return lax.broadcasted_iota(jnp.int32, (rows, LANES), 1) < BS


def mask_amplitudes_kernel(flags, amplitudes, high, low):
    pairs, domv, _ = amplitudes.shape
    left_half = left_of(1)
    for p in range(pairs):
        for j in range(domv // LANES):
            row = pair_row(left_half, flags[2 * j, p], flags[2 * j + 1, p])
            lanes = slice(j * LANES, (j + 1) * LANES)
            for i in range(domv // BS):
                rows = slice(i * BS, (i + 1) * BS)
                top, rest = split(amplitudes[p, rows, lanes] * (row * flags[i, p].astype(jnp.float32)))
                high[p, rows, lanes] = top
                low[p, rows, lanes] = rest


def mask_amplitudes(flags, amplitudes):
    shape = jax.ShapeDtypeStruct(amplitudes.shape, jnp.bfloat16)
    return pl.pallas_call(
        mask_amplitudes_kernel,
        name="mask_amplitudes",
        out_shape=[shape] * 2,
        in_specs=[SMEM_SPEC, VMEM_SPEC],
        out_specs=[VMEM_SPEC] * 2,
        compiler_params=pltpu.CompilerParams(vmem_limit_bytes=VMEM_LIMIT),
        cost_estimate=pl.CostEstimate(flops=4 * amplitudes.size, bytes_accessed=8 * amplitudes.size, transcendentals=0),
    )(flags, amplitudes)


def screen_piece(place, block_mask, piece, q, slot, high, low):
    nq, rows, window = piece.shape
    tiles = window // LANES
    per_slot = rows // BS
    left_half = left_of(1)
    for h in range(per_slot):
        block = (place[0] ^ slot) * per_slot + h
        for t in range(tiles):
            row = pair_row(left_half, block_mask[block, 2 * t], block_mask[block, 2 * t + 1])
            for n in range(nq):
                tile = piece[n, h * BS:(h + 1) * BS, t * LANES:(t + 1) * LANES] * row
                target = pl.ds(pl.multiple_of(slot * rows + h * BS, BS), BS)
                for turn, value in ((0, tile), (1, pltpu.roll(tile, BS, 1))):
                    top, rest = split(value)
                    high[turn * tiles + t, q * nq + n, target, :] = top
                    low[turn * tiles + t, q * nq + n, target, :] = rest


def screen_kernel(keys, place, block_mask, *refs):
    high, low = refs[-2:]
    for (slots, q), pieces in zip(keys, refs):
        for i, slot in enumerate(slots):
            if slot is not None:
                screen_piece(place, block_mask, pieces.at[i], q, slot, high, low)


def screen(place, block_mask, keyed, shape, held=()):
    keys = [(slots, q) for slots, q, _ in keyed]
    pieces = [piece for _, _, piece in keyed]
    size = sum(piece.size for piece in pieces)
    return pl.pallas_call(
        functools.partial(screen_kernel, keys),
        name="screen_factors",
        out_shape=[shape] * 2,
        in_specs=[SMEM_SPEC] * 2 + [VMEM_SPEC] * (len(pieces) + len(held)),
        out_specs=[VMEM_SPEC] * 2,
        input_output_aliases={2 + len(pieces) + i: i for i in range(len(held))},
        compiler_params=pltpu.CompilerParams(vmem_limit_bytes=VMEM_LIMIT),
        cost_estimate=pl.CostEstimate(flops=8 * size, bytes_accessed=12 * size, transcendentals=0),
    )(place, block_mask, *pieces, *held)


def collect_kernel(place, near, mid, crossed, second, far, stack):
    middle = (place[0] > 0) & (place[0] < LINE - 1)
    stack[0] = near[...]

    @pl.when(middle)
    def _():
        stack[1] = crossed[...]
        stack[2] = mid[...]

    @pl.when(jnp.logical_not(middle))
    def _():
        stack[1] = second[...]
        stack[2] = far[...]


def collect(place, near, *received):
    return pl.pallas_call(
        collect_kernel,
        name="collect_pieces",
        out_shape=jax.ShapeDtypeStruct((LINE - 1,) + near.shape, near.dtype),
        in_specs=[SMEM_SPEC] + [VMEM_SPEC] * 5,
        out_specs=VMEM_SPEC,
        compiler_params=pltpu.CompilerParams(vmem_limit_bytes=VMEM_LIMIT),
        cost_estimate=pl.CostEstimate(flops=0, bytes_accessed=2 * (LINE - 1) * near.size * 4, transcendentals=0),
    )(place, near, *received)


def pairs_kernel(row, line, late, place, block_mask, domains, flags, *refs):
    pieces = refs[:len(late)]
    mhigh, mlow, _, _ = refs[len(late):len(late) + 4]
    out, high, low, yhigh, ylow = refs[len(late) + 4:]
    z, r = place[0], place[1]
    for q, piece in zip(late, pieces):

        @pl.loop(1, line)
        def _(slot):
            screen_piece(place, block_mask, piece.at[slot - 1], q, slot, high, low)

    col, pairs, chunk, domv = out.shape
    twice, qs, window, _ = high.shape
    tiles = twice // 2
    rows = window // line
    per_slot = rows // BS
    half = domv // row
    left_half = left_of(BS)
    picks = [r * half + k * chunk for k in range(col)]
    across = (((1,), (1,)), ((), ()))
    dot = functools.partial(lax.dot_general, preferred_element_type=jnp.float32)
    along = (((1,), (0,)), ((), ()))
    for p in range(pairs):
        slot = p % 2
        spans = []
        for i in range(domv // BS):
            block = domains[i, p]
            start = ((block // per_slot) ^ z) * rows + (block % per_slot) * BS
            spans.append(pl.ds(pl.multiple_of(start, BS), BS))
        sources = []
        for j in range(domv // LANES):
            first, second = domains[2 * j, p], domains[2 * j + 1, p]
            from_first = (first % 2) * tiles + first // 2
            from_second = (1 - second % 2) * tiles + second // 2
            sources.append((from_first, from_second))
            for i, span in enumerate(spans):
                for q in range(qs):
                    lanes = slice(q * domv + j * LANES, q * domv + (j + 1) * LANES)
                    for source, target in ((high, yhigh), (low, ylow)):
                        target[slot, i * BS:(i + 1) * BS, lanes] = jnp.where(
                            left_half, source[from_first, q, span, :], source[from_second, q, span, :])
        xs = []
        for source in (high, low):
            rows_of = []
            for q in range(qs):
                for pick in picks:
                    block = domains[pick // BS, p]
                    start = ((block // per_slot) ^ z) * rows + (block % per_slot) * BS + pick % BS
                    span = pl.ds(pl.multiple_of(start, chunk), chunk)
                    rows_of.append(jnp.concatenate([jnp.where(
                        left_of(chunk), source[a, q, span, :], source[b, q, span, :]) for a, b in sources], 1))
            xs.append(jnp.concatenate(rows_of, 0))
        xhigh, xlow = xs
        halfway = dot(xhigh, mhigh[p], along) + dot(xhigh, mlow[p], along) + dot(xlow, mhigh[p], along)
        hhigh, hlow = split(jnp.concatenate([halfway[q * half:(q + 1) * half] for q in range(qs)], 1))
        total = (dot(hhigh, yhigh[slot], across) + dot(hhigh, ylow[slot], across) + dot(hlow, yhigh[slot], across))
        for j in range(domv // LANES):
            weights = pair_row(left_of(1), flags[2 * j, p], flags[2 * j + 1, p])
            for k, pick in enumerate(picks):
                weight = flags[pick // BS, p].astype(jnp.float32)
                out[k, p, :, j * LANES:(j + 1) * LANES] = total[
                    k * chunk:(k + 1) * chunk, j * LANES:(j + 1) * LANES] * (weights * weight)


def contract_pairs(row, col, line, place, block_mask, domains, flags, late, mhigh, mlow, high, low):
    pairs, domv, _ = mhigh.shape
    chunk = domv // (row * col)
    qs = high.shape[1]
    order = range(1, len(late) + 1)
    first = 4 + len(late) + 2
    shape = jax.ShapeDtypeStruct((col, pairs, chunk, domv), jnp.float32)
    terms, _, _ = pl.pallas_call(
        functools.partial(pairs_kernel, row, line, order),
        name="contract_pairs",
        out_shape=[shape] + [jax.ShapeDtypeStruct(high.shape, high.dtype)] * 2,
        in_specs=[SMEM_SPEC] * 4 + [VMEM_SPEC] * (len(late) + 4),
        out_specs=[VMEM_SPEC] * 3,
        scratch_shapes=[pltpu.VMEM((2, domv, qs * domv), jnp.bfloat16)] * 2,
        input_output_aliases={first: 1, first + 1: 2},
        compiler_params=pltpu.CompilerParams(vmem_limit_bytes=VMEM_LIMIT),
        cost_estimate=pl.CostEstimate(flops=6 * pairs * qs * domv ** 3 * 4 // row, bytes_accessed=8 * high.size,
                                      transcendentals=0),
    )(place, block_mask, domains, flags, *late, mhigh, mlow, high, low)
    return terms


def body(wide, row, col, amplitudes, factors, domains, domain_mask, block_mask):
    nq, rows, window = factors.shape
    z, r, c = lax.axis_index("wide"), lax.axis_index("row"), lax.axis_index("col")
    shape = jax.ShapeDtypeStruct((2 * window // LANES, row * nq, window, LANES), jnp.bfloat16)
    domains, flags = domains.T, domain_mask.T
    mhigh, mlow = mask_amplitudes(flags, amplitudes)

    def siblings(piece):
        return [lax.ppermute(piece, "row", [(i, (i + s) % row) for i in range(row)]) for s in range(1, row)]

    if wide == LINE and rows % BS == 0:
        line = wide
        place = jnp.stack([z, r, c]).astype(jnp.int32)
        near = lax.ppermute(factors, "wide", [(0, 1), (1, 0), (2, 3), (3, 2)])
        mid = lax.ppermute(factors, "wide", [(1, 2), (2, 1)])
        crossed = lax.ppermute(near, "wide", [(1, 2), (2, 1)])
        second = lax.ppermute(mid, "wide", [(1, 0), (2, 3)])
        far = lax.ppermute(near, "wide", [(1, 3), (2, 0)])
        early = [((0,), q, piece[None]) for q, piece in enumerate([factors] + siblings(factors))]
        early += [((1,), 0, near[None]), ((3,), 0, mid[None])]
        high, low = screen(place, block_mask, early, shape)
        second, crossed, far, high, low, mhigh, mlow, domains = lax.optimization_barrier(
            (second, crossed, far, high, low, mhigh, mlow, domains))
        stack = collect(place, near, mid, crossed, second, far)
        late = siblings(stack)
        high, low = screen(place, block_mask, [((None, 2, 3), 0, stack)], shape, (high, low))
    else:
        line = 1
        place = jnp.stack([jnp.zeros_like(z), r, c]).astype(jnp.int32)
        whole = lax.all_gather(factors, "wide", axis=1, tiled=True)
        high, low = screen(place, block_mask, [((0,), q, piece[None]) for q, piece in enumerate([whole] + siblings(whole))], shape)
        late = []

    terms = contract_pairs(row, col, line, place, block_mask, domains, flags, late, mhigh, mlow, high, low)
    return jnp.sum(lax.all_to_all(terms, "col", 0, 0, tiled=True), axis=0)


def solution(mesh):
    wide, row, col = (mesh.shape[name] for name in ("wide", "row", "col"))
    return jax.shard_map(
        functools.partial(body, wide, row, col),
        mesh=mesh,
        in_specs=(
            P("wide", None, None),
            P(("row", "col"), "wide", None),
            P("wide", None),
            P("wide", None),
            P(),
        ),
        out_specs=P("wide", ("row", "col"), None),
        check_vma=False,
    )
```

time: 119 us -> 48.8 us (0.41)
  waiting for transfers between devices: 68 us -> 14.2 us
  matrix products: 16.2 us -> 0 us
  blocking collectives: 0 us -> 15 us
  local copies, waits for them, and re-layouts: 18.1 us -> 3.73 us
  between operations: 13.4 us -> 0.12 us
  Pallas kernels: 0 us -> 7.56 us
  starting transfers between devices: 0.04 us -> 7.08 us
  other arithmetic: 2.59 us -> 0.81 us
    reduce_scatter x1 -> x0, waiting for transfers between devices: 37 us -> none  [body(): lax.psum_scatter(partial_terms, ('row', 'col'), scatter_dimension=1, tile...]
    all_gather x1 -> x0, waiting for transfers between devices: 31 us -> none  [body(): gathered = lax.all_gather(factors, 'wide', axis=1, tiled=True)]
    dot_general x12 -> x0, matrix products: 16.2 us -> none  [the longest x6 9.64 us: contract_rows(): jnp.einsum('qxu,uw->qxw', subset, masked, precision=lax.Precision.HIGHEST)]
    all_to_all x0 -> x1, blocking collectives: none -> 15 us  [body(): return jnp.sum(lax.all_to_all(terms, 'col', 0, 0, tiled=True), axis=0)]
    ppermute x0 -> x7, waiting for transfers between devices: none -> 14.2 us  [the longest x1 5.76 us: body(): near = lax.ppermute(factors, 'wide', [(0, 1), (1, 0), (2, 3), (3, 2)])]
    gather x18 -> x0, local copies, waits for them, and re-layouts: 12.8 us -> none  [contract_rows(): subset = screened[:, indices][:, :, indices]]
    pallas_call x0 -> x5, Pallas kernels: none -> 7.56 us  [the longest x1 4.3 us: contract_pairs(): pl.pallas_call(functools.partial(pairs_kernel, row, line, order), name='c...]
    ppermute x0 -> x7, starting transfers between devices: none -> 7.08 us  [the longest x1 3.02 us: body(): near = lax.ppermute(factors, 'wide', [(0, 1), (1, 0), (2, 3), (3, 2)])]
  transfers between devices with their start and end apart: 2 -> 7, of which waited for: 2 -> 4; matrix products, arithmetic and copies ran while one was open for 2% -> 0% of each run, Pallas kernels for 0% -> 6%
where the time goes in v1:
time: 48.8 us; the launch traced here: 48.5 us
  blocking collectives  15 us (31%)
  waiting for transfers between devices  14.2 us (29%)
  Pallas kernels  7.56 us (15%)
  starting transfers between devices  7.08 us (15%)
  local copies, waits for them, and re-layouts  3.73 us (8%)
  other arithmetic  0.81 us (2%)
    all_to_all x1, blocking collectives, body(): return jnp.sum(lax.all_to_all(terms, 'col', 0, 0, tiled=True), axis=0)  15 us
    ppermute x1, waiting for transfers between devices, body(): near = lax.ppermute(factors, 'wide', [(0, 1), (1, 0), (2, 3), (3, 2)])  5.76 us
    pallas_call x1, Pallas kernels, contract_pairs(): pl.pallas_call(functools.partial(pairs_kernel, row, line, order), name='c...  4.3 us
    ppermute x1, waiting for transfers between devices, body(): second = lax.ppermute(mid, 'wide', [(1, 0), (2, 3)])  4.3 us
    unnamed x12, local copies, waits for them, and re-layouts  3.73 us
    ppermute x1, starting transfers between devices, body(): near = lax.ppermute(factors, 'wide', [(0, 1), (1, 0), (2, 3), (3, 2)])  3.02 us
    ppermute x1, waiting for transfers between devices, body(): far = lax.ppermute(near, 'wide', [(1, 3), (2, 0)])  2.66 us
    pallas_call x2, Pallas kernels, screen(): pl.pallas_call(functools.partial(screen_kernel, keys), name='screen_facto...  1.78 us
  transfers between devices with their start and end apart: 7, of which 4 were waited for; matrix products, arithmetic and copies ran while one was open for 0% of the time, Pallas kernels for 6%

profile of v1, /device:TPU:0, one launch (start us, length us, event | category | flops | bytes accessed | tf_op | source)
XLA Modules:
  0.0 48.5 jit_solution(17599305286800241482)
XLA Ops:
  0.0 3.0 %collective-permute-start.2 = (f32[1,128,512]{2,1,0:T(8,128)}, f32[1,128,512]{2,1,0:T(8,128)S(1)}, u32[]{:S(2)}, u32[]{:S(2)}) collective-permute-start(f32[1,128,512]{2,1,0:T(8,128)} %param.6), channel_id=1, source_target_pairs={{0,8},{8,0},{16,24},{24,16},{1,9},{9,1},{17,25},{25,17},{2,10},{10... | collective-permute-start | bytes 786440 | tf_op jit(solution)/shard_map/ppermute | solution.py:226
  3.0 0.7 %collective-permute-start = (f32[1,128,512]{2,1,0:T(8,128)}, f32[1,128,512]{2,1,0:T(8,128)S(1)}, u32[]{:S(2)}, u32[]{:S(2)}) collective-permute-start(f32[1,128,512]{2,1,0:T(8,128)} %param.6), channel_id=1, source_target_pairs={{8,16},{16,8},{9,17},{17,9},{10,18},{18,10},{11,19},{19,11},{12,20... | collective-permute-start | bytes 786440 | tf_op jit(solution)/shard_map/ppermute | solution.py:227
  3.7 0.1 collective-permute-start.5
  3.8 5.8 %collective-permute-done.2.near = f32[1,128,512]{2,1,0:T(8,128)S(1)} collective-permute-done((f32[1,128,512]{2,1,0:T(8,128)}, f32[1,128,512]{2,1,0:T(8,128)S(1)}, u32[]{:S(2)}, u32[]{:S(2)}) %collective-permute-start.2) | collective-permute-done | bytes 262176 | tf_op jit(solution)/shard_map/ppermute | solution.py:226
  9.5 1.3 %collective-permute-start.4 = (f32[1,128,512]{2,1,0:T(8,128)S(1)}, f32[1,128,512]{2,1,0:T(8,128)S(1)}, u32[]{:S(2)}, u32[]{:S(2)}) collective-permute-start(f32[1,128,512]{2,1,0:T(8,128)S(1)} %collective-permute-done.2.near), channel_id=1, source_target_pairs={{8,24},{16,0},{9,25},{17,1},{10,26},{18,2},{11,27},{19,3},{12,28},... | collective-permute-start | bytes 786440 | tf_op jit(solution)/shard_map/ppermute | solution.py:230
  10.8 0.7 %collective-permute-start.3 = (f32[1,128,512]{2,1,0:T(8,128)S(1)}, f32[1,128,512]{2,1,0:T(8,128)S(1)}, u32[]{:S(2)}, u32[]{:S(2)}) collective-permute-start(f32[1,128,512]{2,1,0:T(8,128)S(1)} %collective-permute-done.2.near), channel_id=1, source_target_pairs={{8,16},{16,8},{9,17},{17,9},{10,18},{18,10},{11,19},{19,11},{12,20... | collective-permute-start | bytes 786440 | tf_op jit(solution)/shard_map/ppermute | solution.py:228
  11.5 0.0 collective-permute-done.mid
  11.5 1.3 %collective-permute-start.1 = (f32[1,128,512]{2,1,0:T(8,128)S(1)}, f32[1,128,512]{2,1,0:T(8,128)S(1)}, u32[]{:S(2)}, u32[]{:S(2)}) collective-permute-start(f32[1,128,512]{2,1,0:T(8,128)S(1)} %collective-permute-done.mid), channel_id=1, source_target_pairs={{8,0},{16,24},{9,1},{17,25},{10,2},{18,26},{11,3},{19,27},{12,4},{... | collective-permute-start | bytes 786440 | tf_op jit(solution)/shard_map/ppermute | solution.py:229
  12.8 0.0 copy-start
  12.8 1.4 %copy-done = f32[6,256,256]{2,1,0:T(8,128)S(1)} copy-done((f32[6,256,256]{2,1,0:T(8,128)S(1)}, f32[6,256,256]{2,1,0:T(8,128)}, u32[]{:S(2)}) %copy-start) | copy-done | bytes 1572888
  14.2 0.0 copy-start.4
  14.2 0.7 %copy-done.4 = s32[6,4]{0,1:T(4,128)S(1)} copy-done((s32[6,4]{0,1:T(4,128)S(1)}, s32[6,4]{0,1:T(4,128)}, u32[]{:S(2)}) %copy-start.4) | copy-done | bytes 120
  14.9 0.9 %mask_amplitudes.1 = (bf16[6,256,256]{2,1,0:T(8,128)(2,1)S(1)}, bf16[6,256,256]{2,1,0:T(8,128)(2,1)S(1)}) custom-call(s32[4,6]{1,0:T(4,128)S(1)} %bitcast.13, f32[6,256,256]{2,1,0:T(8,128)S(1)} %copy-done), custom_call_target="tpu_custom_call" | custom-call | flops 1572864 | bytes 3145728 | tf_op jit(solution)/shard_map/mask_amplitudes/pallas_call | solution.py:47
  15.8 0.1 pad_add_fusion.place
  15.9 0.0 collective-permute-done.5
  15.9 0.0 copy-start.1
  15.9 1.0 %copy-done.1 = f32[1,128,512]{2,1,0:T(8,128)S(1)} copy-done((f32[1,128,512]{2,1,0:T(8,128)S(1)}, f32[1,128,512]{2,1,0:T(8,128)}, u32[]{:S(2)}) %copy-start.1) | copy-done | bytes 262168
  16.9 0.0 copy-start.2
  16.9 0.7 %copy-done.2 = s32[8,8]{1,0:T(8,128)S(1)} copy-done((s32[8,8]{1,0:T(8,128)S(1)}, s32[8,8]{1,0:T(8,128)}, u32[]{:S(2)}) %copy-start.2) | copy-done | bytes 280
  17.5 1.0 %screen_factors.2 = (bf16[8,2,512,128]{3,2,1,0:T(8,128)(2,1)S(1)}, bf16[8,2,512,128]{3,2,1,0:T(8,128)(2,1)S(1)}) custom-call(s32[3]{0:T(128)S(1)} %pad_add_fusion.place, s32[8,8]{1,0:T(8,128)S(1)} %copy-done.2, f32[1,1,128,512]{3,2,1,0:T(8,128)S(1)} %bitcast.11, f32[1,1,128,512]{3,2,1,0:T(8,128)S(1)} %bitcast.12, f32[1,1,128,512]{3,2,1,0:T(8,128)S(1)} %bitcast.9, ...), custom_call_target="tpu_custom_call" | custom-call | flops 2097152 | bytes 3145728 | tf_op jit(solution)/shard_map/screen_factors/pallas_call | solution.py:88
  18.5 2.7 %collective-permute-done.4.far = f32[1,128,512]{2,1,0:T(8,128)S(1)} collective-permute-done((f32[1,128,512]{2,1,0:T(8,128)S(1)}, f32[1,128,512]{2,1,0:T(8,128)S(1)}, u32[]{:S(2)}, u32[]{:S(2)}) %collective-permute-start.4) | collective-permute-done | bytes 262176 | tf_op jit(solution)/shard_map/ppermute | solution.py:230
  21.2 0.0 collective-permute-done.3.crossed
  21.2 4.3 %collective-permute-done.1.second = f32[1,128,512]{2,1,0:T(8,128)S(1)} collective-permute-done((f32[1,128,512]{2,1,0:T(8,128)S(1)}, f32[1,128,512]{2,1,0:T(8,128)S(1)}, u32[]{:S(2)}, u32[]{:S(2)}) %collective-permute-start.1) | collective-permute-done | bytes 262176 | tf_op jit(solution)/shard_map/ppermute | solution.py:229
  25.5 0.6 %collect_pieces.1.refs_0_ = f32[3,1,128,512]{3,2,1,0:T(8,128)S(1)} custom-call(s32[3]{0:T(128)S(1)} %pad_add_fusion.place, f32[1,128,512]{2,1,0:T(8,128)S(1)} %collective-permute-done.2.near, f32[1,128,512]{2,1,0:T(8,128)S(1)} %collective-permute-done.mid, f32[1,128,512]{2,1,0:T(8,128)S(1)} %collective-permute-done.3.crossed, ...), custom_call_target="tpu_custom_call" | custom-call | bytes 1572864 | tf_op jit(solution)/shard_map/collect_pieces/pallas_call | solution.py:116
  26.1 0.0 copy-start.3
  26.1 0.0 copy-start.5
  26.1 0.1 collective-permute-start.6
  26.2 0.8 %screen_factors.3 = (bf16[8,2,512,128]{3,2,1,0:T(8,128)(2,1)S(1)}, bf16[8,2,512,128]{3,2,1,0:T(8,128)(2,1)S(1)}) custom-call(s32[3]{0:T(128)S(1)} %pad_add_fusion.place, s32[8,8]{1,0:T(8,128)S(1)} %copy-done.2, f32[3,1,128,512]{3,2,1,0:T(8,128)S(1)} %collect_pieces.1.refs_0_, ...), custom_call_target="tpu_custom_call", output_to_operand_aliasing={{0}: (3, {}), {1}: (4, {})} | custom-call | flops 1572864 | bytes 2359296 | tf_op jit(solution)/shard_map/screen_factors/pallas_call | solution.py:88
  27.0 1.4 %collective-permute-done.6.refs_0_ = f32[3,1,128,512]{3,2,1,0:T(8,128)S(1)} collective-permute-done((f32[3,1,128,512]{3,2,1,0:T(8,128)S(1)}, f32[3,1,128,512]{3,2,1,0:T(8,128)S(1)}, u32[]{:S(2)}, u32[]{:S(2)}) %collective-permute-start.6) | collective-permute-done | bytes 786464 | tf_op jit(solution)/shard_map/ppermute | solution.py:221
  28.4 0.0 copy-done.3
  28.4 0.0 copy-done.5
  28.4 4.3 %contract_pairs.1 = (f32[4,6,32,256]{3,2,1,0:T(8,128)S(1)}, bf16[8,2,512,128]{3,2,1,0:T(8,128)(2,1)S(1)}, bf16[8,2,512,128]{3,2,1,0:T(8,128)(2,1)S(1)}) custom-call(s32[3]{0:T(128)S(1)} %pad_add_fusion.place, s32[8,8]{1,0:T(8,128)S(1)} %copy-done.3, s32[4,6]{1,0:T(4,128)S(1)} %bitcast.15, ...), custom_call_target="tpu_custom_call", output_to_operand_aliasing={{1}: (7, {}), {2}: (8, {})} | custom-call | flops 2415919104 | bytes 8388608 | tf_op jit(solution)/shard_map/contract_pairs/pallas_call | solution.py:198
  32.8 15.0 %all_to_all.5 = f32[4,6,32,256]{3,2,1,0:T(8,128)S(1)} all-to-all(f32[4,6,32,256]{3,2,1,0:T(8,128)S(1)} %get-tuple-element.34), channel_id=1, replica_groups=mesh['wide'=4,'row'=2,'col'=4] {'col'}, dimensions={0} | all-to-all | bytes 1572864 | tf_op jit(solution)/shard_map/all_to_all | solution.py:247
  47.8 0.7 %reduce_sum.9 = f32[6,32,256]{2,1,0:T(8,128)} reduce(f32[4,6,32,256]{3,2,1,0:T(8,128)S(1)} %all_to_all.5, f32[]{:T(128)} %constant.13.clone.1), dimensions={0}, to_apply=%region_0.0 | reduce | flops 147456 | bytes 983044 | tf_op jit(solution)/shard_map/reduce_sum | solution.py:247
Async XLA Ops:
  0.0 9.5 %collective-permute-start.2 = (f32[1,128,512]{2,1,0:T(8,128)}, f32[1,128,512]{2,1,0:T(8,128)S(1)}, u32[]{:S(2)}, u32[]{:S(2)}) collective-permute-start(f32[1,128,512]{2,1,0:T(8,128)} %param.6), channel_id=1, source_target_pairs={{0,8},{8,0},{16,24},{24,16},{1,9},{9,1},{17,25},{25,17},{2,10},{10... | collective-permute-start | bytes 786440 | tf_op jit(solution)/shard_map/ppermute | solution.py:226
  3.0 8.5 %collective-permute-start = (f32[1,128,512]{2,1,0:T(8,128)}, f32[1,128,512]{2,1,0:T(8,128)S(1)}, u32[]{:S(2)}, u32[]{:S(2)}) collective-permute-start(f32[1,128,512]{2,1,0:T(8,128)} %param.6), channel_id=1, source_target_pairs={{8,16},{16,8},{9,17},{17,9},{10,18},{18,10},{11,19},{19,11},{12,20... | collective-permute-start | bytes 786440 | tf_op jit(solution)/shard_map/ppermute | solution.py:227
  3.7 12.2 %collective-permute-start.5 = (f32[1,128,512]{2,1,0:T(8,128)}, f32[1,128,512]{2,1,0:T(8,128)S(1)}, u32[]{:S(2)}, u32[]{:S(2)}) collective-permute-start(f32[1,128,512]{2,1,0:T(8,128)} %param.6), channel_id=1, source_target_pairs={{0,4},{4,0},{1,5},{5,1},{2,6},{6,2},{3,7},{7,3},{8,12},{12,8},{9,1... | collective-permute-start | bytes 786440 | tf_op jit(solution)/shard_map/ppermute | solution.py:221
  9.5 11.6 %collective-permute-start.4 = (f32[1,128,512]{2,1,0:T(8,128)S(1)}, f32[1,128,512]{2,1,0:T(8,128)S(1)}, u32[]{:S(2)}, u32[]{:S(2)}) collective-permute-start(f32[1,128,512]{2,1,0:T(8,128)S(1)} %collective-permute-done.2.near), channel_id=1, source_target_pairs={{8,24},{16,0},{9,25},{17,1},{10,26},{18,2},{11,27},{19,3},{12,28},... | collective-permute-start | bytes 786440 | tf_op jit(solution)/shard_map/ppermute | solution.py:230
  10.8 10.3 %collective-permute-start.3 = (f32[1,128,512]{2,1,0:T(8,128)S(1)}, f32[1,128,512]{2,1,0:T(8,128)S(1)}, u32[]{:S(2)}, u32[]{:S(2)}) collective-permute-start(f32[1,128,512]{2,1,0:T(8,128)S(1)} %collective-permute-done.2.near), channel_id=1, source_target_pairs={{8,16},{16,8},{9,17},{17,9},{10,18},{18,10},{11,19},{19,11},{12,20... | collective-permute-start | bytes 786440 | tf_op jit(solution)/shard_map/ppermute | solution.py:228
  11.5 13.9 %collective-permute-start.1 = (f32[1,128,512]{2,1,0:T(8,128)S(1)}, f32[1,128,512]{2,1,0:T(8,128)S(1)}, u32[]{:S(2)}, u32[]{:S(2)}) collective-permute-start(f32[1,128,512]{2,1,0:T(8,128)S(1)} %collective-permute-done.mid), channel_id=1, source_target_pairs={{8,0},{16,24},{9,1},{17,25},{10,2},{18,26},{11,3},{19,27},{12,4},{... | collective-permute-start | bytes 786440 | tf_op jit(solution)/shard_map/ppermute | solution.py:229
  12.8 1.4 %copy-start = (f32[6,256,256]{2,1,0:T(8,128)S(1)}, f32[6,256,256]{2,1,0:T(8,128)}, u32[]{:S(2)}) copy-start(f32[6,256,256]{2,1,0:T(8,128)} %amplitudes.1) | copy-start | bytes 4718596
  14.2 0.7 %copy-start.4 = (s32[6,4]{0,1:T(4,128)S(1)}, s32[6,4]{0,1:T(4,128)}, u32[]{:S(2)}) copy-start(s32[6,4]{0,1:T(4,128)} %param.8) | copy-start | bytes 292
  15.9 1.0 %copy-start.1 = (f32[1,128,512]{2,1,0:T(8,128)S(1)}, f32[1,128,512]{2,1,0:T(8,128)}, u32[]{:S(2)}) copy-start(f32[1,128,512]{2,1,0:T(8,128)} %param.6) | copy-start | bytes 786436
  16.9 0.7 %copy-start.2 = (s32[8,8]{1,0:T(8,128)S(1)}, s32[8,8]{1,0:T(8,128)}, u32[]{:S(2)}) copy-start(s32[8,8]{1,0:T(8,128)} %block_mask.5) | copy-start | bytes 772
  26.1 2.4 %copy-start.3 = (s32[8,8]{1,0:T(8,128)S(1)}, s32[8,8]{1,0:T(8,128)}, u32[]{:S(2)}) copy-start(s32[8,8]{1,0:T(8,128)} %block_mask.5) | copy-start | bytes 772
  26.1 2.4 %copy-start.5 = (s32[6,4]{0,1:T(4,128)S(1)}, s32[6,4]{0,1:T(4,128)}, u32[]{:S(2)}) copy-start(s32[6,4]{0,1:T(4,128)} %param.7) | copy-start | bytes 292
  26.1 2.4 %collective-permute-start.6 = (f32[3,1,128,512]{3,2,1,0:T(8,128)S(1)}, f32[3,1,128,512]{3,2,1,0:T(8,128)S(1)}, u32[]{:S(2)}, u32[]{:S(2)}) collective-permute-start(f32[3,1,128,512]{3,2,1,0:T(8,128)S(1)} %collect_pieces.1.refs_0_), channel_id=1, source_target_pairs={{0,4},{4,0},{1,5},{5,1},{2,6},{6,2},{3,7},{7,3},{8,12},{12,8},{9,1... | collective-permute-start | bytes 2359304 | tf_op jit(solution)/shard_map/ppermute | solution.py:221

commit v2 on v1

v2 whole, which is shorter than its diff:
```python
import functools

import jax
import jax.numpy as jnp
from jax import lax
from jax.experimental import pallas as pl
from jax.experimental.pallas import tpu as pltpu
from jax.sharding import PartitionSpec as P

BS = 64
LANES = 128
LINE = 4
SLOTS = 3
VMEM_LIMIT = 40 * 1024 * 1024
SMEM_SPEC = pl.BlockSpec(memory_space=pltpu.SMEM)
VMEM_SPEC = pl.BlockSpec(memory_space=pltpu.VMEM)


def split(value):
    top = value.astype(jnp.bfloat16)
    return top, (value - top.astype(jnp.float32)).astype(jnp.bfloat16)


def partner(index, shift, size):
    if size & (size - 1) == 0:
        return index ^ shift
    return (index + shift) % size


def pair_row(left_half, first, second):
    return jnp.where(left_half, first.astype(jnp.float32), second.astype(jnp.float32))


def left_of(rows):
    return lax.broadcasted_iota(jnp.int32, (rows, LANES), 1) < BS


def mask_amplitudes_kernel(flags, amplitudes, high, low):
    pairs, domv, _ = amplitudes.shape
    left_half = left_of(1)
    for p in range(pairs):
        for j in range(domv // LANES):
            row = pair_row(left_half, flags[2 * j, p], flags[2 * j + 1, p])
            lanes = slice(j * LANES, (j + 1) * LANES)
            for i in range(domv // BS):
                rows = slice(i * BS, (i + 1) * BS)
                top, rest = split(amplitudes[p, rows, lanes] * (row * flags[i, p].astype(jnp.float32)))
                high[p, rows, lanes] = top
                low[p, rows, lanes] = rest


def mask_amplitudes(flags, amplitudes):
    shape = jax.ShapeDtypeStruct(amplitudes.shape, jnp.bfloat16)
    return pl.pallas_call(
        mask_amplitudes_kernel,
        name="mask_amplitudes",
        out_shape=[shape] * 2,
        in_specs=[SMEM_SPEC, VMEM_SPEC],
        out_specs=[VMEM_SPEC] * 2,
        compiler_params=pltpu.CompilerParams(vmem_limit_bytes=VMEM_LIMIT),
        cost_estimate=pl.CostEstimate(flops=4 * amplitudes.size, bytes_accessed=8 * amplitudes.size, transcendentals=0),
    )(flags, amplitudes)


def screen_piece(place, block_mask, piece, q, slot, high, low):
    nq, rows, window = piece.shape
    tiles = window // LANES
    per_slot = rows // BS
    left_half = left_of(1)
    for h in range(per_slot):
        block = (place[0] ^ slot) * per_slot + h
        for t in range(tiles):
            row = pair_row(left_half, block_mask[block, 2 * t], block_mask[block, 2 * t + 1])
            for n in range(nq):
                tile = piece[n, h * BS:(h + 1) * BS, t * LANES:(t + 1) * LANES] * row
                target = pl.ds(pl.multiple_of(slot * rows + h * BS, BS), BS)
                for turn, value in ((0, tile), (1, pltpu.roll(tile, BS, 1))):
                    top, rest = split(value)
                    high[turn * tiles + t, q * nq + n, target, :] = top
                    low[turn * tiles + t, q * nq + n, target, :] = rest


def screen_kernel(keys, place, block_mask, *refs):
    high, low = refs[-2:]
    for (slots, q), pieces in zip(keys, refs):
        for i, slot in enumerate(slots):
            if slot is not None:
                screen_piece(place, block_mask, pieces.at[i], q, slot, high, low)


def screen(place, block_mask, keyed, shape, held=()):
    keys = [(slots, q) for slots, q, _ in keyed]
    pieces = [piece for _, _, piece in keyed]
    size = sum(piece.size for piece in pieces)
    return pl.pallas_call(
        functools.partial(screen_kernel, keys),
        name="screen_factors",
        out_shape=[shape] * 2,
        in_specs=[SMEM_SPEC] * 2 + [VMEM_SPEC] * (len(pieces) + len(held)),
        out_specs=[VMEM_SPEC] * 2,
        input_output_aliases={2 + len(pieces) + i: i for i in range(len(held))},
        compiler_params=pltpu.CompilerParams(vmem_limit_bytes=VMEM_LIMIT),
        cost_estimate=pl.CostEstimate(flops=8 * size, bytes_accessed=12 * size, transcendentals=0),
    )(place, block_mask, *pieces, *held)


def pairs_kernel(row, line, layout, late, place, block_mask, domains, flags, *refs):
    pieces = refs[:len(late)]
    mhigh, mlow, _, _ = refs[len(late):len(late) + 4]
    outs = refs[len(late) + 4:len(late) + 4 + len(layout)]
    high, low, xhigh, xlow, hhigh, hlow, yhigh, ylow = refs[len(late) + 4 + len(layout):]
    z, r = place[0], place[1]
    for (slot, q), piece in zip(late, pieces):

        @pl.loop(slot, slot + 1)
        def _(n):
            screen_piece(place, block_mask, piece, q, n, high, low)

    _, pairs, chunk, domv = outs[0].shape
    twice, qs, window, _ = high.shape
    tiles = twice // 2
    rows = window // line
    per_slot = rows // BS
    half = domv // row
    left_half = left_of(BS)
    picks = [r * half + place[at] * chunk for part in layout for at in part]
    targets = [out.at[i] for out, part in zip(outs, layout) for i in range(len(part))]
    across = (((1,), (1,)), ((), ()))
    dot = functools.partial(lax.dot_general, preferred_element_type=jnp.float32)
    along = (((1,), (0,)), ((), ()))

    def gather(p):
        spans = []
        for i in range(domv // BS):
            block = domains[i, p]
            start = ((block // per_slot) ^ z) * rows + (block % per_slot) * BS
            spans.append(pl.ds(pl.multiple_of(start, BS), BS))
        sources = []
        for j in range(domv // LANES):
            first, second = domains[2 * j, p], domains[2 * j + 1, p]
            sources.append(((first % 2) * tiles + first // 2, (1 - second % 2) * tiles + second // 2))
        for source, target in ((high, yhigh), (low, ylow)):
            for j, (a, b) in enumerate(sources):
                for i, span in enumerate(spans):
                    for q in range(qs):
                        lanes = slice(q * domv + j * LANES, q * domv + (j + 1) * LANES)
                        target[p % SLOTS, i * BS:(i + 1) * BS, lanes] = jnp.where(
                            left_half, source[a, q, span, :], source[b, q, span, :])
        for source, target in ((high, xhigh), (low, xlow)):
            for q in range(qs):
                for n, pick in enumerate(picks):
                    block = domains[pick // BS, p]
                    start = ((block // per_slot) ^ z) * rows + (block % per_slot) * BS + pick % BS
                    span = pl.ds(pl.multiple_of(start, chunk), chunk)
                    for j, (a, b) in enumerate(sources):
                        target[p % SLOTS, q * half + n * chunk:q * half + (n + 1) * chunk, j * LANES:(j + 1) * LANES] = (
                            jnp.where(left_of(chunk), source[a, q, span, :], source[b, q, span, :]))

    def first_product(p):
        at = p % SLOTS
        halfway = dot(xhigh[at], mhigh[p], along) + dot(xhigh[at], mlow[p], along) + dot(xlow[at], mhigh[p], along)
        for q in range(qs):
            top, rest = split(halfway[q * half:(q + 1) * half])
            hhigh[at, :, q * domv:(q + 1) * domv] = top
            hlow[at, :, q * domv:(q + 1) * domv] = rest

    def second_product(p):
        at = p % SLOTS
        total = (dot(hhigh[at], yhigh[at], across) + dot(hhigh[at], ylow[at], across)
                 + dot(hlow[at], yhigh[at], across))
        for j in range(domv // LANES):
            weights = pair_row(left_of(1), flags[2 * j, p], flags[2 * j + 1, p])
            for n, (pick, target) in enumerate(zip(picks, targets)):
                weight = flags[pick // BS, p].astype(jnp.float32)
                target[p, :, j * LANES:(j + 1) * LANES] = total[
                    n * chunk:(n + 1) * chunk, j * LANES:(j + 1) * LANES] * (weights * weight)

    for t in range(pairs + 2):
        for stage, act in ((0, gather), (1, first_product), (2, second_product)):
            if 0 <= t - stage < pairs:
                act(t - stage)


def contract_pairs(row, line, layout, place, block_mask, domains, flags, late, mhigh, mlow, high, low):
    pairs, domv, _ = mhigh.shape
    chunk = domv // (row * sum(len(part) for part in layout))
    qs = high.shape[1]
    keys = [(slot, q) for slot, q, _ in late]
    pieces = [piece for _, _, piece in late]
    held = 4 + len(pieces) + 2
    outs = len(layout)
    results = pl.pallas_call(
        functools.partial(pairs_kernel, row, line, layout, keys),
        name="contract_pairs",
        out_shape=[jax.ShapeDtypeStruct((len(part), pairs, chunk, domv), jnp.float32) for part in layout]
        + [jax.ShapeDtypeStruct(high.shape, high.dtype)] * 2,
        in_specs=[SMEM_SPEC] * 4 + [VMEM_SPEC] * (len(pieces) + 4),
        out_specs=[VMEM_SPEC] * (outs + 2),
        scratch_shapes=[pltpu.VMEM((SLOTS, qs * domv // row, domv), jnp.bfloat16)] * 2
        + [pltpu.VMEM((SLOTS, domv // row, qs * domv), jnp.bfloat16)] * 2
        + [pltpu.VMEM((SLOTS, domv, qs * domv), jnp.bfloat16)] * 2,
        input_output_aliases={held: outs, held + 1: outs + 1},
        compiler_params=pltpu.CompilerParams(vmem_limit_bytes=VMEM_LIMIT),
        cost_estimate=pl.CostEstimate(flops=6 * pairs * qs * domv ** 3 * 4 // row, bytes_accessed=8 * high.size,
                                      transcendentals=0),
    )(place, block_mask, domains, flags, *pieces, mhigh, mlow, high, low)
    return results[:outs]


def add_kernel(at, *refs):
    out = refs[-1]
    total = refs[0][at[0]]
    for i, ref in zip(at[1:], refs[1:]):
        total += ref[i]
    out[...] = total


def add_terms(*terms):
    arrays = [array for array, _ in terms]
    return pl.pallas_call(
        functools.partial(add_kernel, [i for _, i in terms]),
        name="add_terms",
        out_shape=jax.ShapeDtypeStruct(arrays[0].shape[1:], jnp.float32),
        in_specs=[VMEM_SPEC] * len(arrays),
        out_specs=VMEM_SPEC,
        compiler_params=pltpu.CompilerParams(vmem_limit_bytes=VMEM_LIMIT),
    )(*arrays)


def body(wide, row, col, amplitudes, factors, domains, domain_mask, block_mask):
    nq, rows, window = factors.shape
    pairs = domains.shape[0]
    z, r, c = lax.axis_index("wide"), lax.axis_index("row"), lax.axis_index("col")
    shape = jax.ShapeDtypeStruct((2 * window // LANES, row * nq, window, LANES), jnp.bfloat16)
    domains, flags = domains.T, domain_mask.T
    mhigh, mlow = mask_amplitudes(flags, amplitudes)

    def siblings(piece):
        return [lax.ppermute(piece, "row", [(i, (i + s) % row) for i in range(row)]) for s in range(1, row)]

    layout = tuple((2 + s,) for s in range(col))
    chunks = [partner(c, s, col) for s in range(col)]

    if wide == LINE and rows % BS == 0:
        line = wide
        place = jnp.stack([z, r] + chunks).astype(jnp.int32)
        near = lax.ppermute(factors, "wide", [(i, i ^ 1) for i in range(line)])
        cross = lax.ppermute(factors, "wide", [(i, i ^ 2) for i in range(line)])
        high, low = screen(place, block_mask, [((0,), 0, factors[None])], shape)
        cross, high, low, mhigh, mlow, domains = lax.optimization_barrier((cross, high, low, mhigh, mlow, domains))
        last = lax.ppermute(cross, "wide", [(i, i ^ 1) for i in range(line)])
        early = [((0,), q + 1, piece[None]) for q, piece in enumerate(siblings(factors))]
        early += [((1,), 0, near[None]), ((2,), 0, cross[None])]
        high, low = screen(place, block_mask, early, shape, (high, low))
        last, cross, near, high, low = lax.optimization_barrier((last, siblings(cross), siblings(near), high, low))
        late = [(3, q + 1, piece) for q, piece in enumerate(siblings(last))]
        held = [((3,), 0, last[None])]
        for slot, pieces in ((1, near), (2, cross)):
            held += [((slot,), q + 1, piece[None]) for q, piece in enumerate(pieces)]
        high, low = screen(place, block_mask, held, shape, (high, low))
    else:
        line = 1
        place = jnp.stack([jnp.zeros_like(z), r] + chunks).astype(jnp.int32)
        whole = lax.all_gather(factors, "wide", axis=1, tiled=True)
        held = [((0,), q, piece[None]) for q, piece in enumerate([whole] + siblings(whole))]
        high, low = screen(place, block_mask, held, shape)
        late = []

    terms = contract_pairs(row, line, layout, place, block_mask, domains, flags, late, mhigh, mlow, high, low)
    moved = [(lax.ppermute(terms[s], "col", [(i, partner(i, s, col)) for i in range(col)]), 0)
             for s in sorted(range(1, col), key=lambda s: -bin(s).count("1"))]
    return add_terms((terms[0], 0), *moved)


def solution(mesh):
    wide, row, col = (mesh.shape[name] for name in ("wide", "row", "col"))
    return jax.shard_map(
        functools.partial(body, wide, row, col),
        mesh=mesh,
        in_specs=(
            P("wide", None, None),
            P(("row", "col"), "wide", None),
            P("wide", None),
            P("wide", None),
            P(),
        ),
        out_specs=P("wide", ("row", "col"), None),
        check_vma=False,
    )
```

time: 48.8 us -> 42.8 us (0.88)
  blocking collectives: 15 us -> 0 us
  waiting for transfers between devices: 14.2 us -> 19 us
  starting transfers between devices: 7.08 us -> 10.4 us
  Pallas kernels: 7.56 us -> 8.63 us
  other arithmetic: 0.81 us -> 0 us
  local copies, waits for them, and re-layouts: 3.73 us -> 4.5 us
    all_to_all x1 -> x0, blocking collectives: 15 us -> none  [body(): return jnp.sum(lax.all_to_all(terms, 'col', 0, 0, tiled=True), axis=0)]
    ppermute x5 -> x6, waiting for transfers between devices: 12.7 us -> 18.4 us  [the longest x3 8.57 us: body(): lax.ppermute(terms[s], 'col', [(i, partner(i, s, col)) for i in range(col)])]
    ppermute x5 -> x6, starting transfers between devices: 6.94 us -> 9.89 us  [the longest x1 4.04 us: body(): cross = lax.ppermute(factors, 'wide', [(i, i ^ 2) for i in range(line)])]
    ppermute x2 -> x4, waiting for transfers between devices: 1.45 us -> 0.63 us  [siblings(): lax.ppermute(piece, 'row', [(i, (i + s) % row) for i in range(row)])]
    pallas_call x2 -> x3, Pallas kernels: 1.78 us -> 2.53 us  [screen(): pl.pallas_call(functools.partial(screen_kernel, keys), name='screen_facto...]
    reduce_sum x1 -> x0, other arithmetic: 0.73 us -> none  [body(): return jnp.sum(lax.all_to_all(terms, 'col', 0, 0, tiled=True), axis=0)]
    unnamed x12, local copies, waits for them, and re-layouts: 3.73 us -> 4.42 us
  transfers between devices with their start and end apart: 7 -> 10, of which waited for: 4 -> 6; matrix products, arithmetic and copies ran while one was open for 0% -> 0% of each run, Pallas kernels for 6% -> 8%
where the time goes in v2:
time: 42.8 us; the launch traced here: 42.6 us
  waiting for transfers between devices  19 us (44%)
  starting transfers between devices  10.4 us (24%)
  Pallas kernels  8.63 us (20%)
  local copies, waits for them, and re-layouts  4.5 us (11%)
    ppermute x3, waiting for transfers between devices, body(): lax.ppermute(terms[s], 'col', [(i, partner(i, s, col)) for i in range(col)])  8.57 us
    ppermute x1, waiting for transfers between devices, body(): cross = lax.ppermute(factors, 'wide', [(i, i ^ 2) for i in range(line)])  5.19 us
    ppermute x1, waiting for transfers between devices, body(): last = lax.ppermute(cross, 'wide', [(i, i ^ 1) for i in range(line)])  4.61 us
    pallas_call x1, Pallas kernels, contract_pairs(): pl.pallas_call(functools.partial(pairs_kernel, row, line, layout, keys),...  4.49 us
    unnamed x12, local copies, waits for them, and re-layouts  4.42 us
    ppermute x1, starting transfers between devices, body(): cross = lax.ppermute(factors, 'wide', [(i, i ^ 2) for i in range(line)])  4.04 us
    ppermute x3, starting transfers between devices, body(): lax.ppermute(terms[s], 'col', [(i, partner(i, s, col)) for i in range(col)])  3.55 us
    pallas_call x3, Pallas kernels, screen(): pl.pallas_call(functools.partial(screen_kernel, keys), name='screen_facto...  2.53 us
  transfers between devices with their start and end apart: 10, of which 6 were waited for; matrix products, arithmetic and copies ran while one was open for 0% of the time, Pallas kernels for 8%

profile of v2, /device:TPU:0, one launch (start us, length us, event | category | flops | bytes accessed | tf_op | source)
XLA Modules:
  0.0 42.6 jit_solution(15048533225112923154)
XLA Ops:
  0.0 4.0 %collective-permute-start = (f32[1,128,512]{2,1,0:T(8,128)}, f32[1,128,512]{2,1,0:T(8,128)S(1)}, u32[]{:S(2)}, u32[]{:S(2)}) collective-permute-start(f32[1,128,512]{2,1,0:T(8,128)} %param.6), channel_id=1, source_target_pairs={{0,16},{8,24},{16,0},{24,8},{1,17},{9,25},{17,1},{25,9},{2,18},{10... | collective-permute-start | bytes 786440 | tf_op jit(solution)/shard_map/ppermute | solution.py:248
  4.0 1.6 %collective-permute-start.3 = (f32[1,128,512]{2,1,0:T(8,128)}, f32[1,128,512]{2,1,0:T(8,128)S(1)}, u32[]{:S(2)}, u32[]{:S(2)}) collective-permute-start(f32[1,128,512]{2,1,0:T(8,128)} %param.6), channel_id=1, source_target_pairs={{0,8},{8,0},{16,24},{24,16},{1,9},{9,1},{17,25},{25,17},{2,10},{10... | collective-permute-start | bytes 786440 | tf_op jit(solution)/shard_map/ppermute | solution.py:247
  5.6 0.0 collective-permute-start.5
  5.6 0.1 stack.27.place
  5.7 0.0 copy-start.1
  5.7 1.0 %copy-done.1 = f32[1,128,512]{2,1,0:T(8,128)S(1)} copy-done((f32[1,128,512]{2,1,0:T(8,128)S(1)}, f32[1,128,512]{2,1,0:T(8,128)}, u32[]{:S(2)}) %copy-start.1) | copy-done | bytes 262168
  6.7 0.0 copy-start.2
  6.7 0.7 %copy-done.2 = s32[8,8]{1,0:T(8,128)S(1)} copy-done((s32[8,8]{1,0:T(8,128)S(1)}, s32[8,8]{1,0:T(8,128)}, u32[]{:S(2)}) %copy-start.2) | copy-done | bytes 280
  7.3 0.7 %screen_factors.3 = (bf16[8,2,512,128]{3,2,1,0:T(8,128)(2,1)S(1)}, bf16[8,2,512,128]{3,2,1,0:T(8,128)(2,1)S(1)}) custom-call(s32[6]{0:T(128)S(1)} %stack.27.place, s32[8,8]{1,0:T(8,128)S(1)} %copy-done.2, f32[1,1,128,512]{3,2,1,0:T(8,128)S(1)} %bitcast.21), custom_call_target="tpu_custom_call" | custom-call | flops 524288 | bytes 786432 | tf_op jit(solution)/shard_map/screen_factors/pallas_call | solution.py:95
  8.1 0.0 copy-start
  8.1 1.4 %copy-done = f32[6,256,256]{2,1,0:T(8,128)S(1)} copy-done((f32[6,256,256]{2,1,0:T(8,128)S(1)}, f32[6,256,256]{2,1,0:T(8,128)}, u32[]{:S(2)}) %copy-start) | copy-done | bytes 1572888
  9.5 0.0 copy-start.4
  9.5 0.7 %copy-done.4 = s32[6,4]{0,1:T(4,128)S(1)} copy-done((s32[6,4]{0,1:T(4,128)S(1)}, s32[6,4]{0,1:T(4,128)}, u32[]{:S(2)}) %copy-start.4) | copy-done | bytes 120
  10.2 0.9 %mask_amplitudes.1 = (bf16[6,256,256]{2,1,0:T(8,128)(2,1)S(1)}, bf16[6,256,256]{2,1,0:T(8,128)(2,1)S(1)}) custom-call(s32[4,6]{1,0:T(4,128)S(1)} %bitcast.22, f32[6,256,256]{2,1,0:T(8,128)S(1)} %copy-done), custom_call_target="tpu_custom_call" | custom-call | flops 1572864 | bytes 3145728 | tf_op jit(solution)/shard_map/mask_amplitudes/pallas_call | solution.py:54
  11.1 5.2 %collective-permute-done = f32[1,128,512]{2,1,0:T(8,128)S(1)} collective-permute-done((f32[1,128,512]{2,1,0:T(8,128)}, f32[1,128,512]{2,1,0:T(8,128)S(1)}, u32[]{:S(2)}, u32[]{:S(2)}) %collective-permute-start) | collective-permute-done | bytes 262176 | tf_op jit(solution)/shard_map/ppermute | solution.py:248
  16.3 0.7 %collective-permute-start.1 = (f32[1,128,512]{2,1,0:T(8,128)S(1)}, f32[1,128,512]{2,1,0:T(8,128)S(1)}, u32[]{:S(2)}, u32[]{:S(2)}) collective-permute-start(f32[1,128,512]{2,1,0:T(8,128)S(1)} %collective-permute-done), channel_id=1, source_target_pairs={{0,8},{8,0},{16,24},{24,16},{1,9},{9,1},{17,25},{25,17},{2,10},{10... | collective-permute-start | bytes 786440 | tf_op jit(solution)/shard_map/ppermute | solution.py:251
  17.0 0.0 collective-permute-start.2
  17.0 0.0 collective-permute-done.3
  17.0 0.5 %collective-permute-start.4 = (f32[1,128,512]{2,1,0:T(8,128)S(1)}, f32[1,128,512]{2,1,0:T(8,128)S(1)}, u32[]{:S(2)}, u32[]{:S(2)}) collective-permute-start(f32[1,128,512]{2,1,0:T(8,128)S(1)} %collective-permute-done.3), channel_id=1, source_target_pairs={{0,4},{4,0},{1,5},{5,1},{2,6},{6,2},{3,7},{7,3},{8,12},{12,8},{9,1... | collective-permute-start | bytes 786440 | tf_op jit(solution)/shard_map/ppermute | solution.py:239
  17.5 0.0 collective-permute-done.5
  17.5 0.0 copy-start.3
  17.5 0.7 %copy-done.3 = s32[8,8]{1,0:T(8,128)S(1)} copy-done((s32[8,8]{1,0:T(8,128)S(1)}, s32[8,8]{1,0:T(8,128)}, u32[]{:S(2)}) %copy-start.3) | copy-done | bytes 280
  18.2 0.9 %screen_factors.4 = (bf16[8,2,512,128]{3,2,1,0:T(8,128)(2,1)S(1)}, bf16[8,2,512,128]{3,2,1,0:T(8,128)(2,1)S(1)}) custom-call(s32[6]{0:T(128)S(1)} %stack.27.place, s32[8,8]{1,0:T(8,128)S(1)} %copy-done.3, f32[1,1,128,512]{3,2,1,0:T(8,128)S(1)} %bitcast.17, f32[1,1,128,512]{3,2,1,0:T(8,128)S(1)} %bitcast.16, ...), custom_call_target="tpu_custom_call", output_to_operand_aliasing={{0}: (5, {}), {1}: (6, {})} | custom-call | flops 1572864 | bytes 2359296 | tf_op jit(solution)/shard_map/screen_factors/pallas_call | solution.py:95
  19.1 4.6 %collective-permute-done.1 = f32[1,128,512]{2,1,0:T(8,128)S(1)} collective-permute-done((f32[1,128,512]{2,1,0:T(8,128)S(1)}, f32[1,128,512]{2,1,0:T(8,128)S(1)}, u32[]{:S(2)}, u32[]{:S(2)}) %collective-permute-start.1) | collective-permute-done | bytes 262176 | tf_op jit(solution)/shard_map/ppermute | solution.py:251
  23.7 0.0 collective-permute-done.2
  23.7 0.0 collective-permute-done.4
  23.7 0.0 collective-permute-start.6
  23.7 0.0 copy-start.5
  23.7 0.9 %screen_factors.5 = (bf16[8,2,512,128]{3,2,1,0:T(8,128)(2,1)S(1)}, bf16[8,2,512,128]{3,2,1,0:T(8,128)(2,1)S(1)}) custom-call(s32[6]{0:T(128)S(1)} %stack.27.place, s32[8,8]{1,0:T(8,128)S(1)} %copy-done.3, f32[1,1,128,512]{3,2,1,0:T(8,128)S(1)} %bitcast.18, f32[1,1,128,512]{3,2,1,0:T(8,128)S(1)} %bitcast.20, ...), custom_call_target="tpu_custom_call", output_to_operand_aliasing={{0}: (5, {}), {1}: (6, {})} | custom-call | flops 1572864 | bytes 2359296 | tf_op jit(solution)/shard_map/screen_factors/pallas_call | solution.py:95
  24.6 0.6 %collective-permute-done.6.refs_0_ = f32[1,128,512]{2,1,0:T(8,128)S(1)} collective-permute-done((f32[1,128,512]{2,1,0:T(8,128)S(1)}, f32[1,128,512]{2,1,0:T(8,128)S(1)}, u32[]{:S(2)}, u32[]{:S(2)}) %collective-permute-start.6) | collective-permute-done | bytes 262176 | tf_op jit(solution)/shard_map/ppermute | solution.py:239
  25.3 0.0 copy-done.5
  25.3 4.5 %contract_pairs.1 = (f32[1,6,32,256]{3,2,1,0:T(8,128)S(1)}, f32[1,6,32,256]{3,2,1,0:T(8,128)S(1)}, f32[1,6,32,256]{3,2,1,0:T(8,128)S(1)}, f32[1,6,32,256]{3,2,1,...) custom-call(s32[6]{0:T(128)S(1)} %stack.27.place, ...), custom_call_target="tpu_custom_call", output_to_operand_aliasing={{4}: (7, {}), {5}: (8, {})} | custom-call | flops 2415919104 | bytes 8388608 | tf_op jit(solution)/shard_map/contract_pairs/pallas_call | solution.py:192
  29.8 2.3 %collective-permute-start.7 = (f32[1,6,32,256]{3,2,1,0:T(8,128)S(1)}, f32[1,6,32,256]{3,2,1,0:T(8,128)S(1)}, u32[]{:S(2)}, u32[]{:S(2)}) collective-permute-start(f32[1,6,32,256]{3,2,1,0:T(8,128)S(1)} %get-tuple-element.48), channel_id=1, source_target_pairs={{0,3},{1,2},{2,1},{3,0},{4,7},{5,6},{6,5},{7,4},{8,11},{9,10},{10,... | collective-permute-start | bytes 589832 | tf_op jit(solution)/shard_map/ppermute | solution.py:270
  32.0 0.5 %collective-permute-start.8 = (f32[1,6,32,256]{3,2,1,0:T(8,128)S(1)}, f32[1,6,32,256]{3,2,1,0:T(8,128)S(1)}, u32[]{:S(2)}, u32[]{:S(2)}) collective-permute-start(f32[1,6,32,256]{3,2,1,0:T(8,128)S(1)} %get-tuple-element.49), channel_id=1, source_target_pairs={{0,1},{1,0},{2,3},{3,2},{4,5},{5,4},{6,7},{7,6},{8,9},{9,8},{10,11... | collective-permute-start | bytes 589832 | tf_op jit(solution)/shard_map/ppermute | solution.py:270
  32.6 0.7 %collective-permute-start.9 = (f32[1,6,32,256]{3,2,1,0:T(8,128)S(1)}, f32[1,6,32,256]{3,2,1,0:T(8,128)S(1)}, u32[]{:S(2)}, u32[]{:S(2)}) collective-permute-start(f32[1,6,32,256]{3,2,1,0:T(8,128)S(1)} %get-tuple-element.50), channel_id=1, source_target_pairs={{0,2},{1,3},{2,0},{3,1},{4,6},{5,7},{6,4},{7,5},{8,10},{9,11},{10,... | collective-permute-start | bytes 589832 | tf_op jit(solution)/shard_map/ppermute | solution.py:270
  33.3 5.2 %collective-permute-done.7.refs_1_ = f32[1,6,32,256]{3,2,1,0:T(8,128)S(1)} collective-permute-done((f32[1,6,32,256]{3,2,1,0:T(8,128)S(1)}, f32[1,6,32,256]{3,2,1,0:T(8,128)S(1)}, u32[]{:S(2)}, u32[]{:S(2)}) %collective-permute-start.7) | collective-permute-done | bytes 196640 | tf_op jit(solution)/shard_map/ppermute | solution.py:270
  38.5 3.2 %collective-permute-done.8.refs_2_ = f32[1,6,32,256]{3,2,1,0:T(8,128)S(1)} collective-permute-done((f32[1,6,32,256]{3,2,1,0:T(8,128)S(1)}, f32[1,6,32,256]{3,2,1,0:T(8,128)S(1)}, u32[]{:S(2)}, u32[]{:S(2)}) %collective-permute-start.8) | collective-permute-done | bytes 196640 | tf_op jit(solution)/shard_map/ppermute | solution.py:270
  41.8 0.1 collective-permute-done.9.refs_3_
  41.9 0.7 %add_terms.1 = f32[6,32,256]{2,1,0:T(8,128)} custom-call(f32[1,6,32,256]{3,2,1,0:T(8,128)S(1)} %get-tuple-element.47.refs_0_, f32[1,6,32,256]{3,2,1,0:T(8,128)S(1)} %collective-permute-done.7.refs_1_, f32[1,6,32,256]{3,2,1,0:T(8,128)S(1)} %collective-permute-done.8.refs_2_, f32[1,6,32,256]{3,2,1,0:T(8,128)S(1)} %collective-permute-done.9.refs_3_), custom_call_target="tpu_custom_call" | custom-call | tf_op jit(solution)/shard_map/add_terms/pallas_call | solution.py:220
Async XLA Ops:
  0.0 16.3 %collective-permute-start = (f32[1,128,512]{2,1,0:T(8,128)}, f32[1,128,512]{2,1,0:T(8,128)S(1)}, u32[]{:S(2)}, u32[]{:S(2)}) collective-permute-start(f32[1,128,512]{2,1,0:T(8,128)} %param.6), channel_id=1, source_target_pairs={{0,16},{8,24},{16,0},{24,8},{1,17},{9,25},{17,1},{25,9},{2,18},{10... | collective-permute-start | bytes 786440 | tf_op jit(solution)/shard_map/ppermute | solution.py:248
  4.0 13.0 %collective-permute-start.3 = (f32[1,128,512]{2,1,0:T(8,128)}, f32[1,128,512]{2,1,0:T(8,128)S(1)}, u32[]{:S(2)}, u32[]{:S(2)}) collective-permute-start(f32[1,128,512]{2,1,0:T(8,128)} %param.6), channel_id=1, source_target_pairs={{0,8},{8,0},{16,24},{24,16},{1,9},{9,1},{17,25},{25,17},{2,10},{10... | collective-permute-start | bytes 786440 | tf_op jit(solution)/shard_map/ppermute | solution.py:247
  5.6 11.9 %collective-permute-start.5 = (f32[1,128,512]{2,1,0:T(8,128)}, f32[1,128,512]{2,1,0:T(8,128)S(1)}, u32[]{:S(2)}, u32[]{:S(2)}) collective-permute-start(f32[1,128,512]{2,1,0:T(8,128)} %param.6), channel_id=1, source_target_pairs={{0,4},{4,0},{1,5},{5,1},{2,6},{6,2},{3,7},{7,3},{8,12},{12,8},{9,1... | collective-permute-start | bytes 786440 | tf_op jit(solution)/shard_map/ppermute | solution.py:239
  5.7 1.0 %copy-start.1 = (f32[1,128,512]{2,1,0:T(8,128)S(1)}, f32[1,128,512]{2,1,0:T(8,128)}, u32[]{:S(2)}) copy-start(f32[1,128,512]{2,1,0:T(8,128)} %param.6) | copy-start | bytes 786436
  6.7 0.7 %copy-start.2 = (s32[8,8]{1,0:T(8,128)S(1)}, s32[8,8]{1,0:T(8,128)}, u32[]{:S(2)}) copy-start(s32[8,8]{1,0:T(8,128)} %block_mask.7) | copy-start | bytes 772
  8.1 1.4 %copy-start = (f32[6,256,256]{2,1,0:T(8,128)S(1)}, f32[6,256,256]{2,1,0:T(8,128)}, u32[]{:S(2)}) copy-start(f32[6,256,256]{2,1,0:T(8,128)} %amplitudes.1) | copy-start | bytes 4718596
  9.5 0.7 %copy-start.4 = (s32[6,4]{0,1:T(4,128)S(1)}, s32[6,4]{0,1:T(4,128)}, u32[]{:S(2)}) copy-start(s32[6,4]{0,1:T(4,128)} %param.8) | copy-start | bytes 292
  16.3 7.4 %collective-permute-start.1 = (f32[1,128,512]{2,1,0:T(8,128)S(1)}, f32[1,128,512]{2,1,0:T(8,128)S(1)}, u32[]{:S(2)}, u32[]{:S(2)}) collective-permute-start(f32[1,128,512]{2,1,0:T(8,128)S(1)} %collective-permute-done), channel_id=1, source_target_pairs={{0,8},{8,0},{16,24},{24,16},{1,9},{9,1},{17,25},{25,17},{2,10},{10... | collective-permute-start | bytes 786440 | tf_op jit(solution)/shard_map/ppermute | solution.py:251
  17.0 6.7 %collective-permute-start.2 = (f32[1,128,512]{2,1,0:T(8,128)S(1)}, f32[1,128,512]{2,1,0:T(8,128)S(1)}, u32[]{:S(2)}, u32[]{:S(2)}) collective-permute-start(f32[1,128,512]{2,1,0:T(8,128)S(1)} %collective-permute-done), channel_id=1, source_target_pairs={{0,4},{4,0},{1,5},{5,1},{2,6},{6,2},{3,7},{7,3},{8,12},{12,8},{9,1... | collective-permute-start | bytes 786440 | tf_op jit(solution)/shard_map/ppermute | solution.py:239
  17.0 6.7 %collective-permute-start.4 = (f32[1,128,512]{2,1,0:T(8,128)S(1)}, f32[1,128,512]{2,1,0:T(8,128)S(1)}, u32[]{:S(2)}, u32[]{:S(2)}) collective-permute-start(f32[1,128,512]{2,1,0:T(8,128)S(1)} %collective-permute-done.3), channel_id=1, source_target_pairs={{0,4},{4,0},{1,5},{5,1},{2,6},{6,2},{3,7},{7,3},{8,12},{12,8},{9,1... | collective-permute-start | bytes 786440 | tf_op jit(solution)/shard_map/ppermute | solution.py:239
  17.5 0.7 %copy-start.3 = (s32[8,8]{1,0:T(8,128)S(1)}, s32[8,8]{1,0:T(8,128)}, u32[]{:S(2)}) copy-start(s32[8,8]{1,0:T(8,128)} %block_mask.7) | copy-start | bytes 772
  23.7 1.5 %collective-permute-start.6 = (f32[1,128,512]{2,1,0:T(8,128)S(1)}, f32[1,128,512]{2,1,0:T(8,128)S(1)}, u32[]{:S(2)}, u32[]{:S(2)}) collective-permute-start(f32[1,128,512]{2,1,0:T(8,128)S(1)} %collective-permute-done.1), channel_id=1, source_target_pairs={{0,4},{4,0},{1,5},{5,1},{2,6},{6,2},{3,7},{7,3},{8,12},{12,8},{9,1... | collective-permute-start | bytes 786440 | tf_op jit(solution)/shard_map/ppermute | solution.py:239
  23.7 1.5 %copy-start.5 = (s32[6,4]{0,1:T(4,128)S(1)}, s32[6,4]{0,1:T(4,128)}, u32[]{:S(2)}) copy-start(s32[6,4]{0,1:T(4,128)} %param.7) | copy-start | bytes 292
  29.8 8.8 %collective-permute-start.7 = (f32[1,6,32,256]{3,2,1,0:T(8,128)S(1)}, f32[1,6,32,256]{3,2,1,0:T(8,128)S(1)}, u32[]{:S(2)}, u32[]{:S(2)}) collective-permute-start(f32[1,6,32,256]{3,2,1,0:T(8,128)S(1)} %get-tuple-element.48), channel_id=1, source_target_pairs={{0,3},{1,2},{2,1},{3,0},{4,7},{5,6},{6,5},{7,4},{8,11},{9,10},{10,... | collective-permute-start | bytes 589832 | tf_op jit(solution)/shard_map/ppermute | solution.py:270
  32.0 9.7 %collective-permute-start.8 = (f32[1,6,32,256]{3,2,1,0:T(8,128)S(1)}, f32[1,6,32,256]{3,2,1,0:T(8,128)S(1)}, u32[]{:S(2)}, u32[]{:S(2)}) collective-permute-start(f32[1,6,32,256]{3,2,1,0:T(8,128)S(1)} %get-tuple-element.49), channel_id=1, source_target_pairs={{0,1},{1,0},{2,3},{3,2},{4,5},{5,4},{6,7},{7,6},{8,9},{9,8},{10,11... | collective-permute-start | bytes 589832 | tf_op jit(solution)/shard_map/ppermute | solution.py:270
  32.6 9.3 %collective-permute-start.9 = (f32[1,6,32,256]{3,2,1,0:T(8,128)S(1)}, f32[1,6,32,256]{3,2,1,0:T(8,128)S(1)}, u32[]{:S(2)}, u32[]{:S(2)}) collective-permute-start(f32[1,6,32,256]{3,2,1,0:T(8,128)S(1)} %get-tuple-element.50), channel_id=1, source_target_pairs={{0,2},{1,3},{2,0},{3,1},{4,6},{5,7},{6,4},{7,5},{8,10},{9,11},{10,... | collective-permute-start | bytes 589832 | tf_op jit(solution)/shard_map/ppermute | solution.py:270

commit v3 on v0

v3 whole, which is shorter than its diff:
```python
import functools

import jax
import jax.numpy as jnp
from jax import lax
from jax.experimental import pallas as pl
from jax.experimental.pallas import tpu as pltpu
from jax.sharding import PartitionSpec as P

BS = 64
LANES = 128
LINE = 4
VMEM_LIMIT = 40 * 1024 * 1024
SMEM_SPEC = pl.BlockSpec(memory_space=pltpu.SMEM)
VMEM_SPEC = pl.BlockSpec(memory_space=pltpu.VMEM)


def split(value):
    top = value.astype(jnp.bfloat16)
    return top, (value - top.astype(jnp.float32)).astype(jnp.bfloat16)


def partner(index, shift, size):
    if size & (size - 1) == 0:
        return index ^ shift
    return (index + shift) % size


def left_of(rows):
    return lax.broadcasted_iota(jnp.int32, (rows, LANES), 1) < BS


class Scalars:
    def __init__(self, info, col, pairs, dom, blocks):
        self.info, self.pairs, self.blocks = info, pairs, blocks
        self.domains = 2 + col
        self.flags = self.domains + dom * pairs
        self.mask = self.flags + dom * pairs

    def place(self, at):
        return self.info[at]

    def domain(self, at, pair):
        return self.info[self.domains + at * self.pairs + pair]

    def flag(self, at, pair):
        return self.info[self.flags + at * self.pairs + pair].astype(jnp.float32)

    def kept(self, first, second):
        return self.info[self.mask + first * self.blocks + second].astype(jnp.float32)


def mask_amplitudes_kernel(read, info, amplitudes, high, low):
    scalars = read(info)
    pairs, domv, _ = amplitudes.shape
    left_half = left_of(1)

    @pl.loop(0, pairs)
    def _(p):
        for j in range(domv // LANES):
            row = jnp.where(left_half, scalars.flag(2 * j, p), scalars.flag(2 * j + 1, p))
            lanes = slice(j * LANES, (j + 1) * LANES)
            for i in range(domv // BS):
                rows = slice(i * BS, (i + 1) * BS)
                top, rest = split(amplitudes[p, rows, lanes] * (row * scalars.flag(i, p)))
                high[p, rows, lanes] = top
                low[p, rows, lanes] = rest


def mask_amplitudes(read, info, amplitudes):
    shape = jax.ShapeDtypeStruct(amplitudes.shape, jnp.bfloat16)
    return pl.pallas_call(
        functools.partial(mask_amplitudes_kernel, read),
        name="mask_amplitudes",
        out_shape=[shape] * 2,
        in_specs=[SMEM_SPEC, VMEM_SPEC],
        out_specs=[VMEM_SPEC] * 2,
        compiler_params=pltpu.CompilerParams(vmem_limit_bytes=VMEM_LIMIT),
        cost_estimate=pl.CostEstimate(flops=4 * amplitudes.size, bytes_accessed=8 * amplitudes.size, transcendentals=0),
    )(info, amplitudes)


def screen_piece(scalars, piece, q, slot, high, low):
    nq, rows, window = piece.shape
    tiles = window // LANES
    per_slot = rows // BS
    left_half = left_of(1)

    @pl.loop(0, tiles)
    def _(t):
        lanes = pl.ds(pl.multiple_of(t * LANES, LANES), LANES)
        for h in range(per_slot):
            block = (scalars.place(0) ^ slot) * per_slot + h
            row = jnp.where(left_half, scalars.kept(block, 2 * t), scalars.kept(block, 2 * t + 1))
            target = slice(slot * rows + h * BS, slot * rows + (h + 1) * BS)
            for n in range(nq):
                tile = piece[n, h * BS:(h + 1) * BS, lanes] * row
                for turn, value in ((0, tile), (1, pltpu.roll(tile, BS, 1))):
                    top, rest = split(value)
                    high[turn * tiles + t, q * nq + n, target, :] = top
                    low[turn * tiles + t, q * nq + n, target, :] = rest


def screen_kernel(read, keys, info, *refs):
    high, low = refs[-2:]
    for (slot, q), piece in zip(keys, refs):
        screen_piece(read(info), piece, q, slot, high, low)


def screen(read, info, keyed, shape, held=()):
    keys = [(slot, q) for slot, q, _ in keyed]
    pieces = [piece for _, _, piece in keyed]
    size = sum(piece.size for piece in pieces)
    return pl.pallas_call(
        functools.partial(screen_kernel, read, keys),
        name="screen_factors",
        out_shape=[shape] * 2,
        in_specs=[SMEM_SPEC] + [VMEM_SPEC] * (len(pieces) + len(held)),
        out_specs=[VMEM_SPEC] * 2,
        input_output_aliases={1 + len(pieces) + i: i for i in range(len(held))},
        compiler_params=pltpu.CompilerParams(vmem_limit_bytes=VMEM_LIMIT),
        cost_estimate=pl.CostEstimate(flops=8 * size, bytes_accessed=12 * size, transcendentals=0),
    )(info, *pieces, *held)


def pairs_kernel(read, row, line, late, info, *refs):
    scalars = read(info)
    pieces = refs[:len(late)]
    mhigh, mlow, _, _ = refs[len(late):len(late) + 4]
    outs = refs[len(late) + 4:-4]
    high, low, yhigh, ylow = refs[-4:]
    z, r = scalars.place(0), scalars.place(1)
    for (slot, q), piece in zip(late, pieces):
        screen_piece(scalars, piece, q, slot, high, low)

    pairs, chunk, domv = outs[0].shape
    twice, qs, window, _ = high.shape
    tiles = twice // 2
    rows = window // line
    per_slot = rows // BS
    half = domv // row
    picks = [r * half + scalars.place(2 + s) * chunk for s in range(len(outs))]
    across = (((1,), (1,)), ((), ()))
    along = (((1,), (0,)), ((), ()))
    dot = functools.partial(lax.dot_general, preferred_element_type=jnp.float32)

    @pl.loop(0, pairs)
    def _(p):
        def rows_of(at, offset, size):
            block = scalars.domain(at, p)
            start = ((block // per_slot) ^ z) * rows + (block % per_slot) * BS + offset
            return pl.ds(pl.multiple_of(start, size), size)

        sources = []
        for j in range(domv // LANES):
            first, second = scalars.domain(2 * j, p), scalars.domain(2 * j + 1, p)
            sources.append(((first % 2) * tiles + first // 2, (1 - second % 2) * tiles + second // 2))
        spans = [rows_of(i, 0, BS) for i in range(domv // BS)]
        xs = []
        for source, target in ((high, yhigh), (low, ylow)):
            for j, (a, b) in enumerate(sources):
                for i, span in enumerate(spans):
                    for q in range(qs):
                        lanes = slice(q * domv + j * LANES, q * domv + (j + 1) * LANES)
                        target[i * BS:(i + 1) * BS, lanes] = jnp.where(
                            left_of(BS), source[a, q, span, :], source[b, q, span, :])
            parts = []
            for q in range(qs):
                for pick in picks:
                    span = rows_of(pick // BS, pick % BS, chunk)
                    parts.append(jnp.concatenate([jnp.where(
                        left_of(chunk), source[a, q, span, :], source[b, q, span, :]) for a, b in sources], 1))
            xs.append(jnp.concatenate(parts, 0))
        xhigh, xlow = xs
        halfway = dot(xhigh, mhigh[p], along) + dot(xhigh, mlow[p], along) + dot(xlow, mhigh[p], along)
        hhigh, hlow = split(jnp.concatenate([halfway[q * half:(q + 1) * half] for q in range(qs)], 1))
        total = dot(hhigh, yhigh[...], across) + dot(hhigh, ylow[...], across) + dot(hlow, yhigh[...], across)
        for j in range(domv // LANES):
            weights = jnp.where(left_of(1), scalars.flag(2 * j, p), scalars.flag(2 * j + 1, p))
            for n, (pick, out) in enumerate(zip(picks, outs)):
                out[p, :, j * LANES:(j + 1) * LANES] = total[
                    n * chunk:(n + 1) * chunk, j * LANES:(j + 1) * LANES] * (weights * scalars.flag(pick // BS, p))


def contract_pairs(read, row, col, line, info, late, mhigh, mlow, high, low):
    pairs, domv, _ = mhigh.shape
    chunk = domv // (row * col)
    qs = high.shape[1]
    keys = [(slot, q) for slot, q, _ in late]
    pieces = [piece for _, _, piece in late]
    held = 1 + len(pieces) + 2
    results = pl.pallas_call(
        functools.partial(pairs_kernel, read, row, line, keys),
        name="contract_pairs",
        out_shape=[jax.ShapeDtypeStruct((pairs, chunk, domv), jnp.float32)] * col
        + [jax.ShapeDtypeStruct(high.shape, high.dtype)] * 2,
        in_specs=[SMEM_SPEC] + [VMEM_SPEC] * (len(pieces) + 4),
        out_specs=[VMEM_SPEC] * (col + 2),
        scratch_shapes=[pltpu.VMEM((domv, qs * domv), jnp.bfloat16)] * 2,
        input_output_aliases={held: col, held + 1: col + 1},
        compiler_params=pltpu.CompilerParams(vmem_limit_bytes=VMEM_LIMIT),
        cost_estimate=pl.CostEstimate(flops=6 * pairs * qs * domv ** 3 * 4 // row, bytes_accessed=8 * high.size,
                                      transcendentals=0),
    )(info, *pieces, mhigh, mlow, high, low)
    return results[:col]


def add_kernel(*refs):
    total = refs[0][...]
    for ref in refs[1:-1]:
        total += ref[...]
    refs[-1][...] = total


def add_terms(*terms):
    return pl.pallas_call(
        add_kernel,
        name="add_terms",
        out_shape=jax.ShapeDtypeStruct(terms[0].shape, jnp.float32),
        in_specs=[VMEM_SPEC] * len(terms),
        out_specs=VMEM_SPEC,
        compiler_params=pltpu.CompilerParams(vmem_limit_bytes=VMEM_LIMIT),
    )(*terms)


def body(wide, row, col, amplitudes, factors, domains, domain_mask, block_mask):
    nq, rows, window = factors.shape
    pairs, dom = domains.shape
    z, r, c = lax.axis_index("wide"), lax.axis_index("row"), lax.axis_index("col")
    line = wide if wide == LINE and rows % BS == 0 else 1
    place = jnp.stack([z if line > 1 else jnp.zeros_like(z), r] + [partner(c, s, col) for s in range(col)])
    info = jnp.concatenate([place.astype(jnp.int32), domains.T.reshape(-1), domain_mask.T.reshape(-1), block_mask.reshape(-1)])

    def read(ref):
        return Scalars(ref, col, pairs, dom, window // BS)

    def siblings(piece):
        return [lax.ppermute(piece, "row", [(i, (i + s) % row) for i in range(row)]) for s in range(1, row)]

    def across(piece, shift):
        return lax.ppermute(piece, "wide", [(i, i ^ shift) for i in range(wide)])

    def others(slot, pieces):
        return [(slot, q + 1, piece) for q, piece in enumerate(pieces)]

    shape = jax.ShapeDtypeStruct((2 * window // LANES, row * nq, window, LANES), jnp.bfloat16)
    prepare = functools.partial(screen, read, info)
    mhigh, mlow = mask_amplitudes(read, info, amplitudes)
    if line > 1:
        near, cross = across(factors, 1), across(factors, 2)
        high, low = prepare([(0, 0, factors)], shape)
        cross, high, low, mhigh, mlow = lax.optimization_barrier((cross, high, low, mhigh, mlow))
        last = across(cross, 1)
        early = others(0, siblings(factors)) + [(1, 0, near), (2, 0, cross)]
        s_cross, s_near = siblings(cross), siblings(near)
        high, low = prepare(early, shape, (high, low))
        last, high, low = lax.optimization_barrier((last, high, low))
        late = others(3, siblings(last))
        high, low = prepare([(3, 0, last)] + others(1, s_near) + others(2, s_cross), shape, (high, low))
    else:
        whole = lax.all_gather(factors, "wide", axis=1, tiled=True)
        late = []
        high, low = prepare([(0, 0, whole)] + others(0, siblings(whole)), shape)

    terms = contract_pairs(read, row, col, line, info, late, mhigh, mlow, high, low)
    moved = [lax.ppermute(terms[s], "col", [(i, partner(i, s, col)) for i in range(col)])
             for s in sorted(range(1, col), key=lambda s: -bin(s).count("1"))]
    return add_terms(terms[0], *moved)


def solution(mesh):
    wide, row, col = (mesh.shape[name] for name in ("wide", "row", "col"))
    return jax.shard_map(
        functools.partial(body, wide, row, col),
        mesh=mesh,
        in_specs=(
            P("wide", None, None),
            P(("row", "col"), "wide", None),
            P("wide", None),
            P("wide", None),
            P(),
        ),
        out_specs=P("wide", ("row", "col"), None),
        check_vma=False,
    )
```

time: 119 us -> 44.4 us (0.37)
  waiting for transfers between devices: 68 us -> 17.5 us
  matrix products: 16.2 us -> 0 us
  local copies, waits for them, and re-layouts: 18.1 us -> 4.73 us
  between operations: 13.4 us -> 0.08 us
  Pallas kernels: 0 us -> 11.5 us
  starting transfers between devices: 0.04 us -> 10.4 us
  other arithmetic: 2.59 us -> 0 us
    reduce_scatter x1 -> x0, waiting for transfers between devices: 37 us -> none  [body(): lax.psum_scatter(partial_terms, ('row', 'col'), scatter_dimension=1, tile...]
    all_gather x1 -> x0, waiting for transfers between devices: 31 us -> none  [body(): gathered = lax.all_gather(factors, 'wide', axis=1, tiled=True)]
    ppermute x0 -> x10, waiting for transfers between devices: none -> 17.5 us  [the longest x3 8.93 us: body(): lax.ppermute(terms[s], 'col', [(i, partner(i, s, col)) for i in range(col)])]
    dot_general x12 -> x0, matrix products: 16.2 us -> none  [the longest x6 9.64 us: contract_rows(): jnp.einsum('qxu,uw->qxw', subset, masked, precision=lax.Precision.HIGHEST)]
    gather x18 -> x0, local copies, waits for them, and re-layouts: 12.8 us -> none  [contract_rows(): subset = screened[:, indices][:, :, indices]]
    pallas_call x0 -> x6, Pallas kernels: none -> 11.5 us  [the longest x1 5.54 us: contract_pairs(): pl.pallas_call(functools.partial(pairs_kernel, read, row, line, keys), na...]
    ppermute x0 -> x10, starting transfers between devices: none -> 10.4 us  [the longest x3 6.33 us: across(): return lax.ppermute(piece, 'wide', [(i, i ^ shift) for i in range(wide)])]
    reshape x0 -> x3, local copies, waits for them, and re-layouts: none -> 2.29 us  [the longest x1 0.77 us: body(): block_mask.reshape(-1)]
  transfers between devices with their start and end apart: 2 -> 10, of which waited for: 2 -> 5; matrix products, arithmetic and copies ran while one was open for 2% -> 5% of each run, Pallas kernels for 0% -> 12%
where the time goes in v3:
time: 44.4 us; the launch traced here: 44.2 us
  waiting for transfers between devices  17.5 us (39%)
  Pallas kernels  11.5 us (26%)
  starting transfers between devices  10.4 us (23%)
  local copies, waits for them, and re-layouts  4.73 us (11%)
    ppermute x3, waiting for transfers between devices, body(): lax.ppermute(terms[s], 'col', [(i, partner(i, s, col)) for i in range(col)])  8.93 us
    ppermute x3, waiting for transfers between devices, across(): return lax.ppermute(piece, 'wide', [(i, i ^ shift) for i in range(wide)])  8.55 us
    ppermute x3, starting transfers between devices, across(): return lax.ppermute(piece, 'wide', [(i, i ^ shift) for i in range(wide)])  6.33 us
    pallas_call x1, Pallas kernels, contract_pairs(): pl.pallas_call(functools.partial(pairs_kernel, read, row, line, keys), na...  5.54 us
    pallas_call x3, Pallas kernels, screen(): pl.pallas_call(functools.partial(screen_kernel, read, keys), name='screen...  4.33 us
    ppermute x3, starting transfers between devices, body(): lax.ppermute(terms[s], 'col', [(i, partner(i, s, col)) for i in range(col)])  3.55 us
    unnamed x4, local copies, waits for them, and re-layouts  2.36 us
    pallas_call x1, Pallas kernels, mask_amplitudes(): pl.pallas_call(functools.partial(mask_amplitudes_kernel, read), name='mas...  0.91 us
  transfers between devices with their start and end apart: 10, of which 5 were waited for; matrix products, arithmetic and copies ran while one was open for 5% of the time, Pallas kernels for 12%

profile of v3, /device:TPU:0, one launch (start us, length us, event | category | flops | bytes accessed | tf_op | source)
XLA Modules:
  0.0 44.2 jit_solution(2731870382147933546)
XLA Ops:
  0.0 4.0 %collective-permute-start = (f32[1,128,512]{2,1,0:T(8,128)}, f32[1,128,512]{2,1,0:T(8,128)S(1)}, u32[]{:S(2)}, u32[]{:S(2)}) collective-permute-start(f32[1,128,512]{2,1,0:T(8,128)} %refs_0_.1), channel_id=1, source_target_pairs={{0,16},{8,24},{16,0},{24,8},{1,17},{9,25},{17,1},{25,9},{2,18},{10... | collective-permute-start | bytes 786440 | tf_op jit(solution)/shard_map/ppermute | solution.py:241
  4.0 1.6 %collective-permute-start.3 = (f32[1,128,512]{2,1,0:T(8,128)}, f32[1,128,512]{2,1,0:T(8,128)S(1)}, u32[]{:S(2)}, u32[]{:S(2)}) collective-permute-start(f32[1,128,512]{2,1,0:T(8,128)} %refs_0_.1), channel_id=1, source_target_pairs={{0,8},{8,0},{16,24},{24,16},{1,9},{9,1},{17,25},{25,17},{2,10},{10... | collective-permute-start | bytes 786440 | tf_op jit(solution)/shard_map/ppermute | solution.py:241
  5.6 0.0 collective-permute-start.2
  5.6 0.8 %reshape.9 = s32[24]{0:T(128)S(1)} reshape(s32[4,6]{1,0:T(4,128)} %bitcast.8) | data formatting | bytes 192 | tf_op jit(solution)/shard_map/reshape | solution.py:232
  6.4 0.8 %reshape.10 = s32[24]{0:T(128)S(1)} reshape(s32[4,6]{1,0:T(4,128)} %bitcast.9) | data formatting | bytes 192 | tf_op jit(solution)/shard_map/reshape | solution.py:232
  7.1 0.8 %reshape.11 = s32[64]{0:T(128)S(1)} reshape(s32[8,8]{1,0:T(8,128)} %param.9) | data formatting | bytes 512 | tf_op jit(solution)/shard_map/reshape | solution.py:232
  7.9 0.1 concatenate.3.info
  8.0 0.0 copy-start.1
  8.0 1.0 %copy-done.1 = f32[1,128,512]{2,1,0:T(8,128)S(1)} copy-done((f32[1,128,512]{2,1,0:T(8,128)S(1)}, f32[1,128,512]{2,1,0:T(8,128)}, u32[]{:S(2)}) %copy-start.1) | copy-done | bytes 262168
  9.0 0.9 %screen_factors.3 = (bf16[8,2,512,128]{3,2,1,0:T(8,128)(2,1)S(1)}, bf16[8,2,512,128]{3,2,1,0:T(8,128)(2,1)S(1)}) custom-call(s32[118]{0:T(128)S(1)} %concatenate.3.info, f32[1,128,512]{2,1,0:T(8,128)S(1)} %copy-done.1), custom_call_target="tpu_custom_call" | custom-call | flops 524288 | bytes 786432 | tf_op jit(solution)/shard_map/screen_factors/pallas_call | solution.py:114
  9.9 0.0 copy-start
  9.9 1.4 %copy-done = f32[6,256,256]{2,1,0:T(8,128)S(1)} copy-done((f32[6,256,256]{2,1,0:T(8,128)S(1)}, f32[6,256,256]{2,1,0:T(8,128)}, u32[]{:S(2)}) %copy-start) | copy-done | bytes 1572888
  11.3 0.9 %mask_amplitudes.1 = (bf16[6,256,256]{2,1,0:T(8,128)(2,1)S(1)}, bf16[6,256,256]{2,1,0:T(8,128)(2,1)S(1)}) custom-call(s32[118]{0:T(128)S(1)} %concatenate.3.info, f32[6,256,256]{2,1,0:T(8,128)S(1)} %copy-done), custom_call_target="tpu_custom_call" | custom-call | flops 1572864 | bytes 3145728 | tf_op jit(solution)/shard_map/mask_amplitudes/pallas_call | solution.py:72
  12.2 4.1 %collective-permute-done.refs_2_ = f32[1,128,512]{2,1,0:T(8,128)S(1)} collective-permute-done((f32[1,128,512]{2,1,0:T(8,128)}, f32[1,128,512]{2,1,0:T(8,128)S(1)}, u32[]{:S(2)}, u32[]{:S(2)}) %collective-permute-start) | collective-permute-done | bytes 262176 | tf_op jit(solution)/shard_map/ppermute | solution.py:241
  16.3 0.7 %collective-permute-start.1 = (f32[1,128,512]{2,1,0:T(8,128)S(1)}, f32[1,128,512]{2,1,0:T(8,128)S(1)}, u32[]{:S(2)}, u32[]{:S(2)}) collective-permute-start(f32[1,128,512]{2,1,0:T(8,128)S(1)} %collective-permute-done.refs_2_), channel_id=1, source_target_pairs={{0,8},{8,0},{16,24},{24,16},{1,9},{9,1},{17,25},{25,17},{2,10},{10... | collective-permute-start | bytes 786440 | tf_op jit(solution)/shard_map/ppermute | solution.py:241
  17.0 0.0 collective-permute-start.6
  17.0 0.0 collective-permute-done.3.refs_1_
  17.0 0.5 %collective-permute-start.5 = (f32[1,128,512]{2,1,0:T(8,128)S(1)}, f32[1,128,512]{2,1,0:T(8,128)S(1)}, u32[]{:S(2)}, u32[]{:S(2)}) collective-permute-start(f32[1,128,512]{2,1,0:T(8,128)S(1)} %collective-permute-done.3.refs_1_), channel_id=1, source_target_pairs={{0,4},{4,0},{1,5},{5,1},{2,6},{6,2},{3,7},{7,3},{8,12},{12,8},{9,1... | collective-permute-start | bytes 786440 | tf_op jit(solution)/shard_map/ppermute | solution.py:238
  17.5 0.0 collective-permute-done.2.refs_0_
  17.5 1.7 %screen_factors.4 = (bf16[8,2,512,128]{3,2,1,0:T(8,128)(2,1)S(1)}, bf16[8,2,512,128]{3,2,1,0:T(8,128)(2,1)S(1)}) custom-call(s32[118]{0:T(128)S(1)} %concatenate.3.info, f32[1,128,512]{2,1,0:T(8,128)S(1)} %collective-permute-done.2.refs_0_, f32[1,128,512]{2,1,0:T(8,128)S(1)} %collective-permute-done.3.refs_1_, ...), custom_call_target="tpu_custom_call", output_to_operand_aliasing={{0}: (4, {}), {1}: (5, {})} | custom-call | flops 1572864 | bytes 2359296 | tf_op jit(solution)/shard_map/screen_factors/pallas_call | solution.py:114
  19.2 4.5 %collective-permute-done.1.refs_0_ = f32[1,128,512]{2,1,0:T(8,128)S(1)} collective-permute-done((f32[1,128,512]{2,1,0:T(8,128)S(1)}, f32[1,128,512]{2,1,0:T(8,128)S(1)}, u32[]{:S(2)}, u32[]{:S(2)}) %collective-permute-start.1) | collective-permute-done | bytes 262176 | tf_op jit(solution)/shard_map/ppermute | solution.py:241
  23.7 0.0 collective-permute-start.4
  23.7 0.0 collective-permute-done.5.refs_1_
  23.7 0.0 collective-permute-done.6.refs_2_
  23.7 1.7 %screen_factors.5 = (bf16[8,2,512,128]{3,2,1,0:T(8,128)(2,1)S(1)}, bf16[8,2,512,128]{3,2,1,0:T(8,128)(2,1)S(1)}) custom-call(s32[118]{0:T(128)S(1)} %concatenate.3.info, f32[1,128,512]{2,1,0:T(8,128)S(1)} %collective-permute-done.1.refs_0_, f32[1,128,512]{2,1,0:T(8,128)S(1)} %collective-permute-done.5.refs_1_, ...), custom_call_target="tpu_custom_call", output_to_operand_aliasing={{0}: (4, {}), {1}: (5, {})} | custom-call | flops 1572864 | bytes 2359296 | tf_op jit(solution)/shard_map/screen_factors/pallas_call | solution.py:114
  25.4 0.0 collective-permute-done.4.refs_0_
  25.4 5.5 %contract_pairs.1 = (f32[6,32,256]{2,1,0:T(8,128)S(1)}, f32[6,32,256]{2,1,0:T(8,128)S(1)}, f32[6,32,256]{2,1,0:T(8,128)S(1)}, f32[6,32,256]{2,1,0:T(8,128)S(1)},...) custom-call(s32[118]{0:T(128)S(1)} %concatenate.3.info, ...), custom_call_target="tpu_custom_call", output_to_operand_aliasing={{4}: (4, {}), {5}: (5, {})} | custom-call | flops 2415919104 | bytes 8388608 | tf_op jit(solution)/shard_map/contract_pairs/pallas_call | solution.py:192
  31.0 2.3 %collective-permute-start.7 = (f32[6,32,256]{2,1,0:T(8,128)S(1)}, f32[6,32,256]{2,1,0:T(8,128)S(1)}, u32[]{:S(2)}, u32[]{:S(2)}) collective-permute-start(f32[6,32,256]{2,1,0:T(8,128)S(1)} %get-tuple-element.42), channel_id=1, source_target_pairs={{0,3},{1,2},{2,1},{3,0},{4,7},{5,6},{6,5},{7,4},{8,11},{9,10},{10,... | collective-permute-start | bytes 589832 | tf_op jit(solution)/shard_map/ppermute | solution.py:266
  33.3 0.5 %collective-permute-start.8 = (f32[6,32,256]{2,1,0:T(8,128)S(1)}, f32[6,32,256]{2,1,0:T(8,128)S(1)}, u32[]{:S(2)}, u32[]{:S(2)}) collective-permute-start(f32[6,32,256]{2,1,0:T(8,128)S(1)} %get-tuple-element.43), channel_id=1, source_target_pairs={{0,1},{1,0},{2,3},{3,2},{4,5},{5,4},{6,7},{7,6},{8,9},{9,8},{10,11... | collective-permute-start | bytes 589832 | tf_op jit(solution)/shard_map/ppermute | solution.py:266
  33.8 0.7 %collective-permute-start.9 = (f32[6,32,256]{2,1,0:T(8,128)S(1)}, f32[6,32,256]{2,1,0:T(8,128)S(1)}, u32[]{:S(2)}, u32[]{:S(2)}) collective-permute-start(f32[6,32,256]{2,1,0:T(8,128)S(1)} %get-tuple-element.44), channel_id=1, source_target_pairs={{0,2},{1,3},{2,0},{3,1},{4,6},{5,7},{6,4},{7,5},{8,10},{9,11},{10,... | collective-permute-start | bytes 589832 | tf_op jit(solution)/shard_map/ppermute | solution.py:266
  34.5 5.2 %collective-permute-done.7.refs_1_ = f32[6,32,256]{2,1,0:T(8,128)S(1)} collective-permute-done((f32[6,32,256]{2,1,0:T(8,128)S(1)}, f32[6,32,256]{2,1,0:T(8,128)S(1)}, u32[]{:S(2)}, u32[]{:S(2)}) %collective-permute-start.7) | collective-permute-done | bytes 196640 | tf_op jit(solution)/shard_map/ppermute | solution.py:266
  39.7 3.7 %collective-permute-done.8.refs_2_ = f32[6,32,256]{2,1,0:T(8,128)S(1)} collective-permute-done((f32[6,32,256]{2,1,0:T(8,128)S(1)}, f32[6,32,256]{2,1,0:T(8,128)S(1)}, u32[]{:S(2)}, u32[]{:S(2)}) %collective-permute-start.8) | collective-permute-done | bytes 196640 | tf_op jit(solution)/shard_map/ppermute | solution.py:266
  43.3 0.1 collective-permute-done.9.refs_3_
  43.5 0.7 %add_terms.1 = f32[6,32,256]{2,1,0:T(8,128)} custom-call(f32[6,32,256]{2,1,0:T(8,128)S(1)} %get-tuple-element.41.refs_0_, f32[6,32,256]{2,1,0:T(8,128)S(1)} %collective-permute-done.7.refs_1_, f32[6,32,256]{2,1,0:T(8,128)S(1)} %collective-permute-done.8.refs_2_, f32[6,32,256]{2,1,0:T(8,128)S(1)} %collective-permute-done.9.refs_3_), custom_call_target="tpu_custom_call" | custom-call | tf_op jit(solution)/shard_map/add_terms/pallas_call | solution.py:216
Async XLA Ops:
  0.0 16.3 %collective-permute-start = (f32[1,128,512]{2,1,0:T(8,128)}, f32[1,128,512]{2,1,0:T(8,128)S(1)}, u32[]{:S(2)}, u32[]{:S(2)}) collective-permute-start(f32[1,128,512]{2,1,0:T(8,128)} %refs_0_.1), channel_id=1, source_target_pairs={{0,16},{8,24},{16,0},{24,8},{1,17},{9,25},{17,1},{25,9},{2,18},{10... | collective-permute-start | bytes 786440 | tf_op jit(solution)/shard_map/ppermute | solution.py:241
  4.0 13.0 %collective-permute-start.3 = (f32[1,128,512]{2,1,0:T(8,128)}, f32[1,128,512]{2,1,0:T(8,128)S(1)}, u32[]{:S(2)}, u32[]{:S(2)}) collective-permute-start(f32[1,128,512]{2,1,0:T(8,128)} %refs_0_.1), channel_id=1, source_target_pairs={{0,8},{8,0},{16,24},{24,16},{1,9},{9,1},{17,25},{25,17},{2,10},{10... | collective-permute-start | bytes 786440 | tf_op jit(solution)/shard_map/ppermute | solution.py:241
  5.6 11.9 %collective-permute-start.2 = (f32[1,128,512]{2,1,0:T(8,128)}, f32[1,128,512]{2,1,0:T(8,128)S(1)}, u32[]{:S(2)}, u32[]{:S(2)}) collective-permute-start(f32[1,128,512]{2,1,0:T(8,128)} %refs_0_.1), channel_id=1, source_target_pairs={{0,4},{4,0},{1,5},{5,1},{2,6},{6,2},{3,7},{7,3},{8,12},{12,8},{9,1... | collective-permute-start | bytes 786440 | tf_op jit(solution)/shard_map/ppermute | solution.py:238
  8.0 1.0 %copy-start.1 = (f32[1,128,512]{2,1,0:T(8,128)S(1)}, f32[1,128,512]{2,1,0:T(8,128)}, u32[]{:S(2)}) copy-start(f32[1,128,512]{2,1,0:T(8,128)} %refs_0_.1) | copy-start | bytes 786436
  9.9 1.4 %copy-start = (f32[6,256,256]{2,1,0:T(8,128)S(1)}, f32[6,256,256]{2,1,0:T(8,128)}, u32[]{:S(2)}) copy-start(f32[6,256,256]{2,1,0:T(8,128)} %amplitudes.1) | copy-start | bytes 4718596
  16.3 7.4 %collective-permute-start.1 = (f32[1,128,512]{2,1,0:T(8,128)S(1)}, f32[1,128,512]{2,1,0:T(8,128)S(1)}, u32[]{:S(2)}, u32[]{:S(2)}) collective-permute-start(f32[1,128,512]{2,1,0:T(8,128)S(1)} %collective-permute-done.refs_2_), channel_id=1, source_target_pairs={{0,8},{8,0},{16,24},{24,16},{1,9},{9,1},{17,25},{25,17},{2,10},{10... | collective-permute-start | bytes 786440 | tf_op jit(solution)/shard_map/ppermute | solution.py:241
  17.0 6.7 %collective-permute-start.6 = (f32[1,128,512]{2,1,0:T(8,128)S(1)}, f32[1,128,512]{2,1,0:T(8,128)S(1)}, u32[]{:S(2)}, u32[]{:S(2)}) collective-permute-start(f32[1,128,512]{2,1,0:T(8,128)S(1)} %collective-permute-done.refs_2_), channel_id=1, source_target_pairs={{0,4},{4,0},{1,5},{5,1},{2,6},{6,2},{3,7},{7,3},{8,12},{12,8},{9,1... | collective-permute-start | bytes 786440 | tf_op jit(solution)/shard_map/ppermute | solution.py:238
  17.0 6.7 %collective-permute-start.5 = (f32[1,128,512]{2,1,0:T(8,128)S(1)}, f32[1,128,512]{2,1,0:T(8,128)S(1)}, u32[]{:S(2)}, u32[]{:S(2)}) collective-permute-start(f32[1,128,512]{2,1,0:T(8,128)S(1)} %collective-permute-done.3.refs_1_), channel_id=1, source_target_pairs={{0,4},{4,0},{1,5},{5,1},{2,6},{6,2},{3,7},{7,3},{8,12},{12,8},{9,1... | collective-permute-start | bytes 786440 | tf_op jit(solution)/shard_map/ppermute | solution.py:238
  23.7 1.7 %collective-permute-start.4 = (f32[1,128,512]{2,1,0:T(8,128)S(1)}, f32[1,128,512]{2,1,0:T(8,128)S(1)}, u32[]{:S(2)}, u32[]{:S(2)}) collective-permute-start(f32[1,128,512]{2,1,0:T(8,128)S(1)} %collective-permute-done.1.refs_0_), channel_id=1, source_target_pairs={{0,4},{4,0},{1,5},{5,1},{2,6},{6,2},{3,7},{7,3},{8,12},{12,8},{9,1... | collective-permute-start | bytes 786440 | tf_op jit(solution)/shard_map/ppermute | solution.py:238
  31.0 8.7 %collective-permute-start.7 = (f32[6,32,256]{2,1,0:T(8,128)S(1)}, f32[6,32,256]{2,1,0:T(8,128)S(1)}, u32[]{:S(2)}, u32[]{:S(2)}) collective-permute-start(f32[6,32,256]{2,1,0:T(8,128)S(1)} %get-tuple-element.42), channel_id=1, source_target_pairs={{0,3},{1,2},{2,1},{3,0},{4,7},{5,6},{6,5},{7,4},{8,11},{9,10},{10,... | collective-permute-start | bytes 589832 | tf_op jit(solution)/shard_map/ppermute | solution.py:266
  33.3 10.1 %collective-permute-start.8 = (f32[6,32,256]{2,1,0:T(8,128)S(1)}, f32[6,32,256]{2,1,0:T(8,128)S(1)}, u32[]{:S(2)}, u32[]{:S(2)}) collective-permute-start(f32[6,32,256]{2,1,0:T(8,128)S(1)} %get-tuple-element.43), channel_id=1, source_target_pairs={{0,1},{1,0},{2,3},{3,2},{4,5},{5,4},{6,7},{7,6},{8,9},{9,8},{10,11... | collective-permute-start | bytes 589832 | tf_op jit(solution)/shard_map/ppermute | solution.py:266
  33.8 9.7 %collective-permute-start.9 = (f32[6,32,256]{2,1,0:T(8,128)S(1)}, f32[6,32,256]{2,1,0:T(8,128)S(1)}, u32[]{:S(2)}, u32[]{:S(2)}) collective-permute-start(f32[6,32,256]{2,1,0:T(8,128)S(1)} %get-tuple-element.44), channel_id=1, source_target_pairs={{0,2},{1,3},{2,0},{3,1},{4,6},{5,7},{6,4},{7,5},{8,10},{9,11},{10,... | collective-permute-start | bytes 589832 | tf_op jit(solution)/shard_map/ppermute | solution.py:266

commit v4 on v3

--- a/solution.py
+++ b/solution.py
@@ -55,8 +55,7 @@
     pairs, domv, _ = amplitudes.shape
     left_half = left_of(1)
 
-    @pl.loop(0, pairs)
-    def _(p):
+    for p in range(pairs):
         for j in range(domv // LANES):
             row = jnp.where(left_half, scalars.flag(2 * j, p), scalars.flag(2 * j + 1, p))
             lanes = slice(j * LANES, (j + 1) * LANES)
@@ -86,9 +85,8 @@
     per_slot = rows // BS
     left_half = left_of(1)
 
-    @pl.loop(0, tiles)
-    def _(t):
-        lanes = pl.ds(pl.multiple_of(t * LANES, LANES), LANES)
+    for t in range(tiles):
+        lanes = slice(t * LANES, (t + 1) * LANES)
         for h in range(per_slot):
             block = (scalars.place(0) ^ slot) * per_slot + h
             row = jnp.where(left_half, scalars.kept(block, 2 * t), scalars.kept(block, 2 * t + 1))
@@ -127,11 +125,14 @@
     scalars = read(info)
     pieces = refs[:len(late)]
     mhigh, mlow, _, _ = refs[len(late):len(late) + 4]
-    outs = refs[len(late) + 4:-4]
-    high, low, yhigh, ylow = refs[-4:]
+    outs = refs[len(late) + 4:-2]
+    high, low = refs[-2:]
     z, r = scalars.place(0), scalars.place(1)
     for (slot, q), piece in zip(late, pieces):
-        screen_piece(scalars, piece, q, slot, high, low)
+
+        @pl.when(z >= 0)
+        def _():
+            screen_piece(scalars, piece, q, slot, high, low)
 
     pairs, chunk, domv = outs[0].shape
     twice, qs, window, _ = high.shape
@@ -144,8 +145,7 @@
     along = (((1,), (0,)), ((), ()))
     dot = functools.partial(lax.dot_general, preferred_element_type=jnp.float32)
 
-    @pl.loop(0, pairs)
-    def _(p):
+    def contract(p):
         def rows_of(at, offset, size):
             block = scalars.domain(at, p)
             start = ((block // per_slot) ^ z) * rows + (block % per_slot) * BS + offset
@@ -155,31 +155,30 @@
         for j in range(domv // LANES):
             first, second = scalars.domain(2 * j, p), scalars.domain(2 * j + 1, p)
             sources.append(((first % 2) * tiles + first // 2, (1 - second % 2) * tiles + second // 2))
+
+        def gather(source, q, spans, size):
+            return jnp.concatenate([jnp.concatenate([
+                jnp.where(left_of(size), source[a, q, span, :], source[b, q, span, :]) for a, b in sources], 1)
+                for span in spans], 0)
+
         spans = [rows_of(i, 0, BS) for i in range(domv // BS)]
-        xs = []
-        for source, target in ((high, yhigh), (low, ylow)):
-            for j, (a, b) in enumerate(sources):
-                for i, span in enumerate(spans):
-                    for q in range(qs):
-                        lanes = slice(q * domv + j * LANES, q * domv + (j + 1) * LANES)
-                        target[i * BS:(i + 1) * BS, lanes] = jnp.where(
-                            left_of(BS), source[a, q, span, :], source[b, q, span, :])
-            parts = []
-            for q in range(qs):
-                for pick in picks:
-                    span = rows_of(pick // BS, pick % BS, chunk)
-                    parts.append(jnp.concatenate([jnp.where(
-                        left_of(chunk), source[a, q, span, :], source[b, q, span, :]) for a, b in sources], 1))
-            xs.append(jnp.concatenate(parts, 0))
-        xhigh, xlow = xs
-        halfway = dot(xhigh, mhigh[p], along) + dot(xhigh, mlow[p], along) + dot(xlow, mhigh[p], along)
+        yhigh, ylow = (jnp.concatenate([gather(source, q, spans, BS) for q in range(qs)], 1) for source in (high, low))
+        spans = [rows_of(pick // BS, pick % BS, chunk) for pick in picks]
+        xhigh, xlow = (jnp.concatenate([gather(source, q, spans, chunk) for q in range(qs)], 0) for source in (high, low))
+        both = dot(jnp.concatenate([xhigh, xlow], 0), mhigh[p], along)
+        size = qs * half
+        halfway = both[:size] + both[size:] + dot(xhigh, mlow[p], along)
         hhigh, hlow = split(jnp.concatenate([halfway[q * half:(q + 1) * half] for q in range(qs)], 1))
-        total = dot(hhigh, yhigh[...], across) + dot(hhigh, ylow[...], across) + dot(hlow, yhigh[...], across)
+        both = dot(jnp.concatenate([hhigh, hlow], 0), yhigh, across)
+        total = both[:half] + both[half:] + dot(hhigh, ylow, across)
         for j in range(domv // LANES):
             weights = jnp.where(left_of(1), scalars.flag(2 * j, p), scalars.flag(2 * j + 1, p))
             for n, (pick, out) in enumerate(zip(picks, outs)):
                 out[p, :, j * LANES:(j + 1) * LANES] = total[
                     n * chunk:(n + 1) * chunk, j * LANES:(j + 1) * LANES] * (weights * scalars.flag(pick // BS, p))
+
+    for p in range(pairs):
+        contract(p)
 
 
 def contract_pairs(read, row, col, line, info, late, mhigh, mlow, high, low):
@@ -196,7 +195,6 @@
         + [jax.ShapeDtypeStruct(high.shape, high.dtype)] * 2,
         in_specs=[SMEM_SPEC] + [VMEM_SPEC] * (len(pieces) + 4),
         out_specs=[VMEM_SPEC] * (col + 2),
-        scratch_shapes=[pltpu.VMEM((domv, qs * domv), jnp.bfloat16)] * 2,
         input_output_aliases={held: col, held + 1: col + 1},
         compiler_params=pltpu.CompilerParams(vmem_limit_bytes=VMEM_LIMIT),
         cost_estimate=pl.CostEstimate(flops=6 * pairs * qs * domv ** 3 * 4 // row, bytes_accessed=8 * high.size,

time: 44.4 us -> 41 us (0.923)
  Pallas kernels: 11.5 us -> 6.62 us
  waiting for transfers between devices: 17.5 us -> 19 us
    pallas_call x1, Pallas kernels: 5.54 us -> 2.7 us  [contract_pairs(): pl.pallas_call(functools.partial(pairs_kernel, read, row, line, keys), na...]
    pallas_call x3, Pallas kernels: 4.33 us -> 2.35 us  [screen(): pl.pallas_call(functools.partial(screen_kernel, read, keys), name='screen...]
    ppermute x3, waiting for transfers between devices: 8.55 us -> 9.71 us  [across(): return lax.ppermute(piece, 'wide', [(i, i ^ shift) for i in range(wide)])]
    ppermute x4, waiting for transfers between devices: 0.01 us -> 0.7 us  [siblings(): lax.ppermute(piece, 'row', [(i, (i + s) % row) for i in range(row)])]
  transfers between devices with their start and end apart: 10 -> 10, of which waited for: 5 -> 6; matrix products, arithmetic and copies ran while one was open for 5% -> 6% of each run, Pallas kernels for 12% -> 8%
where the time goes in v4:
time: 41 us; the launch traced here: 40.8 us
  waiting for transfers between devices  19 us (46%)
  starting transfers between devices  10.4 us (25%)
  Pallas kernels  6.62 us (16%)
  local copies, waits for them, and re-layouts  4.73 us (12%)
    ppermute x3, waiting for transfers between devices, across(): return lax.ppermute(piece, 'wide', [(i, i ^ shift) for i in range(wide)])  9.71 us
    ppermute x3, waiting for transfers between devices, body(): lax.ppermute(terms[s], 'col', [(i, partner(i, s, col)) for i in range(col)])  8.57 us
    ppermute x3, starting transfers between devices, across(): return lax.ppermute(piece, 'wide', [(i, i ^ shift) for i in range(wide)])  6.33 us
    ppermute x3, starting transfers between devices, body(): lax.ppermute(terms[s], 'col', [(i, partner(i, s, col)) for i in range(col)])  3.55 us
    pallas_call x1, Pallas kernels, contract_pairs(): pl.pallas_call(functools.partial(pairs_kernel, read, row, line, keys), na...  2.7 us
    unnamed x4, local copies, waits for them, and re-layouts  2.36 us
    pallas_call x3, Pallas kernels, screen(): pl.pallas_call(functools.partial(screen_kernel, read, keys), name='screen...  2.35 us
    pallas_call x1, Pallas kernels, mask_amplitudes(): pl.pallas_call(functools.partial(mask_amplitudes_kernel, read), name='mas...  0.87 us
  transfers between devices with their start and end apart: 10, of which 6 were waited for; matrix products, arithmetic and copies ran while one was open for 6% of the time, Pallas kernels for 8%

profile of v4, /device:TPU:0, one launch (start us, length us, event | category | flops | bytes accessed | tf_op | source)
XLA Modules:
  0.0 40.8 jit_solution(7803050549347369932)
XLA Ops:
  0.0 4.0 %collective-permute-start = (f32[1,128,512]{2,1,0:T(8,128)}, f32[1,128,512]{2,1,0:T(8,128)S(1)}, u32[]{:S(2)}, u32[]{:S(2)}) collective-permute-start(f32[1,128,512]{2,1,0:T(8,128)} %refs_0_.1), channel_id=1, source_target_pairs={{0,16},{8,24},{16,0},{24,8},{1,17},{9,25},{17,1},{25,9},{2,18},{10... | collective-permute-start | bytes 786440 | tf_op jit(solution)/shard_map/ppermute | solution.py:239
  4.0 1.6 %collective-permute-start.3 = (f32[1,128,512]{2,1,0:T(8,128)}, f32[1,128,512]{2,1,0:T(8,128)S(1)}, u32[]{:S(2)}, u32[]{:S(2)}) collective-permute-start(f32[1,128,512]{2,1,0:T(8,128)} %refs_0_.1), channel_id=1, source_target_pairs={{0,8},{8,0},{16,24},{24,16},{1,9},{9,1},{17,25},{25,17},{2,10},{10... | collective-permute-start | bytes 786440 | tf_op jit(solution)/shard_map/ppermute | solution.py:239
  5.6 0.0 collective-permute-start.2
  5.6 0.8 %reshape.9 = s32[24]{0:T(128)S(1)} reshape(s32[4,6]{1,0:T(4,128)} %bitcast.8) | data formatting | bytes 192 | tf_op jit(solution)/shard_map/reshape | solution.py:230
  6.4 0.8 %reshape.10 = s32[24]{0:T(128)S(1)} reshape(s32[4,6]{1,0:T(4,128)} %bitcast.9) | data formatting | bytes 192 | tf_op jit(solution)/shard_map/reshape | solution.py:230
  7.1 0.8 %reshape.11 = s32[64]{0:T(128)S(1)} reshape(s32[8,8]{1,0:T(8,128)} %param.9) | data formatting | bytes 512 | tf_op jit(solution)/shard_map/reshape | solution.py:230
  7.9 0.1 concatenate.3.info
  8.0 0.0 copy-start.1
  8.0 1.0 %copy-done.1 = f32[1,128,512]{2,1,0:T(8,128)S(1)} copy-done((f32[1,128,512]{2,1,0:T(8,128)S(1)}, f32[1,128,512]{2,1,0:T(8,128)}, u32[]{:S(2)}) %copy-start.1) | copy-done | bytes 262168
  9.0 0.7 %screen_factors.3 = (bf16[8,2,512,128]{3,2,1,0:T(8,128)(2,1)S(1)}, bf16[8,2,512,128]{3,2,1,0:T(8,128)(2,1)S(1)}) custom-call(s32[118]{0:T(128)S(1)} %concatenate.3.info, f32[1,128,512]{2,1,0:T(8,128)S(1)} %copy-done.1), custom_call_target="tpu_custom_call" | custom-call | flops 524288 | bytes 786432 | tf_op jit(solution)/shard_map/screen_factors/pallas_call | solution.py:112
  9.6 0.0 copy-start
  9.7 1.4 %copy-done = f32[6,256,256]{2,1,0:T(8,128)S(1)} copy-done((f32[6,256,256]{2,1,0:T(8,128)S(1)}, f32[6,256,256]{2,1,0:T(8,128)}, u32[]{:S(2)}) %copy-start) | copy-done | bytes 1572888
  11.1 0.9 %mask_amplitudes.1 = (bf16[6,256,256]{2,1,0:T(8,128)(2,1)S(1)}, bf16[6,256,256]{2,1,0:T(8,128)(2,1)S(1)}) custom-call(s32[118]{0:T(128)S(1)} %concatenate.3.info, f32[6,256,256]{2,1,0:T(8,128)S(1)} %copy-done), custom_call_target="tpu_custom_call" | custom-call | flops 1572864 | bytes 3145728 | tf_op jit(solution)/shard_map/mask_amplitudes/pallas_call | solution.py:71
  11.9 4.3 %collective-permute-done.refs_2_ = f32[1,128,512]{2,1,0:T(8,128)S(1)} collective-permute-done((f32[1,128,512]{2,1,0:T(8,128)}, f32[1,128,512]{2,1,0:T(8,128)S(1)}, u32[]{:S(2)}, u32[]{:S(2)}) %collective-permute-start) | collective-permute-done | bytes 262176 | tf_op jit(solution)/shard_map/ppermute | solution.py:239
  16.3 0.7 %collective-permute-start.1 = (f32[1,128,512]{2,1,0:T(8,128)S(1)}, f32[1,128,512]{2,1,0:T(8,128)S(1)}, u32[]{:S(2)}, u32[]{:S(2)}) collective-permute-start(f32[1,128,512]{2,1,0:T(8,128)S(1)} %collective-permute-done.refs_2_), channel_id=1, source_target_pairs={{0,8},{8,0},{16,24},{24,16},{1,9},{9,1},{17,25},{25,17},{2,10},{10... | collective-permute-start | bytes 786440 | tf_op jit(solution)/shard_map/ppermute | solution.py:239
  17.0 0.0 collective-permute-start.6
  17.0 0.0 collective-permute-done.3.refs_1_
  17.0 0.5 %collective-permute-start.5 = (f32[1,128,512]{2,1,0:T(8,128)S(1)}, f32[1,128,512]{2,1,0:T(8,128)S(1)}, u32[]{:S(2)}, u32[]{:S(2)}) collective-permute-start(f32[1,128,512]{2,1,0:T(8,128)S(1)} %collective-permute-done.3.refs_1_), channel_id=1, source_target_pairs={{0,4},{4,0},{1,5},{5,1},{2,6},{6,2},{3,7},{7,3},{8,12},{12,8},{9,1... | collective-permute-start | bytes 786440 | tf_op jit(solution)/shard_map/ppermute | solution.py:236
  17.5 0.0 collective-permute-done.2.refs_0_
  17.5 0.8 %screen_factors.4 = (bf16[8,2,512,128]{3,2,1,0:T(8,128)(2,1)S(1)}, bf16[8,2,512,128]{3,2,1,0:T(8,128)(2,1)S(1)}) custom-call(s32[118]{0:T(128)S(1)} %concatenate.3.info, f32[1,128,512]{2,1,0:T(8,128)S(1)} %collective-permute-done.2.refs_0_, f32[1,128,512]{2,1,0:T(8,128)S(1)} %collective-permute-done.3.refs_1_, ...), custom_call_target="tpu_custom_call", output_to_operand_aliasing={{0}: (4, {}), {1}: (5, {})} | custom-call | flops 1572864 | bytes 2359296 | tf_op jit(solution)/shard_map/screen_factors/pallas_call | solution.py:112
  18.3 5.4 %collective-permute-done.1.refs_0_ = f32[1,128,512]{2,1,0:T(8,128)S(1)} collective-permute-done((f32[1,128,512]{2,1,0:T(8,128)S(1)}, f32[1,128,512]{2,1,0:T(8,128)S(1)}, u32[]{:S(2)}, u32[]{:S(2)}) %collective-permute-start.1) | collective-permute-done | bytes 262176 | tf_op jit(solution)/shard_map/ppermute | solution.py:239
  23.7 0.0 collective-permute-start.4
  23.7 0.0 collective-permute-done.5.refs_1_
  23.7 0.0 collective-permute-done.6.refs_2_
  23.7 0.8 %screen_factors.5 = (bf16[8,2,512,128]{3,2,1,0:T(8,128)(2,1)S(1)}, bf16[8,2,512,128]{3,2,1,0:T(8,128)(2,1)S(1)}) custom-call(s32[118]{0:T(128)S(1)} %concatenate.3.info, f32[1,128,512]{2,1,0:T(8,128)S(1)} %collective-permute-done.1.refs_0_, f32[1,128,512]{2,1,0:T(8,128)S(1)} %collective-permute-done.5.refs_1_, ...), custom_call_target="tpu_custom_call", output_to_operand_aliasing={{0}: (4, {}), {1}: (5, {})} | custom-call | flops 1572864 | bytes 2359296 | tf_op jit(solution)/shard_map/screen_factors/pallas_call | solution.py:112
  24.6 0.7 %collective-permute-done.4.refs_0_ = f32[1,128,512]{2,1,0:T(8,128)S(1)} collective-permute-done((f32[1,128,512]{2,1,0:T(8,128)S(1)}, f32[1,128,512]{2,1,0:T(8,128)S(1)}, u32[]{:S(2)}, u32[]{:S(2)}) %collective-permute-start.4) | collective-permute-done | bytes 262176 | tf_op jit(solution)/shard_map/ppermute | solution.py:236
  25.2 2.7 %contract_pairs.1 = (f32[6,32,256]{2,1,0:T(8,128)S(1)}, f32[6,32,256]{2,1,0:T(8,128)S(1)}, f32[6,32,256]{2,1,0:T(8,128)S(1)}, f32[6,32,256]{2,1,0:T(8,128)S(1)},...) custom-call(s32[118]{0:T(128)S(1)} %concatenate.3.info, ...), custom_call_target="tpu_custom_call", output_to_operand_aliasing={{4}: (4, {}), {5}: (5, {})} | custom-call | flops 2415919104 | bytes 8388608 | tf_op jit(solution)/shard_map/contract_pairs/pallas_call | solution.py:191
  28.0 2.3 %collective-permute-start.7 = (f32[6,32,256]{2,1,0:T(8,128)S(1)}, f32[6,32,256]{2,1,0:T(8,128)S(1)}, u32[]{:S(2)}, u32[]{:S(2)}) collective-permute-start(f32[6,32,256]{2,1,0:T(8,128)S(1)} %get-tuple-element.42), channel_id=1, source_target_pairs={{0,3},{1,2},{2,1},{3,0},{4,7},{5,6},{6,5},{7,4},{8,11},{9,10},{10,... | collective-permute-start | bytes 589832 | tf_op jit(solution)/shard_map/ppermute | solution.py:264
  30.2 0.6 %collective-permute-start.8 = (f32[6,32,256]{2,1,0:T(8,128)S(1)}, f32[6,32,256]{2,1,0:T(8,128)S(1)}, u32[]{:S(2)}, u32[]{:S(2)}) collective-permute-start(f32[6,32,256]{2,1,0:T(8,128)S(1)} %get-tuple-element.43), channel_id=1, source_target_pairs={{0,1},{1,0},{2,3},{3,2},{4,5},{5,4},{6,7},{7,6},{8,9},{9,8},{10,11... | collective-permute-start | bytes 589832 | tf_op jit(solution)/shard_map/ppermute | solution.py:264
  30.8 0.7 %collective-permute-start.9 = (f32[6,32,256]{2,1,0:T(8,128)S(1)}, f32[6,32,256]{2,1,0:T(8,128)S(1)}, u32[]{:S(2)}, u32[]{:S(2)}) collective-permute-start(f32[6,32,256]{2,1,0:T(8,128)S(1)} %get-tuple-element.44), channel_id=1, source_target_pairs={{0,2},{1,3},{2,0},{3,1},{4,6},{5,7},{6,4},{7,5},{8,10},{9,11},{10,... | collective-permute-start | bytes 589832 | tf_op jit(solution)/shard_map/ppermute | solution.py:264
  31.5 5.2 %collective-permute-done.7.refs_1_ = f32[6,32,256]{2,1,0:T(8,128)S(1)} collective-permute-done((f32[6,32,256]{2,1,0:T(8,128)S(1)}, f32[6,32,256]{2,1,0:T(8,128)S(1)}, u32[]{:S(2)}, u32[]{:S(2)}) %collective-permute-start.7) | collective-permute-done | bytes 196640 | tf_op jit(solution)/shard_map/ppermute | solution.py:264
  36.7 3.2 %collective-permute-done.8.refs_2_ = f32[6,32,256]{2,1,0:T(8,128)S(1)} collective-permute-done((f32[6,32,256]{2,1,0:T(8,128)S(1)}, f32[6,32,256]{2,1,0:T(8,128)S(1)}, u32[]{:S(2)}, u32[]{:S(2)}) %collective-permute-start.8) | collective-permute-done | bytes 196640 | tf_op jit(solution)/shard_map/ppermute | solution.py:264
  39.9 0.1 collective-permute-done.9.refs_3_
  40.1 0.7 %add_terms.1 = f32[6,32,256]{2,1,0:T(8,128)} custom-call(f32[6,32,256]{2,1,0:T(8,128)S(1)} %get-tuple-element.41.refs_0_, f32[6,32,256]{2,1,0:T(8,128)S(1)} %collective-permute-done.7.refs_1_, f32[6,32,256]{2,1,0:T(8,128)S(1)} %collective-permute-done.8.refs_2_, f32[6,32,256]{2,1,0:T(8,128)S(1)} %collective-permute-done.9.refs_3_), custom_call_target="tpu_custom_call" | custom-call | tf_op jit(solution)/shard_map/add_terms/pallas_call | solution.py:214
Async XLA Ops:
  0.0 16.3 %collective-permute-start = (f32[1,128,512]{2,1,0:T(8,128)}, f32[1,128,512]{2,1,0:T(8,128)S(1)}, u32[]{:S(2)}, u32[]{:S(2)}) collective-permute-start(f32[1,128,512]{2,1,0:T(8,128)} %refs_0_.1), channel_id=1, source_target_pairs={{0,16},{8,24},{16,0},{24,8},{1,17},{9,25},{17,1},{25,9},{2,18},{10... | collective-permute-start | bytes 786440 | tf_op jit(solution)/shard_map/ppermute | solution.py:239
  4.0 13.0 %collective-permute-start.3 = (f32[1,128,512]{2,1,0:T(8,128)}, f32[1,128,512]{2,1,0:T(8,128)S(1)}, u32[]{:S(2)}, u32[]{:S(2)}) collective-permute-start(f32[1,128,512]{2,1,0:T(8,128)} %refs_0_.1), channel_id=1, source_target_pairs={{0,8},{8,0},{16,24},{24,16},{1,9},{9,1},{17,25},{25,17},{2,10},{10... | collective-permute-start | bytes 786440 | tf_op jit(solution)/shard_map/ppermute | solution.py:239
  5.6 11.9 %collective-permute-start.2 = (f32[1,128,512]{2,1,0:T(8,128)}, f32[1,128,512]{2,1,0:T(8,128)S(1)}, u32[]{:S(2)}, u32[]{:S(2)}) collective-permute-start(f32[1,128,512]{2,1,0:T(8,128)} %refs_0_.1), channel_id=1, source_target_pairs={{0,4},{4,0},{1,5},{5,1},{2,6},{6,2},{3,7},{7,3},{8,12},{12,8},{9,1... | collective-permute-start | bytes 786440 | tf_op jit(solution)/shard_map/ppermute | solution.py:236
  8.0 1.0 %copy-start.1 = (f32[1,128,512]{2,1,0:T(8,128)S(1)}, f32[1,128,512]{2,1,0:T(8,128)}, u32[]{:S(2)}) copy-start(f32[1,128,512]{2,1,0:T(8,128)} %refs_0_.1) | copy-start | bytes 786436
  9.6 1.4 %copy-start = (f32[6,256,256]{2,1,0:T(8,128)S(1)}, f32[6,256,256]{2,1,0:T(8,128)}, u32[]{:S(2)}) copy-start(f32[6,256,256]{2,1,0:T(8,128)} %amplitudes.1) | copy-start | bytes 4718596
  16.3 7.4 %collective-permute-start.1 = (f32[1,128,512]{2,1,0:T(8,128)S(1)}, f32[1,128,512]{2,1,0:T(8,128)S(1)}, u32[]{:S(2)}, u32[]{:S(2)}) collective-permute-start(f32[1,128,512]{2,1,0:T(8,128)S(1)} %collective-permute-done.refs_2_), channel_id=1, source_target_pairs={{0,8},{8,0},{16,24},{24,16},{1,9},{9,1},{17,25},{25,17},{2,10},{10... | collective-permute-start | bytes 786440 | tf_op jit(solution)/shard_map/ppermute | solution.py:239
  17.0 6.7 %collective-permute-start.6 = (f32[1,128,512]{2,1,0:T(8,128)S(1)}, f32[1,128,512]{2,1,0:T(8,128)S(1)}, u32[]{:S(2)}, u32[]{:S(2)}) collective-permute-start(f32[1,128,512]{2,1,0:T(8,128)S(1)} %collective-permute-done.refs_2_), channel_id=1, source_target_pairs={{0,4},{4,0},{1,5},{5,1},{2,6},{6,2},{3,7},{7,3},{8,12},{12,8},{9,1... | collective-permute-start | bytes 786440 | tf_op jit(solution)/shard_map/ppermute | solution.py:236
  17.0 6.7 %collective-permute-start.5 = (f32[1,128,512]{2,1,0:T(8,128)S(1)}, f32[1,128,512]{2,1,0:T(8,128)S(1)}, u32[]{:S(2)}, u32[]{:S(2)}) collective-permute-start(f32[1,128,512]{2,1,0:T(8,128)S(1)} %collective-permute-done.3.refs_1_), channel_id=1, source_target_pairs={{0,4},{4,0},{1,5},{5,1},{2,6},{6,2},{3,7},{7,3},{8,12},{12,8},{9,1... | collective-permute-start | bytes 786440 | tf_op jit(solution)/shard_map/ppermute | solution.py:236
  23.7 1.5 %collective-permute-start.4 = (f32[1,128,512]{2,1,0:T(8,128)S(1)}, f32[1,128,512]{2,1,0:T(8,128)S(1)}, u32[]{:S(2)}, u32[]{:S(2)}) collective-permute-start(f32[1,128,512]{2,1,0:T(8,128)S(1)} %collective-permute-done.1.refs_0_), channel_id=1, source_target_pairs={{0,4},{4,0},{1,5},{5,1},{2,6},{6,2},{3,7},{7,3},{8,12},{12,8},{9,1... | collective-permute-start | bytes 786440 | tf_op jit(solution)/shard_map/ppermute | solution.py:236
  28.0 8.8 %collective-permute-start.7 = (f32[6,32,256]{2,1,0:T(8,128)S(1)}, f32[6,32,256]{2,1,0:T(8,128)S(1)}, u32[]{:S(2)}, u32[]{:S(2)}) collective-permute-start(f32[6,32,256]{2,1,0:T(8,128)S(1)} %get-tuple-element.42), channel_id=1, source_target_pairs={{0,3},{1,2},{2,1},{3,0},{4,7},{5,6},{6,5},{7,4},{8,11},{9,10},{10,... | collective-permute-start | bytes 589832 | tf_op jit(solution)/shard_map/ppermute | solution.py:264
  30.2 9.7 %collective-permute-start.8 = (f32[6,32,256]{2,1,0:T(8,128)S(1)}, f32[6,32,256]{2,1,0:T(8,128)S(1)}, u32[]{:S(2)}, u32[]{:S(2)}) collective-permute-start(f32[6,32,256]{2,1,0:T(8,128)S(1)} %get-tuple-element.43), channel_id=1, source_target_pairs={{0,1},{1,0},{2,3},{3,2},{4,5},{5,4},{6,7},{7,6},{8,9},{9,8},{10,11... | collective-permute-start | bytes 589832 | tf_op jit(solution)/shard_map/ppermute | solution.py:264
  30.8 9.3 %collective-permute-start.9 = (f32[6,32,256]{2,1,0:T(8,128)S(1)}, f32[6,32,256]{2,1,0:T(8,128)S(1)}, u32[]{:S(2)}, u32[]{:S(2)}) collective-permute-start(f32[6,32,256]{2,1,0:T(8,128)S(1)} %get-tuple-element.44), channel_id=1, source_target_pairs={{0,2},{1,3},{2,0},{3,1},{4,6},{5,7},{6,4},{7,5},{8,10},{9,11},{10,... | collective-permute-start | bytes 589832 | tf_op jit(solution)/shard_map/ppermute | solution.py:264

commit v5 on v4

--- a/solution.py
+++ b/solution.py
@@ -20,10 +20,8 @@
     return top, (value - top.astype(jnp.float32)).astype(jnp.bfloat16)
 
 
-def partner(index, shift, size):
-    if size & (size - 1) == 0:
-        return index ^ shift
-    return (index + shift) % size
+def axis_of(r, order):
+    return 1 + (r + order) % 2
 
 
 def left_of(rows):
@@ -31,9 +29,9 @@
 
 
 class Scalars:
-    def __init__(self, info, col, pairs, dom, blocks):
+    def __init__(self, info, places, pairs, dom, blocks):
         self.info, self.pairs, self.blocks = info, pairs, blocks
-        self.domains = 2 + col
+        self.domains = places
         self.flags = self.domains + dom * pairs
         self.mask = self.flags + dom * pairs
 
@@ -121,11 +119,11 @@
     )(info, *pieces, *held)
 
 
-def pairs_kernel(read, row, line, late, info, *refs):
+def pairs_kernel(read, row, line, layout, late, info, *refs):
     scalars = read(info)
     pieces = refs[:len(late)]
     mhigh, mlow, _, _ = refs[len(late):len(late) + 4]
-    outs = refs[len(late) + 4:-2]
+    outs = list(refs[len(late) + 4:-2])
     high, low = refs[-2:]
     z, r = scalars.place(0), scalars.place(1)
     for (slot, q), piece in zip(late, pieces):
@@ -134,18 +132,17 @@
         def _():
             screen_piece(scalars, piece, q, slot, high, low)
 
-    pairs, chunk, domv = outs[0].shape
+    chunk, domv = outs[0].shape[-2:]
     twice, qs, window, _ = high.shape
     tiles = twice // 2
     rows = window // line
     per_slot = rows // BS
     half = domv // row
-    picks = [r * half + scalars.place(2 + s) * chunk for s in range(len(outs))]
     across = (((1,), (1,)), ((), ()))
     along = (((1,), (0,)), ((), ()))
     dot = functools.partial(lax.dot_general, preferred_element_type=jnp.float32)
 
-    def contract(p):
+    def contract(p, picks, targets):
         def rows_of(at, offset, size):
             block = scalars.domain(at, p)
             start = ((block // per_slot) ^ z) * rows + (block % per_slot) * BS + offset
@@ -172,53 +169,83 @@
         both = dot(jnp.concatenate([hhigh, hlow], 0), yhigh, across)
         total = both[:half] + both[half:] + dot(hhigh, ylow, across)
         for j in range(domv // LANES):
+            lanes = slice(j * LANES, (j + 1) * LANES)
             weights = jnp.where(left_of(1), scalars.flag(2 * j, p), scalars.flag(2 * j + 1, p))
-            for n, (pick, out) in enumerate(zip(picks, outs)):
-                out[p, :, j * LANES:(j + 1) * LANES] = total[
-                    n * chunk:(n + 1) * chunk, j * LANES:(j + 1) * LANES] * (weights * scalars.flag(pick // BS, p))
-
-    for p in range(pairs):
-        contract(p)
-
-
-def contract_pairs(read, row, col, line, info, late, mhigh, mlow, high, low):
-    pairs, domv, _ = mhigh.shape
-    chunk = domv // (row * col)
-    qs = high.shape[1]
+            for n, (pick, (target, at, pair)) in enumerate(zip(picks, targets)):
+                target[at, pair, :, lanes] = total[n * chunk:(n + 1) * chunk, lanes] * (weights * scalars.flag(pick // BS, p))
+
+    for first, count, parts in layout:
+        refs_of = [outs.pop(0) for _ in parts]
+        picks = [r * half + scalars.place(at) * chunk for part in parts for at in part]
+        for n in range(count):
+            targets = [(ref, i, n) for ref, part in zip(refs_of, parts) for i in range(len(part))]
+            contract(scalars.place(first) + n, picks, targets)
+
+
+def contract_pairs(read, row, line, layout, info, late, mhigh, mlow, high, low):
+    domv = mhigh.shape[1]
+    chunk = domv // (row * sum(len(part) for part in layout[0][2]))
     keys = [(slot, q) for slot, q, _ in late]
     pieces = [piece for _, _, piece in late]
     held = 1 + len(pieces) + 2
+    shapes = [jax.ShapeDtypeStruct((len(part), count, chunk, domv), jnp.float32) for _, count, parts in layout for part in parts]
+    outs = len(shapes)
     results = pl.pallas_call(
-        functools.partial(pairs_kernel, read, row, line, keys),
+        functools.partial(pairs_kernel, read, row, line, layout, keys),
         name="contract_pairs",
-        out_shape=[jax.ShapeDtypeStruct((pairs, chunk, domv), jnp.float32)] * col
-        + [jax.ShapeDtypeStruct(high.shape, high.dtype)] * 2,
+        out_shape=shapes + [jax.ShapeDtypeStruct(high.shape, high.dtype)] * 2,
         in_specs=[SMEM_SPEC] + [VMEM_SPEC] * (len(pieces) + 4),
-        out_specs=[VMEM_SPEC] * (col + 2),
-        input_output_aliases={held: col, held + 1: col + 1},
-        compiler_params=pltpu.CompilerParams(vmem_limit_bytes=VMEM_LIMIT),
-        cost_estimate=pl.CostEstimate(flops=6 * pairs * qs * domv ** 3 * 4 // row, bytes_accessed=8 * high.size,
-                                      transcendentals=0),
+        out_specs=[VMEM_SPEC] * (outs + 2),
+        input_output_aliases={held: outs, held + 1: outs + 1},
+        compiler_params=pltpu.CompilerParams(vmem_limit_bytes=VMEM_LIMIT),
+        cost_estimate=pl.CostEstimate(flops=6 * mhigh.shape[0] * high.shape[1] * domv ** 3 * 4 // row,
+                                      bytes_accessed=8 * high.size, transcendentals=0),
     )(info, *pieces, mhigh, mlow, high, low)
-    return results[:col]
-
-
-def add_kernel(*refs):
-    total = refs[0][...]
-    for ref in refs[1:-1]:
-        total += ref[...]
-    refs[-1][...] = total
-
-
-def add_terms(*terms):
+    return results[:outs]
+
+
+def add_one_kernel(at, a, b, out):
+    out[...] = a[at] + b[at]
+
+
+def add_one(at, a, b):
     return pl.pallas_call(
-        add_kernel,
-        name="add_terms",
-        out_shape=jax.ShapeDtypeStruct(terms[0].shape, jnp.float32),
-        in_specs=[VMEM_SPEC] * len(terms),
+        functools.partial(add_one_kernel, at),
+        name="add_one",
+        out_shape=jax.ShapeDtypeStruct(a.shape[1:], jnp.float32),
+        in_specs=[VMEM_SPEC] * 2,
         out_specs=VMEM_SPEC,
         compiler_params=pltpu.CompilerParams(vmem_limit_bytes=VMEM_LIMIT),
-    )(*terms)
+    )(a, b)
+
+
+def join_kernel(*refs):
+    out = refs[-1]
+    count = refs[0].shape[1]
+    r = lax.axis_index("row")
+    for order in range(2):
+        kept, other, last = refs[3 * order:3 * order + 3]
+        out[pl.ds((r + order) % 2 * count, count)] = kept[0] + other[0] + last[...]
+
+
+def halve(row, col, terms):
+    def along(order):
+        return [(i * col + k, i * col + (k ^ axis_of(i, order))) for i in range(row) for k in range(col)]
+
+    (sent_a, kept_a, sent_b, kept_b) = terms
+    moved_a = lax.ppermute(sent_a, ("row", "col"), along(0))
+    moved_b = lax.ppermute(sent_b, ("row", "col"), along(1))
+    last_a = lax.ppermute(add_one(1, kept_a, moved_a), ("row", "col"), along(1))
+    last_b = lax.ppermute(add_one(1, kept_b, moved_b), ("row", "col"), along(0))
+    count = kept_a.shape[1]
+    return pl.pallas_call(
+        join_kernel,
+        name="join_groups",
+        out_shape=jax.ShapeDtypeStruct((2 * count,) + kept_a.shape[2:], jnp.float32),
+        in_specs=[VMEM_SPEC] * 6,
+        out_specs=VMEM_SPEC,
+        compiler_params=pltpu.CompilerParams(vmem_limit_bytes=VMEM_LIMIT),
+    )(kept_a, moved_a, last_a, kept_b, moved_b, last_b)
 
 
 def body(wide, row, col, amplitudes, factors, domains, domain_mask, block_mask):
@@ -226,11 +253,23 @@
     pairs, dom = domains.shape
     z, r, c = lax.axis_index("wide"), lax.axis_index("row"), lax.axis_index("col")
     line = wide if wide == LINE and rows % BS == 0 else 1
-    place = jnp.stack([z if line > 1 else jnp.zeros_like(z), r] + [partner(c, s, col) for s in range(col)])
-    info = jnp.concatenate([place.astype(jnp.int32), domains.T.reshape(-1), domain_mask.T.reshape(-1), block_mask.reshape(-1)])
+    halving = col == 4 and pairs % 2 == 0
+    place = [z if line > 1 else 0, r]
+    layout = []
+    if halving:
+        for order in range(2):
+            axis = axis_of(r, order)
+            at = len(place)
+            place += [(r + order) % 2 * (pairs // 2), c ^ axis, c ^ 3, c, c ^ axis ^ 3]
+            layout.append((at, pairs // 2, ((at + 1, at + 2), (at + 3, at + 4))))
+    else:
+        place += [0] + list(range(col))
+        layout.append((2, pairs, (tuple(range(3, 3 + col)),)))
+    place = jnp.stack([jnp.asarray(value, jnp.int32) for value in place])
+    info = jnp.concatenate([place, domains.T.reshape(-1), domain_mask.T.reshape(-1), block_mask.reshape(-1)])
 
     def read(ref):
-        return Scalars(ref, col, pairs, dom, window // BS)
+        return Scalars(ref, place.size, pairs, dom, window // BS)
 
     def siblings(piece):
         return [lax.ppermute(piece, "row", [(i, (i + s) % row) for i in range(row)]) for s in range(1, row)]
@@ -260,10 +299,10 @@
         late = []
         high, low = prepare([(0, 0, whole)] + others(0, siblings(whole)), shape)
 
-    terms = contract_pairs(read, row, col, line, info, late, mhigh, mlow, high, low)
-    moved = [lax.ppermute(terms[s], "col", [(i, partner(i, s, col)) for i in range(col)])
-             for s in sorted(range(1, col), key=lambda s: -bin(s).count("1"))]
-    return add_terms(terms[0], *moved)
+    terms = contract_pairs(read, row, line, layout, info, late, mhigh, mlow, high, low)
+    if halving:
+        return halve(row, col, terms)
+    return jnp.sum(lax.all_to_all(terms[0], "col", 0, 0, tiled=True), axis=0)
 
 
 def solution(mesh):

time: 41 us -> 42.5 us (1.037)
  starting transfers between devices: 10.4 us -> 12.2 us
    ppermute x3 -> x4, starting transfers between devices: 3.55 us -> 5.36 us  [the longest x1 1.54 us: halve(): moved_b = lax.ppermute(sent_b, ('row', 'col'), along(1))]
    ppermute x3 -> x4, waiting for transfers between devices: 8.57 us -> 8.15 us  [the longest x1 4.79 us: halve(): moved_a = lax.ppermute(sent_a, ('row', 'col'), along(0))]
    pallas_call x2 -> x4, Pallas kernels: 3.41 us -> 3.47 us  [the longest x1 2.74 us: contract_pairs(): pl.pallas_call(functools.partial(pairs_kernel, read, row, line, layout, k...]
  transfers between devices with their start and end apart: 10 -> 11, of which waited for: 6 -> 6; matrix products, arithmetic and copies ran while one was open for 6% -> 6% of each run, Pallas kernels for 8% -> 8%
where the time goes in v5:
time: 42.5 us; the launch traced here: 42.2 us
  waiting for transfers between devices  18.6 us (44%)
  starting transfers between devices  12.2 us (29%)
  Pallas kernels  6.68 us (16%)
  local copies, waits for them, and re-layouts  4.73 us (11%)
    ppermute x3, waiting for transfers between devices, across(): return lax.ppermute(piece, 'wide', [(i, i ^ shift) for i in range(wide)])  9.71 us
    ppermute x3, starting transfers between devices, across(): return lax.ppermute(piece, 'wide', [(i, i ^ shift) for i in range(wide)])  6.33 us
    ppermute x1, waiting for transfers between devices, halve(): moved_a = lax.ppermute(sent_a, ('row', 'col'), along(0))  4.79 us
    pallas_call x1, Pallas kernels, contract_pairs(): pl.pallas_call(functools.partial(pairs_kernel, read, row, line, layout, k...  2.74 us
    ppermute x1, waiting for transfers between devices, halve(): last_a = lax.ppermute(add_one(1, kept_a, moved_a), ('row', 'col'), along(1))  2.36 us
    unnamed x4, local copies, waits for them, and re-layouts  2.35 us
    pallas_call x3, Pallas kernels, screen(): pl.pallas_call(functools.partial(screen_kernel, read, keys), name='screen...  2.35 us
    ppermute x1, starting transfers between devices, halve(): moved_b = lax.ppermute(sent_b, ('row', 'col'), along(1))  1.54 us
  transfers between devices with their start and end apart: 11, of which 6 were waited for; matrix products, arithmetic and copies ran while one was open for 6% of the time, Pallas kernels for 8%

profile of v5, /device:TPU:0, one launch (start us, length us, event | category | flops | bytes accessed | tf_op | source)
XLA Modules:
  0.0 42.2 jit_solution(16297716586582369392)
XLA Ops:
  0.0 4.0 %collective-permute-start = (f32[1,128,512]{2,1,0:T(8,128)}, f32[1,128,512]{2,1,0:T(8,128)S(1)}, u32[]{:S(2)}, u32[]{:S(2)}) collective-permute-start(f32[1,128,512]{2,1,0:T(8,128)} %refs_0_.1), channel_id=1, source_target_pairs={{0,16},{8,24},{16,0},{24,8},{1,17},{9,25},{17,1},{25,9},{2,18},{10... | collective-permute-start | bytes 786440 | tf_op jit(solution)/shard_map/ppermute | solution.py:278
  4.0 1.6 %collective-permute-start.3 = (f32[1,128,512]{2,1,0:T(8,128)}, f32[1,128,512]{2,1,0:T(8,128)S(1)}, u32[]{:S(2)}, u32[]{:S(2)}) collective-permute-start(f32[1,128,512]{2,1,0:T(8,128)} %refs_0_.1), channel_id=1, source_target_pairs={{0,8},{8,0},{16,24},{24,16},{1,9},{9,1},{17,25},{25,17},{2,10},{10... | collective-permute-start | bytes 786440 | tf_op jit(solution)/shard_map/ppermute | solution.py:278
  5.6 0.0 collective-permute-start.2
  5.6 0.8 %reshape.9 = s32[24]{0:T(128)S(1)} reshape(s32[4,6]{1,0:T(4,128)} %bitcast.12) | data formatting | bytes 192 | tf_op jit(solution)/shard_map/reshape | solution.py:269
  6.4 0.8 %reshape.10 = s32[24]{0:T(128)S(1)} reshape(s32[4,6]{1,0:T(4,128)} %bitcast.13) | data formatting | bytes 192 | tf_op jit(solution)/shard_map/reshape | solution.py:269
  7.1 0.8 %reshape.11 = s32[64]{0:T(128)S(1)} reshape(s32[8,8]{1,0:T(8,128)} %param.9) | data formatting | bytes 512 | tf_op jit(solution)/shard_map/reshape | solution.py:269
  7.9 0.1 concatenate.3.info
  8.0 0.0 copy-start.1
  8.0 0.9 %copy-done.1 = f32[1,128,512]{2,1,0:T(8,128)S(1)} copy-done((f32[1,128,512]{2,1,0:T(8,128)S(1)}, f32[1,128,512]{2,1,0:T(8,128)}, u32[]{:S(2)}) %copy-start.1) | copy-done | bytes 262168
  9.0 0.7 %screen_factors.3 = (bf16[8,2,512,128]{3,2,1,0:T(8,128)(2,1)S(1)}, bf16[8,2,512,128]{3,2,1,0:T(8,128)(2,1)S(1)}) custom-call(s32[124]{0:T(128)S(1)} %concatenate.3.info, f32[1,128,512]{2,1,0:T(8,128)S(1)} %copy-done.1), custom_call_target="tpu_custom_call" | custom-call | flops 524288 | bytes 786432 | tf_op jit(solution)/shard_map/screen_factors/pallas_call | solution.py:110
  9.6 0.0 copy-start
  9.7 1.4 %copy-done = f32[6,256,256]{2,1,0:T(8,128)S(1)} copy-done((f32[6,256,256]{2,1,0:T(8,128)S(1)}, f32[6,256,256]{2,1,0:T(8,128)}, u32[]{:S(2)}) %copy-start) | copy-done | bytes 1572888
  11.1 0.9 %mask_amplitudes.1 = (bf16[6,256,256]{2,1,0:T(8,128)(2,1)S(1)}, bf16[6,256,256]{2,1,0:T(8,128)(2,1)S(1)}) custom-call(s32[124]{0:T(128)S(1)} %concatenate.3.info, f32[6,256,256]{2,1,0:T(8,128)S(1)} %copy-done), custom_call_target="tpu_custom_call" | custom-call | flops 1572864 | bytes 3145728 | tf_op jit(solution)/shard_map/mask_amplitudes/pallas_call | solution.py:69
  11.9 4.3 %collective-permute-done.refs_2_ = f32[1,128,512]{2,1,0:T(8,128)S(1)} collective-permute-done((f32[1,128,512]{2,1,0:T(8,128)}, f32[1,128,512]{2,1,0:T(8,128)S(1)}, u32[]{:S(2)}, u32[]{:S(2)}) %collective-permute-start) | collective-permute-done | bytes 262176 | tf_op jit(solution)/shard_map/ppermute | solution.py:278
  16.3 0.7 %collective-permute-start.1 = (f32[1,128,512]{2,1,0:T(8,128)S(1)}, f32[1,128,512]{2,1,0:T(8,128)S(1)}, u32[]{:S(2)}, u32[]{:S(2)}) collective-permute-start(f32[1,128,512]{2,1,0:T(8,128)S(1)} %collective-permute-done.refs_2_), channel_id=1, source_target_pairs={{0,8},{8,0},{16,24},{24,16},{1,9},{9,1},{17,25},{25,17},{2,10},{10... | collective-permute-start | bytes 786440 | tf_op jit(solution)/shard_map/ppermute | solution.py:278
  17.0 0.0 collective-permute-start.6
  17.0 0.0 collective-permute-done.3.refs_1_
  17.0 0.5 %collective-permute-start.5 = (f32[1,128,512]{2,1,0:T(8,128)S(1)}, f32[1,128,512]{2,1,0:T(8,128)S(1)}, u32[]{:S(2)}, u32[]{:S(2)}) collective-permute-start(f32[1,128,512]{2,1,0:T(8,128)S(1)} %collective-permute-done.3.refs_1_), channel_id=1, source_target_pairs={{0,4},{4,0},{1,5},{5,1},{2,6},{6,2},{3,7},{7,3},{8,12},{12,8},{9,1... | collective-permute-start | bytes 786440 | tf_op jit(solution)/shard_map/ppermute | solution.py:275
  17.5 0.0 collective-permute-done.2.refs_0_
  17.5 0.8 %screen_factors.4 = (bf16[8,2,512,128]{3,2,1,0:T(8,128)(2,1)S(1)}, bf16[8,2,512,128]{3,2,1,0:T(8,128)(2,1)S(1)}) custom-call(s32[124]{0:T(128)S(1)} %concatenate.3.info, f32[1,128,512]{2,1,0:T(8,128)S(1)} %collective-permute-done.2.refs_0_, f32[1,128,512]{2,1,0:T(8,128)S(1)} %collective-permute-done.3.refs_1_, ...), custom_call_target="tpu_custom_call", output_to_operand_aliasing={{0}: (4, {}), {1}: (5, {})} | custom-call | flops 1572864 | bytes 2359296 | tf_op jit(solution)/shard_map/screen_factors/pallas_call | solution.py:110
  18.3 5.4 %collective-permute-done.1.refs_0_ = f32[1,128,512]{2,1,0:T(8,128)S(1)} collective-permute-done((f32[1,128,512]{2,1,0:T(8,128)S(1)}, f32[1,128,512]{2,1,0:T(8,128)S(1)}, u32[]{:S(2)}, u32[]{:S(2)}) %collective-permute-start.1) | collective-permute-done | bytes 262176 | tf_op jit(solution)/shard_map/ppermute | solution.py:278
  23.7 0.0 collective-permute-start.4
  23.7 0.0 collective-permute-done.5.refs_1_
  23.7 0.0 collective-permute-done.6.refs_2_
  23.7 0.8 %screen_factors.5 = (bf16[8,2,512,128]{3,2,1,0:T(8,128)(2,1)S(1)}, bf16[8,2,512,128]{3,2,1,0:T(8,128)(2,1)S(1)}) custom-call(s32[124]{0:T(128)S(1)} %concatenate.3.info, f32[1,128,512]{2,1,0:T(8,128)S(1)} %collective-permute-done.1.refs_0_, f32[1,128,512]{2,1,0:T(8,128)S(1)} %collective-permute-done.5.refs_1_, ...), custom_call_target="tpu_custom_call", output_to_operand_aliasing={{0}: (4, {}), {1}: (5, {})} | custom-call | flops 1572864 | bytes 2359296 | tf_op jit(solution)/shard_map/screen_factors/pallas_call | solution.py:110
  24.6 0.7 %collective-permute-done.4.refs_0_ = f32[1,128,512]{2,1,0:T(8,128)S(1)} collective-permute-done((f32[1,128,512]{2,1,0:T(8,128)S(1)}, f32[1,128,512]{2,1,0:T(8,128)S(1)}, u32[]{:S(2)}, u32[]{:S(2)}) %collective-permute-start.4) | collective-permute-done | bytes 262176 | tf_op jit(solution)/shard_map/ppermute | solution.py:275
  25.2 2.7 %contract_pairs.1 = (f32[2,3,32,256]{3,2,1,0:T(8,128)S(1)}, f32[2,3,32,256]{3,2,1,0:T(8,128)S(1)}, f32[2,3,32,256]{3,2,1,0:T(8,128)S(1)}, f32[2,3,32,256]{3,2,1,...) custom-call(s32[124]{0:T(128)S(1)} %concatenate.3.info, ...), custom_call_target="tpu_custom_call", output_to_operand_aliasing={{4}: (4, {}), {5}: (5, {})} | custom-call | flops 2415919104 | bytes 8388608 | tf_op jit(solution)/shard_map/contract_pairs/pallas_call | solution.py:193
  28.0 1.3 %collective-permute-start.7 = (f32[2,3,32,256]{3,2,1,0:T(8,128)S(1)}, f32[2,3,32,256]{3,2,1,0:T(8,128)S(1)}, u32[]{:S(2)}, u32[]{:S(2)}) collective-permute-start(f32[2,3,32,256]{3,2,1,0:T(8,128)S(1)} %get-tuple-element.42), channel_id=1, source_target_pairs={{0,1},{1,0},{2,3},{3,2},{4,6},{5,7},{6,4},{7,5},{8,9},{9,8},{10,11... | collective-permute-start | bytes 589832 | tf_op jit(solution)/shard_map/ppermute | solution.py:236
  29.3 1.5 %collective-permute-start.9 = (f32[2,3,32,256]{3,2,1,0:T(8,128)S(1)}, f32[2,3,32,256]{3,2,1,0:T(8,128)S(1)}, u32[]{:S(2)}, u32[]{:S(2)}) collective-permute-start(f32[2,3,32,256]{3,2,1,0:T(8,128)S(1)} %get-tuple-element.44), channel_id=1, source_target_pairs={{0,2},{1,3},{2,0},{3,1},{4,5},{5,4},{6,7},{7,6},{8,10},{9,11},{10,... | collective-permute-start | bytes 589832 | tf_op jit(solution)/shard_map/ppermute | solution.py:237
  30.9 4.8 %collective-permute-done.7.b.refs_1_ = f32[2,3,32,256]{3,2,1,0:T(8,128)S(1)} collective-permute-done((f32[2,3,32,256]{3,2,1,0:T(8,128)S(1)}, f32[2,3,32,256]{3,2,1,0:T(8,128)S(1)}, u32[]{:S(2)}, u32[]{:S(2)}) %collective-permute-start.7) | collective-permute-done | bytes 196640 | tf_op jit(solution)/shard_map/ppermute | solution.py:236
  35.7 1.2 %collective-permute-start.8 = (f32[3,32,256]{2,1,0:T(8,128)S(1)}, f32[3,32,256]{2,1,0:T(8,128)S(1)}, u32[]{:S(2)}, u32[]{:S(2)}) collective-permute-start(f32[3,32,256]{2,1,0:T(8,128)S(1)} %add_one.2), channel_id=1, source_target_pairs={{0,2},{1,3},{2,0},{3,1},{4,5},{5,4},{6,7},{7,6},{8,10},{9,11},{10,... | collective-permute-start | bytes 294920 | tf_op jit(solution)/shard_map/ppermute | solution.py:238
  36.8 0.0 collective-permute-done.9.b.refs_4_
  36.9 1.3 %collective-permute-start.10 = (f32[3,32,256]{2,1,0:T(8,128)S(1)}, f32[3,32,256]{2,1,0:T(8,128)S(1)}, u32[]{:S(2)}, u32[]{:S(2)}) collective-permute-start(f32[3,32,256]{2,1,0:T(8,128)S(1)} %add_one.3), channel_id=1, source_target_pairs={{0,1},{1,0},{2,3},{3,2},{4,6},{5,7},{6,4},{7,5},{8,9},{9,8},{10,11... | collective-permute-start | bytes 294920 | tf_op jit(solution)/shard_map/ppermute | solution.py:239
  38.2 2.4 %collective-permute-done.8.refs_2_ = f32[3,32,256]{2,1,0:T(8,128)S(1)} collective-permute-done((f32[3,32,256]{2,1,0:T(8,128)S(1)}, f32[3,32,256]{2,1,0:T(8,128)S(1)}, u32[]{:S(2)}, u32[]{:S(2)}) %collective-permute-start.8) | collective-permute-done | bytes 98336 | tf_op jit(solution)/shard_map/ppermute | solution.py:238
  40.5 1.0 %collective-permute-done.10.refs_5_ = f32[3,32,256]{2,1,0:T(8,128)S(1)} collective-permute-done((f32[3,32,256]{2,1,0:T(8,128)S(1)}, f32[3,32,256]{2,1,0:T(8,128)S(1)}, u32[]{:S(2)}, u32[]{:S(2)}) %collective-permute-start.10) | collective-permute-done | bytes 98336 | tf_op jit(solution)/shard_map/ppermute | solution.py:239
  41.5 0.7 %join_groups.1 = f32[6,32,256]{2,1,0:T(8,128)} custom-call(f32[2,3,32,256]{3,2,1,0:T(8,128)S(1)} %get-tuple-element.41.a.refs_0_, f32[2,3,32,256]{3,2,1,0:T(8,128)S(1)} %collective-permute-done.7.b.refs_1_, f32[3,32,256]{2,1,0:T(8,128)S(1)} %collective-permute-done.8.refs_2_, f32[2,3,32,256]{3,2,1,0:T(8,128)S(1)} %get-tuple-element.43.a.refs_3_, ...), custom_call_target="tpu_custom_call" | custom-call | tf_op jit(solution)/shard_map/join_groups/pallas_call | solution.py:241
  (2 shorter events, 0.0 us)
Async XLA Ops:
  0.0 16.3 %collective-permute-start = (f32[1,128,512]{2,1,0:T(8,128)}, f32[1,128,512]{2,1,0:T(8,128)S(1)}, u32[]{:S(2)}, u32[]{:S(2)}) collective-permute-start(f32[1,128,512]{2,1,0:T(8,128)} %refs_0_.1), channel_id=1, source_target_pairs={{0,16},{8,24},{16,0},{24,8},{1,17},{9,25},{17,1},{25,9},{2,18},{10... | collective-permute-start | bytes 786440 | tf_op jit(solution)/shard_map/ppermute | solution.py:278
  4.0 13.0 %collective-permute-start.3 = (f32[1,128,512]{2,1,0:T(8,128)}, f32[1,128,512]{2,1,0:T(8,128)S(1)}, u32[]{:S(2)}, u32[]{:S(2)}) collective-permute-start(f32[1,128,512]{2,1,0:T(8,128)} %refs_0_.1), channel_id=1, source_target_pairs={{0,8},{8,0},{16,24},{24,16},{1,9},{9,1},{17,25},{25,17},{2,10},{10... | collective-permute-start | bytes 786440 | tf_op jit(solution)/shard_map/ppermute | solution.py:278
  5.6 11.9 %collective-permute-start.2 = (f32[1,128,512]{2,1,0:T(8,128)}, f32[1,128,512]{2,1,0:T(8,128)S(1)}, u32[]{:S(2)}, u32[]{:S(2)}) collective-permute-start(f32[1,128,512]{2,1,0:T(8,128)} %refs_0_.1), channel_id=1, source_target_pairs={{0,4},{4,0},{1,5},{5,1},{2,6},{6,2},{3,7},{7,3},{8,12},{12,8},{9,1... | collective-permute-start | bytes 786440 | tf_op jit(solution)/shard_map/ppermute | solution.py:275
  8.0 1.0 %copy-start.1 = (f32[1,128,512]{2,1,0:T(8,128)S(1)}, f32[1,128,512]{2,1,0:T(8,128)}, u32[]{:S(2)}) copy-start(f32[1,128,512]{2,1,0:T(8,128)} %refs_0_.1) | copy-start | bytes 786436
  9.6 1.4 %copy-start = (f32[6,256,256]{2,1,0:T(8,128)S(1)}, f32[6,256,256]{2,1,0:T(8,128)}, u32[]{:S(2)}) copy-start(f32[6,256,256]{2,1,0:T(8,128)} %amplitudes.1) | copy-start | bytes 4718596
  16.3 7.4 %collective-permute-start.1 = (f32[1,128,512]{2,1,0:T(8,128)S(1)}, f32[1,128,512]{2,1,0:T(8,128)S(1)}, u32[]{:S(2)}, u32[]{:S(2)}) collective-permute-start(f32[1,128,512]{2,1,0:T(8,128)S(1)} %collective-permute-done.refs_2_), channel_id=1, source_target_pairs={{0,8},{8,0},{16,24},{24,16},{1,9},{9,1},{17,25},{25,17},{2,10},{10... | collective-permute-start | bytes 786440 | tf_op jit(solution)/shard_map/ppermute | solution.py:278
  17.0 6.7 %collective-permute-start.6 = (f32[1,128,512]{2,1,0:T(8,128)S(1)}, f32[1,128,512]{2,1,0:T(8,128)S(1)}, u32[]{:S(2)}, u32[]{:S(2)}) collective-permute-start(f32[1,128,512]{2,1,0:T(8,128)S(1)} %collective-permute-done.refs_2_), channel_id=1, source_target_pairs={{0,4},{4,0},{1,5},{5,1},{2,6},{6,2},{3,7},{7,3},{8,12},{12,8},{9,1... | collective-permute-start | bytes 786440 | tf_op jit(solution)/shard_map/ppermute | solution.py:275
  17.0 6.7 %collective-permute-start.5 = (f32[1,128,512]{2,1,0:T(8,128)S(1)}, f32[1,128,512]{2,1,0:T(8,128)S(1)}, u32[]{:S(2)}, u32[]{:S(2)}) collective-permute-start(f32[1,128,512]{2,1,0:T(8,128)S(1)} %collective-permute-done.3.refs_1_), channel_id=1, source_target_pairs={{0,4},{4,0},{1,5},{5,1},{2,6},{6,2},{3,7},{7,3},{8,12},{12,8},{9,1... | collective-permute-start | bytes 786440 | tf_op jit(solution)/shard_map/ppermute | solution.py:275
  23.7 1.5 %collective-permute-start.4 = (f32[1,128,512]{2,1,0:T(8,128)S(1)}, f32[1,128,512]{2,1,0:T(8,128)S(1)}, u32[]{:S(2)}, u32[]{:S(2)}) collective-permute-start(f32[1,128,512]{2,1,0:T(8,128)S(1)} %collective-permute-done.1.refs_0_), channel_id=1, source_target_pairs={{0,4},{4,0},{1,5},{5,1},{2,6},{6,2},{3,7},{7,3},{8,12},{12,8},{9,1... | collective-permute-start | bytes 786440 | tf_op jit(solution)/shard_map/ppermute | solution.py:275
  28.0 7.7 %collective-permute-start.7 = (f32[2,3,32,256]{3,2,1,0:T(8,128)S(1)}, f32[2,3,32,256]{3,2,1,0:T(8,128)S(1)}, u32[]{:S(2)}, u32[]{:S(2)}) collective-permute-start(f32[2,3,32,256]{3,2,1,0:T(8,128)S(1)} %get-tuple-element.42), channel_id=1, source_target_pairs={{0,1},{1,0},{2,3},{3,2},{4,6},{5,7},{6,4},{7,5},{8,9},{9,8},{10,11... | collective-permute-start | bytes 589832 | tf_op jit(solution)/shard_map/ppermute | solution.py:236
  29.3 7.5 %collective-permute-start.9 = (f32[2,3,32,256]{3,2,1,0:T(8,128)S(1)}, f32[2,3,32,256]{3,2,1,0:T(8,128)S(1)}, u32[]{:S(2)}, u32[]{:S(2)}) collective-permute-start(f32[2,3,32,256]{3,2,1,0:T(8,128)S(1)} %get-tuple-element.44), channel_id=1, source_target_pairs={{0,2},{1,3},{2,0},{3,1},{4,5},{5,4},{6,7},{7,6},{8,10},{9,11},{10,... | collective-permute-start | bytes 589832 | tf_op jit(solution)/shard_map/ppermute | solution.py:237
  35.7 4.9 %collective-permute-start.8 = (f32[3,32,256]{2,1,0:T(8,128)S(1)}, f32[3,32,256]{2,1,0:T(8,128)S(1)}, u32[]{:S(2)}, u32[]{:S(2)}) collective-permute-start(f32[3,32,256]{2,1,0:T(8,128)S(1)} %add_one.2), channel_id=1, source_target_pairs={{0,2},{1,3},{2,0},{3,1},{4,5},{5,4},{6,7},{7,6},{8,10},{9,11},{10,... | collective-permute-start | bytes 294920 | tf_op jit(solution)/shard_map/ppermute | solution.py:238
  36.9 4.7 %collective-permute-start.10 = (f32[3,32,256]{2,1,0:T(8,128)S(1)}, f32[3,32,256]{2,1,0:T(8,128)S(1)}, u32[]{:S(2)}, u32[]{:S(2)}) collective-permute-start(f32[3,32,256]{2,1,0:T(8,128)S(1)} %add_one.3), channel_id=1, source_target_pairs={{0,1},{1,0},{2,3},{3,2},{4,6},{5,7},{6,4},{7,5},{8,9},{9,8},{10,11... | collective-permute-start | bytes 294920 | tf_op jit(solution)/shard_map/ppermute | solution.py:239

commit v6 on v4

v6 whole, which is shorter than its diff:
```python
import functools

import jax
import jax.numpy as jnp
from jax import lax
from jax.experimental import pallas as pl
from jax.experimental.pallas import tpu as pltpu
from jax.sharding import PartitionSpec as P

BS = 64
LANES = 128
LINE = 4
VMEM_LIMIT = 40 * 1024 * 1024
VMEM_SPEC = pl.BlockSpec(memory_space=pltpu.VMEM)


def split(value):
    top = value.astype(jnp.bfloat16)
    return top, (value - top.astype(jnp.float32)).astype(jnp.bfloat16)


def partner(index, shift, size):
    if size & (size - 1) == 0:
        return index ^ shift
    return (index + shift) % size


def left_of(rows):
    return lax.broadcasted_iota(jnp.int32, (rows, LANES), 1) < BS


def mask_amplitudes_kernel(weights, amplitudes, high, low):
    pairs, domv, _ = amplitudes.shape
    for p in range(pairs):
        for i in range(domv // BS):
            rows = slice(i * BS, (i + 1) * BS)
            top, rest = split(amplitudes[p, rows, :] * weights[p, i])
            high[p, rows, :] = top
            low[p, rows, :] = rest


def mask_amplitudes(weights, amplitudes):
    shape = jax.ShapeDtypeStruct(amplitudes.shape, jnp.bfloat16)
    return pl.pallas_call(
        mask_amplitudes_kernel,
        name="mask_amplitudes",
        out_shape=[shape] * 2,
        in_specs=[VMEM_SPEC] * 2,
        out_specs=[VMEM_SPEC] * 2,
        compiler_params=pltpu.CompilerParams(vmem_limit_bytes=VMEM_LIMIT),
        cost_estimate=pl.CostEstimate(flops=4 * amplitudes.size, bytes_accessed=8 * amplitudes.size, transcendentals=0),
    )(weights, amplitudes)


def screen_piece(mask, piece, q, slot, high, low):
    nq, rows, window = piece.shape
    tiles = window // LANES
    for h in range(rows // BS):
        block = slot * (rows // BS) + h
        target = slice(block * BS, (block + 1) * BS)
        for t in range(tiles):
            lanes = slice(t * LANES, (t + 1) * LANES)
            for n in range(nq):
                tile = piece[n, h * BS:(h + 1) * BS, lanes] * mask[block, :, lanes]
                for turn, value in ((0, tile), (1, pltpu.roll(tile, BS, 1))):
                    top, rest = split(value)
                    high[turn * tiles + t, q * nq + n, target, :] = top
                    low[turn * tiles + t, q * nq + n, target, :] = rest


def screen_kernel(keys, mask, *refs):
    high, low = refs[-2:]
    for (slot, q), piece in zip(keys, refs):
        screen_piece(mask, piece, q, slot, high, low)


def screen(mask, keyed, shape, held=()):
    keys = [(slot, q) for slot, q, _ in keyed]
    pieces = [piece for _, _, piece in keyed]
    size = sum(piece.size for piece in pieces)
    return pl.pallas_call(
        functools.partial(screen_kernel, keys),
        name="screen_factors",
        out_shape=[shape] * 2,
        in_specs=[VMEM_SPEC] * (1 + len(pieces) + len(held)),
        out_specs=[VMEM_SPEC] * 2,
        input_output_aliases={1 + len(pieces) + i: i for i in range(len(held))},
        compiler_params=pltpu.CompilerParams(vmem_limit_bytes=VMEM_LIMIT),
        cost_estimate=pl.CostEstimate(flops=8 * size, bytes_accessed=12 * size, transcendentals=0),
    )(mask, *pieces, *held)


def pairs_kernel(row, factors, late, last, count, places, mask, weights, *refs):
    pieces = refs[:len(late)]
    mhigh, mlow = refs[len(late):len(late) + 2]
    held = refs[len(late) + 4:-count - 2]
    outs, (high, low) = refs[-count - 2:-2], refs[-2:]
    at = places[...]
    for (slot, q), piece in zip(late, pieces):

        @pl.when(at[0, 0] >= 0)
        def _():
            screen_piece(mask, piece, q, slot, high, low)

    pairs, chunk, domv = outs[0].shape
    qs = len(factors)
    half = domv // row
    blocks = domv // BS
    tiles = domv // LANES
    across = (((1,), (1,)), ((), ()))
    along = (((1,), (0,)), ((), ()))
    dot = functools.partial(lax.dot_general, preferred_element_type=jnp.float32)

    def contract(p):
        def rows_at(n, size):
            return pl.ds(pl.multiple_of(at[0, n * pairs + p], size), size)

        y_spans = [rows_at(i, BS) for i in range(blocks)]
        x_spans = [rows_at(blocks + n, chunk) for n in range(count)]
        first = blocks + count
        sources = [(at[0, (first + 2 * j) * pairs + p], at[0, (first + 2 * j + 1) * pairs + p]) for j in range(tiles)]

        def gather(source, q, spans, size):
            return jnp.concatenate([jnp.concatenate([
                jnp.where(left_of(size), source[a, q, span, :], source[b, q, span, :]) for a, b in sources], 1)
                for span in spans], 0)

        yhigh, ylow = (jnp.concatenate([gather(source, q, y_spans, BS) for q in factors], 1) for source in (high, low))
        xhigh, xlow = (jnp.concatenate([gather(source, q, x_spans, chunk) for q in factors], 0) for source in (high, low))
        both = dot(jnp.concatenate([xhigh, xlow], 0), mhigh[p], along)
        size = qs * half
        halfway = both[:size] + both[size:] + dot(xhigh, mlow[p], along)
        hhigh, hlow = split(jnp.concatenate([halfway[q * half:(q + 1) * half] for q in range(qs)], 1))
        both = dot(jnp.concatenate([hhigh, hlow], 0), yhigh, across)
        total = both[:half] + both[half:] + dot(hhigh, ylow, across)
        for n, out in enumerate(outs):
            term = total[n * chunk:(n + 1) * chunk]
            if held:
                term += held[n][p]
            out[p] = term * weights[n, p] if last else term

    for p in range(pairs):
        contract(p)


def contract_pairs(row, col, places, mask, weights, factors, last, late, mhigh, mlow, high, low, held=()):
    pairs, domv, _ = mhigh.shape
    chunk = domv // (row * col)
    keys = [(slot, q) for slot, q, _ in late]
    pieces = [piece for _, _, piece in late]
    prepared = 3 + len(pieces) + 2
    results = pl.pallas_call(
        functools.partial(pairs_kernel, row, factors, keys, last, col),
        name="contract_pairs",
        out_shape=[jax.ShapeDtypeStruct((pairs, chunk, domv), jnp.float32)] * col
        + [jax.ShapeDtypeStruct(high.shape, high.dtype)] * 2,
        in_specs=[VMEM_SPEC] * (3 + len(pieces) + 4 + len(held)),
        out_specs=[VMEM_SPEC] * (col + 2),
        input_output_aliases={prepared: col, prepared + 1: col + 1},
        compiler_params=pltpu.CompilerParams(vmem_limit_bytes=VMEM_LIMIT),
        cost_estimate=pl.CostEstimate(flops=6 * pairs * len(factors) * domv ** 3 * 4 // row, bytes_accessed=8 * high.size,
                                      transcendentals=0),
    )(places, mask, weights, *pieces, mhigh, mlow, high, low, *held)
    return results[:col], results[col], results[col + 1]


def add_kernel(*refs):
    total = refs[0][...]
    for ref in refs[1:-1]:
        total += ref[...]
    refs[-1][...] = total


def add_terms(*terms):
    return pl.pallas_call(
        add_kernel,
        name="add_terms",
        out_shape=jax.ShapeDtypeStruct(terms[0].shape, jnp.float32),
        in_specs=[VMEM_SPEC] * len(terms),
        out_specs=VMEM_SPEC,
        compiler_params=pltpu.CompilerParams(vmem_limit_bytes=VMEM_LIMIT),
    )(*terms)


def body(wide, row, col, amplitudes, factors, domains, domain_mask, block_mask):
    nq, rows, window = factors.shape
    pairs, dom = domains.shape
    z, r, c = lax.axis_index("wide"), lax.axis_index("row"), lax.axis_index("col")
    line = wide if wide == LINE and rows % BS == 0 else 1
    plane = z if line > 1 else 0
    blocks = window // BS
    per_slot = blocks // line
    domv = dom * BS
    tiles = window // LANES
    half = domv // row
    chunk = half // col

    def pick(which, table):
        hits = which[:, None] == jnp.arange(table.shape[0])[None, :]
        return jnp.sum(jnp.where(hits[:, :, None], table[None], 0), axis=1)

    blocks_of, flags = domains.T, domain_mask.T
    starts = ((blocks_of // per_slot) ^ plane) * (per_slot * BS) + blocks_of % per_slot * BS
    offsets = r * half + jnp.stack([partner(c, s, col) for s in range(col)]) * chunk
    chosen = pick(offsets // BS, starts) + (offsets % BS)[:, None]
    firsts, seconds = blocks_of[0::2], blocks_of[1::2]
    sources = jnp.stack([firsts % 2 * tiles + firsts // 2, (1 - seconds % 2) * tiles + seconds // 2], 1)
    places = jnp.concatenate([starts, chosen, sources.reshape(-1, pairs)], 0).reshape(1, -1)

    order = jnp.arange(blocks)
    kept = pick(((order // per_slot) ^ plane) * per_slot + order % per_slot, block_mask)
    mask = jnp.repeat(kept, BS, axis=1).astype(jnp.float32)[:, None, :]
    lanes = jnp.repeat(domain_mask, BS, axis=1)
    inner = (domain_mask[:, :, None] * lanes[:, None, :]).astype(jnp.float32)[:, :, None, :]
    outer = (pick(offsets // BS, flags)[:, :, None] * lanes[None]).astype(jnp.float32)[:, :, None, :]

    def siblings(piece):
        return [lax.ppermute(piece, "row", [(i, (i + s) % row) for i in range(row)]) for s in range(1, row)]

    def across(piece, shift):
        return lax.ppermute(piece, "wide", [(i, i ^ shift) for i in range(wide)])

    def others(slot, pieces):
        return [(slot, q + 1, piece) for q, piece in enumerate(pieces)]

    shape = jax.ShapeDtypeStruct((2 * window // LANES, row * nq, window, LANES), jnp.bfloat16)
    prepare = functools.partial(screen, mask)
    mhigh, mlow = mask_amplitudes(inner, amplitudes)
    if line > 1:
        near, cross = across(factors, 1), across(factors, 2)
        high, low = prepare([(0, 0, factors)], shape)
        cross, high, low, mhigh, mlow, places, outer = lax.optimization_barrier(
            (cross, high, low, mhigh, mlow, places, outer))
        last = across(cross, 1)
        early = others(0, siblings(factors)) + [(1, 0, near), (2, 0, cross)]
        s_cross, s_near = siblings(cross), siblings(near)
        high, low = prepare(early, shape, (high, low))
        last, high, low = lax.optimization_barrier((last, high, low))
        contract = functools.partial(contract_pairs, row, col, places, mask, outer)
        sent = others(3, siblings(last)) + others(1, s_near) + others(2, s_cross)
        held, high, low = contract(range(nq), False, [(3, 0, last)], mhigh, mlow, high, low)
        terms, _, _ = contract(range(nq, row * nq), True, sent, mhigh, mlow, high, low, held)
    else:
        whole = lax.all_gather(factors, "wide", axis=1, tiled=True)
        high, low = prepare([(0, 0, whole)] + others(0, siblings(whole)), shape)
        contract = functools.partial(contract_pairs, row, col, places, mask, outer)
        terms, _, _ = contract(range(row * nq), True, [], mhigh, mlow, high, low)

    moved = [lax.ppermute(terms[s], "col", [(i, partner(i, s, col)) for i in range(col)])
             for s in sorted(range(1, col), key=lambda s: -bin(s).count("1"))]
    return add_terms(terms[0], *moved)


def solution(mesh):
    wide, row, col = (mesh.shape[name] for name in ("wide", "row", "col"))
    return jax.shard_map(
        functools.partial(body, wide, row, col),
        mesh=mesh,
        in_specs=(
            P("wide", None, None),
            P(("row", "col"), "wide", None),
            P("wide", None),
            P("wide", None),
            P(),
        ),
        out_specs=P("wide", ("row", "col"), None),
        check_vma=False,
    )
```

time: 41 us -> 40.7 us (level)
  other arithmetic: 0 us -> 2.78 us
  Pallas kernels: 6.62 us -> 4.82 us
  waiting for transfers between devices: 19 us -> 17.3 us
    reshape x3 -> x1, local copies, waits for them, and re-layouts: 2.29 us -> 0.08 us  [body(): jnp.concatenate([starts, chosen, sources.reshape(-1, pairs)], 0)]
    pallas_call x5, Pallas kernels: 5.91 us -> 4.08 us  [the longest x2 3.42 us: contract_pairs(): pl.pallas_call(functools.partial(pairs_kernel, row, factors, keys, last,...]
    reduce_sum x0 -> x2, other arithmetic: none -> 1.55 us  [pick(): return jnp.sum(jnp.where(hits[:, :, None], table[None], 0), axis=1)]
    slice x0 -> x2, local copies, waits for them, and re-layouts: none -> 1.4 us  [body(): firsts, seconds = (blocks_of[0::2], blocks_of[1::2])]
    ppermute x3, waiting for transfers between devices: 9.71 us -> 8.4 us  [across(): return lax.ppermute(piece, 'wide', [(i, i ^ shift) for i in range(wide)])]
    add x0 -> x3, other arithmetic: none -> 0.77 us  [the longest x1 0.69 us: body(): (blocks_of // per_slot ^ plane) * (per_slot * BS)]
    unnamed x4 -> x5, local copies, waits for them, and re-layouts: 2.36 us -> 3.12 us
    ppermute x4, waiting for transfers between devices: 0.7 us -> 0.01 us  [siblings(): lax.ppermute(piece, 'row', [(i, (i + s) % row) for i in range(row)])]
  transfers between devices with their start and end apart: 10 -> 10, of which waited for: 6 -> 5; matrix products, arithmetic and copies ran while one was open for 6% -> 13% of each run, Pallas kernels for 8% -> 6%
where the time goes in v6:
time: 40.7 us; the launch traced here: 40.4 us
  waiting for transfers between devices  17.3 us (43%)
  starting transfers between devices  10.4 us (26%)
  local copies, waits for them, and re-layouts  4.92 us (12%)
  Pallas kernels  4.82 us (12%)
  other arithmetic  2.78 us (7%)
    ppermute x3, waiting for transfers between devices, body(): lax.ppermute(terms[s], 'col', [(i, partner(i, s, col)) for i in range(col)])  8.93 us
    ppermute x3, waiting for transfers between devices, across(): return lax.ppermute(piece, 'wide', [(i, i ^ shift) for i in range(wide)])  8.4 us
    ppermute x3, starting transfers between devices, across(): return lax.ppermute(piece, 'wide', [(i, i ^ shift) for i in range(wide)])  6.33 us
    ppermute x3, starting transfers between devices, body(): lax.ppermute(terms[s], 'col', [(i, partner(i, s, col)) for i in range(col)])  3.55 us
    pallas_call x2, Pallas kernels, contract_pairs(): pl.pallas_call(functools.partial(pairs_kernel, row, factors, keys, last,...  3.42 us
    unnamed x5, local copies, waits for them, and re-layouts  3.12 us
    reduce_sum x2, other arithmetic, pick(): return jnp.sum(jnp.where(hits[:, :, None], table[None], 0), axis=1)  1.55 us
    slice x2, local copies, waits for them, and re-layouts, body(): firsts, seconds = (blocks_of[0::2], blocks_of[1::2])  1.4 us
  transfers between devices with their start and end apart: 10, of which 5 were waited for; matrix products, arithmetic and copies ran while one was open for 13% of the time, Pallas kernels for 6%

profile of v6, /device:TPU:0, one launch (start us, length us, event | category | flops | bytes accessed | tf_op | source)
XLA Modules:
  0.0 40.4 jit_solution(1862484031391203139)
XLA Ops:
  0.0 4.0 %collective-permute-start = (f32[1,128,512]{2,1,0:T(8,128)}, f32[1,128,512]{2,1,0:T(8,128)S(1)}, u32[]{:S(2)}, u32[]{:S(2)}) collective-permute-start(f32[1,128,512]{2,1,0:T(8,128)} %refs_0_.1), channel_id=1, source_target_pairs={{0,16},{8,24},{16,0},{24,8},{1,17},{9,25},{17,1},{25,9},{2,18},{10... | collective-permute-start | bytes 786440 | tf_op jit(solution)/shard_map/ppermute | solution.py:221
  4.0 1.6 %collective-permute-start.3 = (f32[1,128,512]{2,1,0:T(8,128)}, f32[1,128,512]{2,1,0:T(8,128)S(1)}, u32[]{:S(2)}, u32[]{:S(2)}) collective-permute-start(f32[1,128,512]{2,1,0:T(8,128)} %refs_0_.1), channel_id=1, source_target_pairs={{0,8},{8,0},{16,24},{24,16},{1,9},{9,1},{17,25},{25,17},{2,10},{10... | collective-permute-start | bytes 786440 | tf_op jit(solution)/shard_map/ppermute | solution.py:221
  5.6 0.0 collective-permute-start.2
  5.6 0.7 %slice.6 = s32[2,6]{1,0:T(2,128)S(1)} slice(s32[4,6]{1,0:T(4,128)} %bitcast.14), slice={[0:4:2], [0:6:1]} | slice | bytes 96 | tf_op jit(solution)/shard_map/slice | solution.py:206
  6.3 0.7 %slice.7 = s32[2,6]{1,0:T(2,128)S(1)} slice(s32[4,6]{1,0:T(4,128)} %bitcast.15), slice={[1:4:2], [0:6:1]} | slice | bytes 96 | tf_op jit(solution)/shard_map/slice | solution.py:206
  7.0 0.7 %fusion.2 = s32[4,6]{1,0:T(4,128)S(1)} fusion(s32[]{:T(128)S(6)} %axis_index.33, s32[6,4]{0,1:T(4,128)} %param.7), kind=kLoop, calls=%fused_computation.14 | loop fusion | flops 552 | bytes 196 | tf_op jit(solution)/shard_map/add | solution.py:203
  7.7 0.1 and_select_fusion.4
  7.8 0.1 iota_compare_fusion.1
  7.9 0.1 iota_compare_fusion
  8.0 0.8 %copy.18 = s32[6,4]{1,0:T(8,128)S(1)} copy(s32[6,4]{0,1:T(4,128)} %param.8) | data formatting | bytes 192 | tf_op args[3]
  8.8 0.1 broadcast_in_dim.77
  8.9 0.1 mul.76
  8.9 0.1 multiply_convert_fusion.1.weights
  9.0 0.8 %select_reduce_fusion = s32[8,8]{1,0:T(8,128)S(1)} fusion(s32[8,8]{1,0:T(8,128)} %param.9, pred[8,8]{1,0:T(8,128)(4,1)S(1)} %iota_compare_fusion), kind=kLoop, calls=%fused_computation | loop fusion | flops 960 | bytes 576 | tf_op jit(solution)/shard_map/reduce_sum | solution.py:200
  9.8 0.8 %select_reduce_fusion.1 = (s32[4,6]{1,0:T(4,128)S(1)}, s32[4,6]{1,0:T(4,128)S(1)}) fusion(s32[4,6]{1,0:T(4,128)} %bitcast.12, pred[4,4]{1,0:T(4,128)(4,1)S(1)} %iota_compare_fusion.1, s32[4,6]{1,0:T(4,128)S(1)} %fusion.2), kind=kLoop, calls=%fused_computation.4 | loop fusion | flops 336 | bytes 400 | tf_op jit(solution)/shard_map/reduce_sum | solution.py:200
  10.6 0.1 broadcast_add_fusion
  10.7 0.1 reshape.185.places
  10.8 0.1 broadcast_in_dim.76
  10.8 0.1 convert_element_type.35.mask
  10.9 0.0 copy-start.1
  11.0 0.9 %copy-done.1 = f32[1,128,512]{2,1,0:T(8,128)S(1)} copy-done((f32[1,128,512]{2,1,0:T(8,128)S(1)}, f32[1,128,512]{2,1,0:T(8,128)}, u32[]{:S(2)}) %copy-start.1) | copy-done | bytes 262168
  11.9 0.1 screen_factors.2
  12.0 0.0 copy-start
  12.1 1.4 %copy-done = f32[6,256,256]{2,1,0:T(8,128)S(1)} copy-done((f32[6,256,256]{2,1,0:T(8,128)S(1)}, f32[6,256,256]{2,1,0:T(8,128)}, u32[]{:S(2)}) %copy-start) | copy-done | bytes 1572888
  13.4 0.2 mask_amplitudes.1
  13.7 0.1 multiply_convert_fusion.weights
  13.8 2.5 %collective-permute-done.refs_2_ = f32[1,128,512]{2,1,0:T(8,128)S(1)} collective-permute-done((f32[1,128,512]{2,1,0:T(8,128)}, f32[1,128,512]{2,1,0:T(8,128)S(1)}, u32[]{:S(2)}, u32[]{:S(2)}) %collective-permute-start) | collective-permute-done | bytes 262176 | tf_op jit(solution)/shard_map/ppermute | solution.py:221
  16.3 0.7 %collective-permute-start.1 = (f32[1,128,512]{2,1,0:T(8,128)S(1)}, f32[1,128,512]{2,1,0:T(8,128)S(1)}, u32[]{:S(2)}, u32[]{:S(2)}) collective-permute-start(f32[1,128,512]{2,1,0:T(8,128)S(1)} %collective-permute-done.refs_2_), channel_id=1, source_target_pairs={{0,8},{8,0},{16,24},{24,16},{1,9},{9,1},{17,25},{25,17},{2,10},{10... | collective-permute-start | bytes 786440 | tf_op jit(solution)/shard_map/ppermute | solution.py:221
  17.0 0.0 collective-permute-start.6
  17.0 0.0 collective-permute-done.3.refs_1_
  17.0 0.5 %collective-permute-start.5 = (f32[1,128,512]{2,1,0:T(8,128)S(1)}, f32[1,128,512]{2,1,0:T(8,128)S(1)}, u32[]{:S(2)}, u32[]{:S(2)}) collective-permute-start(f32[1,128,512]{2,1,0:T(8,128)S(1)} %collective-permute-done.3.refs_1_), channel_id=1, source_target_pairs={{0,4},{4,0},{1,5},{5,1},{2,6},{6,2},{3,7},{7,3},{8,12},{12,8},{9,1... | collective-permute-start | bytes 786440 | tf_op jit(solution)/shard_map/ppermute | solution.py:218
  17.5 0.0 collective-permute-done.2.refs_0_
  17.5 0.3 screen_factors.3
  17.8 5.9 %collective-permute-done.1.refs_0_ = f32[1,128,512]{2,1,0:T(8,128)S(1)} collective-permute-done((f32[1,128,512]{2,1,0:T(8,128)S(1)}, f32[1,128,512]{2,1,0:T(8,128)S(1)}, u32[]{:S(2)}, u32[]{:S(2)}) %collective-permute-start.1) | collective-permute-done | bytes 262176 | tf_op jit(solution)/shard_map/ppermute | solution.py:221
  23.7 0.0 collective-permute-start.4
  23.7 1.6 %contract_pairs.2 = (f32[6,32,256]{2,1,0:T(8,128)S(1)}, f32[6,32,256]{2,1,0:T(8,128)S(1)}, f32[6,32,256]{2,1,0:T(8,128)S(1)}, f32[6,32,256]{2,1,0:T(8,128)S(1)},...) custom-call(s32[1,72]{1,0:T(1,128)S(1)} %reshape.185.places, ...), custom_call_target="tpu_custom_call", output_to_operand_aliasing={{4}: (6, {}), {5}: (7, {})} | custom-call | flops 1207959552 | bytes 8388608 | tf_op jit(solution)/shard_map/contract_pairs/pallas_call | solution.py:152
  25.3 0.0 collective-permute-done.5.refs_1_
  25.4 0.0 collective-permute-done.6.refs_2_
  25.4 0.0 collective-permute-done.4.refs_0_
  25.4 1.8 %contract_pairs.3 = (f32[6,32,256]{2,1,0:T(8,128)S(1)}, f32[6,32,256]{2,1,0:T(8,128)S(1)}, f32[6,32,256]{2,1,0:T(8,128)S(1)}, f32[6,32,256]{2,1,0:T(8,128)S(1)},...) custom-call(s32[1,72]{1,0:T(1,128)S(1)} %reshape.185.places, ...), custom_call_target="tpu_custom_call", output_to_operand_aliasing={{4}: (8, {}), {5}: (9, {})} | custom-call | flops 1207959552 | bytes 8388608 | tf_op jit(solution)/shard_map/contract_pairs/pallas_call | solution.py:152
  27.2 2.3 %collective-permute-start.7 = (f32[6,32,256]{2,1,0:T(8,128)S(1)}, f32[6,32,256]{2,1,0:T(8,128)S(1)}, u32[]{:S(2)}, u32[]{:S(2)}) collective-permute-start(f32[6,32,256]{2,1,0:T(8,128)S(1)} %get-tuple-element.54), channel_id=1, source_target_pairs={{0,3},{1,2},{2,1},{3,0},{4,7},{5,6},{6,5},{7,4},{8,11},{9,10},{10,... | collective-permute-start | bytes 589832 | tf_op jit(solution)/shard_map/ppermute | solution.py:249
  29.5 0.5 %collective-permute-start.8 = (f32[6,32,256]{2,1,0:T(8,128)S(1)}, f32[6,32,256]{2,1,0:T(8,128)S(1)}, u32[]{:S(2)}, u32[]{:S(2)}) collective-permute-start(f32[6,32,256]{2,1,0:T(8,128)S(1)} %get-tuple-element.55), channel_id=1, source_target_pairs={{0,1},{1,0},{2,3},{3,2},{4,5},{5,4},{6,7},{7,6},{8,9},{9,8},{10,11... | collective-permute-start | bytes 589832 | tf_op jit(solution)/shard_map/ppermute | solution.py:249
  30.0 0.7 %collective-permute-start.9 = (f32[6,32,256]{2,1,0:T(8,128)S(1)}, f32[6,32,256]{2,1,0:T(8,128)S(1)}, u32[]{:S(2)}, u32[]{:S(2)}) collective-permute-start(f32[6,32,256]{2,1,0:T(8,128)S(1)} %get-tuple-element.56), channel_id=1, source_target_pairs={{0,2},{1,3},{2,0},{3,1},{4,6},{5,7},{6,4},{7,5},{8,10},{9,11},{10,... | collective-permute-start | bytes 589832 | tf_op jit(solution)/shard_map/ppermute | solution.py:249
  30.7 5.1 %collective-permute-done.7.refs_1_ = f32[6,32,256]{2,1,0:T(8,128)S(1)} collective-permute-done((f32[6,32,256]{2,1,0:T(8,128)S(1)}, f32[6,32,256]{2,1,0:T(8,128)S(1)}, u32[]{:S(2)}, u32[]{:S(2)}) %collective-permute-start.7) | collective-permute-done | bytes 196640 | tf_op jit(solution)/shard_map/ppermute | solution.py:249
  35.9 3.7 %collective-permute-done.8.refs_2_ = f32[6,32,256]{2,1,0:T(8,128)S(1)} collective-permute-done((f32[6,32,256]{2,1,0:T(8,128)S(1)}, f32[6,32,256]{2,1,0:T(8,128)S(1)}, u32[]{:S(2)}, u32[]{:S(2)}) %collective-permute-start.8) | collective-permute-done | bytes 196640 | tf_op jit(solution)/shard_map/ppermute | solution.py:249
  39.6 0.1 collective-permute-done.9.refs_3_
  39.7 0.7 %add_terms.1 = f32[6,32,256]{2,1,0:T(8,128)} custom-call(f32[6,32,256]{2,1,0:T(8,128)S(1)} %get-tuple-element.53.refs_0_, f32[6,32,256]{2,1,0:T(8,128)S(1)} %collective-permute-done.7.refs_1_, f32[6,32,256]{2,1,0:T(8,128)S(1)} %collective-permute-done.8.refs_2_, f32[6,32,256]{2,1,0:T(8,128)S(1)} %collective-permute-done.9.refs_3_), custom_call_target="tpu_custom_call" | custom-call | tf_op jit(solution)/shard_map/add_terms/pallas_call | solution.py:175
  (7 shorter events, 0.1 us)
Async XLA Ops:
  0.0 16.3 %collective-permute-start = (f32[1,128,512]{2,1,0:T(8,128)}, f32[1,128,512]{2,1,0:T(8,128)S(1)}, u32[]{:S(2)}, u32[]{:S(2)}) collective-permute-start(f32[1,128,512]{2,1,0:T(8,128)} %refs_0_.1), channel_id=1, source_target_pairs={{0,16},{8,24},{16,0},{24,8},{1,17},{9,25},{17,1},{25,9},{2,18},{10... | collective-permute-start | bytes 786440 | tf_op jit(solution)/shard_map/ppermute | solution.py:221
  4.0 13.0 %collective-permute-start.3 = (f32[1,128,512]{2,1,0:T(8,128)}, f32[1,128,512]{2,1,0:T(8,128)S(1)}, u32[]{:S(2)}, u32[]{:S(2)}) collective-permute-start(f32[1,128,512]{2,1,0:T(8,128)} %refs_0_.1), channel_id=1, source_target_pairs={{0,8},{8,0},{16,24},{24,16},{1,9},{9,1},{17,25},{25,17},{2,10},{10... | collective-permute-start | bytes 786440 | tf_op jit(solution)/shard_map/ppermute | solution.py:221
  5.6 11.9 %collective-permute-start.2 = (f32[1,128,512]{2,1,0:T(8,128)}, f32[1,128,512]{2,1,0:T(8,128)S(1)}, u32[]{:S(2)}, u32[]{:S(2)}) collective-permute-start(f32[1,128,512]{2,1,0:T(8,128)} %refs_0_.1), channel_id=1, source_target_pairs={{0,4},{4,0},{1,5},{5,1},{2,6},{6,2},{3,7},{7,3},{8,12},{12,8},{9,1... | collective-permute-start | bytes 786440 | tf_op jit(solution)/shard_map/ppermute | solution.py:218
  10.9 1.0 %copy-start.1 = (f32[1,128,512]{2,1,0:T(8,128)S(1)}, f32[1,128,512]{2,1,0:T(8,128)}, u32[]{:S(2)}) copy-start(f32[1,128,512]{2,1,0:T(8,128)} %refs_0_.1) | copy-start | bytes 786436
  12.0 1.4 %copy-start = (f32[6,256,256]{2,1,0:T(8,128)S(1)}, f32[6,256,256]{2,1,0:T(8,128)}, u32[]{:S(2)}) copy-start(f32[6,256,256]{2,1,0:T(8,128)} %amplitudes.1) | copy-start | bytes 4718596
  16.3 7.4 %collective-permute-start.1 = (f32[1,128,512]{2,1,0:T(8,128)S(1)}, f32[1,128,512]{2,1,0:T(8,128)S(1)}, u32[]{:S(2)}, u32[]{:S(2)}) collective-permute-start(f32[1,128,512]{2,1,0:T(8,128)S(1)} %collective-permute-done.refs_2_), channel_id=1, source_target_pairs={{0,8},{8,0},{16,24},{24,16},{1,9},{9,1},{17,25},{25,17},{2,10},{10... | collective-permute-start | bytes 786440 | tf_op jit(solution)/shard_map/ppermute | solution.py:221
  17.0 8.4 %collective-permute-start.6 = (f32[1,128,512]{2,1,0:T(8,128)S(1)}, f32[1,128,512]{2,1,0:T(8,128)S(1)}, u32[]{:S(2)}, u32[]{:S(2)}) collective-permute-start(f32[1,128,512]{2,1,0:T(8,128)S(1)} %collective-permute-done.refs_2_), channel_id=1, source_target_pairs={{0,4},{4,0},{1,5},{5,1},{2,6},{6,2},{3,7},{7,3},{8,12},{12,8},{9,1... | collective-permute-start | bytes 786440 | tf_op jit(solution)/shard_map/ppermute | solution.py:218
  17.0 8.3 %collective-permute-start.5 = (f32[1,128,512]{2,1,0:T(8,128)S(1)}, f32[1,128,512]{2,1,0:T(8,128)S(1)}, u32[]{:S(2)}, u32[]{:S(2)}) collective-permute-start(f32[1,128,512]{2,1,0:T(8,128)S(1)} %collective-permute-done.3.refs_1_), channel_id=1, source_target_pairs={{0,4},{4,0},{1,5},{5,1},{2,6},{6,2},{3,7},{7,3},{8,12},{12,8},{9,1... | collective-permute-start | bytes 786440 | tf_op jit(solution)/shard_map/ppermute | solution.py:218
  23.7 1.7 %collective-permute-start.4 = (f32[1,128,512]{2,1,0:T(8,128)S(1)}, f32[1,128,512]{2,1,0:T(8,128)S(1)}, u32[]{:S(2)}, u32[]{:S(2)}) collective-permute-start(f32[1,128,512]{2,1,0:T(8,128)S(1)} %collective-permute-done.1.refs_0_), channel_id=1, source_target_pairs={{0,4},{4,0},{1,5},{5,1},{2,6},{6,2},{3,7},{7,3},{8,12},{12,8},{9,1... | collective-permute-start | bytes 786440 | tf_op jit(solution)/shard_map/ppermute | solution.py:218
  27.2 8.7 %collective-permute-start.7 = (f32[6,32,256]{2,1,0:T(8,128)S(1)}, f32[6,32,256]{2,1,0:T(8,128)S(1)}, u32[]{:S(2)}, u32[]{:S(2)}) collective-permute-start(f32[6,32,256]{2,1,0:T(8,128)S(1)} %get-tuple-element.54), channel_id=1, source_target_pairs={{0,3},{1,2},{2,1},{3,0},{4,7},{5,6},{6,5},{7,4},{8,11},{9,10},{10,... | collective-permute-start | bytes 589832 | tf_op jit(solution)/shard_map/ppermute | solution.py:249
  29.5 10.1 %collective-permute-start.8 = (f32[6,32,256]{2,1,0:T(8,128)S(1)}, f32[6,32,256]{2,1,0:T(8,128)S(1)}, u32[]{:S(2)}, u32[]{:S(2)}) collective-permute-start(f32[6,32,256]{2,1,0:T(8,128)S(1)} %get-tuple-element.55), channel_id=1, source_target_pairs={{0,1},{1,0},{2,3},{3,2},{4,5},{5,4},{6,7},{7,6},{8,9},{9,8},{10,11... | collective-permute-start | bytes 589832 | tf_op jit(solution)/shard_map/ppermute | solution.py:249
  30.0 9.7 %collective-permute-start.9 = (f32[6,32,256]{2,1,0:T(8,128)S(1)}, f32[6,32,256]{2,1,0:T(8,128)S(1)}, u32[]{:S(2)}, u32[]{:S(2)}) collective-permute-start(f32[6,32,256]{2,1,0:T(8,128)S(1)} %get-tuple-element.56), channel_id=1, source_target_pairs={{0,2},{1,3},{2,0},{3,1},{4,6},{5,7},{6,4},{7,5},{8,10},{9,11},{10,... | collective-permute-start | bytes 589832 | tf_op jit(solution)/shard_map/ppermute | solution.py:249

commit v7 on v6

--- a/solution.py
+++ b/solution.py
@@ -90,9 +90,10 @@
     )(mask, *pieces, *held)
 
 
-def pairs_kernel(row, factors, late, last, count, places, mask, weights, *refs):
+def pairs_kernel(row, col, factors, late, last, shifts, places, mask, weights, *refs):
     pieces = refs[:len(late)]
     mhigh, mlow = refs[len(late):len(late) + 2]
+    count = len(shifts)
     held = refs[len(late) + 4:-count - 2]
     outs, (high, low) = refs[-count - 2:-2], refs[-2:]
     at = places[...]
@@ -104,7 +105,7 @@
 
     pairs, chunk, domv = outs[0].shape
     qs = len(factors)
-    half = domv // row
+    size = count * chunk
     blocks = domv // BS
     tiles = domv // LANES
     across = (((1,), (1,)), ((), ()))
@@ -116,8 +117,8 @@
             return pl.ds(pl.multiple_of(at[0, n * pairs + p], size), size)
 
         y_spans = [rows_at(i, BS) for i in range(blocks)]
-        x_spans = [rows_at(blocks + n, chunk) for n in range(count)]
-        first = blocks + count
+        x_spans = [rows_at(blocks + n, chunk) for n in shifts]
+        first = blocks + col
         sources = [(at[0, (first + 2 * j) * pairs + p], at[0, (first + 2 * j + 1) * pairs + p]) for j in range(tiles)]
 
         def gather(source, q, spans, size):
@@ -128,40 +129,40 @@
         yhigh, ylow = (jnp.concatenate([gather(source, q, y_spans, BS) for q in factors], 1) for source in (high, low))
         xhigh, xlow = (jnp.concatenate([gather(source, q, x_spans, chunk) for q in factors], 0) for source in (high, low))
         both = dot(jnp.concatenate([xhigh, xlow], 0), mhigh[p], along)
-        size = qs * half
-        halfway = both[:size] + both[size:] + dot(xhigh, mlow[p], along)
-        hhigh, hlow = split(jnp.concatenate([halfway[q * half:(q + 1) * half] for q in range(qs)], 1))
+        halfway = both[:qs * size] + both[qs * size:] + dot(xhigh, mlow[p], along)
+        hhigh, hlow = split(jnp.concatenate([halfway[q * size:(q + 1) * size] for q in range(qs)], 1))
         both = dot(jnp.concatenate([hhigh, hlow], 0), yhigh, across)
-        total = both[:half] + both[half:] + dot(hhigh, ylow, across)
-        for n, out in enumerate(outs):
+        total = both[:size] + both[size:] + dot(hhigh, ylow, across)
+        for n, (shift, out) in enumerate(zip(shifts, outs)):
             term = total[n * chunk:(n + 1) * chunk]
             if held:
-                term += held[n][p]
-            out[p] = term * weights[n, p] if last else term
+                term += held[shift][p]
+            out[p] = term * weights[shift, p] if last else term
 
     for p in range(pairs):
         contract(p)
 
 
-def contract_pairs(row, col, places, mask, weights, factors, last, late, mhigh, mlow, high, low, held=()):
+def contract_pairs(row, col, places, mask, weights, factors, last, shifts, late, mhigh, mlow, high, low, held=()):
     pairs, domv, _ = mhigh.shape
     chunk = domv // (row * col)
     keys = [(slot, q) for slot, q, _ in late]
     pieces = [piece for _, _, piece in late]
     prepared = 3 + len(pieces) + 2
+    count = len(shifts)
     results = pl.pallas_call(
-        functools.partial(pairs_kernel, row, factors, keys, last, col),
+        functools.partial(pairs_kernel, row, col, factors, keys, last, shifts),
         name="contract_pairs",
-        out_shape=[jax.ShapeDtypeStruct((pairs, chunk, domv), jnp.float32)] * col
+        out_shape=[jax.ShapeDtypeStruct((pairs, chunk, domv), jnp.float32)] * count
         + [jax.ShapeDtypeStruct(high.shape, high.dtype)] * 2,
         in_specs=[VMEM_SPEC] * (3 + len(pieces) + 4 + len(held)),
-        out_specs=[VMEM_SPEC] * (col + 2),
-        input_output_aliases={prepared: col, prepared + 1: col + 1},
-        compiler_params=pltpu.CompilerParams(vmem_limit_bytes=VMEM_LIMIT),
-        cost_estimate=pl.CostEstimate(flops=6 * pairs * len(factors) * domv ** 3 * 4 // row, bytes_accessed=8 * high.size,
+        out_specs=[VMEM_SPEC] * (count + 2),
+        input_output_aliases={prepared: count, prepared + 1: count + 1},
+        compiler_params=pltpu.CompilerParams(vmem_limit_bytes=VMEM_LIMIT),
+        cost_estimate=pl.CostEstimate(flops=6 * pairs * len(factors) * domv ** 3 * 4 * count // (row * col), bytes_accessed=8 * high.size,
                                       transcendentals=0),
     )(places, mask, weights, *pieces, mhigh, mlow, high, low, *held)
-    return results[:col], results[col], results[col + 1]
+    return results[:count], results[count], results[count + 1]
 
 
 def add_kernel(*refs):
@@ -171,7 +172,7 @@
     refs[-1][...] = total
 
 
-def add_terms(*terms):
+def add_terms(*terms, ahead=0):
     return pl.pallas_call(
         add_kernel,
         name="add_terms",
@@ -179,6 +180,7 @@
         in_specs=[VMEM_SPEC] * len(terms),
         out_specs=VMEM_SPEC,
         compiler_params=pltpu.CompilerParams(vmem_limit_bytes=VMEM_LIMIT),
+        cost_estimate=pl.CostEstimate(flops=0, bytes_accessed=ahead + 4 * len(terms) * terms[0].size, transcendentals=0),
     )(*terms)
 
 
@@ -198,6 +200,8 @@
     def pick(which, table):
         hits = which[:, None] == jnp.arange(table.shape[0])[None, :]
         return jnp.sum(jnp.where(hits[:, :, None], table[None], 0), axis=1)
+
+    shifts = sorted(range(col), key=lambda s: -bin(s).count("1"))
 
     blocks_of, flags = domains.T, domain_mask.T
     starts = ((blocks_of // per_slot) ^ plane) * (per_slot * BS) + blocks_of % per_slot * BS
@@ -238,17 +242,19 @@
         last, high, low = lax.optimization_barrier((last, high, low))
         contract = functools.partial(contract_pairs, row, col, places, mask, outer)
         sent = others(3, siblings(last)) + others(1, s_near) + others(2, s_cross)
-        held, high, low = contract(range(nq), False, [(3, 0, last)], mhigh, mlow, high, low)
-        terms, _, _ = contract(range(nq, row * nq), True, sent, mhigh, mlow, high, low, held)
+        held, high, low = contract(range(nq), False, range(col), [(3, 0, last)], mhigh, mlow, high, low)
+        far, high, low = contract(range(nq, row * nq), True, shifts[:1], sent, mhigh, mlow, high, low, held)
+        rest, _, _ = contract(range(nq, row * nq), True, shifts[1:], [], mhigh, mlow, high, low, held)
+        terms = dict(zip(shifts, far + rest))
     else:
         whole = lax.all_gather(factors, "wide", axis=1, tiled=True)
         high, low = prepare([(0, 0, whole)] + others(0, siblings(whole)), shape)
         contract = functools.partial(contract_pairs, row, col, places, mask, outer)
-        terms, _, _ = contract(range(row * nq), True, [], mhigh, mlow, high, low)
-
-    moved = [lax.ppermute(terms[s], "col", [(i, partner(i, s, col)) for i in range(col)])
-             for s in sorted(range(1, col), key=lambda s: -bin(s).count("1"))]
-    return add_terms(terms[0], *moved)
+        rest, _, _ = contract(range(row * nq), True, shifts, [], mhigh, mlow, high, low)
+        terms = dict(zip(shifts, rest))
+
+    moved = [lax.ppermute(terms[s], "col", [(i, partner(i, s, col)) for i in range(col)]) for s in shifts if s]
+    return add_terms(add_terms(terms[0], moved[0], ahead=1 << 24), *moved[1:])
 
 
 def solution(mesh):

time: 40.7 us -> 40.4 us (level)
  waiting for transfers between devices: 17.3 us -> 15.9 us
  Pallas kernels: 4.82 us -> 5.82 us
    ppermute x3, waiting for transfers between devices: 8.93 us -> 7.48 us  [body(): lax.ppermute(terms[s], 'col', [(i, partner(i, s, col)) for i in range(col)])]
    pallas_call x2 -> x3, Pallas kernels: 3.42 us -> 4.43 us  [contract_pairs(): pl.pallas_call(functools.partial(pairs_kernel, row, col, factors, keys, l...]
  transfers between devices with their start and end apart: 10 -> 10, of which waited for: 5 -> 5; matrix products, arithmetic and copies ran while one was open for 13% -> 13% of each run, Pallas kernels for 6% -> 9%
where the time goes in v7:
time: 40.4 us; the launch traced here: 40.1 us
  waiting for transfers between devices  15.9 us (39%)
  starting transfers between devices  10.5 us (26%)
  Pallas kernels  5.82 us (14%)
  local copies, waits for them, and re-layouts  4.92 us (12%)
  other arithmetic  2.78 us (7%)
    ppermute x3, waiting for transfers between devices, across(): return lax.ppermute(piece, 'wide', [(i, i ^ shift) for i in range(wide)])  8.39 us
    ppermute x3, waiting for transfers between devices, body(): lax.ppermute(terms[s], 'col', [(i, partner(i, s, col)) for i in range(col)])  7.48 us
    ppermute x3, starting transfers between devices, across(): return lax.ppermute(piece, 'wide', [(i, i ^ shift) for i in range(wide)])  6.33 us
    pallas_call x3, Pallas kernels, contract_pairs(): pl.pallas_call(functools.partial(pairs_kernel, row, col, factors, keys, l...  4.43 us
    ppermute x3, starting transfers between devices, body(): lax.ppermute(terms[s], 'col', [(i, partner(i, s, col)) for i in range(col)])  3.65 us
    unnamed x5, local copies, waits for them, and re-layouts  3.12 us
    reduce_sum x2, other arithmetic, pick(): return jnp.sum(jnp.where(hits[:, :, None], table[None], 0), axis=1)  1.54 us
    slice x2, local copies, waits for them, and re-layouts, body(): firsts, seconds = (blocks_of[0::2], blocks_of[1::2])  1.4 us
  transfers between devices with their start and end apart: 10, of which 5 were waited for; matrix products, arithmetic and copies ran while one was open for 13% of the time, Pallas kernels for 9%

profile of v7, /device:TPU:0, one launch (start us, length us, event | category | flops | bytes accessed | tf_op | source)
XLA Modules:
  0.0 40.1 jit_solution(12179681304842919484)
XLA Ops:
  0.0 4.0 %collective-permute-start = (f32[1,128,512]{2,1,0:T(8,128)}, f32[1,128,512]{2,1,0:T(8,128)S(1)}, u32[]{:S(2)}, u32[]{:S(2)}) collective-permute-start(f32[1,128,512]{2,1,0:T(8,128)} %refs_0_.1), channel_id=1, source_target_pairs={{0,16},{8,24},{16,0},{24,8},{1,17},{9,25},{17,1},{25,9},{2,18},{10... | collective-permute-start | bytes 786440 | tf_op jit(solution)/shard_map/ppermute | solution.py:225
  4.0 1.6 %collective-permute-start.3 = (f32[1,128,512]{2,1,0:T(8,128)}, f32[1,128,512]{2,1,0:T(8,128)S(1)}, u32[]{:S(2)}, u32[]{:S(2)}) collective-permute-start(f32[1,128,512]{2,1,0:T(8,128)} %refs_0_.1), channel_id=1, source_target_pairs={{0,8},{8,0},{16,24},{24,16},{1,9},{9,1},{17,25},{25,17},{2,10},{10... | collective-permute-start | bytes 786440 | tf_op jit(solution)/shard_map/ppermute | solution.py:225
  5.6 0.0 collective-permute-start.2
  5.6 0.7 %slice.6 = s32[2,6]{1,0:T(2,128)S(1)} slice(s32[4,6]{1,0:T(4,128)} %bitcast.14), slice={[0:4:2], [0:6:1]} | slice | bytes 96 | tf_op jit(solution)/shard_map/slice | solution.py:210
  6.3 0.7 %slice.7 = s32[2,6]{1,0:T(2,128)S(1)} slice(s32[4,6]{1,0:T(4,128)} %bitcast.15), slice={[1:4:2], [0:6:1]} | slice | bytes 96 | tf_op jit(solution)/shard_map/slice | solution.py:210
  7.0 0.7 %fusion.2 = s32[4,6]{1,0:T(4,128)S(1)} fusion(s32[]{:T(128)S(6)} %axis_index.33, s32[6,4]{0,1:T(4,128)} %param.7), kind=kLoop, calls=%fused_computation.14 | loop fusion | flops 552 | bytes 196 | tf_op jit(solution)/shard_map/add | solution.py:207
  7.7 0.1 and_select_fusion.4
  7.8 0.1 iota_compare_fusion.1
  7.9 0.8 %copy.20 = s32[6,4]{1,0:T(8,128)S(1)} copy(s32[6,4]{0,1:T(4,128)} %param.8) | data formatting | bytes 192 | tf_op args[3]
  8.7 0.1 broadcast_in_dim.77
  8.8 0.1 mul.76
  8.9 0.1 iota_compare_fusion
  8.9 0.1 multiply_convert_fusion.1.weights
  9.1 0.8 %select_reduce_fusion.1 = (s32[4,6]{1,0:T(4,128)S(1)}, s32[4,6]{1,0:T(4,128)S(1)}) fusion(s32[4,6]{1,0:T(4,128)} %bitcast.12, pred[4,4]{1,0:T(4,128)(4,1)S(1)} %iota_compare_fusion.1, s32[4,6]{1,0:T(4,128)S(1)} %fusion.2), kind=kLoop, calls=%fused_computation.4 | loop fusion | flops 336 | bytes 400 | tf_op jit(solution)/shard_map/reduce_sum | solution.py:202
  9.8 0.1 broadcast_add_fusion
  9.9 0.8 %select_reduce_fusion = s32[8,8]{1,0:T(8,128)S(1)} fusion(s32[8,8]{1,0:T(8,128)} %param.9, pred[8,8]{1,0:T(8,128)(4,1)S(1)} %iota_compare_fusion), kind=kLoop, calls=%fused_computation | loop fusion | flops 960 | bytes 576 | tf_op jit(solution)/shard_map/reduce_sum | solution.py:202
  10.7 0.1 reshape.185.places
  10.8 0.1 broadcast_in_dim.76
  10.9 0.1 convert_element_type.35.mask
  11.0 0.0 copy-start.1
  11.0 0.9 %copy-done.1 = f32[1,128,512]{2,1,0:T(8,128)S(1)} copy-done((f32[1,128,512]{2,1,0:T(8,128)S(1)}, f32[1,128,512]{2,1,0:T(8,128)}, u32[]{:S(2)}) %copy-start.1) | copy-done | bytes 262168
  11.9 0.1 screen_factors.2
  12.0 0.0 copy-start
  12.1 1.4 %copy-done = f32[6,256,256]{2,1,0:T(8,128)S(1)} copy-done((f32[6,256,256]{2,1,0:T(8,128)S(1)}, f32[6,256,256]{2,1,0:T(8,128)}, u32[]{:S(2)}) %copy-start) | copy-done | bytes 1572888
  13.5 0.2 mask_amplitudes.1
  13.7 0.1 multiply_convert_fusion.weights
  13.8 2.5 %collective-permute-done.refs_2_ = f32[1,128,512]{2,1,0:T(8,128)S(1)} collective-permute-done((f32[1,128,512]{2,1,0:T(8,128)}, f32[1,128,512]{2,1,0:T(8,128)S(1)}, u32[]{:S(2)}, u32[]{:S(2)}) %collective-permute-start) | collective-permute-done | bytes 262176 | tf_op jit(solution)/shard_map/ppermute | solution.py:225
  16.3 0.7 %collective-permute-start.1 = (f32[1,128,512]{2,1,0:T(8,128)S(1)}, f32[1,128,512]{2,1,0:T(8,128)S(1)}, u32[]{:S(2)}, u32[]{:S(2)}) collective-permute-start(f32[1,128,512]{2,1,0:T(8,128)S(1)} %collective-permute-done.refs_2_), channel_id=1, source_target_pairs={{0,8},{8,0},{16,24},{24,16},{1,9},{9,1},{17,25},{25,17},{2,10},{10... | collective-permute-start | bytes 786440 | tf_op jit(solution)/shard_map/ppermute | solution.py:225
  17.0 0.0 collective-permute-start.6
  17.0 0.0 collective-permute-done.3.refs_1_
  17.0 0.5 %collective-permute-start.5 = (f32[1,128,512]{2,1,0:T(8,128)S(1)}, f32[1,128,512]{2,1,0:T(8,128)S(1)}, u32[]{:S(2)}, u32[]{:S(2)}) collective-permute-start(f32[1,128,512]{2,1,0:T(8,128)S(1)} %collective-permute-done.3.refs_1_), channel_id=1, source_target_pairs={{0,4},{4,0},{1,5},{5,1},{2,6},{6,2},{3,7},{7,3},{8,12},{12,8},{9,1... | collective-permute-start | bytes 786440 | tf_op jit(solution)/shard_map/ppermute | solution.py:222
  17.5 0.0 collective-permute-done.2.refs_0_
  17.5 0.3 screen_factors.3
  17.8 5.9 %collective-permute-done.1.refs_0_ = f32[1,128,512]{2,1,0:T(8,128)S(1)} collective-permute-done((f32[1,128,512]{2,1,0:T(8,128)S(1)}, f32[1,128,512]{2,1,0:T(8,128)S(1)}, u32[]{:S(2)}, u32[]{:S(2)}) %collective-permute-start.1) | collective-permute-done | bytes 262176 | tf_op jit(solution)/shard_map/ppermute | solution.py:225
  23.7 0.0 collective-permute-start.4
  23.7 1.6 %contract_pairs.3 = (f32[6,32,256]{2,1,0:T(8,128)S(1)}, f32[6,32,256]{2,1,0:T(8,128)S(1)}, f32[6,32,256]{2,1,0:T(8,128)S(1)}, f32[6,32,256]{2,1,0:T(8,128)S(1)},...) custom-call(s32[1,72]{1,0:T(1,128)S(1)} %reshape.185.places, ...), custom_call_target="tpu_custom_call", output_to_operand_aliasing={{4}: (6, {}), {5}: (7, {})} | custom-call | flops 1207959552 | bytes 8388608 | tf_op jit(solution)/shard_map/contract_pairs/pallas_call | solution.py:153
  25.3 0.0 collective-permute-done.6.refs_2_
  25.4 0.0 collective-permute-done.5.refs_1_
  25.4 0.0 collective-permute-done.4.refs_0_
  25.4 1.5 %contract_pairs.4 = (f32[6,32,256]{2,1,0:T(8,128)S(1)}, bf16[8,2,512,128]{3,2,1,0:T(8,128)(2,1)S(1)}, bf16[8,2,512,128]{3,2,1,0:T(8,128)(2,1)S(1)}) custom-call(s32[1,72]{1,0:T(1,128)S(1)} %reshape.185.places, f32[8,1,512]{2,1,0:T(1,128)S(1)} %convert_element_type.35.mask, ...), custom_call_target="tpu_custom_call", output_to_operand_aliasing={{1}: (8, {}), {2}: (9, {})} | custom-call | flops 301989888 | bytes 8388608 | tf_op jit(solution)/shard_map/contract_pairs/pallas_call | solution.py:153
  26.8 2.3 %collective-permute-start.7 = (f32[6,32,256]{2,1,0:T(8,128)S(1)}, f32[6,32,256]{2,1,0:T(8,128)S(1)}, u32[]{:S(2)}, u32[]{:S(2)}) collective-permute-start(f32[6,32,256]{2,1,0:T(8,128)S(1)} %get-tuple-element.58), channel_id=1, source_target_pairs={{0,3},{1,2},{2,1},{3,0},{4,7},{5,6},{6,5},{7,4},{8,11},{9,10},{10,... | collective-permute-start | bytes 589832 | tf_op jit(solution)/shard_map/ppermute | solution.py:256
  29.1 1.3 %contract_pairs.5 = (f32[6,32,256]{2,1,0:T(8,128)S(1)}, f32[6,32,256]{2,1,0:T(8,128)S(1)}, f32[6,32,256]{2,1,0:T(8,128)S(1)}, bf16[8,2,512,128]{3,2,1,0:T(8,128)(2,1)S(1)}, bf16[8,2,512,128]{3,2,1,0:T(8,128)(2,1)S(1)}) custom-call(s32[1,72]{1,0:T(1,128)S(1)} %reshape.185.places, ...), custom_call_target="tpu_custom_call", output_to_operand_aliasing={{3}: (5, {}), {4}: (6, {})} | custom-call | flops 905969664 | bytes 8388608 | tf_op jit(solution)/shard_map/contract_pairs/pallas_call | solution.py:153
  30.5 0.6 %collective-permute-start.8 = (f32[6,32,256]{2,1,0:T(8,128)S(1)}, f32[6,32,256]{2,1,0:T(8,128)S(1)}, u32[]{:S(2)}, u32[]{:S(2)}) collective-permute-start(f32[6,32,256]{2,1,0:T(8,128)S(1)} %get-tuple-element.59), channel_id=1, source_target_pairs={{0,1},{1,0},{2,3},{3,2},{4,5},{5,4},{6,7},{7,6},{8,9},{9,8},{10,11... | collective-permute-start | bytes 589832 | tf_op jit(solution)/shard_map/ppermute | solution.py:256
  31.1 0.7 %collective-permute-start.9 = (f32[6,32,256]{2,1,0:T(8,128)S(1)}, f32[6,32,256]{2,1,0:T(8,128)S(1)}, u32[]{:S(2)}, u32[]{:S(2)}) collective-permute-start(f32[6,32,256]{2,1,0:T(8,128)S(1)} %get-tuple-element.60), channel_id=1, source_target_pairs={{0,2},{1,3},{2,0},{3,1},{4,6},{5,7},{6,4},{7,5},{8,10},{9,11},{10,... | collective-permute-start | bytes 589832 | tf_op jit(solution)/shard_map/ppermute | solution.py:256
  31.8 3.7 %collective-permute-done.7.refs_1_ = f32[6,32,256]{2,1,0:T(8,128)S(1)} collective-permute-done((f32[6,32,256]{2,1,0:T(8,128)S(1)}, f32[6,32,256]{2,1,0:T(8,128)S(1)}, u32[]{:S(2)}, u32[]{:S(2)}) %collective-permute-start.7) | collective-permute-done | bytes 196640 | tf_op jit(solution)/shard_map/ppermute | solution.py:256
  35.5 3.7 %collective-permute-done.8.refs_1_ = f32[6,32,256]{2,1,0:T(8,128)S(1)} collective-permute-done((f32[6,32,256]{2,1,0:T(8,128)S(1)}, f32[6,32,256]{2,1,0:T(8,128)S(1)}, u32[]{:S(2)}, u32[]{:S(2)}) %collective-permute-start.8) | collective-permute-done | bytes 196640 | tf_op jit(solution)/shard_map/ppermute | solution.py:256
  39.2 0.1 collective-permute-done.9.refs_2_
  39.3 0.7 %add_terms.3 = f32[6,32,256]{2,1,0:T(8,128)} custom-call(f32[6,32,256]{2,1,0:T(8,128)S(1)} %add_terms.2.refs_0_, f32[6,32,256]{2,1,0:T(8,128)S(1)} %collective-permute-done.8.refs_1_, f32[6,32,256]{2,1,0:T(8,128)S(1)} %collective-permute-done.9.refs_2_), custom_call_target="tpu_custom_call" | custom-call | bytes 589824 | tf_op jit(solution)/shard_map/add_terms/pallas_call | solution.py:176
  (8 shorter events, 0.1 us)
Async XLA Ops:
  0.0 16.3 %collective-permute-start = (f32[1,128,512]{2,1,0:T(8,128)}, f32[1,128,512]{2,1,0:T(8,128)S(1)}, u32[]{:S(2)}, u32[]{:S(2)}) collective-permute-start(f32[1,128,512]{2,1,0:T(8,128)} %refs_0_.1), channel_id=1, source_target_pairs={{0,16},{8,24},{16,0},{24,8},{1,17},{9,25},{17,1},{25,9},{2,18},{10... | collective-permute-start | bytes 786440 | tf_op jit(solution)/shard_map/ppermute | solution.py:225
  4.0 13.0 %collective-permute-start.3 = (f32[1,128,512]{2,1,0:T(8,128)}, f32[1,128,512]{2,1,0:T(8,128)S(1)}, u32[]{:S(2)}, u32[]{:S(2)}) collective-permute-start(f32[1,128,512]{2,1,0:T(8,128)} %refs_0_.1), channel_id=1, source_target_pairs={{0,8},{8,0},{16,24},{24,16},{1,9},{9,1},{17,25},{25,17},{2,10},{10... | collective-permute-start | bytes 786440 | tf_op jit(solution)/shard_map/ppermute | solution.py:225
  5.6 11.9 %collective-permute-start.2 = (f32[1,128,512]{2,1,0:T(8,128)}, f32[1,128,512]{2,1,0:T(8,128)S(1)}, u32[]{:S(2)}, u32[]{:S(2)}) collective-permute-start(f32[1,128,512]{2,1,0:T(8,128)} %refs_0_.1), channel_id=1, source_target_pairs={{0,4},{4,0},{1,5},{5,1},{2,6},{6,2},{3,7},{7,3},{8,12},{12,8},{9,1... | collective-permute-start | bytes 786440 | tf_op jit(solution)/shard_map/ppermute | solution.py:222
  11.0 1.0 %copy-start.1 = (f32[1,128,512]{2,1,0:T(8,128)S(1)}, f32[1,128,512]{2,1,0:T(8,128)}, u32[]{:S(2)}) copy-start(f32[1,128,512]{2,1,0:T(8,128)} %refs_0_.1) | copy-start | bytes 786436
  12.0 1.4 %copy-start = (f32[6,256,256]{2,1,0:T(8,128)S(1)}, f32[6,256,256]{2,1,0:T(8,128)}, u32[]{:S(2)}) copy-start(f32[6,256,256]{2,1,0:T(8,128)} %amplitudes.1) | copy-start | bytes 4718596
  16.3 7.4 %collective-permute-start.1 = (f32[1,128,512]{2,1,0:T(8,128)S(1)}, f32[1,128,512]{2,1,0:T(8,128)S(1)}, u32[]{:S(2)}, u32[]{:S(2)}) collective-permute-start(f32[1,128,512]{2,1,0:T(8,128)S(1)} %collective-permute-done.refs_2_), channel_id=1, source_target_pairs={{0,8},{8,0},{16,24},{24,16},{1,9},{9,1},{17,25},{25,17},{2,10},{10... | collective-permute-start | bytes 786440 | tf_op jit(solution)/shard_map/ppermute | solution.py:225
  17.0 8.3 %collective-permute-start.6 = (f32[1,128,512]{2,1,0:T(8,128)S(1)}, f32[1,128,512]{2,1,0:T(8,128)S(1)}, u32[]{:S(2)}, u32[]{:S(2)}) collective-permute-start(f32[1,128,512]{2,1,0:T(8,128)S(1)} %collective-permute-done.refs_2_), channel_id=1, source_target_pairs={{0,4},{4,0},{1,5},{5,1},{2,6},{6,2},{3,7},{7,3},{8,12},{12,8},{9,1... | collective-permute-start | bytes 786440 | tf_op jit(solution)/shard_map/ppermute | solution.py:222
  17.0 8.3 %collective-permute-start.5 = (f32[1,128,512]{2,1,0:T(8,128)S(1)}, f32[1,128,512]{2,1,0:T(8,128)S(1)}, u32[]{:S(2)}, u32[]{:S(2)}) collective-permute-start(f32[1,128,512]{2,1,0:T(8,128)S(1)} %collective-permute-done.3.refs_1_), channel_id=1, source_target_pairs={{0,4},{4,0},{1,5},{5,1},{2,6},{6,2},{3,7},{7,3},{8,12},{12,8},{9,1... | collective-permute-start | bytes 786440 | tf_op jit(solution)/shard_map/ppermute | solution.py:222
  23.7 1.7 %collective-permute-start.4 = (f32[1,128,512]{2,1,0:T(8,128)S(1)}, f32[1,128,512]{2,1,0:T(8,128)S(1)}, u32[]{:S(2)}, u32[]{:S(2)}) collective-permute-start(f32[1,128,512]{2,1,0:T(8,128)S(1)} %collective-permute-done.1.refs_0_), channel_id=1, source_target_pairs={{0,4},{4,0},{1,5},{5,1},{2,6},{6,2},{3,7},{7,3},{8,12},{12,8},{9,1... | collective-permute-start | bytes 786440 | tf_op jit(solution)/shard_map/ppermute | solution.py:222
  26.8 8.7 %collective-permute-start.7 = (f32[6,32,256]{2,1,0:T(8,128)S(1)}, f32[6,32,256]{2,1,0:T(8,128)S(1)}, u32[]{:S(2)}, u32[]{:S(2)}) collective-permute-start(f32[6,32,256]{2,1,0:T(8,128)S(1)} %get-tuple-element.58), channel_id=1, source_target_pairs={{0,3},{1,2},{2,1},{3,0},{4,7},{5,6},{6,5},{7,4},{8,11},{9,10},{10,... | collective-permute-start | bytes 589832 | tf_op jit(solution)/shard_map/ppermute | solution.py:256
  30.5 8.7 %collective-permute-start.8 = (f32[6,32,256]{2,1,0:T(8,128)S(1)}, f32[6,32,256]{2,1,0:T(8,128)S(1)}, u32[]{:S(2)}, u32[]{:S(2)}) collective-permute-start(f32[6,32,256]{2,1,0:T(8,128)S(1)} %get-tuple-element.59), channel_id=1, source_target_pairs={{0,1},{1,0},{2,3},{3,2},{4,5},{5,4},{6,7},{7,6},{8,9},{9,8},{10,11... | collective-permute-start | bytes 589832 | tf_op jit(solution)/shard_map/ppermute | solution.py:256
  31.1 8.2 %collective-permute-start.9 = (f32[6,32,256]{2,1,0:T(8,128)S(1)}, f32[6,32,256]{2,1,0:T(8,128)S(1)}, u32[]{:S(2)}, u32[]{:S(2)}) collective-permute-start(f32[6,32,256]{2,1,0:T(8,128)S(1)} %get-tuple-element.60), channel_id=1, source_target_pairs={{0,2},{1,3},{2,0},{3,1},{4,6},{5,7},{6,4},{7,5},{8,10},{9,11},{10,... | collective-permute-start | bytes 589832 | tf_op jit(solution)/shard_map/ppermute | solution.py:256

commit v8 on v7

--- a/solution.py
+++ b/solution.py
@@ -136,7 +136,7 @@
         for n, (shift, out) in enumerate(zip(shifts, outs)):
             term = total[n * chunk:(n + 1) * chunk]
             if held:
-                term += held[shift][p]
+                term += held[n][p]
             out[p] = term * weights[shift, p] if last else term
 
     for p in range(pairs):
@@ -241,10 +241,11 @@
         high, low = prepare(early, shape, (high, low))
         last, high, low = lax.optimization_barrier((last, high, low))
         contract = functools.partial(contract_pairs, row, col, places, mask, outer)
-        sent = others(3, siblings(last)) + others(1, s_near) + others(2, s_cross)
-        held, high, low = contract(range(nq), False, range(col), [(3, 0, last)], mhigh, mlow, high, low)
-        far, high, low = contract(range(nq, row * nq), True, shifts[:1], sent, mhigh, mlow, high, low, held)
-        rest, _, _ = contract(range(nq, row * nq), True, shifts[1:], [], mhigh, mlow, high, low, held)
+        s_last = siblings(last)
+        ready = [(3, 0, last)] + others(1, s_near) + others(2, s_cross)
+        held, high, low = contract(range(nq), False, shifts[:1], ready, mhigh, mlow, high, low)
+        far, high, low = contract(range(nq, row * nq), True, shifts[:1], others(3, s_last), mhigh, mlow, high, low, held)
+        rest, _, _ = contract(range(row * nq), True, shifts[1:], [], mhigh, mlow, high, low)
         terms = dict(zip(shifts, far + rest))
     else:
         whole = lax.all_gather(factors, "wide", axis=1, tiled=True)

time: 40.4 us -> 40.1 us (level)
  waiting for transfers between devices: 15.9 us -> 15.1 us
  Pallas kernels: 5.82 us -> 6.29 us
    ppermute x3, waiting for transfers between devices: 7.48 us -> 6.69 us  [body(): lax.ppermute(terms[s], 'col', [(i, partner(i, s, col)) for i in range(col)])]
    pallas_call x3, Pallas kernels: 4.43 us -> 4.91 us  [contract_pairs(): pl.pallas_call(functools.partial(pairs_kernel, row, col, factors, keys, l...]
  transfers between devices with their start and end apart: 10 -> 10, of which waited for: 5 -> 6; matrix products, arithmetic and copies ran while one was open for 13% -> 13% of each run, Pallas kernels for 9% -> 11%
where the time goes in v8:
time: 40.1 us; the launch traced here: 39.8 us
  waiting for transfers between devices  15.1 us (38%)
  starting transfers between devices  10.5 us (26%)
  Pallas kernels  6.29 us (16%)
  local copies, waits for them, and re-layouts  4.92 us (12%)
  other arithmetic  2.78 us (7%)
    ppermute x3, waiting for transfers between devices, across(): return lax.ppermute(piece, 'wide', [(i, i ^ shift) for i in range(wide)])  8.39 us
    ppermute x3, waiting for transfers between devices, body(): lax.ppermute(terms[s], 'col', [(i, partner(i, s, col)) for i in range(col)])  6.69 us
    ppermute x3, starting transfers between devices, across(): return lax.ppermute(piece, 'wide', [(i, i ^ shift) for i in range(wide)])  6.33 us
    pallas_call x3, Pallas kernels, contract_pairs(): pl.pallas_call(functools.partial(pairs_kernel, row, col, factors, keys, l...  4.91 us
    ppermute x3, starting transfers between devices, body(): lax.ppermute(terms[s], 'col', [(i, partner(i, s, col)) for i in range(col)])  3.63 us
    unnamed x5, local copies, waits for them, and re-layouts  3.12 us
    reduce_sum x2, other arithmetic, pick(): return jnp.sum(jnp.where(hits[:, :, None], table[None], 0), axis=1)  1.55 us
    slice x2, local copies, waits for them, and re-layouts, body(): firsts, seconds = (blocks_of[0::2], blocks_of[1::2])  1.4 us
  transfers between devices with their start and end apart: 10, of which 6 were waited for; matrix products, arithmetic and copies ran while one was open for 13% of the time, Pallas kernels for 11%

profile of v8, /device:TPU:0, one launch (start us, length us, event | category | flops | bytes accessed | tf_op | source)
XLA Modules:
  0.0 39.8 jit_solution(13678608885558045781)
XLA Ops:
  0.0 4.0 %collective-permute-start = (f32[1,128,512]{2,1,0:T(8,128)}, f32[1,128,512]{2,1,0:T(8,128)S(1)}, u32[]{:S(2)}, u32[]{:S(2)}) collective-permute-start(f32[1,128,512]{2,1,0:T(8,128)} %refs_0_.1), channel_id=1, source_target_pairs={{0,16},{8,24},{16,0},{24,8},{1,17},{9,25},{17,1},{25,9},{2,18},{10... | collective-permute-start | bytes 786440 | tf_op jit(solution)/shard_map/ppermute | solution.py:225
  4.0 1.6 %collective-permute-start.3 = (f32[1,128,512]{2,1,0:T(8,128)}, f32[1,128,512]{2,1,0:T(8,128)S(1)}, u32[]{:S(2)}, u32[]{:S(2)}) collective-permute-start(f32[1,128,512]{2,1,0:T(8,128)} %refs_0_.1), channel_id=1, source_target_pairs={{0,8},{8,0},{16,24},{24,16},{1,9},{9,1},{17,25},{25,17},{2,10},{10... | collective-permute-start | bytes 786440 | tf_op jit(solution)/shard_map/ppermute | solution.py:225
  5.6 0.0 collective-permute-start.2
  5.6 0.7 %slice.6 = s32[2,6]{1,0:T(2,128)S(1)} slice(s32[4,6]{1,0:T(4,128)} %bitcast.14), slice={[0:4:2], [0:6:1]} | slice | bytes 96 | tf_op jit(solution)/shard_map/slice | solution.py:210
  6.3 0.7 %slice.7 = s32[2,6]{1,0:T(2,128)S(1)} slice(s32[4,6]{1,0:T(4,128)} %bitcast.15), slice={[1:4:2], [0:6:1]} | slice | bytes 96 | tf_op jit(solution)/shard_map/slice | solution.py:210
  7.0 0.7 %fusion.2 = s32[4,6]{1,0:T(4,128)S(1)} fusion(s32[]{:T(128)S(6)} %axis_index.33, s32[6,4]{0,1:T(4,128)} %param.7), kind=kLoop, calls=%fused_computation.14 | loop fusion | flops 552 | bytes 196 | tf_op jit(solution)/shard_map/add | solution.py:207
  7.7 0.1 and_select_fusion.4
  7.8 0.1 iota_compare_fusion.1
  7.9 0.8 %copy.20 = s32[6,4]{1,0:T(8,128)S(1)} copy(s32[6,4]{0,1:T(4,128)} %param.8) | data formatting | bytes 192 | tf_op args[3]
  8.7 0.1 broadcast_in_dim.77
  8.8 0.1 mul.76
  8.8 0.1 multiply_convert_fusion.1.weights
  8.9 0.8 %select_reduce_fusion.1 = (s32[4,6]{1,0:T(4,128)S(1)}, s32[4,6]{1,0:T(4,128)S(1)}) fusion(s32[4,6]{1,0:T(4,128)} %bitcast.12, pred[4,4]{1,0:T(4,128)(4,1)S(1)} %iota_compare_fusion.1, s32[4,6]{1,0:T(4,128)S(1)} %fusion.2), kind=kLoop, calls=%fused_computation.4 | loop fusion | flops 336 | bytes 400 | tf_op jit(solution)/shard_map/reduce_sum | solution.py:202
  9.7 0.1 multiply_convert_fusion.weights
  9.8 0.1 iota_compare_fusion
  9.9 0.1 broadcast_add_fusion
  10.0 0.8 %select_reduce_fusion = s32[8,8]{1,0:T(8,128)S(1)} fusion(s32[8,8]{1,0:T(8,128)} %param.9, pred[8,8]{1,0:T(8,128)(4,1)S(1)} %iota_compare_fusion), kind=kLoop, calls=%fused_computation | loop fusion | flops 960 | bytes 576 | tf_op jit(solution)/shard_map/reduce_sum | solution.py:202
  10.8 0.1 reshape.185.places
  10.9 0.1 broadcast_in_dim.76
  11.0 0.1 convert_element_type.35.mask
  11.1 0.0 copy-start.1
  11.1 0.9 %copy-done.1 = f32[1,128,512]{2,1,0:T(8,128)S(1)} copy-done((f32[1,128,512]{2,1,0:T(8,128)S(1)}, f32[1,128,512]{2,1,0:T(8,128)}, u32[]{:S(2)}) %copy-start.1) | copy-done | bytes 262168
  12.0 0.1 screen_factors.2
  12.2 0.0 copy-start
  12.2 1.4 %copy-done = f32[6,256,256]{2,1,0:T(8,128)S(1)} copy-done((f32[6,256,256]{2,1,0:T(8,128)S(1)}, f32[6,256,256]{2,1,0:T(8,128)}, u32[]{:S(2)}) %copy-start) | copy-done | bytes 1572888
  13.6 0.2 mask_amplitudes.1
  13.8 2.5 %collective-permute-done.refs_2_ = f32[1,128,512]{2,1,0:T(8,128)S(1)} collective-permute-done((f32[1,128,512]{2,1,0:T(8,128)}, f32[1,128,512]{2,1,0:T(8,128)S(1)}, u32[]{:S(2)}, u32[]{:S(2)}) %collective-permute-start) | collective-permute-done | bytes 262176 | tf_op jit(solution)/shard_map/ppermute | solution.py:225
  16.3 0.7 %collective-permute-start.1 = (f32[1,128,512]{2,1,0:T(8,128)S(1)}, f32[1,128,512]{2,1,0:T(8,128)S(1)}, u32[]{:S(2)}, u32[]{:S(2)}) collective-permute-start(f32[1,128,512]{2,1,0:T(8,128)S(1)} %collective-permute-done.refs_2_), channel_id=1, source_target_pairs={{0,8},{8,0},{16,24},{24,16},{1,9},{9,1},{17,25},{25,17},{2,10},{10... | collective-permute-start | bytes 786440 | tf_op jit(solution)/shard_map/ppermute | solution.py:225
  17.0 0.0 collective-permute-start.6
  17.0 0.0 collective-permute-done.3.refs_1_
  17.0 0.5 %collective-permute-start.5 = (f32[1,128,512]{2,1,0:T(8,128)S(1)}, f32[1,128,512]{2,1,0:T(8,128)S(1)}, u32[]{:S(2)}, u32[]{:S(2)}) collective-permute-start(f32[1,128,512]{2,1,0:T(8,128)S(1)} %collective-permute-done.3.refs_1_), channel_id=1, source_target_pairs={{0,4},{4,0},{1,5},{5,1},{2,6},{6,2},{3,7},{7,3},{8,12},{12,8},{9,1... | collective-permute-start | bytes 786440 | tf_op jit(solution)/shard_map/ppermute | solution.py:222
  17.5 0.0 collective-permute-done.2.refs_0_
  17.5 0.3 screen_factors.3
  17.8 5.9 %collective-permute-done.1.refs_0_ = f32[1,128,512]{2,1,0:T(8,128)S(1)} collective-permute-done((f32[1,128,512]{2,1,0:T(8,128)S(1)}, f32[1,128,512]{2,1,0:T(8,128)S(1)}, u32[]{:S(2)}, u32[]{:S(2)}) %collective-permute-start.1) | collective-permute-done | bytes 262176 | tf_op jit(solution)/shard_map/ppermute | solution.py:225
  23.7 0.0 collective-permute-start.4
  23.7 0.0 collective-permute-done.6.refs_2_
  23.7 0.0 collective-permute-done.5.refs_1_
  23.7 1.5 %contract_pairs.3 = (f32[6,32,256]{2,1,0:T(8,128)S(1)}, bf16[8,2,512,128]{3,2,1,0:T(8,128)(2,1)S(1)}, bf16[8,2,512,128]{3,2,1,0:T(8,128)(2,1)S(1)}) custom-call(s32[1,72]{1,0:T(1,128)S(1)} %reshape.185.places, f32[8,1,512]{2,1,0:T(1,128)S(1)} %convert_element_type.35.mask, ...), custom_call_target="tpu_custom_call", output_to_operand_aliasing={{1}: (8, {}), {2}: (9, {})} | custom-call | flops 301989888 | bytes 8388608 | tf_op jit(solution)/shard_map/contract_pairs/pallas_call | solution.py:153
  25.2 0.1 collective-permute-done.4.refs_0_
  25.2 1.3 %contract_pairs.4 = (f32[6,32,256]{2,1,0:T(8,128)S(1)}, bf16[8,2,512,128]{3,2,1,0:T(8,128)(2,1)S(1)}, bf16[8,2,512,128]{3,2,1,0:T(8,128)(2,1)S(1)}) custom-call(s32[1,72]{1,0:T(1,128)S(1)} %reshape.185.places, f32[8,1,512]{2,1,0:T(1,128)S(1)} %convert_element_type.35.mask, ...), custom_call_target="tpu_custom_call", output_to_operand_aliasing={{1}: (6, {}), {2}: (7, {})} | custom-call | flops 301989888 | bytes 8388608 | tf_op jit(solution)/shard_map/contract_pairs/pallas_call | solution.py:153
  26.6 2.3 %collective-permute-start.7 = (f32[6,32,256]{2,1,0:T(8,128)S(1)}, f32[6,32,256]{2,1,0:T(8,128)S(1)}, u32[]{:S(2)}, u32[]{:S(2)}) collective-permute-start(f32[6,32,256]{2,1,0:T(8,128)S(1)} %get-tuple-element.52), channel_id=1, source_target_pairs={{0,3},{1,2},{2,1},{3,0},{4,7},{5,6},{6,5},{7,4},{8,11},{9,10},{10,... | collective-permute-start | bytes 589832 | tf_op jit(solution)/shard_map/ppermute | solution.py:257
  28.9 2.1 %contract_pairs.5 = (f32[6,32,256]{2,1,0:T(8,128)S(1)}, f32[6,32,256]{2,1,0:T(8,128)S(1)}, f32[6,32,256]{2,1,0:T(8,128)S(1)}, bf16[8,2,512,128]{3,2,1,0:T(8,128)(2,1)S(1)}, bf16[8,2,512,128]{3,2,1,0:T(8,128)(2,1)S(1)}) custom-call(s32[1,72]{1,0:T(1,128)S(1)} %reshape.185.places, ...), custom_call_target="tpu_custom_call", output_to_operand_aliasing={{3}: (5, {}), {4}: (6, {})} | custom-call | flops 1811939328 | bytes 8388608 | tf_op jit(solution)/shard_map/contract_pairs/pallas_call | solution.py:153
  31.0 0.6 %collective-permute-start.8 = (f32[6,32,256]{2,1,0:T(8,128)S(1)}, f32[6,32,256]{2,1,0:T(8,128)S(1)}, u32[]{:S(2)}, u32[]{:S(2)}) collective-permute-start(f32[6,32,256]{2,1,0:T(8,128)S(1)} %get-tuple-element.53), channel_id=1, source_target_pairs={{0,1},{1,0},{2,3},{3,2},{4,5},{5,4},{6,7},{7,6},{8,9},{9,8},{10,11... | collective-permute-start | bytes 589832 | tf_op jit(solution)/shard_map/ppermute | solution.py:257
  31.6 0.7 %collective-permute-start.9 = (f32[6,32,256]{2,1,0:T(8,128)S(1)}, f32[6,32,256]{2,1,0:T(8,128)S(1)}, u32[]{:S(2)}, u32[]{:S(2)}) collective-permute-start(f32[6,32,256]{2,1,0:T(8,128)S(1)} %get-tuple-element.54), channel_id=1, source_target_pairs={{0,2},{1,3},{2,0},{3,1},{4,6},{5,7},{6,4},{7,5},{8,10},{9,11},{10,... | collective-permute-start | bytes 589832 | tf_op jit(solution)/shard_map/ppermute | solution.py:257
  32.3 2.9 %collective-permute-done.7.refs_1_ = f32[6,32,256]{2,1,0:T(8,128)S(1)} collective-permute-done((f32[6,32,256]{2,1,0:T(8,128)S(1)}, f32[6,32,256]{2,1,0:T(8,128)S(1)}, u32[]{:S(2)}, u32[]{:S(2)}) %collective-permute-start.7) | collective-permute-done | bytes 196640 | tf_op jit(solution)/shard_map/ppermute | solution.py:257
  35.3 3.6 %collective-permute-done.8.refs_1_ = f32[6,32,256]{2,1,0:T(8,128)S(1)} collective-permute-done((f32[6,32,256]{2,1,0:T(8,128)S(1)}, f32[6,32,256]{2,1,0:T(8,128)S(1)}, u32[]{:S(2)}, u32[]{:S(2)}) %collective-permute-start.8) | collective-permute-done | bytes 196640 | tf_op jit(solution)/shard_map/ppermute | solution.py:257
  38.9 0.2 collective-permute-done.9.refs_2_
  39.0 0.7 %add_terms.3 = f32[6,32,256]{2,1,0:T(8,128)} custom-call(f32[6,32,256]{2,1,0:T(8,128)S(1)} %add_terms.2.refs_0_, f32[6,32,256]{2,1,0:T(8,128)S(1)} %collective-permute-done.8.refs_1_, f32[6,32,256]{2,1,0:T(8,128)S(1)} %collective-permute-done.9.refs_2_), custom_call_target="tpu_custom_call" | custom-call | bytes 589824 | tf_op jit(solution)/shard_map/add_terms/pallas_call | solution.py:176
  (8 shorter events, 0.1 us)
Async XLA Ops:
  0.0 16.3 %collective-permute-start = (f32[1,128,512]{2,1,0:T(8,128)}, f32[1,128,512]{2,1,0:T(8,128)S(1)}, u32[]{:S(2)}, u32[]{:S(2)}) collective-permute-start(f32[1,128,512]{2,1,0:T(8,128)} %refs_0_.1), channel_id=1, source_target_pairs={{0,16},{8,24},{16,0},{24,8},{1,17},{9,25},{17,1},{25,9},{2,18},{10... | collective-permute-start | bytes 786440 | tf_op jit(solution)/shard_map/ppermute | solution.py:225
  4.0 13.0 %collective-permute-start.3 = (f32[1,128,512]{2,1,0:T(8,128)}, f32[1,128,512]{2,1,0:T(8,128)S(1)}, u32[]{:S(2)}, u32[]{:S(2)}) collective-permute-start(f32[1,128,512]{2,1,0:T(8,128)} %refs_0_.1), channel_id=1, source_target_pairs={{0,8},{8,0},{16,24},{24,16},{1,9},{9,1},{17,25},{25,17},{2,10},{10... | collective-permute-start | bytes 786440 | tf_op jit(solution)/shard_map/ppermute | solution.py:225
  5.6 11.9 %collective-permute-start.2 = (f32[1,128,512]{2,1,0:T(8,128)}, f32[1,128,512]{2,1,0:T(8,128)S(1)}, u32[]{:S(2)}, u32[]{:S(2)}) collective-permute-start(f32[1,128,512]{2,1,0:T(8,128)} %refs_0_.1), channel_id=1, source_target_pairs={{0,4},{4,0},{1,5},{5,1},{2,6},{6,2},{3,7},{7,3},{8,12},{12,8},{9,1... | collective-permute-start | bytes 786440 | tf_op jit(solution)/shard_map/ppermute | solution.py:222
  11.1 1.0 %copy-start.1 = (f32[1,128,512]{2,1,0:T(8,128)S(1)}, f32[1,128,512]{2,1,0:T(8,128)}, u32[]{:S(2)}) copy-start(f32[1,128,512]{2,1,0:T(8,128)} %refs_0_.1) | copy-start | bytes 786436
  12.2 1.4 %copy-start = (f32[6,256,256]{2,1,0:T(8,128)S(1)}, f32[6,256,256]{2,1,0:T(8,128)}, u32[]{:S(2)}) copy-start(f32[6,256,256]{2,1,0:T(8,128)} %amplitudes.1) | copy-start | bytes 4718596
  16.3 7.4 %collective-permute-start.1 = (f32[1,128,512]{2,1,0:T(8,128)S(1)}, f32[1,128,512]{2,1,0:T(8,128)S(1)}, u32[]{:S(2)}, u32[]{:S(2)}) collective-permute-start(f32[1,128,512]{2,1,0:T(8,128)S(1)} %collective-permute-done.refs_2_), channel_id=1, source_target_pairs={{0,8},{8,0},{16,24},{24,16},{1,9},{9,1},{17,25},{25,17},{2,10},{10... | collective-permute-start | bytes 786440 | tf_op jit(solution)/shard_map/ppermute | solution.py:225
  17.0 6.7 %collective-permute-start.6 = (f32[1,128,512]{2,1,0:T(8,128)S(1)}, f32[1,128,512]{2,1,0:T(8,128)S(1)}, u32[]{:S(2)}, u32[]{:S(2)}) collective-permute-start(f32[1,128,512]{2,1,0:T(8,128)S(1)} %collective-permute-done.refs_2_), channel_id=1, source_target_pairs={{0,4},{4,0},{1,5},{5,1},{2,6},{6,2},{3,7},{7,3},{8,12},{12,8},{9,1... | collective-permute-start | bytes 786440 | tf_op jit(solution)/shard_map/ppermute | solution.py:222
  17.0 6.7 %collective-permute-start.5 = (f32[1,128,512]{2,1,0:T(8,128)S(1)}, f32[1,128,512]{2,1,0:T(8,128)S(1)}, u32[]{:S(2)}, u32[]{:S(2)}) collective-permute-start(f32[1,128,512]{2,1,0:T(8,128)S(1)} %collective-permute-done.3.refs_1_), channel_id=1, source_target_pairs={{0,4},{4,0},{1,5},{5,1},{2,6},{6,2},{3,7},{7,3},{8,12},{12,8},{9,1... | collective-permute-start | bytes 786440 | tf_op jit(solution)/shard_map/ppermute | solution.py:222
  23.7 1.5 %collective-permute-start.4 = (f32[1,128,512]{2,1,0:T(8,128)S(1)}, f32[1,128,512]{2,1,0:T(8,128)S(1)}, u32[]{:S(2)}, u32[]{:S(2)}) collective-permute-start(f32[1,128,512]{2,1,0:T(8,128)S(1)} %collective-permute-done.1.refs_0_), channel_id=1, source_target_pairs={{0,4},{4,0},{1,5},{5,1},{2,6},{6,2},{3,7},{7,3},{8,12},{12,8},{9,1... | collective-permute-start | bytes 786440 | tf_op jit(solution)/shard_map/ppermute | solution.py:222
  26.6 8.7 %collective-permute-start.7 = (f32[6,32,256]{2,1,0:T(8,128)S(1)}, f32[6,32,256]{2,1,0:T(8,128)S(1)}, u32[]{:S(2)}, u32[]{:S(2)}) collective-permute-start(f32[6,32,256]{2,1,0:T(8,128)S(1)} %get-tuple-element.52), channel_id=1, source_target_pairs={{0,3},{1,2},{2,1},{3,0},{4,7},{5,6},{6,5},{7,4},{8,11},{9,10},{10,... | collective-permute-start | bytes 589832 | tf_op jit(solution)/shard_map/ppermute | solution.py:257
  31.0 7.9 %collective-permute-start.8 = (f32[6,32,256]{2,1,0:T(8,128)S(1)}, f32[6,32,256]{2,1,0:T(8,128)S(1)}, u32[]{:S(2)}, u32[]{:S(2)}) collective-permute-start(f32[6,32,256]{2,1,0:T(8,128)S(1)} %get-tuple-element.53), channel_id=1, source_target_pairs={{0,1},{1,0},{2,3},{3,2},{4,5},{5,4},{6,7},{7,6},{8,9},{9,8},{10,11... | collective-permute-start | bytes 589832 | tf_op jit(solution)/shard_map/ppermute | solution.py:257
  31.6 7.4 %collective-permute-start.9 = (f32[6,32,256]{2,1,0:T(8,128)S(1)}, f32[6,32,256]{2,1,0:T(8,128)S(1)}, u32[]{:S(2)}, u32[]{:S(2)}) collective-permute-start(f32[6,32,256]{2,1,0:T(8,128)S(1)} %get-tuple-element.54), channel_id=1, source_target_pairs={{0,2},{1,3},{2,0},{3,1},{4,6},{5,7},{6,4},{7,5},{8,10},{9,11},{10,... | collective-permute-start | bytes 589832 | tf_op jit(solution)/shard_map/ppermute | solution.py:257

commit v9 on v8

--- a/solution.py
+++ b/solution.py
@@ -90,19 +90,10 @@
     )(mask, *pieces, *held)
 
 
-def pairs_kernel(row, col, factors, late, last, shifts, places, mask, weights, *refs):
-    pieces = refs[:len(late)]
-    mhigh, mlow = refs[len(late):len(late) + 2]
+def pairs_kernel(row, col, factors, last, shifts, places, weights, mhigh, mlow, high, low, *refs):
     count = len(shifts)
-    held = refs[len(late) + 4:-count - 2]
-    outs, (high, low) = refs[-count - 2:-2], refs[-2:]
+    held, outs = refs[:-count], refs[-count:]
     at = places[...]
-    for (slot, q), piece in zip(late, pieces):
-
-        @pl.when(at[0, 0] >= 0)
-        def _():
-            screen_piece(mask, piece, q, slot, high, low)
-
     pairs, chunk, domv = outs[0].shape
     qs = len(factors)
     size = count * chunk
@@ -143,26 +134,20 @@
         contract(p)
 
 
-def contract_pairs(row, col, places, mask, weights, factors, last, shifts, late, mhigh, mlow, high, low, held=()):
+def contract_pairs(row, col, places, weights, factors, last, shifts, mhigh, mlow, high, low, held=()):
     pairs, domv, _ = mhigh.shape
     chunk = domv // (row * col)
-    keys = [(slot, q) for slot, q, _ in late]
-    pieces = [piece for _, _, piece in late]
-    prepared = 3 + len(pieces) + 2
     count = len(shifts)
-    results = pl.pallas_call(
-        functools.partial(pairs_kernel, row, col, factors, keys, last, shifts),
+    return pl.pallas_call(
+        functools.partial(pairs_kernel, row, col, factors, last, shifts),
         name="contract_pairs",
-        out_shape=[jax.ShapeDtypeStruct((pairs, chunk, domv), jnp.float32)] * count
-        + [jax.ShapeDtypeStruct(high.shape, high.dtype)] * 2,
-        in_specs=[VMEM_SPEC] * (3 + len(pieces) + 4 + len(held)),
-        out_specs=[VMEM_SPEC] * (count + 2),
-        input_output_aliases={prepared: count, prepared + 1: count + 1},
-        compiler_params=pltpu.CompilerParams(vmem_limit_bytes=VMEM_LIMIT),
-        cost_estimate=pl.CostEstimate(flops=6 * pairs * len(factors) * domv ** 3 * 4 * count // (row * col), bytes_accessed=8 * high.size,
-                                      transcendentals=0),
-    )(places, mask, weights, *pieces, mhigh, mlow, high, low, *held)
-    return results[:count], results[count], results[count + 1]
+        out_shape=[jax.ShapeDtypeStruct((pairs, chunk, domv), jnp.float32)] * count,
+        in_specs=[VMEM_SPEC] * (6 + len(held)),
+        out_specs=[VMEM_SPEC] * count,
+        compiler_params=pltpu.CompilerParams(vmem_limit_bytes=VMEM_LIMIT),
+        cost_estimate=pl.CostEstimate(flops=6 * pairs * len(factors) * domv ** 3 * 4 * count // (row * col),
+                                      bytes_accessed=8 * high.size, transcendentals=0),
+    )(places, weights, mhigh, mlow, high, low, *held)
 
 
 def add_kernel(*refs):
@@ -240,18 +225,20 @@
         s_cross, s_near = siblings(cross), siblings(near)
         high, low = prepare(early, shape, (high, low))
         last, high, low = lax.optimization_barrier((last, high, low))
-        contract = functools.partial(contract_pairs, row, col, places, mask, outer)
+        contract = functools.partial(contract_pairs, row, col, places, outer)
         s_last = siblings(last)
-        ready = [(3, 0, last)] + others(1, s_near) + others(2, s_cross)
-        held, high, low = contract(range(nq), False, shifts[:1], ready, mhigh, mlow, high, low)
-        far, high, low = contract(range(nq, row * nq), True, shifts[:1], others(3, s_last), mhigh, mlow, high, low, held)
-        rest, _, _ = contract(range(row * nq), True, shifts[1:], [], mhigh, mlow, high, low)
+        high, low = prepare([(3, 0, last)] + others(1, s_near) + others(2, s_cross), shape, (high, low))
+        held = contract(range(nq), False, shifts[:1], mhigh, mlow, high, low)
+        high, low = prepare(others(3, s_last), shape, (high, low))
+        far = contract(range(nq, row * nq), True, shifts[:1], mhigh, mlow, high, low, held)
+        far, high, low = lax.optimization_barrier((far, high, low))
+        rest = contract(range(row * nq), True, shifts[1:], mhigh, mlow, high, low)
         terms = dict(zip(shifts, far + rest))
     else:
         whole = lax.all_gather(factors, "wide", axis=1, tiled=True)
         high, low = prepare([(0, 0, whole)] + others(0, siblings(whole)), shape)
-        contract = functools.partial(contract_pairs, row, col, places, mask, outer)
-        rest, _, _ = contract(range(row * nq), True, shifts, [], mhigh, mlow, high, low)
+        contract = functools.partial(contract_pairs, row, col, places, outer)
+        rest = contract(range(row * nq), True, shifts, mhigh, mlow, high, low)
         terms = dict(zip(shifts, rest))
 
     moved = [lax.ppermute(terms[s], "col", [(i, partner(i, s, col)) for i in range(col)]) for s in shifts if s]

time: 40.1 us -> 40 us (level)
    pallas_call x3, Pallas kernels: 4.91 us -> 4.42 us  [contract_pairs(): pl.pallas_call(functools.partial(pairs_kernel, row, col, factors, last, s...]
    pallas_call x2 -> x4, Pallas kernels: 0.41 us -> 0.83 us  [screen(): pl.pallas_call(functools.partial(screen_kernel, keys), name='screen_facto...]
where the time goes in v9:
time: 40 us; the launch traced here: 39.7 us
  waiting for transfers between devices  15.1 us (38%)
  starting transfers between devices  10.5 us (26%)
  Pallas kernels  6.21 us (16%)
  local copies, waits for them, and re-layouts  4.92 us (12%)
  other arithmetic  2.78 us (7%)
    ppermute x3, waiting for transfers between devices, across(): return lax.ppermute(piece, 'wide', [(i, i ^ shift) for i in range(wide)])  8.39 us
    ppermute x3, waiting for transfers between devices, body(): lax.ppermute(terms[s], 'col', [(i, partner(i, s, col)) for i in range(col)])  6.65 us
    ppermute x3, starting transfers between devices, across(): return lax.ppermute(piece, 'wide', [(i, i ^ shift) for i in range(wide)])  6.33 us
    pallas_call x3, Pallas kernels, contract_pairs(): pl.pallas_call(functools.partial(pairs_kernel, row, col, factors, last, s...  4.42 us
    ppermute x3, starting transfers between devices, body(): lax.ppermute(terms[s], 'col', [(i, partner(i, s, col)) for i in range(col)])  3.64 us
    unnamed x5, local copies, waits for them, and re-layouts  3.12 us
    reduce_sum x2, other arithmetic, pick(): return jnp.sum(jnp.where(hits[:, :, None], table[None], 0), axis=1)  1.55 us
    slice x2, local copies, waits for them, and re-layouts, body(): firsts, seconds = (blocks_of[0::2], blocks_of[1::2])  1.4 us
  transfers between devices with their start and end apart: 10, of which 6 were waited for; matrix products, arithmetic and copies ran while one was open for 13% of the time, Pallas kernels for 11%

profile of v9, /device:TPU:0, one launch (start us, length us, event | category | flops | bytes accessed | tf_op | source)
XLA Modules:
  0.0 39.7 jit_solution(8723189111829211091)
XLA Ops:
  0.0 4.0 %collective-permute-start = (f32[1,128,512]{2,1,0:T(8,128)}, f32[1,128,512]{2,1,0:T(8,128)S(1)}, u32[]{:S(2)}, u32[]{:S(2)}) collective-permute-start(f32[1,128,512]{2,1,0:T(8,128)} %refs_0_.1), channel_id=1, source_target_pairs={{0,16},{8,24},{16,0},{24,8},{1,17},{9,25},{17,1},{25,9},{2,18},{10... | collective-permute-start | bytes 786440 | tf_op jit(solution)/shard_map/ppermute | solution.py:210
  4.0 1.6 %collective-permute-start.3 = (f32[1,128,512]{2,1,0:T(8,128)}, f32[1,128,512]{2,1,0:T(8,128)S(1)}, u32[]{:S(2)}, u32[]{:S(2)}) collective-permute-start(f32[1,128,512]{2,1,0:T(8,128)} %refs_0_.1), channel_id=1, source_target_pairs={{0,8},{8,0},{16,24},{24,16},{1,9},{9,1},{17,25},{25,17},{2,10},{10... | collective-permute-start | bytes 786440 | tf_op jit(solution)/shard_map/ppermute | solution.py:210
  5.6 0.0 collective-permute-start.2
  5.6 0.7 %slice.6 = s32[2,6]{1,0:T(2,128)S(1)} slice(s32[4,6]{1,0:T(4,128)} %bitcast.14), slice={[0:4:2], [0:6:1]} | slice | bytes 96 | tf_op jit(solution)/shard_map/slice | solution.py:195
  6.3 0.7 %slice.7 = s32[2,6]{1,0:T(2,128)S(1)} slice(s32[4,6]{1,0:T(4,128)} %bitcast.15), slice={[1:4:2], [0:6:1]} | slice | bytes 96 | tf_op jit(solution)/shard_map/slice | solution.py:195
  7.0 0.7 %fusion.2 = s32[4,6]{1,0:T(4,128)S(1)} fusion(s32[]{:T(128)S(6)} %axis_index.33, s32[6,4]{0,1:T(4,128)} %param.7), kind=kLoop, calls=%fused_computation.14 | loop fusion | flops 552 | bytes 196 | tf_op jit(solution)/shard_map/add | solution.py:192
  7.7 0.1 and_select_fusion.4
  7.8 0.1 iota_compare_fusion.1
  7.9 0.8 %copy.18 = s32[6,4]{1,0:T(8,128)S(1)} copy(s32[6,4]{0,1:T(4,128)} %param.8) | data formatting | bytes 192 | tf_op args[3]
  8.7 0.1 broadcast_in_dim.77
  8.8 0.1 mul.76
  8.8 0.1 multiply_convert_fusion.1.weights
  8.9 0.8 %select_reduce_fusion.1 = (s32[4,6]{1,0:T(4,128)S(1)}, s32[4,6]{1,0:T(4,128)S(1)}) fusion(s32[4,6]{1,0:T(4,128)} %bitcast.12, pred[4,4]{1,0:T(4,128)(4,1)S(1)} %iota_compare_fusion.1, s32[4,6]{1,0:T(4,128)S(1)} %fusion.2), kind=kLoop, calls=%fused_computation.4 | loop fusion | flops 336 | bytes 400 | tf_op jit(solution)/shard_map/reduce_sum | solution.py:187
  9.7 0.1 multiply_convert_fusion.weights
  9.8 0.1 iota_compare_fusion
  9.9 0.1 broadcast_add_fusion
  10.0 0.8 %select_reduce_fusion = s32[8,8]{1,0:T(8,128)S(1)} fusion(s32[8,8]{1,0:T(8,128)} %param.9, pred[8,8]{1,0:T(8,128)(4,1)S(1)} %iota_compare_fusion), kind=kLoop, calls=%fused_computation | loop fusion | flops 960 | bytes 576 | tf_op jit(solution)/shard_map/reduce_sum | solution.py:187
  10.8 0.1 reshape.185.places
  10.9 0.1 broadcast_in_dim.76
  11.0 0.1 convert_element_type.35.mask
  11.1 0.0 copy-start.1
  11.1 0.9 %copy-done.1 = f32[1,128,512]{2,1,0:T(8,128)S(1)} copy-done((f32[1,128,512]{2,1,0:T(8,128)S(1)}, f32[1,128,512]{2,1,0:T(8,128)}, u32[]{:S(2)}) %copy-start.1) | copy-done | bytes 262168
  12.0 0.1 screen_factors.4
  12.2 0.0 copy-start
  12.2 1.4 %copy-done = f32[6,256,256]{2,1,0:T(8,128)S(1)} copy-done((f32[6,256,256]{2,1,0:T(8,128)S(1)}, f32[6,256,256]{2,1,0:T(8,128)}, u32[]{:S(2)}) %copy-start) | copy-done | bytes 1572888
  13.6 0.2 mask_amplitudes.1
  13.8 2.5 %collective-permute-done.refs_2_ = f32[1,128,512]{2,1,0:T(8,128)S(1)} collective-permute-done((f32[1,128,512]{2,1,0:T(8,128)}, f32[1,128,512]{2,1,0:T(8,128)S(1)}, u32[]{:S(2)}, u32[]{:S(2)}) %collective-permute-start) | collective-permute-done | bytes 262176 | tf_op jit(solution)/shard_map/ppermute | solution.py:210
  16.3 0.7 %collective-permute-start.1 = (f32[1,128,512]{2,1,0:T(8,128)S(1)}, f32[1,128,512]{2,1,0:T(8,128)S(1)}, u32[]{:S(2)}, u32[]{:S(2)}) collective-permute-start(f32[1,128,512]{2,1,0:T(8,128)S(1)} %collective-permute-done.refs_2_), channel_id=1, source_target_pairs={{0,8},{8,0},{16,24},{24,16},{1,9},{9,1},{17,25},{25,17},{2,10},{10... | collective-permute-start | bytes 786440 | tf_op jit(solution)/shard_map/ppermute | solution.py:210
  17.0 0.0 collective-permute-start.6
  17.0 0.0 collective-permute-done.3.refs_1_
  17.0 0.5 %collective-permute-start.5 = (f32[1,128,512]{2,1,0:T(8,128)S(1)}, f32[1,128,512]{2,1,0:T(8,128)S(1)}, u32[]{:S(2)}, u32[]{:S(2)}) collective-permute-start(f32[1,128,512]{2,1,0:T(8,128)S(1)} %collective-permute-done.3.refs_1_), channel_id=1, source_target_pairs={{0,4},{4,0},{1,5},{5,1},{2,6},{6,2},{3,7},{7,3},{8,12},{12,8},{9,1... | collective-permute-start | bytes 786440 | tf_op jit(solution)/shard_map/ppermute | solution.py:207
  17.5 0.0 collective-permute-done.2.refs_0_
  17.5 0.3 screen_factors.5
  17.8 5.9 %collective-permute-done.1.refs_0_ = f32[1,128,512]{2,1,0:T(8,128)S(1)} collective-permute-done((f32[1,128,512]{2,1,0:T(8,128)S(1)}, f32[1,128,512]{2,1,0:T(8,128)S(1)}, u32[]{:S(2)}, u32[]{:S(2)}) %collective-permute-start.1) | collective-permute-done | bytes 262176 | tf_op jit(solution)/shard_map/ppermute | solution.py:210
  23.7 0.0 collective-permute-start.4
  23.7 0.0 collective-permute-done.6.refs_2_
  23.7 0.0 collective-permute-done.5.refs_1_
  23.7 0.3 screen_factors.6
  24.0 1.1 %contract_pairs.3.refs_0_ = f32[6,32,256]{2,1,0:T(8,128)S(1)} custom-call(s32[1,72]{1,0:T(1,128)S(1)} %reshape.185.places, f32[4,6,1,256]{3,2,1,0:T(1,128)S(1)} %multiply_convert_fusion.weights, bf16[6,256,256]{2,1,0:T(8,128)(2,1)S(1)} %get-tuple-element.37.mhigh, bf16[6,256,256]{2,1,0:T(8,128)(2,1)S(1)} %get-tuple-element.38.mlow, ...), custom_call_target="tpu_custom_call" | custom-call | flops 301989888 | bytes 8388608 | tf_op jit(solution)/shard_map/contract_pairs/pallas_call | solution.py:141
  25.2 0.1 collective-permute-done.4.refs_0_
  25.2 0.1 screen_factors.7
  25.4 1.1 %contract_pairs.4 = f32[6,32,256]{2,1,0:T(8,128)S(1)} custom-call(s32[1,72]{1,0:T(1,128)S(1)} %reshape.185.places, f32[4,6,1,256]{3,2,1,0:T(1,128)S(1)} %multiply_convert_fusion.weights, bf16[6,256,256]{2,1,0:T(8,128)(2,1)S(1)} %get-tuple-element.37.mhigh, bf16[6,256,256]{2,1,0:T(8,128)(2,1)S(1)} %get-tuple-element.38.mlow, ...), custom_call_target="tpu_custom_call" | custom-call | flops 301989888 | bytes 8388608 | tf_op jit(solution)/shard_map/contract_pairs/pallas_call | solution.py:141
  26.5 2.3 %collective-permute-start.7 = (f32[6,32,256]{2,1,0:T(8,128)S(1)}, f32[6,32,256]{2,1,0:T(8,128)S(1)}, u32[]{:S(2)}, u32[]{:S(2)}) collective-permute-start(f32[6,32,256]{2,1,0:T(8,128)S(1)} %contract_pairs.4), channel_id=1, source_target_pairs={{0,3},{1,2},{2,1},{3,0},{4,7},{5,6},{6,5},{7,4},{8,11},{9,10},{10,... | collective-permute-start | bytes 589832 | tf_op jit(solution)/shard_map/ppermute | solution.py:244
  28.8 2.1 %contract_pairs.5 = (f32[6,32,256]{2,1,0:T(8,128)S(1)}, f32[6,32,256]{2,1,0:T(8,128)S(1)}, f32[6,32,256]{2,1,0:T(8,128)S(1)}) custom-call(s32[1,72]{1,0:T(1,128)S(1)} %reshape.185.places, f32[4,6,1,256]{3,2,1,0:T(1,128)S(1)} %multiply_convert_fusion.weights, bf16[6,256,256]{2,1,0:T(8,128)(2,1)S(1)} %get-tuple-element.37.mhigh, ...), custom_call_target="tpu_custom_call" | custom-call | flops 1811939328 | bytes 8388608 | tf_op jit(solution)/shard_map/contract_pairs/pallas_call | solution.py:141
  31.0 0.6 %collective-permute-start.8 = (f32[6,32,256]{2,1,0:T(8,128)S(1)}, f32[6,32,256]{2,1,0:T(8,128)S(1)}, u32[]{:S(2)}, u32[]{:S(2)}) collective-permute-start(f32[6,32,256]{2,1,0:T(8,128)S(1)} %get-tuple-element.55), channel_id=1, source_target_pairs={{0,1},{1,0},{2,3},{3,2},{4,5},{5,4},{6,7},{7,6},{8,9},{9,8},{10,11... | collective-permute-start | bytes 589832 | tf_op jit(solution)/shard_map/ppermute | solution.py:244
  31.6 0.7 %collective-permute-start.9 = (f32[6,32,256]{2,1,0:T(8,128)S(1)}, f32[6,32,256]{2,1,0:T(8,128)S(1)}, u32[]{:S(2)}, u32[]{:S(2)}) collective-permute-start(f32[6,32,256]{2,1,0:T(8,128)S(1)} %get-tuple-element.56), channel_id=1, source_target_pairs={{0,2},{1,3},{2,0},{3,1},{4,6},{5,7},{6,4},{7,5},{8,10},{9,11},{10,... | collective-permute-start | bytes 589832 | tf_op jit(solution)/shard_map/ppermute | solution.py:244
  32.3 2.9 %collective-permute-done.7.refs_1_ = f32[6,32,256]{2,1,0:T(8,128)S(1)} collective-permute-done((f32[6,32,256]{2,1,0:T(8,128)S(1)}, f32[6,32,256]{2,1,0:T(8,128)S(1)}, u32[]{:S(2)}, u32[]{:S(2)}) %collective-permute-start.7) | collective-permute-done | bytes 196640 | tf_op jit(solution)/shard_map/ppermute | solution.py:244
  35.2 3.6 %collective-permute-done.8.refs_1_ = f32[6,32,256]{2,1,0:T(8,128)S(1)} collective-permute-done((f32[6,32,256]{2,1,0:T(8,128)S(1)}, f32[6,32,256]{2,1,0:T(8,128)S(1)}, u32[]{:S(2)}, u32[]{:S(2)}) %collective-permute-start.8) | collective-permute-done | bytes 196640 | tf_op jit(solution)/shard_map/ppermute | solution.py:244
  38.8 0.2 collective-permute-done.9.refs_2_
  39.0 0.7 %add_terms.3 = f32[6,32,256]{2,1,0:T(8,128)} custom-call(f32[6,32,256]{2,1,0:T(8,128)S(1)} %add_terms.2.refs_0_, f32[6,32,256]{2,1,0:T(8,128)S(1)} %collective-permute-done.8.refs_1_, f32[6,32,256]{2,1,0:T(8,128)S(1)} %collective-permute-done.9.refs_2_), custom_call_target="tpu_custom_call" | custom-call | bytes 589824 | tf_op jit(solution)/shard_map/add_terms/pallas_call | solution.py:161
  (8 shorter events, 0.1 us)
Async XLA Ops:
  0.0 16.3 %collective-permute-start = (f32[1,128,512]{2,1,0:T(8,128)}, f32[1,128,512]{2,1,0:T(8,128)S(1)}, u32[]{:S(2)}, u32[]{:S(2)}) collective-permute-start(f32[1,128,512]{2,1,0:T(8,128)} %refs_0_.1), channel_id=1, source_target_pairs={{0,16},{8,24},{16,0},{24,8},{1,17},{9,25},{17,1},{25,9},{2,18},{10... | collective-permute-start | bytes 786440 | tf_op jit(solution)/shard_map/ppermute | solution.py:210
  4.0 13.0 %collective-permute-start.3 = (f32[1,128,512]{2,1,0:T(8,128)}, f32[1,128,512]{2,1,0:T(8,128)S(1)}, u32[]{:S(2)}, u32[]{:S(2)}) collective-permute-start(f32[1,128,512]{2,1,0:T(8,128)} %refs_0_.1), channel_id=1, source_target_pairs={{0,8},{8,0},{16,24},{24,16},{1,9},{9,1},{17,25},{25,17},{2,10},{10... | collective-permute-start | bytes 786440 | tf_op jit(solution)/shard_map/ppermute | solution.py:210
  5.6 11.9 %collective-permute-start.2 = (f32[1,128,512]{2,1,0:T(8,128)}, f32[1,128,512]{2,1,0:T(8,128)S(1)}, u32[]{:S(2)}, u32[]{:S(2)}) collective-permute-start(f32[1,128,512]{2,1,0:T(8,128)} %refs_0_.1), channel_id=1, source_target_pairs={{0,4},{4,0},{1,5},{5,1},{2,6},{6,2},{3,7},{7,3},{8,12},{12,8},{9,1... | collective-permute-start | bytes 786440 | tf_op jit(solution)/shard_map/ppermute | solution.py:207
  11.1 1.0 %copy-start.1 = (f32[1,128,512]{2,1,0:T(8,128)S(1)}, f32[1,128,512]{2,1,0:T(8,128)}, u32[]{:S(2)}) copy-start(f32[1,128,512]{2,1,0:T(8,128)} %refs_0_.1) | copy-start | bytes 786436
  12.2 1.4 %copy-start = (f32[6,256,256]{2,1,0:T(8,128)S(1)}, f32[6,256,256]{2,1,0:T(8,128)}, u32[]{:S(2)}) copy-start(f32[6,256,256]{2,1,0:T(8,128)} %amplitudes.1) | copy-start | bytes 4718596
  16.3 7.4 %collective-permute-start.1 = (f32[1,128,512]{2,1,0:T(8,128)S(1)}, f32[1,128,512]{2,1,0:T(8,128)S(1)}, u32[]{:S(2)}, u32[]{:S(2)}) collective-permute-start(f32[1,128,512]{2,1,0:T(8,128)S(1)} %collective-permute-done.refs_2_), channel_id=1, source_target_pairs={{0,8},{8,0},{16,24},{24,16},{1,9},{9,1},{17,25},{25,17},{2,10},{10... | collective-permute-start | bytes 786440 | tf_op jit(solution)/shard_map/ppermute | solution.py:210
  17.0 6.7 %collective-permute-start.6 = (f32[1,128,512]{2,1,0:T(8,128)S(1)}, f32[1,128,512]{2,1,0:T(8,128)S(1)}, u32[]{:S(2)}, u32[]{:S(2)}) collective-permute-start(f32[1,128,512]{2,1,0:T(8,128)S(1)} %collective-permute-done.refs_2_), channel_id=1, source_target_pairs={{0,4},{4,0},{1,5},{5,1},{2,6},{6,2},{3,7},{7,3},{8,12},{12,8},{9,1... | collective-permute-start | bytes 786440 | tf_op jit(solution)/shard_map/ppermute | solution.py:207
  17.0 6.7 %collective-permute-start.5 = (f32[1,128,512]{2,1,0:T(8,128)S(1)}, f32[1,128,512]{2,1,0:T(8,128)S(1)}, u32[]{:S(2)}, u32[]{:S(2)}) collective-permute-start(f32[1,128,512]{2,1,0:T(8,128)S(1)} %collective-permute-done.3.refs_1_), channel_id=1, source_target_pairs={{0,4},{4,0},{1,5},{5,1},{2,6},{6,2},{3,7},{7,3},{8,12},{12,8},{9,1... | collective-permute-start | bytes 786440 | tf_op jit(solution)/shard_map/ppermute | solution.py:207
  23.7 1.5 %collective-permute-start.4 = (f32[1,128,512]{2,1,0:T(8,128)S(1)}, f32[1,128,512]{2,1,0:T(8,128)S(1)}, u32[]{:S(2)}, u32[]{:S(2)}) collective-permute-start(f32[1,128,512]{2,1,0:T(8,128)S(1)} %collective-permute-done.1.refs_0_), channel_id=1, source_target_pairs={{0,4},{4,0},{1,5},{5,1},{2,6},{6,2},{3,7},{7,3},{8,12},{12,8},{9,1... | collective-permute-start | bytes 786440 | tf_op jit(solution)/shard_map/ppermute | solution.py:207
  26.5 8.7 %collective-permute-start.7 = (f32[6,32,256]{2,1,0:T(8,128)S(1)}, f32[6,32,256]{2,1,0:T(8,128)S(1)}, u32[]{:S(2)}, u32[]{:S(2)}) collective-permute-start(f32[6,32,256]{2,1,0:T(8,128)S(1)} %contract_pairs.4), channel_id=1, source_target_pairs={{0,3},{1,2},{2,1},{3,0},{4,7},{5,6},{6,5},{7,4},{8,11},{9,10},{10,... | collective-permute-start | bytes 589832 | tf_op jit(solution)/shard_map/ppermute | solution.py:244
  31.0 7.8 %collective-permute-start.8 = (f32[6,32,256]{2,1,0:T(8,128)S(1)}, f32[6,32,256]{2,1,0:T(8,128)S(1)}, u32[]{:S(2)}, u32[]{:S(2)}) collective-permute-start(f32[6,32,256]{2,1,0:T(8,128)S(1)} %get-tuple-element.55), channel_id=1, source_target_pairs={{0,1},{1,0},{2,3},{3,2},{4,5},{5,4},{6,7},{7,6},{8,9},{9,8},{10,11... | collective-permute-start | bytes 589832 | tf_op jit(solution)/shard_map/ppermute | solution.py:244
  31.6 7.4 %collective-permute-start.9 = (f32[6,32,256]{2,1,0:T(8,128)S(1)}, f32[6,32,256]{2,1,0:T(8,128)S(1)}, u32[]{:S(2)}, u32[]{:S(2)}) collective-permute-start(f32[6,32,256]{2,1,0:T(8,128)S(1)} %get-tuple-element.56), channel_id=1, source_target_pairs={{0,2},{1,3},{2,0},{3,1},{4,6},{5,7},{6,4},{7,5},{8,10},{9,11},{10,... | collective-permute-start | bytes 589832 | tf_op jit(solution)/shard_map/ppermute | solution.py:244

commit v10 on v9

--- a/solution.py
+++ b/solution.py
@@ -52,26 +52,29 @@
     )(weights, amplitudes)
 
 
-def screen_piece(mask, piece, q, slot, high, low):
+def screen_piece(mask, piece, q, slot, packed):
     nq, rows, window = piece.shape
-    tiles = window // LANES
+    blocks = window // BS
+    left_half = left_of(BS)
     for h in range(rows // BS):
         block = slot * (rows // BS) + h
         target = slice(block * BS, (block + 1) * BS)
-        for t in range(tiles):
+        for t in range(window // LANES):
             lanes = slice(t * LANES, (t + 1) * LANES)
             for n in range(nq):
                 tile = piece[n, h * BS:(h + 1) * BS, lanes] * mask[block, :, lanes]
-                for turn, value in ((0, tile), (1, pltpu.roll(tile, BS, 1))):
-                    top, rest = split(value)
-                    high[turn * tiles + t, q * nq + n, target, :] = top
-                    low[turn * tiles + t, q * nq + n, target, :] = rest
+                high, low = split(tile)
+                turned_high, turned_low = split(pltpu.roll(tile, BS, 1))
+                at = q * nq + n
+                packed[2 * t, at, target, :] = jnp.where(left_half, high, turned_low)
+                packed[2 * t + 1, at, target, :] = jnp.where(left_half, turned_high, low)
+                packed[blocks + 2 * t, at, target, :] = jnp.where(left_half, low, turned_high)
+                packed[blocks + 2 * t + 1, at, target, :] = jnp.where(left_half, turned_low, high)
 
 
 def screen_kernel(keys, mask, *refs):
-    high, low = refs[-2:]
     for (slot, q), piece in zip(keys, refs):
-        screen_piece(mask, piece, q, slot, high, low)
+        screen_piece(mask, piece, q, slot, refs[-1])
 
 
 def screen(mask, keyed, shape, held=()):
@@ -81,16 +84,16 @@
     return pl.pallas_call(
         functools.partial(screen_kernel, keys),
         name="screen_factors",
-        out_shape=[shape] * 2,
+        out_shape=shape,
         in_specs=[VMEM_SPEC] * (1 + len(pieces) + len(held)),
-        out_specs=[VMEM_SPEC] * 2,
-        input_output_aliases={1 + len(pieces) + i: i for i in range(len(held))},
+        out_specs=VMEM_SPEC,
+        input_output_aliases={1 + len(pieces): 0} if held else {},
         compiler_params=pltpu.CompilerParams(vmem_limit_bytes=VMEM_LIMIT),
         cost_estimate=pl.CostEstimate(flops=8 * size, bytes_accessed=12 * size, transcendentals=0),
     )(mask, *pieces, *held)
 
 
-def pairs_kernel(row, col, factors, last, shifts, places, weights, mhigh, mlow, high, low, *refs):
+def pairs_kernel(row, col, factors, last, shifts, places, weights, mhigh, mlow, packed, *refs):
     count = len(shifts)
     held, outs = refs[:-count], refs[-count:]
     at = places[...]
@@ -98,7 +101,7 @@
     qs = len(factors)
     size = count * chunk
     blocks = domv // BS
-    tiles = domv // LANES
+    turned = packed.shape[0] // 2
     across = (((1,), (1,)), ((), ()))
     along = (((1,), (0,)), ((), ()))
     dot = functools.partial(lax.dot_general, preferred_element_type=jnp.float32)
@@ -109,21 +112,28 @@
 
         y_spans = [rows_at(i, BS) for i in range(blocks)]
         x_spans = [rows_at(blocks + n, chunk) for n in shifts]
-        first = blocks + col
-        sources = [(at[0, (first + 2 * j) * pairs + p], at[0, (first + 2 * j + 1) * pairs + p]) for j in range(tiles)]
-
-        def gather(source, q, spans, size):
-            return jnp.concatenate([jnp.concatenate([
-                jnp.where(left_of(size), source[a, q, span, :], source[b, q, span, :]) for a, b in sources], 1)
-                for span in spans], 0)
-
-        yhigh, ylow = (jnp.concatenate([gather(source, q, y_spans, BS) for q in factors], 1) for source in (high, low))
-        xhigh, xlow = (jnp.concatenate([gather(source, q, x_spans, chunk) for q in factors], 0) for source in (high, low))
+        columns = [at[0, (blocks + col + i) * pairs + p] for i in range(blocks)]
+
+        def x_part(q, low):
+            return jnp.concatenate([jnp.concatenate([jnp.where(
+                left_of(chunk), packed[columns[i] + low * turned, q, span, :], packed[columns[i + 1] + (1 - low) * turned, q, span, :])
+                for i in range(0, blocks, 2)], 1) for span in x_spans], 0)
+
+        xhigh, xlow = (jnp.concatenate([x_part(q, low) for q in factors], 0) for low in range(2))
         both = dot(jnp.concatenate([xhigh, xlow], 0), mhigh[p], along)
         halfway = both[:qs * size] + both[qs * size:] + dot(xhigh, mlow[p], along)
-        hhigh, hlow = split(jnp.concatenate([halfway[q * size:(q + 1) * size] for q in range(qs)], 1))
-        both = dot(jnp.concatenate([hhigh, hlow], 0), yhigh, across)
-        total = both[:size] + both[size:] + dot(hhigh, ylow, across)
+
+        doubled = []
+        for q in range(qs):
+            for j in range(domv // LANES):
+                tile = halfway[q * size:(q + 1) * size, j * LANES:(j + 1) * LANES]
+                other = pltpu.roll(tile, BS, 1)
+                doubled += [jnp.where(left_of(size), tile, other), jnp.where(left_of(size), other, tile)]
+        hhigh, hlow = split(jnp.concatenate(doubled, 1))
+        y = jnp.concatenate([jnp.concatenate([packed[column, q, span, :] for q in factors for column in columns], 1)
+                             for span in y_spans], 0)
+        both = dot(jnp.concatenate([hhigh, hlow], 0), y, across)
+        total = both[:size] + both[size:]
         for n, (shift, out) in enumerate(zip(shifts, outs)):
             term = total[n * chunk:(n + 1) * chunk]
             if held:
@@ -134,7 +144,7 @@
         contract(p)
 
 
-def contract_pairs(row, col, places, weights, factors, last, shifts, mhigh, mlow, high, low, held=()):
+def contract_pairs(row, col, places, weights, factors, last, shifts, mhigh, mlow, packed, held=()):
     pairs, domv, _ = mhigh.shape
     chunk = domv // (row * col)
     count = len(shifts)
@@ -142,12 +152,12 @@
         functools.partial(pairs_kernel, row, col, factors, last, shifts),
         name="contract_pairs",
         out_shape=[jax.ShapeDtypeStruct((pairs, chunk, domv), jnp.float32)] * count,
-        in_specs=[VMEM_SPEC] * (6 + len(held)),
+        in_specs=[VMEM_SPEC] * (5 + len(held)),
         out_specs=[VMEM_SPEC] * count,
         compiler_params=pltpu.CompilerParams(vmem_limit_bytes=VMEM_LIMIT),
         cost_estimate=pl.CostEstimate(flops=6 * pairs * len(factors) * domv ** 3 * 4 * count // (row * col),
-                                      bytes_accessed=8 * high.size, transcendentals=0),
-    )(places, weights, mhigh, mlow, high, low, *held)
+                                      bytes_accessed=4 * packed.size, transcendentals=0),
+    )(places, weights, mhigh, mlow, packed, *held)
 
 
 def add_kernel(*refs):
@@ -178,7 +188,6 @@
     blocks = window // BS
     per_slot = blocks // line
     domv = dom * BS
-    tiles = window // LANES
     half = domv // row
     chunk = half // col
 
@@ -192,9 +201,7 @@
     starts = ((blocks_of // per_slot) ^ plane) * (per_slot * BS) + blocks_of % per_slot * BS
     offsets = r * half + jnp.stack([partner(c, s, col) for s in range(col)]) * chunk
     chosen = pick(offsets // BS, starts) + (offsets % BS)[:, None]
-    firsts, seconds = blocks_of[0::2], blocks_of[1::2]
-    sources = jnp.stack([firsts % 2 * tiles + firsts // 2, (1 - seconds % 2) * tiles + seconds // 2], 1)
-    places = jnp.concatenate([starts, chosen, sources.reshape(-1, pairs)], 0).reshape(1, -1)
+    places = jnp.concatenate([starts, chosen, blocks_of], 0).reshape(1, -1)
 
     order = jnp.arange(blocks)
     kept = pick(((order // per_slot) ^ plane) * per_slot + order % per_slot, block_mask)
@@ -212,33 +219,33 @@
     def others(slot, pieces):
         return [(slot, q + 1, piece) for q, piece in enumerate(pieces)]
 
-    shape = jax.ShapeDtypeStruct((2 * window // LANES, row * nq, window, LANES), jnp.bfloat16)
+    shape = jax.ShapeDtypeStruct((2 * blocks, row * nq, window, LANES), jnp.bfloat16)
     prepare = functools.partial(screen, mask)
     mhigh, mlow = mask_amplitudes(inner, amplitudes)
     if line > 1:
         near, cross = across(factors, 1), across(factors, 2)
-        high, low = prepare([(0, 0, factors)], shape)
-        cross, high, low, mhigh, mlow, places, outer = lax.optimization_barrier(
-            (cross, high, low, mhigh, mlow, places, outer))
+        packed = prepare([(0, 0, factors)], shape)
+        cross, packed, mhigh, mlow, places, outer = lax.optimization_barrier(
+            (cross, packed, mhigh, mlow, places, outer))
         last = across(cross, 1)
         early = others(0, siblings(factors)) + [(1, 0, near), (2, 0, cross)]
         s_cross, s_near = siblings(cross), siblings(near)
-        high, low = prepare(early, shape, (high, low))
-        last, high, low = lax.optimization_barrier((last, high, low))
+        packed = prepare(early, shape, (packed,))
+        last, packed = lax.optimization_barrier((last, packed))
         contract = functools.partial(contract_pairs, row, col, places, outer)
         s_last = siblings(last)
-        high, low = prepare([(3, 0, last)] + others(1, s_near) + others(2, s_cross), shape, (high, low))
-        held = contract(range(nq), False, shifts[:1], mhigh, mlow, high, low)
-        high, low = prepare(others(3, s_last), shape, (high, low))
-        far = contract(range(nq, row * nq), True, shifts[:1], mhigh, mlow, high, low, held)
-        far, high, low = lax.optimization_barrier((far, high, low))
-        rest = contract(range(row * nq), True, shifts[1:], mhigh, mlow, high, low)
+        packed = prepare([(3, 0, last)] + others(1, s_near) + others(2, s_cross), shape, (packed,))
+        held = contract(range(nq), False, shifts[:1], mhigh, mlow, packed)
+        packed = prepare(others(3, s_last), shape, (packed,))
+        far = contract(range(nq, row * nq), True, shifts[:1], mhigh, mlow, packed, held)
+        _, packed = lax.optimization_barrier((far, packed))
+        rest = contract(range(row * nq), True, shifts[1:], mhigh, mlow, packed)
         terms = dict(zip(shifts, far + rest))
     else:
         whole = lax.all_gather(factors, "wide", axis=1, tiled=True)
-        high, low = prepare([(0, 0, whole)] + others(0, siblings(whole)), shape)
+        packed = prepare([(0, 0, whole)] + others(0, siblings(whole)), shape)
         contract = functools.partial(contract_pairs, row, col, places, outer)
-        rest = contract(range(row * nq), True, shifts, mhigh, mlow, high, low)
+        rest = contract(range(row * nq), True, shifts, mhigh, mlow, packed)
         terms = dict(zip(shifts, rest))
 
     moved = [lax.ppermute(terms[s], "col", [(i, partner(i, s, col)) for i in range(col)]) for s in shifts if s]

time: 40 us -> 40.4 us (1.010)
  local copies, waits for them, and re-layouts: 4.92 us -> 2.12 us
  waiting for transfers between devices: 15.1 us -> 17 us
  Pallas kernels: 6.21 us -> 7 us
  other arithmetic: 2.78 us -> 3.45 us
    ppermute x3, waiting for transfers between devices: 8.39 us -> 10.4 us  [across(): return lax.ppermute(piece, 'wide', [(i, i ^ shift) for i in range(wide)])]
    slice x2 -> x0, local copies, waits for them, and re-layouts: 1.4 us -> none  [body(): firsts, seconds = (blocks_of[0::2], blocks_of[1::2])]
    unnamed x5, local copies, waits for them, and re-layouts: 3.12 us -> 1.72 us
    concatenate x1, other arithmetic: 0.01 us -> 0.69 us  [body(): places = jnp.concatenate([starts, chosen, blocks_of], 0).reshape(1, -1)]
    pallas_call x3, Pallas kernels: 4.42 us -> 4.96 us  [contract_pairs(): pl.pallas_call(functools.partial(pairs_kernel, row, col, factors, last, s...]
  transfers between devices with their start and end apart: 10 -> 10, of which waited for: 6 -> 5; matrix products, arithmetic and copies ran while one was open for 13% -> 12% of each run, Pallas kernels for 11% -> 12%
where the time goes in v10:
time: 40.4 us; the launch traced here: 40.1 us
  waiting for transfers between devices  17 us (42%)
  starting transfers between devices  10.5 us (26%)
  Pallas kernels  7 us (17%)
  other arithmetic  3.45 us (9%)
  local copies, waits for them, and re-layouts  2.12 us (5%)
    ppermute x3, waiting for transfers between devices, across(): return lax.ppermute(piece, 'wide', [(i, i ^ shift) for i in range(wide)])  10.4 us
    ppermute x3, waiting for transfers between devices, body(): lax.ppermute(terms[s], 'col', [(i, partner(i, s, col)) for i in range(col)])  6.51 us
    ppermute x3, starting transfers between devices, across(): return lax.ppermute(piece, 'wide', [(i, i ^ shift) for i in range(wide)])  6.33 us
    pallas_call x3, Pallas kernels, contract_pairs(): pl.pallas_call(functools.partial(pairs_kernel, row, col, factors, last, s...  4.96 us
    ppermute x3, starting transfers between devices, body(): lax.ppermute(terms[s], 'col', [(i, partner(i, s, col)) for i in range(col)])  3.62 us
    unnamed x5, local copies, waits for them, and re-layouts  1.72 us
    reduce_sum x2, other arithmetic, pick(): return jnp.sum(jnp.where(hits[:, :, None], table[None], 0), axis=1)  1.54 us
    pallas_call x4, Pallas kernels, screen(): pl.pallas_call(functools.partial(screen_kernel, keys), name='screen_facto...  1.07 us
  transfers between devices with their start and end apart: 10, of which 5 were waited for; matrix products, arithmetic and copies ran while one was open for 12% of the time, Pallas kernels for 12%

profile of v10, /device:TPU:0, one launch (start us, length us, event | category | flops | bytes accessed | tf_op | source)
XLA Modules:
  0.0 40.1 jit_solution(14316930711383142135)
XLA Ops:
  0.0 0.0 copy-start
  0.0 4.0 %collective-permute-start = (f32[1,128,512]{2,1,0:T(8,128)}, f32[1,128,512]{2,1,0:T(8,128)S(1)}, u32[]{:S(2)}, u32[]{:S(2)}) collective-permute-start(f32[1,128,512]{2,1,0:T(8,128)} %refs_0_.1), channel_id=1, source_target_pairs={{0,16},{8,24},{16,0},{24,8},{1,17},{9,25},{17,1},{25,9},{2,18},{10... | collective-permute-start | bytes 786440 | tf_op jit(solution)/shard_map/ppermute | solution.py:217
  4.0 1.6 %collective-permute-start.3 = (f32[1,128,512]{2,1,0:T(8,128)}, f32[1,128,512]{2,1,0:T(8,128)S(1)}, u32[]{:S(2)}, u32[]{:S(2)}) collective-permute-start(f32[1,128,512]{2,1,0:T(8,128)} %refs_0_.1), channel_id=1, source_target_pairs={{0,8},{8,0},{16,24},{24,16},{1,9},{9,1},{17,25},{25,17},{2,10},{10... | collective-permute-start | bytes 786440 | tf_op jit(solution)/shard_map/ppermute | solution.py:217
  5.6 0.0 collective-permute-start.2
  5.6 0.1 and_select_fusion
  5.7 0.1 iota_compare_fusion.1
  5.8 0.7 %fusion.2 = s32[4,6]{1,0:T(4,128)S(1)} fusion(s32[]{:T(128)S(6)} %axis_index.33, s32[6,4]{0,1:T(4,128)} %param.7), kind=kLoop, calls=%fused_computation.14 | loop fusion | flops 552 | bytes 196 | tf_op jit(solution)/shard_map/add | solution.py:201
  6.5 0.8 %copy.13 = s32[6,4]{1,0:T(8,128)S(1)} copy(s32[6,4]{0,1:T(4,128)} %param.8) | data formatting | bytes 192 | tf_op args[3]
  7.3 0.1 broadcast_in_dim.77
  7.3 0.1 mul.70
  7.4 0.1 multiply_convert_fusion.1.weights
  7.5 0.8 %select_reduce_fusion.1 = (s32[4,6]{1,0:T(4,128)S(1)}, s32[4,6]{1,0:T(4,128)S(1)}) fusion(s32[4,6]{1,0:T(4,128)} %bitcast.7, pred[4,4]{1,0:T(4,128)(4,1)S(1)} %iota_compare_fusion.1, s32[4,6]{1,0:T(4,128)S(1)} %fusion.2), kind=kLoop, calls=%fused_computation.4 | loop fusion | flops 336 | bytes 400 | tf_op jit(solution)/shard_map/reduce_sum | solution.py:196
  8.3 0.1 multiply_convert_fusion.weights
  8.4 0.1 broadcast_add_fusion
  8.5 0.1 iota_compare_fusion
  8.5 0.8 %select_reduce_fusion = s32[8,8]{1,0:T(8,128)S(1)} fusion(s32[8,8]{1,0:T(8,128)} %param.9, pred[8,8]{1,0:T(8,128)(4,1)S(1)} %iota_compare_fusion), kind=kLoop, calls=%fused_computation | loop fusion | flops 960 | bytes 576 | tf_op jit(solution)/shard_map/reduce_sum | solution.py:196
  9.3 0.7 %pad_add_fusion = s32[12,6]{1,0:T(8,128)S(1)} fusion(s32[4,6]{1,0:T(4,128)} %bitcast.8, s32[4,6]{1,0:T(4,128)S(1)} %broadcast_add_fusion, s32[4,6]{1,0:T(4,128)S(1)} %fusion.2), kind=kLoop, calls=%fused_computation.3 | loop fusion | flops 144 | bytes 576 | tf_op jit(solution)/shard_map/concatenate | solution.py:204
  10.0 0.1 reshape.181.places
  10.1 0.1 broadcast_in_dim.76
  10.2 0.1 convert_element_type.35.mask
  10.3 0.0 copy-start.1
  10.3 0.9 %copy-done.1 = f32[1,128,512]{2,1,0:T(8,128)S(1)} copy-done((f32[1,128,512]{2,1,0:T(8,128)S(1)}, f32[1,128,512]{2,1,0:T(8,128)}, u32[]{:S(2)}) %copy-start.1) | copy-done | bytes 262168
  11.2 0.2 screen_factors.4.refs_3_
  11.4 0.0 copy-done
  11.4 0.2 mask_amplitudes.1
  11.7 4.6 %collective-permute-done.refs_2_ = f32[1,128,512]{2,1,0:T(8,128)S(1)} collective-permute-done((f32[1,128,512]{2,1,0:T(8,128)}, f32[1,128,512]{2,1,0:T(8,128)S(1)}, u32[]{:S(2)}, u32[]{:S(2)}) %collective-permute-start) | collective-permute-done | bytes 262176 | tf_op jit(solution)/shard_map/ppermute | solution.py:217
  16.3 0.7 %collective-permute-start.1 = (f32[1,128,512]{2,1,0:T(8,128)S(1)}, f32[1,128,512]{2,1,0:T(8,128)S(1)}, u32[]{:S(2)}, u32[]{:S(2)}) collective-permute-start(f32[1,128,512]{2,1,0:T(8,128)S(1)} %collective-permute-done.refs_2_), channel_id=1, source_target_pairs={{0,8},{8,0},{16,24},{24,16},{1,9},{9,1},{17,25},{25,17},{2,10},{10... | collective-permute-start | bytes 786440 | tf_op jit(solution)/shard_map/ppermute | solution.py:217
  17.0 0.0 collective-permute-start.6
  17.0 0.0 collective-permute-done.3.refs_1_
  17.0 0.5 %collective-permute-start.5 = (f32[1,128,512]{2,1,0:T(8,128)S(1)}, f32[1,128,512]{2,1,0:T(8,128)S(1)}, u32[]{:S(2)}, u32[]{:S(2)}) collective-permute-start(f32[1,128,512]{2,1,0:T(8,128)S(1)} %collective-permute-done.3.refs_1_), channel_id=1, source_target_pairs={{0,4},{4,0},{1,5},{5,1},{2,6},{6,2},{3,7},{7,3},{8,12},{12,8},{9,1... | collective-permute-start | bytes 786440 | tf_op jit(solution)/shard_map/ppermute | solution.py:214
  17.5 0.0 collective-permute-done.2.refs_0_
  17.5 0.4 screen_factors.5.refs_3_
  17.9 5.8 %collective-permute-done.1.refs_0_ = f32[1,128,512]{2,1,0:T(8,128)S(1)} collective-permute-done((f32[1,128,512]{2,1,0:T(8,128)S(1)}, f32[1,128,512]{2,1,0:T(8,128)S(1)}, u32[]{:S(2)}, u32[]{:S(2)}) %collective-permute-start.1) | collective-permute-done | bytes 262176 | tf_op jit(solution)/shard_map/ppermute | solution.py:217
  23.7 0.0 collective-permute-start.4
  23.7 0.0 collective-permute-done.6.refs_2_
  23.7 0.0 collective-permute-done.5.refs_1_
  23.7 0.4 screen_factors.6.refs_1_.packed
  24.1 1.3 %contract_pairs.3.refs_0_ = f32[6,32,256]{2,1,0:T(8,128)S(1)} custom-call(s32[1,72]{1,0:T(1,128)S(1)} %reshape.181.places, f32[4,6,1,256]{3,2,1,0:T(1,128)S(1)} %multiply_convert_fusion.weights, bf16[6,256,256]{2,1,0:T(8,128)(2,1)S(1)} %get-tuple-element.23.mhigh, bf16[6,256,256]{2,1,0:T(8,128)(2,1)S(1)} %get-tuple-element.24.mlow, ...), custom_call_target="tpu_custom_call" | custom-call | flops 301989888 | bytes 8388608 | tf_op jit(solution)/shard_map/contract_pairs/pallas_call | solution.py:151
  25.4 0.0 collective-permute-done.4.refs_0_
  25.4 0.2 screen_factors.7.packed
  25.6 1.3 %contract_pairs.4 = f32[6,32,256]{2,1,0:T(8,128)S(1)} custom-call(s32[1,72]{1,0:T(1,128)S(1)} %reshape.181.places, f32[4,6,1,256]{3,2,1,0:T(1,128)S(1)} %multiply_convert_fusion.weights, bf16[6,256,256]{2,1,0:T(8,128)(2,1)S(1)} %get-tuple-element.23.mhigh, bf16[6,256,256]{2,1,0:T(8,128)(2,1)S(1)} %get-tuple-element.24.mlow, ...), custom_call_target="tpu_custom_call" | custom-call | flops 301989888 | bytes 8388608 | tf_op jit(solution)/shard_map/contract_pairs/pallas_call | solution.py:151
  26.9 2.3 %collective-permute-start.7 = (f32[6,32,256]{2,1,0:T(8,128)S(1)}, f32[6,32,256]{2,1,0:T(8,128)S(1)}, u32[]{:S(2)}, u32[]{:S(2)}) collective-permute-start(f32[6,32,256]{2,1,0:T(8,128)S(1)} %contract_pairs.4), channel_id=1, source_target_pairs={{0,3},{1,2},{2,1},{3,0},{4,7},{5,6},{6,5},{7,4},{8,11},{9,10},{10,... | collective-permute-start | bytes 589832 | tf_op jit(solution)/shard_map/ppermute | solution.py:251
  29.2 2.3 %contract_pairs.5 = (f32[6,32,256]{2,1,0:T(8,128)S(1)}, f32[6,32,256]{2,1,0:T(8,128)S(1)}, f32[6,32,256]{2,1,0:T(8,128)S(1)}) custom-call(s32[1,72]{1,0:T(1,128)S(1)} %reshape.181.places, f32[4,6,1,256]{3,2,1,0:T(1,128)S(1)} %multiply_convert_fusion.weights, bf16[6,256,256]{2,1,0:T(8,128)(2,1)S(1)} %get-tuple-element.23.mhigh, ...), custom_call_target="tpu_custom_call" | custom-call | flops 1811939328 | bytes 8388608 | tf_op jit(solution)/shard_map/contract_pairs/pallas_call | solution.py:151
  31.6 0.6 %collective-permute-start.8 = (f32[6,32,256]{2,1,0:T(8,128)S(1)}, f32[6,32,256]{2,1,0:T(8,128)S(1)}, u32[]{:S(2)}, u32[]{:S(2)}) collective-permute-start(f32[6,32,256]{2,1,0:T(8,128)S(1)} %get-tuple-element.31), channel_id=1, source_target_pairs={{0,1},{1,0},{2,3},{3,2},{4,5},{5,4},{6,7},{7,6},{8,9},{9,8},{10,11... | collective-permute-start | bytes 589832 | tf_op jit(solution)/shard_map/ppermute | solution.py:251
  32.2 0.7 %collective-permute-start.9 = (f32[6,32,256]{2,1,0:T(8,128)S(1)}, f32[6,32,256]{2,1,0:T(8,128)S(1)}, u32[]{:S(2)}, u32[]{:S(2)}) collective-permute-start(f32[6,32,256]{2,1,0:T(8,128)S(1)} %get-tuple-element.32), channel_id=1, source_target_pairs={{0,2},{1,3},{2,0},{3,1},{4,6},{5,7},{6,4},{7,5},{8,10},{9,11},{10,... | collective-permute-start | bytes 589832 | tf_op jit(solution)/shard_map/ppermute | solution.py:251
  32.9 2.7 %collective-permute-done.7.refs_1_ = f32[6,32,256]{2,1,0:T(8,128)S(1)} collective-permute-done((f32[6,32,256]{2,1,0:T(8,128)S(1)}, f32[6,32,256]{2,1,0:T(8,128)S(1)}, u32[]{:S(2)}, u32[]{:S(2)}) %collective-permute-start.7) | collective-permute-done | bytes 196640 | tf_op jit(solution)/shard_map/ppermute | solution.py:251
  35.6 3.6 %collective-permute-done.8.refs_1_ = f32[6,32,256]{2,1,0:T(8,128)S(1)} collective-permute-done((f32[6,32,256]{2,1,0:T(8,128)S(1)}, f32[6,32,256]{2,1,0:T(8,128)S(1)}, u32[]{:S(2)}, u32[]{:S(2)}) %collective-permute-start.8) | collective-permute-done | bytes 196640 | tf_op jit(solution)/shard_map/ppermute | solution.py:251
  39.3 0.2 collective-permute-done.9.refs_2_
  39.4 0.7 %add_terms.3 = f32[6,32,256]{2,1,0:T(8,128)} custom-call(f32[6,32,256]{2,1,0:T(8,128)S(1)} %add_terms.2.refs_0_, f32[6,32,256]{2,1,0:T(8,128)S(1)} %collective-permute-done.8.refs_1_, f32[6,32,256]{2,1,0:T(8,128)S(1)} %collective-permute-done.9.refs_2_), custom_call_target="tpu_custom_call" | custom-call | bytes 589824 | tf_op jit(solution)/shard_map/add_terms/pallas_call | solution.py:171
  (4 shorter events, 0.0 us)
Async XLA Ops:
  0.0 11.4 %copy-start = (f32[6,256,256]{2,1,0:T(8,128)S(1)}, f32[6,256,256]{2,1,0:T(8,128)}, u32[]{:S(2)}) copy-start(f32[6,256,256]{2,1,0:T(8,128)} %amplitudes.1) | copy-start | bytes 4718596
  0.0 16.3 %collective-permute-start = (f32[1,128,512]{2,1,0:T(8,128)}, f32[1,128,512]{2,1,0:T(8,128)S(1)}, u32[]{:S(2)}, u32[]{:S(2)}) collective-permute-start(f32[1,128,512]{2,1,0:T(8,128)} %refs_0_.1), channel_id=1, source_target_pairs={{0,16},{8,24},{16,0},{24,8},{1,17},{9,25},{17,1},{25,9},{2,18},{10... | collective-permute-start | bytes 786440 | tf_op jit(solution)/shard_map/ppermute | solution.py:217
  4.0 13.0 %collective-permute-start.3 = (f32[1,128,512]{2,1,0:T(8,128)}, f32[1,128,512]{2,1,0:T(8,128)S(1)}, u32[]{:S(2)}, u32[]{:S(2)}) collective-permute-start(f32[1,128,512]{2,1,0:T(8,128)} %refs_0_.1), channel_id=1, source_target_pairs={{0,8},{8,0},{16,24},{24,16},{1,9},{9,1},{17,25},{25,17},{2,10},{10... | collective-permute-start | bytes 786440 | tf_op jit(solution)/shard_map/ppermute | solution.py:217
  5.6 11.9 %collective-permute-start.2 = (f32[1,128,512]{2,1,0:T(8,128)}, f32[1,128,512]{2,1,0:T(8,128)S(1)}, u32[]{:S(2)}, u32[]{:S(2)}) collective-permute-start(f32[1,128,512]{2,1,0:T(8,128)} %refs_0_.1), channel_id=1, source_target_pairs={{0,4},{4,0},{1,5},{5,1},{2,6},{6,2},{3,7},{7,3},{8,12},{12,8},{9,1... | collective-permute-start | bytes 786440 | tf_op jit(solution)/shard_map/ppermute | solution.py:214
  10.3 1.0 %copy-start.1 = (f32[1,128,512]{2,1,0:T(8,128)S(1)}, f32[1,128,512]{2,1,0:T(8,128)}, u32[]{:S(2)}) copy-start(f32[1,128,512]{2,1,0:T(8,128)} %refs_0_.1) | copy-start | bytes 786436
  16.3 7.4 %collective-permute-start.1 = (f32[1,128,512]{2,1,0:T(8,128)S(1)}, f32[1,128,512]{2,1,0:T(8,128)S(1)}, u32[]{:S(2)}, u32[]{:S(2)}) collective-permute-start(f32[1,128,512]{2,1,0:T(8,128)S(1)} %collective-permute-done.refs_2_), channel_id=1, source_target_pairs={{0,8},{8,0},{16,24},{24,16},{1,9},{9,1},{17,25},{25,17},{2,10},{10... | collective-permute-start | bytes 786440 | tf_op jit(solution)/shard_map/ppermute | solution.py:217
  17.0 6.7 %collective-permute-start.6 = (f32[1,128,512]{2,1,0:T(8,128)S(1)}, f32[1,128,512]{2,1,0:T(8,128)S(1)}, u32[]{:S(2)}, u32[]{:S(2)}) collective-permute-start(f32[1,128,512]{2,1,0:T(8,128)S(1)} %collective-permute-done.refs_2_), channel_id=1, source_target_pairs={{0,4},{4,0},{1,5},{5,1},{2,6},{6,2},{3,7},{7,3},{8,12},{12,8},{9,1... | collective-permute-start | bytes 786440 | tf_op jit(solution)/shard_map/ppermute | solution.py:214
  17.0 6.7 %collective-permute-start.5 = (f32[1,128,512]{2,1,0:T(8,128)S(1)}, f32[1,128,512]{2,1,0:T(8,128)S(1)}, u32[]{:S(2)}, u32[]{:S(2)}) collective-permute-start(f32[1,128,512]{2,1,0:T(8,128)S(1)} %collective-permute-done.3.refs_1_), channel_id=1, source_target_pairs={{0,4},{4,0},{1,5},{5,1},{2,6},{6,2},{3,7},{7,3},{8,12},{12,8},{9,1... | collective-permute-start | bytes 786440 | tf_op jit(solution)/shard_map/ppermute | solution.py:214
  23.7 1.7 %collective-permute-start.4 = (f32[1,128,512]{2,1,0:T(8,128)S(1)}, f32[1,128,512]{2,1,0:T(8,128)S(1)}, u32[]{:S(2)}, u32[]{:S(2)}) collective-permute-start(f32[1,128,512]{2,1,0:T(8,128)S(1)} %collective-permute-done.1.refs_0_), channel_id=1, source_target_pairs={{0,4},{4,0},{1,5},{5,1},{2,6},{6,2},{3,7},{7,3},{8,12},{12,8},{9,1... | collective-permute-start | bytes 786440 | tf_op jit(solution)/shard_map/ppermute | solution.py:214
  26.9 8.7 %collective-permute-start.7 = (f32[6,32,256]{2,1,0:T(8,128)S(1)}, f32[6,32,256]{2,1,0:T(8,128)S(1)}, u32[]{:S(2)}, u32[]{:S(2)}) collective-permute-start(f32[6,32,256]{2,1,0:T(8,128)S(1)} %contract_pairs.4), channel_id=1, source_target_pairs={{0,3},{1,2},{2,1},{3,0},{4,7},{5,6},{6,5},{7,4},{8,11},{9,10},{10,... | collective-permute-start | bytes 589832 | tf_op jit(solution)/shard_map/ppermute | solution.py:251
  31.6 7.7 %collective-permute-start.8 = (f32[6,32,256]{2,1,0:T(8,128)S(1)}, f32[6,32,256]{2,1,0:T(8,128)S(1)}, u32[]{:S(2)}, u32[]{:S(2)}) collective-permute-start(f32[6,32,256]{2,1,0:T(8,128)S(1)} %get-tuple-element.31), channel_id=1, source_target_pairs={{0,1},{1,0},{2,3},{3,2},{4,5},{5,4},{6,7},{7,6},{8,9},{9,8},{10,11... | collective-permute-start | bytes 589832 | tf_op jit(solution)/shard_map/ppermute | solution.py:251
  32.2 7.3 %collective-permute-start.9 = (f32[6,32,256]{2,1,0:T(8,128)S(1)}, f32[6,32,256]{2,1,0:T(8,128)S(1)}, u32[]{:S(2)}, u32[]{:S(2)}) collective-permute-start(f32[6,32,256]{2,1,0:T(8,128)S(1)} %get-tuple-element.32), channel_id=1, source_target_pairs={{0,2},{1,3},{2,0},{3,1},{4,6},{5,7},{6,4},{7,5},{8,10},{9,11},{10,... | collective-permute-start | bytes 589832 | tf_op jit(solution)/shard_map/ppermute | solution.py:251

commit v11 on v9

--- a/solution.py
+++ b/solution.py
@@ -103,25 +103,26 @@
     along = (((1,), (0,)), ((), ()))
     dot = functools.partial(lax.dot_general, preferred_element_type=jnp.float32)
 
-    def contract(p):
-        def rows_at(n, size):
-            return pl.ds(pl.multiple_of(at[0, n * pairs + p], size), size)
-
-        y_spans = [rows_at(i, BS) for i in range(blocks)]
-        x_spans = [rows_at(blocks + n, chunk) for n in shifts]
+    def rows_at(n, p, size):
+        return pl.ds(pl.multiple_of(at[0, n * pairs + p], size), size)
+
+    def gather(source, p, q, spans, size):
         first = blocks + col
         sources = [(at[0, (first + 2 * j) * pairs + p], at[0, (first + 2 * j + 1) * pairs + p]) for j in range(tiles)]
-
-        def gather(source, q, spans, size):
-            return jnp.concatenate([jnp.concatenate([
-                jnp.where(left_of(size), source[a, q, span, :], source[b, q, span, :]) for a, b in sources], 1)
-                for span in spans], 0)
-
-        yhigh, ylow = (jnp.concatenate([gather(source, q, y_spans, BS) for q in factors], 1) for source in (high, low))
-        xhigh, xlow = (jnp.concatenate([gather(source, q, x_spans, chunk) for q in factors], 0) for source in (high, low))
+        return jnp.concatenate([jnp.concatenate([
+            jnp.where(left_of(size), source[a, q, span, :], source[b, q, span, :]) for a, b in sources], 1)
+            for span in spans], 0)
+
+    def first_product(p):
+        spans = [rows_at(blocks + n, p, chunk) for n in shifts]
+        xhigh, xlow = (jnp.concatenate([gather(source, p, q, spans, chunk) for q in factors], 0) for source in (high, low))
         both = dot(jnp.concatenate([xhigh, xlow], 0), mhigh[p], along)
         halfway = both[:qs * size] + both[qs * size:] + dot(xhigh, mlow[p], along)
-        hhigh, hlow = split(jnp.concatenate([halfway[q * size:(q + 1) * size] for q in range(qs)], 1))
+        return split(jnp.concatenate([halfway[q * size:(q + 1) * size] for q in range(qs)], 1))
+
+    def second_product(p, hhigh, hlow):
+        spans = [rows_at(i, p, BS) for i in range(blocks)]
+        yhigh, ylow = (jnp.concatenate([gather(source, p, q, spans, BS) for q in factors], 1) for source in (high, low))
         both = dot(jnp.concatenate([hhigh, hlow], 0), yhigh, across)
         total = both[:size] + both[size:] + dot(hhigh, ylow, across)
         for n, (shift, out) in enumerate(zip(shifts, outs)):
@@ -130,8 +131,12 @@
                 term += held[n][p]
             out[p] = term * weights[shift, p] if last else term
 
-    for p in range(pairs):
-        contract(p)
+    together = pairs if count == 1 else 1
+    for start in range(0, pairs, together):
+        group = range(start, start + together)
+        parts = [first_product(p) for p in group]
+        for p, (hhigh, hlow) in zip(group, parts):
+            second_product(p, hhigh, hlow)
 
 
 def contract_pairs(row, col, places, weights, factors, last, shifts, mhigh, mlow, high, low, held=()):

time: 40 us -> 39.6 us (0.990)
  transfers between devices with their start and end apart: 10 -> 10, of which waited for: 6 -> 6; matrix products, arithmetic and copies ran while one was open for 13% -> 14% of each run, Pallas kernels for 11% -> 10%
where the time goes in v11:
time: 39.6 us; the launch traced here: 39.3 us
  waiting for transfers between devices  15.1 us (38%)
  starting transfers between devices  10.5 us (27%)
  Pallas kernels  5.84 us (15%)
  local copies, waits for them, and re-layouts  4.92 us (12%)
  other arithmetic  2.78 us (7%)
    ppermute x3, waiting for transfers between devices, across(): return lax.ppermute(piece, 'wide', [(i, i ^ shift) for i in range(wide)])  8.39 us
    ppermute x3, waiting for transfers between devices, body(): lax.ppermute(terms[s], 'col', [(i, partner(i, s, col)) for i in range(col)])  6.49 us
    ppermute x3, starting transfers between devices, across(): return lax.ppermute(piece, 'wide', [(i, i ^ shift) for i in range(wide)])  6.33 us
    pallas_call x3, Pallas kernels, contract_pairs(): pl.pallas_call(functools.partial(pairs_kernel, row, col, factors, last, s...  4.05 us
    ppermute x3, starting transfers between devices, body(): lax.ppermute(terms[s], 'col', [(i, partner(i, s, col)) for i in range(col)])  3.62 us
    unnamed x5, local copies, waits for them, and re-layouts  3.12 us
    reduce_sum x2, other arithmetic, pick(): return jnp.sum(jnp.where(hits[:, :, None], table[None], 0), axis=1)  1.55 us
    slice x2, local copies, waits for them, and re-layouts, body(): firsts, seconds = (blocks_of[0::2], blocks_of[1::2])  1.4 us
  transfers between devices with their start and end apart: 10, of which 6 were waited for; matrix products, arithmetic and copies ran while one was open for 14% of the time, Pallas kernels for 10%

profile of v11, /device:TPU:0, one launch (start us, length us, event | category | flops | bytes accessed | tf_op | source)
XLA Modules:
  0.0 39.3 jit_solution(14536185691448733434)
XLA Ops:
  0.0 4.0 %collective-permute-start = (f32[1,128,512]{2,1,0:T(8,128)}, f32[1,128,512]{2,1,0:T(8,128)S(1)}, u32[]{:S(2)}, u32[]{:S(2)}) collective-permute-start(f32[1,128,512]{2,1,0:T(8,128)} %refs_0_.1), channel_id=1, source_target_pairs={{0,16},{8,24},{16,0},{24,8},{1,17},{9,25},{17,1},{25,9},{2,18},{10... | collective-permute-start | bytes 786440 | tf_op jit(solution)/shard_map/ppermute | solution.py:215
  4.0 1.6 %collective-permute-start.3 = (f32[1,128,512]{2,1,0:T(8,128)}, f32[1,128,512]{2,1,0:T(8,128)S(1)}, u32[]{:S(2)}, u32[]{:S(2)}) collective-permute-start(f32[1,128,512]{2,1,0:T(8,128)} %refs_0_.1), channel_id=1, source_target_pairs={{0,8},{8,0},{16,24},{24,16},{1,9},{9,1},{17,25},{25,17},{2,10},{10... | collective-permute-start | bytes 786440 | tf_op jit(solution)/shard_map/ppermute | solution.py:215
  5.6 0.0 collective-permute-start.2
  5.6 0.7 %slice.6 = s32[2,6]{1,0:T(2,128)S(1)} slice(s32[4,6]{1,0:T(4,128)} %bitcast.14), slice={[0:4:2], [0:6:1]} | slice | bytes 96 | tf_op jit(solution)/shard_map/slice | solution.py:200
  6.3 0.7 %slice.7 = s32[2,6]{1,0:T(2,128)S(1)} slice(s32[4,6]{1,0:T(4,128)} %bitcast.15), slice={[1:4:2], [0:6:1]} | slice | bytes 96 | tf_op jit(solution)/shard_map/slice | solution.py:200
  7.0 0.7 %fusion.2 = s32[4,6]{1,0:T(4,128)S(1)} fusion(s32[]{:T(128)S(6)} %axis_index.33, s32[6,4]{0,1:T(4,128)} %param.7), kind=kLoop, calls=%fused_computation.14 | loop fusion | flops 552 | bytes 196 | tf_op jit(solution)/shard_map/add | solution.py:197
  7.7 0.1 and_select_fusion.4
  7.8 0.1 iota_compare_fusion.1
  7.9 0.8 %copy.18 = s32[6,4]{1,0:T(8,128)S(1)} copy(s32[6,4]{0,1:T(4,128)} %param.8) | data formatting | bytes 192 | tf_op args[3]
  8.7 0.1 broadcast_in_dim.77
  8.8 0.1 mul.76
  8.8 0.1 multiply_convert_fusion.1.weights
  8.9 0.8 %select_reduce_fusion.1 = (s32[4,6]{1,0:T(4,128)S(1)}, s32[4,6]{1,0:T(4,128)S(1)}) fusion(s32[4,6]{1,0:T(4,128)} %bitcast.12, pred[4,4]{1,0:T(4,128)(4,1)S(1)} %iota_compare_fusion.1, s32[4,6]{1,0:T(4,128)S(1)} %fusion.2), kind=kLoop, calls=%fused_computation.4 | loop fusion | flops 336 | bytes 400 | tf_op jit(solution)/shard_map/reduce_sum | solution.py:192
  9.7 0.1 multiply_convert_fusion.weights
  9.8 0.1 iota_compare_fusion
  9.9 0.1 broadcast_add_fusion
  10.0 0.8 %select_reduce_fusion = s32[8,8]{1,0:T(8,128)S(1)} fusion(s32[8,8]{1,0:T(8,128)} %param.9, pred[8,8]{1,0:T(8,128)(4,1)S(1)} %iota_compare_fusion), kind=kLoop, calls=%fused_computation | loop fusion | flops 960 | bytes 576 | tf_op jit(solution)/shard_map/reduce_sum | solution.py:192
  10.8 0.1 reshape.185.places
  10.9 0.1 broadcast_in_dim.76
  11.0 0.1 convert_element_type.35.mask
  11.1 0.0 copy-start.1
  11.1 0.9 %copy-done.1 = f32[1,128,512]{2,1,0:T(8,128)S(1)} copy-done((f32[1,128,512]{2,1,0:T(8,128)S(1)}, f32[1,128,512]{2,1,0:T(8,128)}, u32[]{:S(2)}) %copy-start.1) | copy-done | bytes 262168
  12.0 0.1 screen_factors.4
  12.2 0.0 copy-start
  12.2 1.4 %copy-done = f32[6,256,256]{2,1,0:T(8,128)S(1)} copy-done((f32[6,256,256]{2,1,0:T(8,128)S(1)}, f32[6,256,256]{2,1,0:T(8,128)}, u32[]{:S(2)}) %copy-start) | copy-done | bytes 1572888
  13.6 0.2 mask_amplitudes.1
  13.8 2.5 %collective-permute-done.refs_2_ = f32[1,128,512]{2,1,0:T(8,128)S(1)} collective-permute-done((f32[1,128,512]{2,1,0:T(8,128)}, f32[1,128,512]{2,1,0:T(8,128)S(1)}, u32[]{:S(2)}, u32[]{:S(2)}) %collective-permute-start) | collective-permute-done | bytes 262176 | tf_op jit(solution)/shard_map/ppermute | solution.py:215
  16.3 0.7 %collective-permute-start.1 = (f32[1,128,512]{2,1,0:T(8,128)S(1)}, f32[1,128,512]{2,1,0:T(8,128)S(1)}, u32[]{:S(2)}, u32[]{:S(2)}) collective-permute-start(f32[1,128,512]{2,1,0:T(8,128)S(1)} %collective-permute-done.refs_2_), channel_id=1, source_target_pairs={{0,8},{8,0},{16,24},{24,16},{1,9},{9,1},{17,25},{25,17},{2,10},{10... | collective-permute-start | bytes 786440 | tf_op jit(solution)/shard_map/ppermute | solution.py:215
  17.0 0.0 collective-permute-start.6
  17.0 0.0 collective-permute-done.3.refs_1_
  17.0 0.5 %collective-permute-start.5 = (f32[1,128,512]{2,1,0:T(8,128)S(1)}, f32[1,128,512]{2,1,0:T(8,128)S(1)}, u32[]{:S(2)}, u32[]{:S(2)}) collective-permute-start(f32[1,128,512]{2,1,0:T(8,128)S(1)} %collective-permute-done.3.refs_1_), channel_id=1, source_target_pairs={{0,4},{4,0},{1,5},{5,1},{2,6},{6,2},{3,7},{7,3},{8,12},{12,8},{9,1... | collective-permute-start | bytes 786440 | tf_op jit(solution)/shard_map/ppermute | solution.py:212
  17.5 0.0 collective-permute-done.2.refs_0_
  17.5 0.3 screen_factors.5
  17.8 5.9 %collective-permute-done.1.refs_0_ = f32[1,128,512]{2,1,0:T(8,128)S(1)} collective-permute-done((f32[1,128,512]{2,1,0:T(8,128)S(1)}, f32[1,128,512]{2,1,0:T(8,128)S(1)}, u32[]{:S(2)}, u32[]{:S(2)}) %collective-permute-start.1) | collective-permute-done | bytes 262176 | tf_op jit(solution)/shard_map/ppermute | solution.py:215
  23.7 0.0 collective-permute-start.4
  23.7 0.0 collective-permute-done.6.refs_2_
  23.7 0.0 collective-permute-done.5.refs_1_
  23.7 0.3 screen_factors.6
  24.0 1.0 %contract_pairs.3.refs_0_ = f32[6,32,256]{2,1,0:T(8,128)S(1)} custom-call(s32[1,72]{1,0:T(1,128)S(1)} %reshape.185.places, f32[4,6,1,256]{3,2,1,0:T(1,128)S(1)} %multiply_convert_fusion.weights, bf16[6,256,256]{2,1,0:T(8,128)(2,1)S(1)} %get-tuple-element.37.mhigh, bf16[6,256,256]{2,1,0:T(8,128)(2,1)S(1)} %get-tuple-element.38.mlow, ...), custom_call_target="tpu_custom_call" | custom-call | flops 301989888 | bytes 8388608 | tf_op jit(solution)/shard_map/contract_pairs/pallas_call | solution.py:146
  25.0 0.3 collective-permute-done.4.refs_0_
  25.2 0.1 screen_factors.7
  25.4 1.0 %contract_pairs.4 = f32[6,32,256]{2,1,0:T(8,128)S(1)} custom-call(s32[1,72]{1,0:T(1,128)S(1)} %reshape.185.places, f32[4,6,1,256]{3,2,1,0:T(1,128)S(1)} %multiply_convert_fusion.weights, bf16[6,256,256]{2,1,0:T(8,128)(2,1)S(1)} %get-tuple-element.37.mhigh, bf16[6,256,256]{2,1,0:T(8,128)(2,1)S(1)} %get-tuple-element.38.mlow, ...), custom_call_target="tpu_custom_call" | custom-call | flops 301989888 | bytes 8388608 | tf_op jit(solution)/shard_map/contract_pairs/pallas_call | solution.py:146
  26.4 2.3 %collective-permute-start.7 = (f32[6,32,256]{2,1,0:T(8,128)S(1)}, f32[6,32,256]{2,1,0:T(8,128)S(1)}, u32[]{:S(2)}, u32[]{:S(2)}) collective-permute-start(f32[6,32,256]{2,1,0:T(8,128)S(1)} %contract_pairs.4), channel_id=1, source_target_pairs={{0,3},{1,2},{2,1},{3,0},{4,7},{5,6},{6,5},{7,4},{8,11},{9,10},{10,... | collective-permute-start | bytes 589832 | tf_op jit(solution)/shard_map/ppermute | solution.py:249
  28.7 2.1 %contract_pairs.5 = (f32[6,32,256]{2,1,0:T(8,128)S(1)}, f32[6,32,256]{2,1,0:T(8,128)S(1)}, f32[6,32,256]{2,1,0:T(8,128)S(1)}) custom-call(s32[1,72]{1,0:T(1,128)S(1)} %reshape.185.places, f32[4,6,1,256]{3,2,1,0:T(1,128)S(1)} %multiply_convert_fusion.weights, bf16[6,256,256]{2,1,0:T(8,128)(2,1)S(1)} %get-tuple-element.37.mhigh, ...), custom_call_target="tpu_custom_call" | custom-call | flops 1811939328 | bytes 8388608 | tf_op jit(solution)/shard_map/contract_pairs/pallas_call | solution.py:146
  30.8 0.6 %collective-permute-start.8 = (f32[6,32,256]{2,1,0:T(8,128)S(1)}, f32[6,32,256]{2,1,0:T(8,128)S(1)}, u32[]{:S(2)}, u32[]{:S(2)}) collective-permute-start(f32[6,32,256]{2,1,0:T(8,128)S(1)} %get-tuple-element.55), channel_id=1, source_target_pairs={{0,1},{1,0},{2,3},{3,2},{4,5},{5,4},{6,7},{7,6},{8,9},{9,8},{10,11... | collective-permute-start | bytes 589832 | tf_op jit(solution)/shard_map/ppermute | solution.py:249
  31.4 0.7 %collective-permute-start.9 = (f32[6,32,256]{2,1,0:T(8,128)S(1)}, f32[6,32,256]{2,1,0:T(8,128)S(1)}, u32[]{:S(2)}, u32[]{:S(2)}) collective-permute-start(f32[6,32,256]{2,1,0:T(8,128)S(1)} %get-tuple-element.56), channel_id=1, source_target_pairs={{0,2},{1,3},{2,0},{3,1},{4,6},{5,7},{6,4},{7,5},{8,10},{9,11},{10,... | collective-permute-start | bytes 589832 | tf_op jit(solution)/shard_map/ppermute | solution.py:249
  32.1 3.0 %collective-permute-done.7.refs_1_ = f32[6,32,256]{2,1,0:T(8,128)S(1)} collective-permute-done((f32[6,32,256]{2,1,0:T(8,128)S(1)}, f32[6,32,256]{2,1,0:T(8,128)S(1)}, u32[]{:S(2)}, u32[]{:S(2)}) %collective-permute-start.7) | collective-permute-done | bytes 196640 | tf_op jit(solution)/shard_map/ppermute | solution.py:249
  35.1 3.4 %collective-permute-done.8.refs_1_ = f32[6,32,256]{2,1,0:T(8,128)S(1)} collective-permute-done((f32[6,32,256]{2,1,0:T(8,128)S(1)}, f32[6,32,256]{2,1,0:T(8,128)S(1)}, u32[]{:S(2)}, u32[]{:S(2)}) %collective-permute-start.8) | collective-permute-done | bytes 196640 | tf_op jit(solution)/shard_map/ppermute | solution.py:249
  38.4 0.2 collective-permute-done.9.refs_2_
  38.6 0.7 %add_terms.3 = f32[6,32,256]{2,1,0:T(8,128)} custom-call(f32[6,32,256]{2,1,0:T(8,128)S(1)} %add_terms.2.refs_0_, f32[6,32,256]{2,1,0:T(8,128)S(1)} %collective-permute-done.8.refs_1_, f32[6,32,256]{2,1,0:T(8,128)S(1)} %collective-permute-done.9.refs_2_), custom_call_target="tpu_custom_call" | custom-call | bytes 589824 | tf_op jit(solution)/shard_map/add_terms/pallas_call | solution.py:166
  (8 shorter events, 0.1 us)
Async XLA Ops:
  0.0 16.3 %collective-permute-start = (f32[1,128,512]{2,1,0:T(8,128)}, f32[1,128,512]{2,1,0:T(8,128)S(1)}, u32[]{:S(2)}, u32[]{:S(2)}) collective-permute-start(f32[1,128,512]{2,1,0:T(8,128)} %refs_0_.1), channel_id=1, source_target_pairs={{0,16},{8,24},{16,0},{24,8},{1,17},{9,25},{17,1},{25,9},{2,18},{10... | collective-permute-start | bytes 786440 | tf_op jit(solution)/shard_map/ppermute | solution.py:215
  4.0 13.0 %collective-permute-start.3 = (f32[1,128,512]{2,1,0:T(8,128)}, f32[1,128,512]{2,1,0:T(8,128)S(1)}, u32[]{:S(2)}, u32[]{:S(2)}) collective-permute-start(f32[1,128,512]{2,1,0:T(8,128)} %refs_0_.1), channel_id=1, source_target_pairs={{0,8},{8,0},{16,24},{24,16},{1,9},{9,1},{17,25},{25,17},{2,10},{10... | collective-permute-start | bytes 786440 | tf_op jit(solution)/shard_map/ppermute | solution.py:215
  5.6 11.9 %collective-permute-start.2 = (f32[1,128,512]{2,1,0:T(8,128)}, f32[1,128,512]{2,1,0:T(8,128)S(1)}, u32[]{:S(2)}, u32[]{:S(2)}) collective-permute-start(f32[1,128,512]{2,1,0:T(8,128)} %refs_0_.1), channel_id=1, source_target_pairs={{0,4},{4,0},{1,5},{5,1},{2,6},{6,2},{3,7},{7,3},{8,12},{12,8},{9,1... | collective-permute-start | bytes 786440 | tf_op jit(solution)/shard_map/ppermute | solution.py:212
  11.1 1.0 %copy-start.1 = (f32[1,128,512]{2,1,0:T(8,128)S(1)}, f32[1,128,512]{2,1,0:T(8,128)}, u32[]{:S(2)}) copy-start(f32[1,128,512]{2,1,0:T(8,128)} %refs_0_.1) | copy-start | bytes 786436
  12.2 1.4 %copy-start = (f32[6,256,256]{2,1,0:T(8,128)S(1)}, f32[6,256,256]{2,1,0:T(8,128)}, u32[]{:S(2)}) copy-start(f32[6,256,256]{2,1,0:T(8,128)} %amplitudes.1) | copy-start | bytes 4718596
  16.3 7.4 %collective-permute-start.1 = (f32[1,128,512]{2,1,0:T(8,128)S(1)}, f32[1,128,512]{2,1,0:T(8,128)S(1)}, u32[]{:S(2)}, u32[]{:S(2)}) collective-permute-start(f32[1,128,512]{2,1,0:T(8,128)S(1)} %collective-permute-done.refs_2_), channel_id=1, source_target_pairs={{0,8},{8,0},{16,24},{24,16},{1,9},{9,1},{17,25},{25,17},{2,10},{10... | collective-permute-start | bytes 786440 | tf_op jit(solution)/shard_map/ppermute | solution.py:215
  17.0 6.7 %collective-permute-start.6 = (f32[1,128,512]{2,1,0:T(8,128)S(1)}, f32[1,128,512]{2,1,0:T(8,128)S(1)}, u32[]{:S(2)}, u32[]{:S(2)}) collective-permute-start(f32[1,128,512]{2,1,0:T(8,128)S(1)} %collective-permute-done.refs_2_), channel_id=1, source_target_pairs={{0,4},{4,0},{1,5},{5,1},{2,6},{6,2},{3,7},{7,3},{8,12},{12,8},{9,1... | collective-permute-start | bytes 786440 | tf_op jit(solution)/shard_map/ppermute | solution.py:212
  17.0 6.7 %collective-permute-start.5 = (f32[1,128,512]{2,1,0:T(8,128)S(1)}, f32[1,128,512]{2,1,0:T(8,128)S(1)}, u32[]{:S(2)}, u32[]{:S(2)}) collective-permute-start(f32[1,128,512]{2,1,0:T(8,128)S(1)} %collective-permute-done.3.refs_1_), channel_id=1, source_target_pairs={{0,4},{4,0},{1,5},{5,1},{2,6},{6,2},{3,7},{7,3},{8,12},{12,8},{9,1... | collective-permute-start | bytes 786440 | tf_op jit(solution)/shard_map/ppermute | solution.py:212
  23.7 1.5 %collective-permute-start.4 = (f32[1,128,512]{2,1,0:T(8,128)S(1)}, f32[1,128,512]{2,1,0:T(8,128)S(1)}, u32[]{:S(2)}, u32[]{:S(2)}) collective-permute-start(f32[1,128,512]{2,1,0:T(8,128)S(1)} %collective-permute-done.1.refs_0_), channel_id=1, source_target_pairs={{0,4},{4,0},{1,5},{5,1},{2,6},{6,2},{3,7},{7,3},{8,12},{12,8},{9,1... | collective-permute-start | bytes 786440 | tf_op jit(solution)/shard_map/ppermute | solution.py:212
  26.4 8.7 %collective-permute-start.7 = (f32[6,32,256]{2,1,0:T(8,128)S(1)}, f32[6,32,256]{2,1,0:T(8,128)S(1)}, u32[]{:S(2)}, u32[]{:S(2)}) collective-permute-start(f32[6,32,256]{2,1,0:T(8,128)S(1)} %contract_pairs.4), channel_id=1, source_target_pairs={{0,3},{1,2},{2,1},{3,0},{4,7},{5,6},{6,5},{7,4},{8,11},{9,10},{10,... | collective-permute-start | bytes 589832 | tf_op jit(solution)/shard_map/ppermute | solution.py:249
  30.8 7.7 %collective-permute-start.8 = (f32[6,32,256]{2,1,0:T(8,128)S(1)}, f32[6,32,256]{2,1,0:T(8,128)S(1)}, u32[]{:S(2)}, u32[]{:S(2)}) collective-permute-start(f32[6,32,256]{2,1,0:T(8,128)S(1)} %get-tuple-element.55), channel_id=1, source_target_pairs={{0,1},{1,0},{2,3},{3,2},{4,5},{5,4},{6,7},{7,6},{8,9},{9,8},{10,11... | collective-permute-start | bytes 589832 | tf_op jit(solution)/shard_map/ppermute | solution.py:249
  31.4 7.2 %collective-permute-start.9 = (f32[6,32,256]{2,1,0:T(8,128)S(1)}, f32[6,32,256]{2,1,0:T(8,128)S(1)}, u32[]{:S(2)}, u32[]{:S(2)}) collective-permute-start(f32[6,32,256]{2,1,0:T(8,128)S(1)} %get-tuple-element.56), channel_id=1, source_target_pairs={{0,2},{1,3},{2,0},{3,1},{4,6},{5,7},{6,4},{7,5},{8,10},{9,11},{10,... | collective-permute-start | bytes 589832 | tf_op jit(solution)/shard_map/ppermute | solution.py:249

commit v12 on v11

--- a/solution.py
+++ b/solution.py
@@ -131,9 +131,9 @@
                 term += held[n][p]
             out[p] = term * weights[shift, p] if last else term
 
-    together = pairs if count == 1 else 1
+    together = pairs if count == 1 else max(1, pairs // 2)
     for start in range(0, pairs, together):
-        group = range(start, start + together)
+        group = range(start, min(start + together, pairs))
         parts = [first_product(p) for p in group]
         for p, (hhigh, hlow) in zip(group, parts):
             second_product(p, hhigh, hlow)

time: 39.6 us -> 39.6 us (level)
  no operation moved by 1% of the time
where the time goes in v12:
time: 39.6 us; the launch traced here: 39.3 us
  waiting for transfers between devices  15.4 us (39%)
  starting transfers between devices  10.5 us (27%)
  Pallas kernels  5.6 us (14%)
  local copies, waits for them, and re-layouts  4.92 us (12%)
  other arithmetic  2.78 us (7%)
    ppermute x3, waiting for transfers between devices, across(): return lax.ppermute(piece, 'wide', [(i, i ^ shift) for i in range(wide)])  8.39 us
    ppermute x3, waiting for transfers between devices, body(): lax.ppermute(terms[s], 'col', [(i, partner(i, s, col)) for i in range(col)])  6.74 us
    ppermute x3, starting transfers between devices, across(): return lax.ppermute(piece, 'wide', [(i, i ^ shift) for i in range(wide)])  6.33 us
    pallas_call x3, Pallas kernels, contract_pairs(): pl.pallas_call(functools.partial(pairs_kernel, row, col, factors, last, s...  3.8 us
    ppermute x3, starting transfers between devices, body(): lax.ppermute(terms[s], 'col', [(i, partner(i, s, col)) for i in range(col)])  3.62 us
    unnamed x5, local copies, waits for them, and re-layouts  3.12 us
    reduce_sum x2, other arithmetic, pick(): return jnp.sum(jnp.where(hits[:, :, None], table[None], 0), axis=1)  1.55 us
    slice x2, local copies, waits for them, and re-layouts, body(): firsts, seconds = (blocks_of[0::2], blocks_of[1::2])  1.4 us
  transfers between devices with their start and end apart: 10, of which 6 were waited for; matrix products, arithmetic and copies ran while one was open for 14% of the time, Pallas kernels for 10%

profile of v12, /device:TPU:0, one launch (start us, length us, event | category | flops | bytes accessed | tf_op | source)
XLA Modules:
  0.0 39.3 jit_solution(16380742911016470968)
XLA Ops:
  0.0 4.0 %collective-permute-start = (f32[1,128,512]{2,1,0:T(8,128)}, f32[1,128,512]{2,1,0:T(8,128)S(1)}, u32[]{:S(2)}, u32[]{:S(2)}) collective-permute-start(f32[1,128,512]{2,1,0:T(8,128)} %refs_0_.1), channel_id=1, source_target_pairs={{0,16},{8,24},{16,0},{24,8},{1,17},{9,25},{17,1},{25,9},{2,18},{10... | collective-permute-start | bytes 786440 | tf_op jit(solution)/shard_map/ppermute | solution.py:215
  4.0 1.6 %collective-permute-start.3 = (f32[1,128,512]{2,1,0:T(8,128)}, f32[1,128,512]{2,1,0:T(8,128)S(1)}, u32[]{:S(2)}, u32[]{:S(2)}) collective-permute-start(f32[1,128,512]{2,1,0:T(8,128)} %refs_0_.1), channel_id=1, source_target_pairs={{0,8},{8,0},{16,24},{24,16},{1,9},{9,1},{17,25},{25,17},{2,10},{10... | collective-permute-start | bytes 786440 | tf_op jit(solution)/shard_map/ppermute | solution.py:215
  5.6 0.0 collective-permute-start.2
  5.6 0.7 %slice.6 = s32[2,6]{1,0:T(2,128)S(1)} slice(s32[4,6]{1,0:T(4,128)} %bitcast.14), slice={[0:4:2], [0:6:1]} | slice | bytes 96 | tf_op jit(solution)/shard_map/slice | solution.py:200
  6.3 0.7 %slice.7 = s32[2,6]{1,0:T(2,128)S(1)} slice(s32[4,6]{1,0:T(4,128)} %bitcast.15), slice={[1:4:2], [0:6:1]} | slice | bytes 96 | tf_op jit(solution)/shard_map/slice | solution.py:200
  7.0 0.7 %fusion.2 = s32[4,6]{1,0:T(4,128)S(1)} fusion(s32[]{:T(128)S(6)} %axis_index.33, s32[6,4]{0,1:T(4,128)} %param.7), kind=kLoop, calls=%fused_computation.14 | loop fusion | flops 552 | bytes 196 | tf_op jit(solution)/shard_map/add | solution.py:197
  7.7 0.1 and_select_fusion.4
  7.8 0.1 iota_compare_fusion.1
  7.9 0.8 %copy.18 = s32[6,4]{1,0:T(8,128)S(1)} copy(s32[6,4]{0,1:T(4,128)} %param.8) | data formatting | bytes 192 | tf_op args[3]
  8.7 0.1 broadcast_in_dim.77
  8.8 0.1 mul.76
  8.8 0.1 multiply_convert_fusion.1.weights
  8.9 0.8 %select_reduce_fusion.1 = (s32[4,6]{1,0:T(4,128)S(1)}, s32[4,6]{1,0:T(4,128)S(1)}) fusion(s32[4,6]{1,0:T(4,128)} %bitcast.12, pred[4,4]{1,0:T(4,128)(4,1)S(1)} %iota_compare_fusion.1, s32[4,6]{1,0:T(4,128)S(1)} %fusion.2), kind=kLoop, calls=%fused_computation.4 | loop fusion | flops 336 | bytes 400 | tf_op jit(solution)/shard_map/reduce_sum | solution.py:192
  9.7 0.1 multiply_convert_fusion.weights
  9.8 0.1 iota_compare_fusion
  9.9 0.1 broadcast_add_fusion
  10.0 0.8 %select_reduce_fusion = s32[8,8]{1,0:T(8,128)S(1)} fusion(s32[8,8]{1,0:T(8,128)} %param.9, pred[8,8]{1,0:T(8,128)(4,1)S(1)} %iota_compare_fusion), kind=kLoop, calls=%fused_computation | loop fusion | flops 960 | bytes 576 | tf_op jit(solution)/shard_map/reduce_sum | solution.py:192
  10.8 0.1 reshape.185.places
  10.9 0.1 broadcast_in_dim.76
  11.0 0.1 convert_element_type.35.mask
  11.1 0.0 copy-start.1
  11.1 0.9 %copy-done.1 = f32[1,128,512]{2,1,0:T(8,128)S(1)} copy-done((f32[1,128,512]{2,1,0:T(8,128)S(1)}, f32[1,128,512]{2,1,0:T(8,128)}, u32[]{:S(2)}) %copy-start.1) | copy-done | bytes 262168
  12.0 0.1 screen_factors.4
  12.2 0.0 copy-start
  12.2 1.4 %copy-done = f32[6,256,256]{2,1,0:T(8,128)S(1)} copy-done((f32[6,256,256]{2,1,0:T(8,128)S(1)}, f32[6,256,256]{2,1,0:T(8,128)}, u32[]{:S(2)}) %copy-start) | copy-done | bytes 1572888
  13.6 0.2 mask_amplitudes.1
  13.8 2.5 %collective-permute-done.refs_2_ = f32[1,128,512]{2,1,0:T(8,128)S(1)} collective-permute-done((f32[1,128,512]{2,1,0:T(8,128)}, f32[1,128,512]{2,1,0:T(8,128)S(1)}, u32[]{:S(2)}, u32[]{:S(2)}) %collective-permute-start) | collective-permute-done | bytes 262176 | tf_op jit(solution)/shard_map/ppermute | solution.py:215
  16.3 0.7 %collective-permute-start.1 = (f32[1,128,512]{2,1,0:T(8,128)S(1)}, f32[1,128,512]{2,1,0:T(8,128)S(1)}, u32[]{:S(2)}, u32[]{:S(2)}) collective-permute-start(f32[1,128,512]{2,1,0:T(8,128)S(1)} %collective-permute-done.refs_2_), channel_id=1, source_target_pairs={{0,8},{8,0},{16,24},{24,16},{1,9},{9,1},{17,25},{25,17},{2,10},{10... | collective-permute-start | bytes 786440 | tf_op jit(solution)/shard_map/ppermute | solution.py:215
  17.0 0.0 collective-permute-start.6
  17.0 0.0 collective-permute-done.3.refs_1_
  17.0 0.5 %collective-permute-start.5 = (f32[1,128,512]{2,1,0:T(8,128)S(1)}, f32[1,128,512]{2,1,0:T(8,128)S(1)}, u32[]{:S(2)}, u32[]{:S(2)}) collective-permute-start(f32[1,128,512]{2,1,0:T(8,128)S(1)} %collective-permute-done.3.refs_1_), channel_id=1, source_target_pairs={{0,4},{4,0},{1,5},{5,1},{2,6},{6,2},{3,7},{7,3},{8,12},{12,8},{9,1... | collective-permute-start | bytes 786440 | tf_op jit(solution)/shard_map/ppermute | solution.py:212
  17.5 0.0 collective-permute-done.2.refs_0_
  17.5 0.3 screen_factors.5
  17.8 5.9 %collective-permute-done.1.refs_0_ = f32[1,128,512]{2,1,0:T(8,128)S(1)} collective-permute-done((f32[1,128,512]{2,1,0:T(8,128)S(1)}, f32[1,128,512]{2,1,0:T(8,128)S(1)}, u32[]{:S(2)}, u32[]{:S(2)}) %collective-permute-start.1) | collective-permute-done | bytes 262176 | tf_op jit(solution)/shard_map/ppermute | solution.py:215
  23.7 0.0 collective-permute-start.4
  23.7 0.0 collective-permute-done.6.refs_2_
  23.7 0.0 collective-permute-done.5.refs_1_
  23.7 0.3 screen_factors.6
  24.0 1.0 %contract_pairs.3.refs_0_ = f32[6,32,256]{2,1,0:T(8,128)S(1)} custom-call(s32[1,72]{1,0:T(1,128)S(1)} %reshape.185.places, f32[4,6,1,256]{3,2,1,0:T(1,128)S(1)} %multiply_convert_fusion.weights, bf16[6,256,256]{2,1,0:T(8,128)(2,1)S(1)} %get-tuple-element.37.mhigh, bf16[6,256,256]{2,1,0:T(8,128)(2,1)S(1)} %get-tuple-element.38.mlow, ...), custom_call_target="tpu_custom_call" | custom-call | flops 301989888 | bytes 8388608 | tf_op jit(solution)/shard_map/contract_pairs/pallas_call | solution.py:146
  25.0 0.3 collective-permute-done.4.refs_0_
  25.2 0.1 screen_factors.7
  25.4 1.0 %contract_pairs.4 = f32[6,32,256]{2,1,0:T(8,128)S(1)} custom-call(s32[1,72]{1,0:T(1,128)S(1)} %reshape.185.places, f32[4,6,1,256]{3,2,1,0:T(1,128)S(1)} %multiply_convert_fusion.weights, bf16[6,256,256]{2,1,0:T(8,128)(2,1)S(1)} %get-tuple-element.37.mhigh, bf16[6,256,256]{2,1,0:T(8,128)(2,1)S(1)} %get-tuple-element.38.mlow, ...), custom_call_target="tpu_custom_call" | custom-call | flops 301989888 | bytes 8388608 | tf_op jit(solution)/shard_map/contract_pairs/pallas_call | solution.py:146
  26.4 2.3 %collective-permute-start.7 = (f32[6,32,256]{2,1,0:T(8,128)S(1)}, f32[6,32,256]{2,1,0:T(8,128)S(1)}, u32[]{:S(2)}, u32[]{:S(2)}) collective-permute-start(f32[6,32,256]{2,1,0:T(8,128)S(1)} %contract_pairs.4), channel_id=1, source_target_pairs={{0,3},{1,2},{2,1},{3,0},{4,7},{5,6},{6,5},{7,4},{8,11},{9,10},{10,... | collective-permute-start | bytes 589832 | tf_op jit(solution)/shard_map/ppermute | solution.py:249
  28.7 1.9 %contract_pairs.5 = (f32[6,32,256]{2,1,0:T(8,128)S(1)}, f32[6,32,256]{2,1,0:T(8,128)S(1)}, f32[6,32,256]{2,1,0:T(8,128)S(1)}) custom-call(s32[1,72]{1,0:T(1,128)S(1)} %reshape.185.places, f32[4,6,1,256]{3,2,1,0:T(1,128)S(1)} %multiply_convert_fusion.weights, bf16[6,256,256]{2,1,0:T(8,128)(2,1)S(1)} %get-tuple-element.37.mhigh, ...), custom_call_target="tpu_custom_call" | custom-call | flops 1811939328 | bytes 8388608 | tf_op jit(solution)/shard_map/contract_pairs/pallas_call | solution.py:146
  30.5 0.6 %collective-permute-start.8 = (f32[6,32,256]{2,1,0:T(8,128)S(1)}, f32[6,32,256]{2,1,0:T(8,128)S(1)}, u32[]{:S(2)}, u32[]{:S(2)}) collective-permute-start(f32[6,32,256]{2,1,0:T(8,128)S(1)} %get-tuple-element.55), channel_id=1, source_target_pairs={{0,1},{1,0},{2,3},{3,2},{4,5},{5,4},{6,7},{7,6},{8,9},{9,8},{10,11... | collective-permute-start | bytes 589832 | tf_op jit(solution)/shard_map/ppermute | solution.py:249
  31.1 0.7 %collective-permute-start.9 = (f32[6,32,256]{2,1,0:T(8,128)S(1)}, f32[6,32,256]{2,1,0:T(8,128)S(1)}, u32[]{:S(2)}, u32[]{:S(2)}) collective-permute-start(f32[6,32,256]{2,1,0:T(8,128)S(1)} %get-tuple-element.56), channel_id=1, source_target_pairs={{0,2},{1,3},{2,0},{3,1},{4,6},{5,7},{6,4},{7,5},{8,10},{9,11},{10,... | collective-permute-start | bytes 589832 | tf_op jit(solution)/shard_map/ppermute | solution.py:249
  31.9 3.2 %collective-permute-done.7.refs_1_ = f32[6,32,256]{2,1,0:T(8,128)S(1)} collective-permute-done((f32[6,32,256]{2,1,0:T(8,128)S(1)}, f32[6,32,256]{2,1,0:T(8,128)S(1)}, u32[]{:S(2)}, u32[]{:S(2)}) %collective-permute-start.7) | collective-permute-done | bytes 196640 | tf_op jit(solution)/shard_map/ppermute | solution.py:249
  35.1 3.4 %collective-permute-done.8.refs_1_ = f32[6,32,256]{2,1,0:T(8,128)S(1)} collective-permute-done((f32[6,32,256]{2,1,0:T(8,128)S(1)}, f32[6,32,256]{2,1,0:T(8,128)S(1)}, u32[]{:S(2)}, u32[]{:S(2)}) %collective-permute-start.8) | collective-permute-done | bytes 196640 | tf_op jit(solution)/shard_map/ppermute | solution.py:249
  38.4 0.2 collective-permute-done.9.refs_2_
  38.6 0.7 %add_terms.3 = f32[6,32,256]{2,1,0:T(8,128)} custom-call(f32[6,32,256]{2,1,0:T(8,128)S(1)} %add_terms.2.refs_0_, f32[6,32,256]{2,1,0:T(8,128)S(1)} %collective-permute-done.8.refs_1_, f32[6,32,256]{2,1,0:T(8,128)S(1)} %collective-permute-done.9.refs_2_), custom_call_target="tpu_custom_call" | custom-call | bytes 589824 | tf_op jit(solution)/shard_map/add_terms/pallas_call | solution.py:166
  (8 shorter events, 0.1 us)
Async XLA Ops:
  0.0 16.3 %collective-permute-start = (f32[1,128,512]{2,1,0:T(8,128)}, f32[1,128,512]{2,1,0:T(8,128)S(1)}, u32[]{:S(2)}, u32[]{:S(2)}) collective-permute-start(f32[1,128,512]{2,1,0:T(8,128)} %refs_0_.1), channel_id=1, source_target_pairs={{0,16},{8,24},{16,0},{24,8},{1,17},{9,25},{17,1},{25,9},{2,18},{10... | collective-permute-start | bytes 786440 | tf_op jit(solution)/shard_map/ppermute | solution.py:215
  4.0 13.0 %collective-permute-start.3 = (f32[1,128,512]{2,1,0:T(8,128)}, f32[1,128,512]{2,1,0:T(8,128)S(1)}, u32[]{:S(2)}, u32[]{:S(2)}) collective-permute-start(f32[1,128,512]{2,1,0:T(8,128)} %refs_0_.1), channel_id=1, source_target_pairs={{0,8},{8,0},{16,24},{24,16},{1,9},{9,1},{17,25},{25,17},{2,10},{10... | collective-permute-start | bytes 786440 | tf_op jit(solution)/shard_map/ppermute | solution.py:215
  5.6 11.9 %collective-permute-start.2 = (f32[1,128,512]{2,1,0:T(8,128)}, f32[1,128,512]{2,1,0:T(8,128)S(1)}, u32[]{:S(2)}, u32[]{:S(2)}) collective-permute-start(f32[1,128,512]{2,1,0:T(8,128)} %refs_0_.1), channel_id=1, source_target_pairs={{0,4},{4,0},{1,5},{5,1},{2,6},{6,2},{3,7},{7,3},{8,12},{12,8},{9,1... | collective-permute-start | bytes 786440 | tf_op jit(solution)/shard_map/ppermute | solution.py:212
  11.1 1.0 %copy-start.1 = (f32[1,128,512]{2,1,0:T(8,128)S(1)}, f32[1,128,512]{2,1,0:T(8,128)}, u32[]{:S(2)}) copy-start(f32[1,128,512]{2,1,0:T(8,128)} %refs_0_.1) | copy-start | bytes 786436
  12.2 1.4 %copy-start = (f32[6,256,256]{2,1,0:T(8,128)S(1)}, f32[6,256,256]{2,1,0:T(8,128)}, u32[]{:S(2)}) copy-start(f32[6,256,256]{2,1,0:T(8,128)} %amplitudes.1) | copy-start | bytes 4718596
  16.3 7.4 %collective-permute-start.1 = (f32[1,128,512]{2,1,0:T(8,128)S(1)}, f32[1,128,512]{2,1,0:T(8,128)S(1)}, u32[]{:S(2)}, u32[]{:S(2)}) collective-permute-start(f32[1,128,512]{2,1,0:T(8,128)S(1)} %collective-permute-done.refs_2_), channel_id=1, source_target_pairs={{0,8},{8,0},{16,24},{24,16},{1,9},{9,1},{17,25},{25,17},{2,10},{10... | collective-permute-start | bytes 786440 | tf_op jit(solution)/shard_map/ppermute | solution.py:215
  17.0 6.7 %collective-permute-start.6 = (f32[1,128,512]{2,1,0:T(8,128)S(1)}, f32[1,128,512]{2,1,0:T(8,128)S(1)}, u32[]{:S(2)}, u32[]{:S(2)}) collective-permute-start(f32[1,128,512]{2,1,0:T(8,128)S(1)} %collective-permute-done.refs_2_), channel_id=1, source_target_pairs={{0,4},{4,0},{1,5},{5,1},{2,6},{6,2},{3,7},{7,3},{8,12},{12,8},{9,1... | collective-permute-start | bytes 786440 | tf_op jit(solution)/shard_map/ppermute | solution.py:212
  17.0 6.7 %collective-permute-start.5 = (f32[1,128,512]{2,1,0:T(8,128)S(1)}, f32[1,128,512]{2,1,0:T(8,128)S(1)}, u32[]{:S(2)}, u32[]{:S(2)}) collective-permute-start(f32[1,128,512]{2,1,0:T(8,128)S(1)} %collective-permute-done.3.refs_1_), channel_id=1, source_target_pairs={{0,4},{4,0},{1,5},{5,1},{2,6},{6,2},{3,7},{7,3},{8,12},{12,8},{9,1... | collective-permute-start | bytes 786440 | tf_op jit(solution)/shard_map/ppermute | solution.py:212
  23.7 1.5 %collective-permute-start.4 = (f32[1,128,512]{2,1,0:T(8,128)S(1)}, f32[1,128,512]{2,1,0:T(8,128)S(1)}, u32[]{:S(2)}, u32[]{:S(2)}) collective-permute-start(f32[1,128,512]{2,1,0:T(8,128)S(1)} %collective-permute-done.1.refs_0_), channel_id=1, source_target_pairs={{0,4},{4,0},{1,5},{5,1},{2,6},{6,2},{3,7},{7,3},{8,12},{12,8},{9,1... | collective-permute-start | bytes 786440 | tf_op jit(solution)/shard_map/ppermute | solution.py:212
  26.4 8.7 %collective-permute-start.7 = (f32[6,32,256]{2,1,0:T(8,128)S(1)}, f32[6,32,256]{2,1,0:T(8,128)S(1)}, u32[]{:S(2)}, u32[]{:S(2)}) collective-permute-start(f32[6,32,256]{2,1,0:T(8,128)S(1)} %contract_pairs.4), channel_id=1, source_target_pairs={{0,3},{1,2},{2,1},{3,0},{4,7},{5,6},{6,5},{7,4},{8,11},{9,10},{10,... | collective-permute-start | bytes 589832 | tf_op jit(solution)/shard_map/ppermute | solution.py:249
  30.5 7.9 %collective-permute-start.8 = (f32[6,32,256]{2,1,0:T(8,128)S(1)}, f32[6,32,256]{2,1,0:T(8,128)S(1)}, u32[]{:S(2)}, u32[]{:S(2)}) collective-permute-start(f32[6,32,256]{2,1,0:T(8,128)S(1)} %get-tuple-element.55), channel_id=1, source_target_pairs={{0,1},{1,0},{2,3},{3,2},{4,5},{5,4},{6,7},{7,6},{8,9},{9,8},{10,11... | collective-permute-start | bytes 589832 | tf_op jit(solution)/shard_map/ppermute | solution.py:249
  31.1 7.5 %collective-permute-start.9 = (f32[6,32,256]{2,1,0:T(8,128)S(1)}, f32[6,32,256]{2,1,0:T(8,128)S(1)}, u32[]{:S(2)}, u32[]{:S(2)}) collective-permute-start(f32[6,32,256]{2,1,0:T(8,128)S(1)} %get-tuple-element.56), channel_id=1, source_target_pairs={{0,2},{1,3},{2,0},{3,1},{4,6},{5,7},{6,4},{7,5},{8,10},{9,11},{10,... | collective-permute-start | bytes 589832 | tf_op jit(solution)/shard_map/ppermute | solution.py:249

commit v13 on v11

--- a/solution.py
+++ b/solution.py
@@ -123,8 +123,13 @@
     def second_product(p, hhigh, hlow):
         spans = [rows_at(i, p, BS) for i in range(blocks)]
         yhigh, ylow = (jnp.concatenate([gather(source, p, q, spans, BS) for q in factors], 1) for source in (high, low))
-        both = dot(jnp.concatenate([hhigh, hlow], 0), yhigh, across)
-        total = both[:size] + both[size:] + dot(hhigh, ylow, across)
+        halves = jnp.concatenate([hhigh, hlow], 0)
+        if count == 1:
+            both = dot(halves, jnp.concatenate([yhigh, ylow], 0), across)
+            total = both[:size, :domv] + both[size:, :domv] + (both[:size, domv:] + both[size:, domv:])
+        else:
+            both = dot(halves, yhigh, across)
+            total = both[:size] + both[size:] + dot(hhigh, ylow, across)
         for n, (shift, out) in enumerate(zip(shifts, outs)):
             term = total[n * chunk:(n + 1) * chunk]
             if held:

time: 39.6 us -> 39.7 us (level)
  no operation moved by 1% of the time
where the time goes in v13:
time: 39.7 us; the launch traced here: 39.3 us
  waiting for transfers between devices  15.2 us (38%)
  starting transfers between devices  10.5 us (26%)
  Pallas kernels  5.85 us (15%)
  local copies, waits for them, and re-layouts  4.92 us (12%)
  other arithmetic  2.78 us (7%)
    ppermute x3, waiting for transfers between devices, across(): return lax.ppermute(piece, 'wide', [(i, i ^ shift) for i in range(wide)])  8.39 us
    ppermute x3, waiting for transfers between devices, body(): lax.ppermute(terms[s], 'col', [(i, partner(i, s, col)) for i in range(col)])  6.5 us
    ppermute x3, starting transfers between devices, across(): return lax.ppermute(piece, 'wide', [(i, i ^ shift) for i in range(wide)])  6.33 us
    pallas_call x3, Pallas kernels, contract_pairs(): pl.pallas_call(functools.partial(pairs_kernel, row, col, factors, last, s...  4.06 us
    ppermute x3, starting transfers between devices, body(): lax.ppermute(terms[s], 'col', [(i, partner(i, s, col)) for i in range(col)])  3.62 us
    unnamed x5, local copies, waits for them, and re-layouts  3.12 us
    reduce_sum x2, other arithmetic, pick(): return jnp.sum(jnp.where(hits[:, :, None], table[None], 0), axis=1)  1.55 us
    slice x2, local copies, waits for them, and re-layouts, body(): firsts, seconds = (blocks_of[0::2], blocks_of[1::2])  1.4 us
  transfers between devices with their start and end apart: 10, of which 6 were waited for; matrix products, arithmetic and copies ran while one was open for 14% of the time, Pallas kernels for 10%

profile of v13, /device:TPU:0, one launch (start us, length us, event | category | flops | bytes accessed | tf_op | source)
XLA Modules:
  0.0 39.3 jit_solution(17989422733775579054)
XLA Ops:
  0.0 4.0 %collective-permute-start = (f32[1,128,512]{2,1,0:T(8,128)}, f32[1,128,512]{2,1,0:T(8,128)S(1)}, u32[]{:S(2)}, u32[]{:S(2)}) collective-permute-start(f32[1,128,512]{2,1,0:T(8,128)} %refs_0_.1), channel_id=1, source_target_pairs={{0,16},{8,24},{16,0},{24,8},{1,17},{9,25},{17,1},{25,9},{2,18},{10... | collective-permute-start | bytes 786440 | tf_op jit(solution)/shard_map/ppermute | solution.py:220
  4.0 1.6 %collective-permute-start.3 = (f32[1,128,512]{2,1,0:T(8,128)}, f32[1,128,512]{2,1,0:T(8,128)S(1)}, u32[]{:S(2)}, u32[]{:S(2)}) collective-permute-start(f32[1,128,512]{2,1,0:T(8,128)} %refs_0_.1), channel_id=1, source_target_pairs={{0,8},{8,0},{16,24},{24,16},{1,9},{9,1},{17,25},{25,17},{2,10},{10... | collective-permute-start | bytes 786440 | tf_op jit(solution)/shard_map/ppermute | solution.py:220
  5.6 0.0 collective-permute-start.2
  5.6 0.7 %slice.6 = s32[2,6]{1,0:T(2,128)S(1)} slice(s32[4,6]{1,0:T(4,128)} %bitcast.14), slice={[0:4:2], [0:6:1]} | slice | bytes 96 | tf_op jit(solution)/shard_map/slice | solution.py:205
  6.3 0.7 %slice.7 = s32[2,6]{1,0:T(2,128)S(1)} slice(s32[4,6]{1,0:T(4,128)} %bitcast.15), slice={[1:4:2], [0:6:1]} | slice | bytes 96 | tf_op jit(solution)/shard_map/slice | solution.py:205
  7.0 0.7 %fusion.2 = s32[4,6]{1,0:T(4,128)S(1)} fusion(s32[]{:T(128)S(6)} %axis_index.33, s32[6,4]{0,1:T(4,128)} %param.7), kind=kLoop, calls=%fused_computation.14 | loop fusion | flops 552 | bytes 196 | tf_op jit(solution)/shard_map/add | solution.py:202
  7.7 0.1 and_select_fusion.4
  7.8 0.1 iota_compare_fusion.1
  7.9 0.8 %copy.18 = s32[6,4]{1,0:T(8,128)S(1)} copy(s32[6,4]{0,1:T(4,128)} %param.8) | data formatting | bytes 192 | tf_op args[3]
  8.7 0.1 broadcast_in_dim.77
  8.8 0.1 mul.76
  8.8 0.1 multiply_convert_fusion.1.weights
  8.9 0.8 %select_reduce_fusion.1 = (s32[4,6]{1,0:T(4,128)S(1)}, s32[4,6]{1,0:T(4,128)S(1)}) fusion(s32[4,6]{1,0:T(4,128)} %bitcast.12, pred[4,4]{1,0:T(4,128)(4,1)S(1)} %iota_compare_fusion.1, s32[4,6]{1,0:T(4,128)S(1)} %fusion.2), kind=kLoop, calls=%fused_computation.4 | loop fusion | flops 336 | bytes 400 | tf_op jit(solution)/shard_map/reduce_sum | solution.py:197
  9.7 0.1 multiply_convert_fusion.weights
  9.8 0.1 iota_compare_fusion
  9.9 0.1 broadcast_add_fusion
  10.0 0.8 %select_reduce_fusion = s32[8,8]{1,0:T(8,128)S(1)} fusion(s32[8,8]{1,0:T(8,128)} %param.9, pred[8,8]{1,0:T(8,128)(4,1)S(1)} %iota_compare_fusion), kind=kLoop, calls=%fused_computation | loop fusion | flops 960 | bytes 576 | tf_op jit(solution)/shard_map/reduce_sum | solution.py:197
  10.8 0.1 reshape.185.places
  10.9 0.1 broadcast_in_dim.76
  11.0 0.1 convert_element_type.35.mask
  11.1 0.0 copy-start.1
  11.1 0.9 %copy-done.1 = f32[1,128,512]{2,1,0:T(8,128)S(1)} copy-done((f32[1,128,512]{2,1,0:T(8,128)S(1)}, f32[1,128,512]{2,1,0:T(8,128)}, u32[]{:S(2)}) %copy-start.1) | copy-done | bytes 262168
  12.0 0.1 screen_factors.4
  12.2 0.0 copy-start
  12.2 1.4 %copy-done = f32[6,256,256]{2,1,0:T(8,128)S(1)} copy-done((f32[6,256,256]{2,1,0:T(8,128)S(1)}, f32[6,256,256]{2,1,0:T(8,128)}, u32[]{:S(2)}) %copy-start) | copy-done | bytes 1572888
  13.6 0.2 mask_amplitudes.1
  13.8 2.5 %collective-permute-done.refs_2_ = f32[1,128,512]{2,1,0:T(8,128)S(1)} collective-permute-done((f32[1,128,512]{2,1,0:T(8,128)}, f32[1,128,512]{2,1,0:T(8,128)S(1)}, u32[]{:S(2)}, u32[]{:S(2)}) %collective-permute-start) | collective-permute-done | bytes 262176 | tf_op jit(solution)/shard_map/ppermute | solution.py:220
  16.3 0.7 %collective-permute-start.1 = (f32[1,128,512]{2,1,0:T(8,128)S(1)}, f32[1,128,512]{2,1,0:T(8,128)S(1)}, u32[]{:S(2)}, u32[]{:S(2)}) collective-permute-start(f32[1,128,512]{2,1,0:T(8,128)S(1)} %collective-permute-done.refs_2_), channel_id=1, source_target_pairs={{0,8},{8,0},{16,24},{24,16},{1,9},{9,1},{17,25},{25,17},{2,10},{10... | collective-permute-start | bytes 786440 | tf_op jit(solution)/shard_map/ppermute | solution.py:220
  17.0 0.0 collective-permute-start.6
  17.0 0.0 collective-permute-done.3.refs_1_
  17.0 0.5 %collective-permute-start.5 = (f32[1,128,512]{2,1,0:T(8,128)S(1)}, f32[1,128,512]{2,1,0:T(8,128)S(1)}, u32[]{:S(2)}, u32[]{:S(2)}) collective-permute-start(f32[1,128,512]{2,1,0:T(8,128)S(1)} %collective-permute-done.3.refs_1_), channel_id=1, source_target_pairs={{0,4},{4,0},{1,5},{5,1},{2,6},{6,2},{3,7},{7,3},{8,12},{12,8},{9,1... | collective-permute-start | bytes 786440 | tf_op jit(solution)/shard_map/ppermute | solution.py:217
  17.5 0.0 collective-permute-done.2.refs_0_
  17.5 0.3 screen_factors.5
  17.8 5.9 %collective-permute-done.1.refs_0_ = f32[1,128,512]{2,1,0:T(8,128)S(1)} collective-permute-done((f32[1,128,512]{2,1,0:T(8,128)S(1)}, f32[1,128,512]{2,1,0:T(8,128)S(1)}, u32[]{:S(2)}, u32[]{:S(2)}) %collective-permute-start.1) | collective-permute-done | bytes 262176 | tf_op jit(solution)/shard_map/ppermute | solution.py:220
  23.7 0.0 collective-permute-start.4
  23.7 0.0 collective-permute-done.6.refs_2_
  23.7 0.0 collective-permute-done.5.refs_1_
  23.7 0.3 screen_factors.6
  24.0 1.0 %contract_pairs.3.refs_0_ = f32[6,32,256]{2,1,0:T(8,128)S(1)} custom-call(s32[1,72]{1,0:T(1,128)S(1)} %reshape.185.places, f32[4,6,1,256]{3,2,1,0:T(1,128)S(1)} %multiply_convert_fusion.weights, bf16[6,256,256]{2,1,0:T(8,128)(2,1)S(1)} %get-tuple-element.37.mhigh, bf16[6,256,256]{2,1,0:T(8,128)(2,1)S(1)} %get-tuple-element.38.mlow, ...), custom_call_target="tpu_custom_call" | custom-call | flops 301989888 | bytes 8388608 | tf_op jit(solution)/shard_map/contract_pairs/pallas_call | solution.py:151
  25.0 0.3 collective-permute-done.4.refs_0_
  25.2 0.1 screen_factors.7
  25.4 1.0 %contract_pairs.4 = f32[6,32,256]{2,1,0:T(8,128)S(1)} custom-call(s32[1,72]{1,0:T(1,128)S(1)} %reshape.185.places, f32[4,6,1,256]{3,2,1,0:T(1,128)S(1)} %multiply_convert_fusion.weights, bf16[6,256,256]{2,1,0:T(8,128)(2,1)S(1)} %get-tuple-element.37.mhigh, bf16[6,256,256]{2,1,0:T(8,128)(2,1)S(1)} %get-tuple-element.38.mlow, ...), custom_call_target="tpu_custom_call" | custom-call | flops 301989888 | bytes 8388608 | tf_op jit(solution)/shard_map/contract_pairs/pallas_call | solution.py:151
  26.4 2.3 %collective-permute-start.7 = (f32[6,32,256]{2,1,0:T(8,128)S(1)}, f32[6,32,256]{2,1,0:T(8,128)S(1)}, u32[]{:S(2)}, u32[]{:S(2)}) collective-permute-start(f32[6,32,256]{2,1,0:T(8,128)S(1)} %contract_pairs.4), channel_id=1, source_target_pairs={{0,3},{1,2},{2,1},{3,0},{4,7},{5,6},{6,5},{7,4},{8,11},{9,10},{10,... | collective-permute-start | bytes 589832 | tf_op jit(solution)/shard_map/ppermute | solution.py:254
  28.7 2.1 %contract_pairs.5 = (f32[6,32,256]{2,1,0:T(8,128)S(1)}, f32[6,32,256]{2,1,0:T(8,128)S(1)}, f32[6,32,256]{2,1,0:T(8,128)S(1)}) custom-call(s32[1,72]{1,0:T(1,128)S(1)} %reshape.185.places, f32[4,6,1,256]{3,2,1,0:T(1,128)S(1)} %multiply_convert_fusion.weights, bf16[6,256,256]{2,1,0:T(8,128)(2,1)S(1)} %get-tuple-element.37.mhigh, ...), custom_call_target="tpu_custom_call" | custom-call | flops 1811939328 | bytes 8388608 | tf_op jit(solution)/shard_map/contract_pairs/pallas_call | solution.py:151
  30.8 0.6 %collective-permute-start.8 = (f32[6,32,256]{2,1,0:T(8,128)S(1)}, f32[6,32,256]{2,1,0:T(8,128)S(1)}, u32[]{:S(2)}, u32[]{:S(2)}) collective-permute-start(f32[6,32,256]{2,1,0:T(8,128)S(1)} %get-tuple-element.55), channel_id=1, source_target_pairs={{0,1},{1,0},{2,3},{3,2},{4,5},{5,4},{6,7},{7,6},{8,9},{9,8},{10,11... | collective-permute-start | bytes 589832 | tf_op jit(solution)/shard_map/ppermute | solution.py:254
  31.4 0.7 %collective-permute-start.9 = (f32[6,32,256]{2,1,0:T(8,128)S(1)}, f32[6,32,256]{2,1,0:T(8,128)S(1)}, u32[]{:S(2)}, u32[]{:S(2)}) collective-permute-start(f32[6,32,256]{2,1,0:T(8,128)S(1)} %get-tuple-element.56), channel_id=1, source_target_pairs={{0,2},{1,3},{2,0},{3,1},{4,6},{5,7},{6,4},{7,5},{8,10},{9,11},{10,... | collective-permute-start | bytes 589832 | tf_op jit(solution)/shard_map/ppermute | solution.py:254
  32.1 3.0 %collective-permute-done.7.refs_1_ = f32[6,32,256]{2,1,0:T(8,128)S(1)} collective-permute-done((f32[6,32,256]{2,1,0:T(8,128)S(1)}, f32[6,32,256]{2,1,0:T(8,128)S(1)}, u32[]{:S(2)}, u32[]{:S(2)}) %collective-permute-start.7) | collective-permute-done | bytes 196640 | tf_op jit(solution)/shard_map/ppermute | solution.py:254
  35.1 3.4 %collective-permute-done.8.refs_1_ = f32[6,32,256]{2,1,0:T(8,128)S(1)} collective-permute-done((f32[6,32,256]{2,1,0:T(8,128)S(1)}, f32[6,32,256]{2,1,0:T(8,128)S(1)}, u32[]{:S(2)}, u32[]{:S(2)}) %collective-permute-start.8) | collective-permute-done | bytes 196640 | tf_op jit(solution)/shard_map/ppermute | solution.py:254
  38.5 0.2 collective-permute-done.9.refs_2_
  38.6 0.7 %add_terms.3 = f32[6,32,256]{2,1,0:T(8,128)} custom-call(f32[6,32,256]{2,1,0:T(8,128)S(1)} %add_terms.2.refs_0_, f32[6,32,256]{2,1,0:T(8,128)S(1)} %collective-permute-done.8.refs_1_, f32[6,32,256]{2,1,0:T(8,128)S(1)} %collective-permute-done.9.refs_2_), custom_call_target="tpu_custom_call" | custom-call | bytes 589824 | tf_op jit(solution)/shard_map/add_terms/pallas_call | solution.py:171
  (8 shorter events, 0.1 us)
Async XLA Ops:
  0.0 16.3 %collective-permute-start = (f32[1,128,512]{2,1,0:T(8,128)}, f32[1,128,512]{2,1,0:T(8,128)S(1)}, u32[]{:S(2)}, u32[]{:S(2)}) collective-permute-start(f32[1,128,512]{2,1,0:T(8,128)} %refs_0_.1), channel_id=1, source_target_pairs={{0,16},{8,24},{16,0},{24,8},{1,17},{9,25},{17,1},{25,9},{2,18},{10... | collective-permute-start | bytes 786440 | tf_op jit(solution)/shard_map/ppermute | solution.py:220
  4.0 13.0 %collective-permute-start.3 = (f32[1,128,512]{2,1,0:T(8,128)}, f32[1,128,512]{2,1,0:T(8,128)S(1)}, u32[]{:S(2)}, u32[]{:S(2)}) collective-permute-start(f32[1,128,512]{2,1,0:T(8,128)} %refs_0_.1), channel_id=1, source_target_pairs={{0,8},{8,0},{16,24},{24,16},{1,9},{9,1},{17,25},{25,17},{2,10},{10... | collective-permute-start | bytes 786440 | tf_op jit(solution)/shard_map/ppermute | solution.py:220
  5.6 11.9 %collective-permute-start.2 = (f32[1,128,512]{2,1,0:T(8,128)}, f32[1,128,512]{2,1,0:T(8,128)S(1)}, u32[]{:S(2)}, u32[]{:S(2)}) collective-permute-start(f32[1,128,512]{2,1,0:T(8,128)} %refs_0_.1), channel_id=1, source_target_pairs={{0,4},{4,0},{1,5},{5,1},{2,6},{6,2},{3,7},{7,3},{8,12},{12,8},{9,1... | collective-permute-start | bytes 786440 | tf_op jit(solution)/shard_map/ppermute | solution.py:217
  11.1 1.0 %copy-start.1 = (f32[1,128,512]{2,1,0:T(8,128)S(1)}, f32[1,128,512]{2,1,0:T(8,128)}, u32[]{:S(2)}) copy-start(f32[1,128,512]{2,1,0:T(8,128)} %refs_0_.1) | copy-start | bytes 786436
  12.2 1.4 %copy-start = (f32[6,256,256]{2,1,0:T(8,128)S(1)}, f32[6,256,256]{2,1,0:T(8,128)}, u32[]{:S(2)}) copy-start(f32[6,256,256]{2,1,0:T(8,128)} %amplitudes.1) | copy-start | bytes 4718596
  16.3 7.4 %collective-permute-start.1 = (f32[1,128,512]{2,1,0:T(8,128)S(1)}, f32[1,128,512]{2,1,0:T(8,128)S(1)}, u32[]{:S(2)}, u32[]{:S(2)}) collective-permute-start(f32[1,128,512]{2,1,0:T(8,128)S(1)} %collective-permute-done.refs_2_), channel_id=1, source_target_pairs={{0,8},{8,0},{16,24},{24,16},{1,9},{9,1},{17,25},{25,17},{2,10},{10... | collective-permute-start | bytes 786440 | tf_op jit(solution)/shard_map/ppermute | solution.py:220
  17.0 6.7 %collective-permute-start.6 = (f32[1,128,512]{2,1,0:T(8,128)S(1)}, f32[1,128,512]{2,1,0:T(8,128)S(1)}, u32[]{:S(2)}, u32[]{:S(2)}) collective-permute-start(f32[1,128,512]{2,1,0:T(8,128)S(1)} %collective-permute-done.refs_2_), channel_id=1, source_target_pairs={{0,4},{4,0},{1,5},{5,1},{2,6},{6,2},{3,7},{7,3},{8,12},{12,8},{9,1... | collective-permute-start | bytes 786440 | tf_op jit(solution)/shard_map/ppermute | solution.py:217
  17.0 6.7 %collective-permute-start.5 = (f32[1,128,512]{2,1,0:T(8,128)S(1)}, f32[1,128,512]{2,1,0:T(8,128)S(1)}, u32[]{:S(2)}, u32[]{:S(2)}) collective-permute-start(f32[1,128,512]{2,1,0:T(8,128)S(1)} %collective-permute-done.3.refs_1_), channel_id=1, source_target_pairs={{0,4},{4,0},{1,5},{5,1},{2,6},{6,2},{3,7},{7,3},{8,12},{12,8},{9,1... | collective-permute-start | bytes 786440 | tf_op jit(solution)/shard_map/ppermute | solution.py:217
  23.7 1.5 %collective-permute-start.4 = (f32[1,128,512]{2,1,0:T(8,128)S(1)}, f32[1,128,512]{2,1,0:T(8,128)S(1)}, u32[]{:S(2)}, u32[]{:S(2)}) collective-permute-start(f32[1,128,512]{2,1,0:T(8,128)S(1)} %collective-permute-done.1.refs_0_), channel_id=1, source_target_pairs={{0,4},{4,0},{1,5},{5,1},{2,6},{6,2},{3,7},{7,3},{8,12},{12,8},{9,1... | collective-permute-start | bytes 786440 | tf_op jit(solution)/shard_map/ppermute | solution.py:217
  26.4 8.7 %collective-permute-start.7 = (f32[6,32,256]{2,1,0:T(8,128)S(1)}, f32[6,32,256]{2,1,0:T(8,128)S(1)}, u32[]{:S(2)}, u32[]{:S(2)}) collective-permute-start(f32[6,32,256]{2,1,0:T(8,128)S(1)} %contract_pairs.4), channel_id=1, source_target_pairs={{0,3},{1,2},{2,1},{3,0},{4,7},{5,6},{6,5},{7,4},{8,11},{9,10},{10,... | collective-permute-start | bytes 589832 | tf_op jit(solution)/shard_map/ppermute | solution.py:254
  30.8 7.7 %collective-permute-start.8 = (f32[6,32,256]{2,1,0:T(8,128)S(1)}, f32[6,32,256]{2,1,0:T(8,128)S(1)}, u32[]{:S(2)}, u32[]{:S(2)}) collective-permute-start(f32[6,32,256]{2,1,0:T(8,128)S(1)} %get-tuple-element.55), channel_id=1, source_target_pairs={{0,1},{1,0},{2,3},{3,2},{4,5},{5,4},{6,7},{7,6},{8,9},{9,8},{10,11... | collective-permute-start | bytes 589832 | tf_op jit(solution)/shard_map/ppermute | solution.py:254
  31.4 7.3 %collective-permute-start.9 = (f32[6,32,256]{2,1,0:T(8,128)S(1)}, f32[6,32,256]{2,1,0:T(8,128)S(1)}, u32[]{:S(2)}, u32[]{:S(2)}) collective-permute-start(f32[6,32,256]{2,1,0:T(8,128)S(1)} %get-tuple-element.56), channel_id=1, source_target_pairs={{0,2},{1,3},{2,0},{3,1},{4,6},{5,7},{6,4},{7,5},{8,10},{9,11},{10,... | collective-permute-start | bytes 589832 | tf_op jit(solution)/shard_map/ppermute | solution.py:254

commit v14 on v11

--- a/solution.py
+++ b/solution.py
@@ -19,10 +19,12 @@
     return top, (value - top.astype(jnp.float32)).astype(jnp.bfloat16)
 
 
-def partner(index, shift, size):
-    if size & (size - 1) == 0:
-        return index ^ shift
-    return (index + shift) % size
+def partner(r, c, shift, col):
+    if col == 4 and shift in (1, 2):
+        return c ^ (shift if r % 2 == 0 else 3 - shift)
+    if col & (col - 1) == 0:
+        return c ^ shift
+    return (c + shift) % col
 
 
 def left_of(rows):
@@ -195,7 +197,7 @@
 
     blocks_of, flags = domains.T, domain_mask.T
     starts = ((blocks_of // per_slot) ^ plane) * (per_slot * BS) + blocks_of % per_slot * BS
-    offsets = r * half + jnp.stack([partner(c, s, col) for s in range(col)]) * chunk
+    offsets = r * half + jnp.stack([jnp.where(r % 2 == 0, partner(0, c, s, col), partner(1, c, s, col)) for s in range(col)]) * chunk
     chosen = pick(offsets // BS, starts) + (offsets % BS)[:, None]
     firsts, seconds = blocks_of[0::2], blocks_of[1::2]
     sources = jnp.stack([firsts % 2 * tiles + firsts // 2, (1 - seconds % 2) * tiles + seconds // 2], 1)
@@ -246,7 +248,8 @@
         rest = contract(range(row * nq), True, shifts, mhigh, mlow, high, low)
         terms = dict(zip(shifts, rest))
 
-    moved = [lax.ppermute(terms[s], "col", [(i, partner(i, s, col)) for i in range(col)]) for s in shifts if s]
+    moved = [lax.ppermute(terms[s], ("row", "col"), [(i * col + k, i * col + partner(i, k, s, col)) for i in range(row) for k in range(col)])
+             for s in shifts if s]
     return add_terms(add_terms(terms[0], moved[0], ahead=1 << 24), *moved[1:])
 
 

time: 39.6 us -> 39.6 us (level)
  no operation moved by 1% of the time
where the time goes in v14:
time: 39.6 us; the launch traced here: 39.3 us
  waiting for transfers between devices  15.1 us (38%)
  starting transfers between devices  10.5 us (27%)
  Pallas kernels  5.84 us (15%)
  local copies, waits for them, and re-layouts  4.92 us (12%)
  other arithmetic  2.79 us (7%)
    ppermute x3, waiting for transfers between devices, across(): return lax.ppermute(piece, 'wide', [(i, i ^ shift) for i in range(wide)])  8.39 us
    ppermute x3, waiting for transfers between devices, body(): lax.ppermute(terms[s], ('row', 'col'), [(i * col + k, i * col + partner(i...  6.49 us
    ppermute x3, starting transfers between devices, across(): return lax.ppermute(piece, 'wide', [(i, i ^ shift) for i in range(wide)])  6.33 us
    pallas_call x3, Pallas kernels, contract_pairs(): pl.pallas_call(functools.partial(pairs_kernel, row, col, factors, last, s...  4.05 us
    ppermute x3, starting transfers between devices, body(): lax.ppermute(terms[s], ('row', 'col'), [(i * col + k, i * col + partner(i...  3.62 us
    unnamed x5, local copies, waits for them, and re-layouts  3.12 us
    reduce_sum x2, other arithmetic, pick(): return jnp.sum(jnp.where(hits[:, :, None], table[None], 0), axis=1)  1.55 us
    slice x2, local copies, waits for them, and re-layouts, body(): firsts, seconds = (blocks_of[0::2], blocks_of[1::2])  1.4 us
  transfers between devices with their start and end apart: 10, of which 6 were waited for; matrix products, arithmetic and copies ran while one was open for 14% of the time, Pallas kernels for 10%

profile of v14, /device:TPU:0, one launch (start us, length us, event | category | flops | bytes accessed | tf_op | source)
XLA Modules:
  0.0 39.3 jit_solution(13298277471364244010)
XLA Ops:
  0.0 4.0 %collective-permute-start = (f32[1,128,512]{2,1,0:T(8,128)}, f32[1,128,512]{2,1,0:T(8,128)S(1)}, u32[]{:S(2)}, u32[]{:S(2)}) collective-permute-start(f32[1,128,512]{2,1,0:T(8,128)} %refs_0_.1), channel_id=1, source_target_pairs={{0,16},{8,24},{16,0},{24,8},{1,17},{9,25},{17,1},{25,9},{2,18},{10... | collective-permute-start | bytes 786440 | tf_op jit(solution)/shard_map/ppermute | solution.py:217
  4.0 1.6 %collective-permute-start.3 = (f32[1,128,512]{2,1,0:T(8,128)}, f32[1,128,512]{2,1,0:T(8,128)S(1)}, u32[]{:S(2)}, u32[]{:S(2)}) collective-permute-start(f32[1,128,512]{2,1,0:T(8,128)} %refs_0_.1), channel_id=1, source_target_pairs={{0,8},{8,0},{16,24},{24,16},{1,9},{9,1},{17,25},{25,17},{2,10},{10... | collective-permute-start | bytes 786440 | tf_op jit(solution)/shard_map/ppermute | solution.py:217
  5.6 0.0 collective-permute-start.2
  5.6 0.7 %slice.6 = s32[2,6]{1,0:T(2,128)S(1)} slice(s32[4,6]{1,0:T(4,128)} %bitcast.14), slice={[0:4:2], [0:6:1]} | slice | bytes 96 | tf_op jit(solution)/shard_map/slice | solution.py:202
  6.3 0.7 %slice.7 = s32[2,6]{1,0:T(2,128)S(1)} slice(s32[4,6]{1,0:T(4,128)} %bitcast.15), slice={[1:4:2], [0:6:1]} | slice | bytes 96 | tf_op jit(solution)/shard_map/slice | solution.py:202
  7.0 0.7 %fusion.2 = s32[4,6]{1,0:T(4,128)S(1)} fusion(s32[]{:T(128)S(6)} %axis_index.33, s32[6,4]{0,1:T(4,128)} %param.7), kind=kLoop, calls=%fused_computation.14 | loop fusion | flops 552 | bytes 196 | tf_op jit(solution)/shard_map/add | solution.py:199
  7.7 0.1 and_select_fusion.4
  7.8 0.1 iota_compare_fusion.1
  7.9 0.8 %copy.18 = s32[6,4]{1,0:T(8,128)S(1)} copy(s32[6,4]{0,1:T(4,128)} %param.8) | data formatting | bytes 192 | tf_op args[3]
  8.7 0.1 broadcast_in_dim.77
  8.8 0.1 mul.76
  8.8 0.1 multiply_convert_fusion.1.weights
  8.9 0.8 %select_reduce_fusion.1 = (s32[4,6]{1,0:T(4,128)S(1)}, s32[4,6]{1,0:T(4,128)S(1)}) fusion(s32[4,6]{1,0:T(4,128)} %bitcast.12, pred[4,4]{1,0:T(4,128)(4,1)S(1)} %iota_compare_fusion.1, s32[4,6]{1,0:T(4,128)S(1)} %fusion.2), kind=kLoop, calls=%fused_computation.4 | loop fusion | flops 336 | bytes 400 | tf_op jit(solution)/shard_map/reduce_sum | solution.py:194
  9.7 0.1 multiply_convert_fusion.weights
  9.8 0.1 iota_compare_fusion
  9.9 0.1 broadcast_add_fusion
  10.0 0.8 %select_reduce_fusion = s32[8,8]{1,0:T(8,128)S(1)} fusion(s32[8,8]{1,0:T(8,128)} %param.9, pred[8,8]{1,0:T(8,128)(4,1)S(1)} %iota_compare_fusion), kind=kLoop, calls=%fused_computation | loop fusion | flops 960 | bytes 576 | tf_op jit(solution)/shard_map/reduce_sum | solution.py:194
  10.8 0.1 reshape.185.places
  10.9 0.1 broadcast_in_dim.76
  11.0 0.1 convert_element_type.35.mask
  11.1 0.0 copy-start.1
  11.1 0.9 %copy-done.1 = f32[1,128,512]{2,1,0:T(8,128)S(1)} copy-done((f32[1,128,512]{2,1,0:T(8,128)S(1)}, f32[1,128,512]{2,1,0:T(8,128)}, u32[]{:S(2)}) %copy-start.1) | copy-done | bytes 262168
  12.0 0.1 screen_factors.4
  12.2 0.0 copy-start
  12.2 1.4 %copy-done = f32[6,256,256]{2,1,0:T(8,128)S(1)} copy-done((f32[6,256,256]{2,1,0:T(8,128)S(1)}, f32[6,256,256]{2,1,0:T(8,128)}, u32[]{:S(2)}) %copy-start) | copy-done | bytes 1572888
  13.6 0.2 mask_amplitudes.1
  13.8 2.5 %collective-permute-done.refs_2_ = f32[1,128,512]{2,1,0:T(8,128)S(1)} collective-permute-done((f32[1,128,512]{2,1,0:T(8,128)}, f32[1,128,512]{2,1,0:T(8,128)S(1)}, u32[]{:S(2)}, u32[]{:S(2)}) %collective-permute-start) | collective-permute-done | bytes 262176 | tf_op jit(solution)/shard_map/ppermute | solution.py:217
  16.3 0.7 %collective-permute-start.1 = (f32[1,128,512]{2,1,0:T(8,128)S(1)}, f32[1,128,512]{2,1,0:T(8,128)S(1)}, u32[]{:S(2)}, u32[]{:S(2)}) collective-permute-start(f32[1,128,512]{2,1,0:T(8,128)S(1)} %collective-permute-done.refs_2_), channel_id=1, source_target_pairs={{0,8},{8,0},{16,24},{24,16},{1,9},{9,1},{17,25},{25,17},{2,10},{10... | collective-permute-start | bytes 786440 | tf_op jit(solution)/shard_map/ppermute | solution.py:217
  17.0 0.0 collective-permute-start.6
  17.0 0.0 collective-permute-done.3.refs_1_
  17.0 0.5 %collective-permute-start.5 = (f32[1,128,512]{2,1,0:T(8,128)S(1)}, f32[1,128,512]{2,1,0:T(8,128)S(1)}, u32[]{:S(2)}, u32[]{:S(2)}) collective-permute-start(f32[1,128,512]{2,1,0:T(8,128)S(1)} %collective-permute-done.3.refs_1_), channel_id=1, source_target_pairs={{0,4},{4,0},{1,5},{5,1},{2,6},{6,2},{3,7},{7,3},{8,12},{12,8},{9,1... | collective-permute-start | bytes 786440 | tf_op jit(solution)/shard_map/ppermute | solution.py:214
  17.5 0.0 collective-permute-done.2.refs_0_
  17.5 0.3 screen_factors.5
  17.8 5.9 %collective-permute-done.1.refs_0_ = f32[1,128,512]{2,1,0:T(8,128)S(1)} collective-permute-done((f32[1,128,512]{2,1,0:T(8,128)S(1)}, f32[1,128,512]{2,1,0:T(8,128)S(1)}, u32[]{:S(2)}, u32[]{:S(2)}) %collective-permute-start.1) | collective-permute-done | bytes 262176 | tf_op jit(solution)/shard_map/ppermute | solution.py:217
  23.7 0.0 collective-permute-start.4
  23.7 0.0 collective-permute-done.6.refs_2_
  23.7 0.0 collective-permute-done.5.refs_1_
  23.7 0.3 screen_factors.6
  24.0 1.0 %contract_pairs.3.refs_0_ = f32[6,32,256]{2,1,0:T(8,128)S(1)} custom-call(s32[1,72]{1,0:T(1,128)S(1)} %reshape.185.places, f32[4,6,1,256]{3,2,1,0:T(1,128)S(1)} %multiply_convert_fusion.weights, bf16[6,256,256]{2,1,0:T(8,128)(2,1)S(1)} %get-tuple-element.37.mhigh, bf16[6,256,256]{2,1,0:T(8,128)(2,1)S(1)} %get-tuple-element.38.mlow, ...), custom_call_target="tpu_custom_call" | custom-call | flops 301989888 | bytes 8388608 | tf_op jit(solution)/shard_map/contract_pairs/pallas_call | solution.py:148
  25.0 0.3 collective-permute-done.4.refs_0_
  25.2 0.1 screen_factors.7
  25.4 1.0 %contract_pairs.4 = f32[6,32,256]{2,1,0:T(8,128)S(1)} custom-call(s32[1,72]{1,0:T(1,128)S(1)} %reshape.185.places, f32[4,6,1,256]{3,2,1,0:T(1,128)S(1)} %multiply_convert_fusion.weights, bf16[6,256,256]{2,1,0:T(8,128)(2,1)S(1)} %get-tuple-element.37.mhigh, bf16[6,256,256]{2,1,0:T(8,128)(2,1)S(1)} %get-tuple-element.38.mlow, ...), custom_call_target="tpu_custom_call" | custom-call | flops 301989888 | bytes 8388608 | tf_op jit(solution)/shard_map/contract_pairs/pallas_call | solution.py:148
  26.4 2.3 %collective-permute-start.7 = (f32[6,32,256]{2,1,0:T(8,128)S(1)}, f32[6,32,256]{2,1,0:T(8,128)S(1)}, u32[]{:S(2)}, u32[]{:S(2)}) collective-permute-start(f32[6,32,256]{2,1,0:T(8,128)S(1)} %contract_pairs.4), channel_id=1, source_target_pairs={{0,3},{1,2},{2,1},{3,0},{4,7},{5,6},{6,5},{7,4},{8,11},{9,10},{10,... | collective-permute-start | bytes 589832 | tf_op jit(solution)/shard_map/ppermute | solution.py:251
  28.7 2.1 %contract_pairs.5 = (f32[6,32,256]{2,1,0:T(8,128)S(1)}, f32[6,32,256]{2,1,0:T(8,128)S(1)}, f32[6,32,256]{2,1,0:T(8,128)S(1)}) custom-call(s32[1,72]{1,0:T(1,128)S(1)} %reshape.185.places, f32[4,6,1,256]{3,2,1,0:T(1,128)S(1)} %multiply_convert_fusion.weights, bf16[6,256,256]{2,1,0:T(8,128)(2,1)S(1)} %get-tuple-element.37.mhigh, ...), custom_call_target="tpu_custom_call" | custom-call | flops 1811939328 | bytes 8388608 | tf_op jit(solution)/shard_map/contract_pairs/pallas_call | solution.py:148
  30.8 0.6 %collective-permute-start.8 = (f32[6,32,256]{2,1,0:T(8,128)S(1)}, f32[6,32,256]{2,1,0:T(8,128)S(1)}, u32[]{:S(2)}, u32[]{:S(2)}) collective-permute-start(f32[6,32,256]{2,1,0:T(8,128)S(1)} %get-tuple-element.55), channel_id=1, source_target_pairs={{0,1},{1,0},{2,3},{3,2},{4,6},{5,7},{6,4},{7,5},{8,9},{9,8},{10,11... | collective-permute-start | bytes 589832 | tf_op jit(solution)/shard_map/ppermute | solution.py:251
  31.4 0.7 %collective-permute-start.9 = (f32[6,32,256]{2,1,0:T(8,128)S(1)}, f32[6,32,256]{2,1,0:T(8,128)S(1)}, u32[]{:S(2)}, u32[]{:S(2)}) collective-permute-start(f32[6,32,256]{2,1,0:T(8,128)S(1)} %get-tuple-element.56), channel_id=1, source_target_pairs={{0,2},{1,3},{2,0},{3,1},{4,5},{5,4},{6,7},{7,6},{8,10},{9,11},{10,... | collective-permute-start | bytes 589832 | tf_op jit(solution)/shard_map/ppermute | solution.py:251
  32.1 2.4 %collective-permute-done.7.refs_1_ = f32[6,32,256]{2,1,0:T(8,128)S(1)} collective-permute-done((f32[6,32,256]{2,1,0:T(8,128)S(1)}, f32[6,32,256]{2,1,0:T(8,128)S(1)}, u32[]{:S(2)}, u32[]{:S(2)}) %collective-permute-start.7) | collective-permute-done | bytes 196640 | tf_op jit(solution)/shard_map/ppermute | solution.py:251
  34.5 3.9 %collective-permute-done.8.refs_1_ = f32[6,32,256]{2,1,0:T(8,128)S(1)} collective-permute-done((f32[6,32,256]{2,1,0:T(8,128)S(1)}, f32[6,32,256]{2,1,0:T(8,128)S(1)}, u32[]{:S(2)}, u32[]{:S(2)}) %collective-permute-start.8) | collective-permute-done | bytes 196640 | tf_op jit(solution)/shard_map/ppermute | solution.py:251
  38.4 0.2 collective-permute-done.9.refs_2_
  38.6 0.7 %add_terms.3 = f32[6,32,256]{2,1,0:T(8,128)} custom-call(f32[6,32,256]{2,1,0:T(8,128)S(1)} %add_terms.2.refs_0_, f32[6,32,256]{2,1,0:T(8,128)S(1)} %collective-permute-done.8.refs_1_, f32[6,32,256]{2,1,0:T(8,128)S(1)} %collective-permute-done.9.refs_2_), custom_call_target="tpu_custom_call" | custom-call | bytes 589824 | tf_op jit(solution)/shard_map/add_terms/pallas_call | solution.py:168
  (8 shorter events, 0.1 us)
Async XLA Ops:
  0.0 16.3 %collective-permute-start = (f32[1,128,512]{2,1,0:T(8,128)}, f32[1,128,512]{2,1,0:T(8,128)S(1)}, u32[]{:S(2)}, u32[]{:S(2)}) collective-permute-start(f32[1,128,512]{2,1,0:T(8,128)} %refs_0_.1), channel_id=1, source_target_pairs={{0,16},{8,24},{16,0},{24,8},{1,17},{9,25},{17,1},{25,9},{2,18},{10... | collective-permute-start | bytes 786440 | tf_op jit(solution)/shard_map/ppermute | solution.py:217
  4.0 13.0 %collective-permute-start.3 = (f32[1,128,512]{2,1,0:T(8,128)}, f32[1,128,512]{2,1,0:T(8,128)S(1)}, u32[]{:S(2)}, u32[]{:S(2)}) collective-permute-start(f32[1,128,512]{2,1,0:T(8,128)} %refs_0_.1), channel_id=1, source_target_pairs={{0,8},{8,0},{16,24},{24,16},{1,9},{9,1},{17,25},{25,17},{2,10},{10... | collective-permute-start | bytes 786440 | tf_op jit(solution)/shard_map/ppermute | solution.py:217
  5.6 11.9 %collective-permute-start.2 = (f32[1,128,512]{2,1,0:T(8,128)}, f32[1,128,512]{2,1,0:T(8,128)S(1)}, u32[]{:S(2)}, u32[]{:S(2)}) collective-permute-start(f32[1,128,512]{2,1,0:T(8,128)} %refs_0_.1), channel_id=1, source_target_pairs={{0,4},{4,0},{1,5},{5,1},{2,6},{6,2},{3,7},{7,3},{8,12},{12,8},{9,1... | collective-permute-start | bytes 786440 | tf_op jit(solution)/shard_map/ppermute | solution.py:214
  11.1 1.0 %copy-start.1 = (f32[1,128,512]{2,1,0:T(8,128)S(1)}, f32[1,128,512]{2,1,0:T(8,128)}, u32[]{:S(2)}) copy-start(f32[1,128,512]{2,1,0:T(8,128)} %refs_0_.1) | copy-start | bytes 786436
  12.2 1.4 %copy-start = (f32[6,256,256]{2,1,0:T(8,128)S(1)}, f32[6,256,256]{2,1,0:T(8,128)}, u32[]{:S(2)}) copy-start(f32[6,256,256]{2,1,0:T(8,128)} %amplitudes.1) | copy-start | bytes 4718596
  16.3 7.4 %collective-permute-start.1 = (f32[1,128,512]{2,1,0:T(8,128)S(1)}, f32[1,128,512]{2,1,0:T(8,128)S(1)}, u32[]{:S(2)}, u32[]{:S(2)}) collective-permute-start(f32[1,128,512]{2,1,0:T(8,128)S(1)} %collective-permute-done.refs_2_), channel_id=1, source_target_pairs={{0,8},{8,0},{16,24},{24,16},{1,9},{9,1},{17,25},{25,17},{2,10},{10... | collective-permute-start | bytes 786440 | tf_op jit(solution)/shard_map/ppermute | solution.py:217
  17.0 6.7 %collective-permute-start.6 = (f32[1,128,512]{2,1,0:T(8,128)S(1)}, f32[1,128,512]{2,1,0:T(8,128)S(1)}, u32[]{:S(2)}, u32[]{:S(2)}) collective-permute-start(f32[1,128,512]{2,1,0:T(8,128)S(1)} %collective-permute-done.refs_2_), channel_id=1, source_target_pairs={{0,4},{4,0},{1,5},{5,1},{2,6},{6,2},{3,7},{7,3},{8,12},{12,8},{9,1... | collective-permute-start | bytes 786440 | tf_op jit(solution)/shard_map/ppermute | solution.py:214
  17.0 6.7 %collective-permute-start.5 = (f32[1,128,512]{2,1,0:T(8,128)S(1)}, f32[1,128,512]{2,1,0:T(8,128)S(1)}, u32[]{:S(2)}, u32[]{:S(2)}) collective-permute-start(f32[1,128,512]{2,1,0:T(8,128)S(1)} %collective-permute-done.3.refs_1_), channel_id=1, source_target_pairs={{0,4},{4,0},{1,5},{5,1},{2,6},{6,2},{3,7},{7,3},{8,12},{12,8},{9,1... | collective-permute-start | bytes 786440 | tf_op jit(solution)/shard_map/ppermute | solution.py:214
  23.7 1.5 %collective-permute-start.4 = (f32[1,128,512]{2,1,0:T(8,128)S(1)}, f32[1,128,512]{2,1,0:T(8,128)S(1)}, u32[]{:S(2)}, u32[]{:S(2)}) collective-permute-start(f32[1,128,512]{2,1,0:T(8,128)S(1)} %collective-permute-done.1.refs_0_), channel_id=1, source_target_pairs={{0,4},{4,0},{1,5},{5,1},{2,6},{6,2},{3,7},{7,3},{8,12},{12,8},{9,1... | collective-permute-start | bytes 786440 | tf_op jit(solution)/shard_map/ppermute | solution.py:214
  26.4 8.1 %collective-permute-start.7 = (f32[6,32,256]{2,1,0:T(8,128)S(1)}, f32[6,32,256]{2,1,0:T(8,128)S(1)}, u32[]{:S(2)}, u32[]{:S(2)}) collective-permute-start(f32[6,32,256]{2,1,0:T(8,128)S(1)} %contract_pairs.4), channel_id=1, source_target_pairs={{0,3},{1,2},{2,1},{3,0},{4,7},{5,6},{6,5},{7,4},{8,11},{9,10},{10,... | collective-permute-start | bytes 589832 | tf_op jit(solution)/shard_map/ppermute | solution.py:251
  30.8 7.7 %collective-permute-start.8 = (f32[6,32,256]{2,1,0:T(8,128)S(1)}, f32[6,32,256]{2,1,0:T(8,128)S(1)}, u32[]{:S(2)}, u32[]{:S(2)}) collective-permute-start(f32[6,32,256]{2,1,0:T(8,128)S(1)} %get-tuple-element.55), channel_id=1, source_target_pairs={{0,1},{1,0},{2,3},{3,2},{4,6},{5,7},{6,4},{7,5},{8,9},{9,8},{10,11... | collective-permute-start | bytes 589832 | tf_op jit(solution)/shard_map/ppermute | solution.py:251
  31.4 7.2 %collective-permute-start.9 = (f32[6,32,256]{2,1,0:T(8,128)S(1)}, f32[6,32,256]{2,1,0:T(8,128)S(1)}, u32[]{:S(2)}, u32[]{:S(2)}) collective-permute-start(f32[6,32,256]{2,1,0:T(8,128)S(1)} %get-tuple-element.56), channel_id=1, source_target_pairs={{0,2},{1,3},{2,0},{3,1},{4,5},{5,4},{6,7},{7,6},{8,10},{9,11},{10,... | collective-permute-start | bytes 589832 | tf_op jit(solution)/shard_map/ppermute | solution.py:251
